TPU v7x, 32 devices: a whole 2x2x4 slice. The times are simulated.
32 devices in a mesh: groups: 2 (over x), src: 2 (over core), chan: 8 (over z, y).
Axes of the slice: x: 2, y: 2, z: 4, core: 2. Of those that a mesh axis runs over, the one named last changes fastest.
Arguments:
- residual_input: bfloat16 [32, 8192], P('groups', ('src', 'chan')), parts along dimension 0, may hold values from -6 to 6
- query_heads: bfloat16 [32, 8192], P(('groups', 'src', 'chan')), parts along dimension 0, may hold values from -9 to 9
- new_keyval: bfloat16 [32, 2048], P(('groups', 'src', 'chan')), parts along dimension 0, may hold values from -6 to 6
- cache_pages: bfloat16 [256, 16, 2048], P(('groups', 'src', 'chan')), parts along dimension 0, may hold values from -6 to 6
- prompt_lengths: int32 [32], P('groups'), parts along dimension 0, may hold values from 1 to 256, as said below
- page_owner: int32 [256], P(('groups', 'src', 'chan')), parts along dimension 0, may hold values from 0 to 15, as said below
- page_index: int32 [256], P(('groups', 'src', 'chan')), parts along dimension 0, may hold values from 0 to 15, as said below
- mamba_state: float32 [32, 16, 8192], P(('groups', 'src', 'chan')), parts along dimension 0, may hold values from -6 to 6
- conv_state: float32 [32, 3, 8192], P(('groups', 'src', 'chan')), parts along dimension 0, may hold values from -6 to 6
- out_heads: bfloat16 [8192, 8192], P(None, ('src', 'chan')), may hold values from -0.125 to 0.125
- in_values: bfloat16 [8192, 8192], P(None, ('src', 'chan')), may hold values from -0.0625 to 0.0625
- in_gates: bfloat16 [8192, 8192], P(None, ('src', 'chan')), may hold values from -0.0625 to 0.0625
- conv_taps: float32 [4, 8192], P(None, ('src', 'chan')), may hold values from -3 to 3
- conv_offset: float32 [8192], P(('src', 'chan')), may hold values from -0.6 to 0.6
- state_proj: bfloat16 [8192, 544], P(('src', 'chan')), may hold values from -0.0625 to 0.0625
- step_proj: bfloat16 [512, 8192], P(None, ('src', 'chan')), may hold values from -0.25 to 0.25
- step_bias: float32 [8192], P(('src', 'chan')), may hold values from -4 to -1
- decay_log: float32 [16, 8192], P(None, ('src', 'chan')), may hold values from 0 to 2.77
- skip_gain: float32 [8192], P(('src', 'chan')), may hold values from 0.5 to 1.5
- mamba_down: bfloat16 [8192, 8192], P(('src', 'chan')), may hold values from -0.09375 to 0.09375
Outputs:
- hidden_out: bfloat16 [32, 8192], P('groups', ('src', 'chan')), parts along dimension 0
- mamba_next: float32 [32, 16, 8192], P('groups', None, ('src', 'chan')), parts along dimension 0
- conv_next: float32 [32, 3, 8192], P('groups', None, ('src', 'chan')), parts along dimension 0
There are 2 independent parts, one for each index of `groups`. A program takes and returns all parts, laid end to end along the dimension named above; an argument that names none is the same for every part. Nothing has to cross between parts.
Inputs may be any that keep to these rules, and one draw needn't show every extreme that they name: Request r has ceil(prompt_lengths[r] / 16) cache pages, at most 16; some request has 16 full pages. `page_owner`: every cache page belongs to a request; the 8 pages held by one prefill shard belong to different requests. `page_index`: the pages of request r carry the places 0 to ceil(prompt_lengths[r] / 16) - 1, each once.
All inputs are finite; a program needn't handle non-finite values.
Results may differ from a plain program's by a relative error of at most 0.0065.
Values may be sent and summed in bfloat16 or wider, within the bound.
No kernel may reach another device: no remote copies, remote signals or barrier semaphores. Data moves between devices by JAX's collectives and lax.ppermute only.
A program may use at most 128 MiB of HBM per device.

v0:
```python
import math

import jax
import jax.numpy as jnp
from jax import lax
from jax.sharding import PartitionSpec as P

D = 8192
NS = 16
DTR = 512
QH = 64
KVH = 8
HD = 128


NEGATIVE = -1e30


def page_terms(scores, usable, values):
    masked = jnp.where(usable[:, None, None, :], scores, NEGATIVE)
    page_peak = jnp.max(masked, axis=-1)
    weights = jnp.where(usable[:, None, None, :], jnp.exp(masked - page_peak[..., None]), 0.0)
    page_total = jnp.sum(weights, axis=-1)
    page_sum = jnp.einsum(
        "skgt,stkd->skgd", weights.astype(jnp.bfloat16), values, preferred_element_type=jnp.float32
    )
    return (page_peak, page_total, page_sum)


def combine(page_peak, page_total, page_sum, queries, new_token, score_scale):
    own_score = (
        jnp.einsum("kgd,kd->kg", queries, new_token[0], preferred_element_type=jnp.float32)
        * score_scale
    )
    row_peak = jnp.maximum(own_score, jnp.max(page_peak, axis=0))
    factor = jnp.exp(page_peak - row_peak[None])
    own_factor = jnp.exp(own_score - row_peak)
    numer = (
        jnp.sum(factor[..., None] * page_sum, axis=0)
        + own_factor[..., None] * new_token[1].astype(jnp.float32)[:, None, :]
    )
    denom = jnp.sum(factor * page_total, axis=0) + own_factor
    return (numer / denom[..., None]).reshape(1, -1).astype(jnp.bfloat16)


def on_device(
    residual_input,
    query_heads,
    new_keyval,
    cache_pages,
    prompt_lengths,
    page_owner,
    page_index,
    mamba_state,
    conv_state,
    out_heads,
    in_values,
    in_gates,
    conv_taps,
    conv_offset,
    state_proj,
    step_proj,
    step_bias,
    decay_log,
    skip_gain,
    mamba_down,
):
    devices_here = lax.axis_size(("src", "chan"))
    group_size = QH // KVH
    score_scale = 1.0 / math.sqrt(HD)
    held_pages = cache_pages.shape[0]
    tokens = cache_pages.shape[1]
    state_here, conv_here = (
        lax.all_to_all(mamba_state, ("src", "chan"), split_axis=2, concat_axis=0, tiled=True),
        lax.all_to_all(conv_state, ("src", "chan"), split_axis=2, concat_axis=0, tiled=True),
    )
    offsets = jnp.arange(tokens, dtype=jnp.int32)
    owners = jnp.arange(devices_here, dtype=jnp.int32)
    queries = query_heads.reshape(KVH, group_size, HD)
    new_token = new_keyval.reshape(2, KVH, HD)
    onehot = page_owner[None, :] == owners[:, None]
    outgoing = jnp.dot(
        onehot.astype(jnp.bfloat16),
        cache_pages.reshape(held_pages, -1),
        preferred_element_type=jnp.float32,
    ).astype(jnp.bfloat16)
    slot_index = jnp.sum(jnp.where(onehot, page_index[None, :] + 1, 0), axis=1, keepdims=True) - 1
    arrived, arrived_index = (
        lax.all_to_all(outgoing, ("src", "chan"), split_axis=0, concat_axis=0, tiled=True),
        lax.all_to_all(slot_index, ("src", "chan"), split_axis=0, concat_axis=0, tiled=True),
    )
    own_index = lax.axis_index(("src", "chan"))
    own_length = jnp.sum(jnp.where(owners == own_index, prompt_lengths, 0))
    blocks = arrived.reshape(devices_here, tokens, 2, KVH, HD)
    usable = (arrived_index >= 0) & (arrived_index * tokens + offsets[None, :] < own_length)
    scores = (
        jnp.einsum("kgd,stkd->skgt", queries, blocks[:, :, 0], preferred_element_type=jnp.float32)
        * score_scale
    )
    page_peak, page_total, page_sum = page_terms(scores, usable, blocks[:, :, 1])
    attended = combine(page_peak, page_total, page_sum, queries, new_token, score_scale)
    attention_out = jnp.dot(
        lax.all_gather(attended, ("src", "chan"), axis=0, tiled=True),
        out_heads,
        preferred_element_type=jnp.float32,
    )
    hidden_mid = (residual_input.astype(jnp.float32) + attention_out).astype(jnp.bfloat16)
    fragment = lax.all_gather(hidden_mid, ("src", "chan"), axis=1, tiled=True)
    widened = fragment.astype(jnp.float32)
    sum_values = jnp.dot(fragment, in_values, preferred_element_type=jnp.float32)
    sum_gates = jnp.dot(fragment, in_gates, preferred_element_type=jnp.float32)
    squares = jnp.sum(widened * widened, axis=1)
    inverse_rms = lax.rsqrt(squares / D + 1e-06)
    value_proj = sum_values * inverse_rms[:, None]
    gate_proj = sum_gates * inverse_rms[:, None]
    window = jnp.concatenate([conv_here, value_proj[:, None, :]], axis=1)
    conv_next = window[:, 1:, :]
    x_act = jax.nn.silu(jnp.sum(window * conv_taps[None], axis=1) + conv_offset[None, :])
    x_low = x_act.astype(jnp.bfloat16)
    projected = lax.psum(
        jnp.dot(x_low, state_proj, preferred_element_type=jnp.float32), ("src", "chan")
    )
    step_low = projected[:, :DTR].astype(jnp.bfloat16)
    b_part = projected[:, DTR : DTR + NS]
    c_part = projected[:, DTR + NS :]
    step = jax.nn.softplus(
        jnp.dot(step_low, step_proj, preferred_element_type=jnp.float32) + step_bias[None, :]
    )
    decay_factor = jnp.exp(-step[:, None, :] * jnp.exp(decay_log)[None])
    mamba_next = decay_factor * state_here + (step * x_act)[:, None, :] * b_part[:, :, None]
    gated = (
        (jnp.sum(mamba_next * c_part[:, :, None], axis=1) + skip_gain[None, :] * x_act)
        * jax.nn.silu(gate_proj)
    ).astype(jnp.bfloat16)
    down_sum = lax.psum_scatter(
        lax.dot_general(
            mamba_down, gated, (((0,), (1,)), ((), ())), preferred_element_type=jnp.float32
        ),
        ("src", "chan"),
        scatter_dimension=0,
        tiled=True,
    )
    hidden_out = (hidden_mid.astype(jnp.float32) + down_sum.T).astype(jnp.bfloat16)
    return (hidden_out, mamba_next, conv_next)


def solution(mesh):
    placed = (
        P("groups", ("src", "chan")),
        P(("groups", "src", "chan"), None),
        P(("groups", "src", "chan"), None),
        P(("groups", "src", "chan"), None, None),
        P("groups"),
        P(("groups", "src", "chan")),
        P(("groups", "src", "chan")),
        P(("groups", "src", "chan"), None, None),
        P(("groups", "src", "chan"), None, None),
        P(None, ("src", "chan")),
        P(None, ("src", "chan")),
        P(None, ("src", "chan")),
        P(None, ("src", "chan")),
        P(("src", "chan")),
        P(("src", "chan"), None),
        P(None, ("src", "chan")),
        P(("src", "chan")),
        P(None, ("src", "chan")),
        P(("src", "chan")),
        P(("src", "chan"), None),
    )
    return jax.shard_map(
        on_device,
        mesh=mesh,
        in_specs=placed,
        out_specs=(
            P("groups", ("src", "chan")),
            P("groups", None, ("src", "chan")),
            P("groups", None, ("src", "chan")),
        ),
        check_vma=False,
    )
```

profile of v0, /device:TPU:0, one launch (start us, length us, event | category | flops | bytes accessed | tf_op | source)
XLA Modules:
  0.0 401.2 jit_solution(14309717734615232371)
XLA Ops:
  7.2 0.0 copy-start
  7.2 0.7 broadcast_add_fusion
  7.9 0.7 select_reduce_fusion
  8.6 0.7 copy.72
  9.3 7.4 %all-to-all-start = ((s32[16,1,1]{2,1,0:T(1,128)}), s32[16,1,1]{2,1,0:T(1,128)S(1)}, u32[]{:S(2)}, u32[]{:S(2)}) async-start(s32[16,1,1]{2,1,0:T(1,128)} %copy.72), calls=%async_computation | async-start | bytes 16384 | tf_op jit(solution)/shard_map/all_to_all | solution.py:90
  16.7 0.0 copy-start.1
  16.7 8.1 %copy.78 = f32[1,3,8192]{1,0,2:T(1,128)} copy(f32[1,3,8192]{2,0,1:T(1,128)} %param.28) | data formatting | bytes 196608 | tf_op args[8]
  24.8 0.5 broadcast.128
  25.3 38.3 %reduce.9 = f32[8192,3]{1,0:T(8,128)} reduce(f32[8192,1,3]{2,1,0:T(1,128)} %bitcast.72, f32[]{:T(128)} %broadcast.128), dimensions={1}, to_apply=%bitcast.55.reduce_sub_computation | reduce | bytes 196612
  63.6 5.2 %reshape.189 = f32[16,1,1536]{2,1,0:T(1,128)} reshape(f32[8192,3]{1,0:T(8,128)} %reduce.9) | data formatting | bytes 196608
  68.9 6.3 %all-to-all-start.2 = ((f32[16,1,1536]{2,1,0:T(1,128)}), f32[16,1,1536]{2,1,0:T(1,128)S(1)}, u32[]{:S(2)}, u32[]{:S(2)}) async-start(f32[16,1,1536]{2,1,0:T(1,128)} %reshape.189), calls=%async_computation.2 | async-start | bytes 196608 | tf_op jit(solution)/shard_map/all_to_all | solution.py:75
  75.2 0.0 copy-start.3
  75.2 6.4 %copy.80 = f32[1,16,8192]{1,0,2:T(1,128)} copy(f32[1,16,8192]{2,1,0:T(8,128)S(1)} %copy-done.1) | data formatting | bytes 1048576 | tf_op args[7]
  81.6 38.3 %reduce.11 = f32[8192,16]{1,0:T(8,128)} reduce(f32[8192,1,16]{2,1,0:T(1,128)} %bitcast.74, f32[]{:T(128)} %broadcast.128), dimensions={1}, to_apply=%bitcast.53.reduce_sub_computation | reduce | bytes 1048580
  120.0 4.2 %reshape.187 = f32[16,1,8192]{2,1,0:T(1,128)} reshape(f32[8192,16]{1,0:T(8,128)} %reduce.11) | data formatting | bytes 1048576
  124.2 6.1 %all-to-all-start.3 = ((f32[16,1,8192]{2,1,0:T(1,128)}), f32[16,1,8192]{2,1,0:T(1,128)S(1)}, u32[]{:S(2)}, u32[]{:S(2)}) async-start(f32[16,1,8192]{2,1,0:T(1,128)} %reshape.187), calls=%async_computation.3 | async-start | bytes 1048576 | tf_op jit(solution)/shard_map/all_to_all | solution.py:74
  130.4 0.3 copy.93
  130.7 0.5 fusion
  131.2 0.5 broadcast.127
  131.7 1.4 reduce.8
  133.2 1.6 reshape.185
  134.8 11.4 %all-to-all-done.3 = f32[16,1,8192]{2,1,0:T(1,128)S(1)} async-done(((f32[16,1,8192]{2,1,0:T(1,128)}), f32[16,1,8192]{2,1,0:T(1,128)S(1)}, u32[]{:S(2)}, u32[]{:S(2)}) %all-to-all-start.3) | async-done | bytes 524320 | tf_op jit(solution)/shard_map/all_to_all | solution.py:74
  146.2 4.4 %all-to-all-start.1 = ((bf16[16,2,16384]{2,1,0:T(2,128)(2,1)}), bf16[16,2,16384]{2,1,0:T(2,128)(2,1)}, u32[]{:S(2)}, u32[]{:S(2)}) async-start(bf16[16,2,16384]{2,1,0:T(2,128)(2,1)} %reshape.185), calls=%async_computation.1 | async-start | bytes 2097152 | tf_op jit(solution)/shard_map/all_to_all | solution.py:89
  150.5 0.6 reduce-scatter.2.cloned.1.call-start
  151.1 0.1 reduce.4
  151.2 0.6 fusion.30
  151.9 0.1 fusion.18
  152.0 0.4 compare_reduce_fusion
  152.4 0.4 multiply_reduce_fusion.3
  152.8 0.7 fusion.26
  153.5 0.8 reduce.10
  154.3 7.4 %reshape.190 = f32[8192,1,3]{2,1,0:T(1,128)} reshape(f32[16,1536]{1,0:T(8,128)S(1)} %reduce.10) | data formatting | bytes 196608
  161.7 2.8 copy.88
  164.6 1.8 reduce.12
  166.4 9.2 %reshape.188 = f32[8192,1,16]{2,1,0:T(1,128)} reshape(f32[16,8192]{1,0:T(8,128)S(1)} %reduce.12) | data formatting | bytes 1048576
  175.6 2.9 copy.89
  178.5 4.5 %reshape.186 = bf16[16,1,32768]{2,1,0:T(2,128)(2,1)S(1)} reshape(bf16[16,2,16384]{2,1,0:T(2,128)(2,1)} %all-to-all-done.1) | data formatting | bytes 2097152
  183.0 7.4 %reduce.3 = bf16[16,32768]{1,0:T(8,128)(2,1)} reduce(bf16[16,1,32768]{2,1,0:T(2,128)(2,1)S(1)} %reshape.186, bf16[]{:T(256)} %constant.50), dimensions={1}, to_apply=%all_to_all.38.reduce_sub_computation | reduce | bytes 2097154 | tf_op jit(solution)/shard_map/all_to_all | solution.py:89
  190.4 1.4 copy.94
  191.8 0.3 fusion.35
  192.1 1.4 fusion.38
  193.5 0.4 fusion.7
  194.0 0.3 fusion.3
  194.3 0.1 divide_convert_fusion
  194.4 35.6 %all-gather = bf16[16,1,8192]{2,1,0:T(2,128)(2,1)S(1)} all-gather(bf16[1,1,8192]{2,1,0:T(2,128)(2,1)S(1)} %reshape.172), channel_id=1, replica_groups=mesh['groups'=2,'src'=2,'chan'=8] {'src','chan'}, dimensions={0}, use_global_device_ids=true | all-gather | bytes 278528 | tf_op jit(solution)/shard_map/all_gather | solution.py:103
  230.0 4.6 %fusion.5 = bf16[16,512]{1,0:T(8,128)(2,1)S(1)} fusion(bf16[8192,512]{1,0:T(8,128)(2,1)} %param.29, bf16[16,1,8192]{2,1,0:T(2,128)(2,1)S(1)} %all-gather, bf16[16,512]{1,0:T(8,128)(2,1)S(1)} %copy-done.7), kind=kOutput, calls=%fused_computation.13 | convolution fusion | flops 134242304 | bytes 8683520 | tf_op jit(solution)/shard_map/dot_general | solution.py:102
  234.6 29.9 %all_gather.7 = bf16[16,8192]{1,0:T(8,128)(2,1)S(1)} all-gather(bf16[16,512]{1,0:T(8,128)(2,1)S(1)} %fusion.5), channel_id=1, replica_groups=mesh['groups'=2,'src'=2,'chan'=8] {'src','chan'}, dimensions={1}, use_global_device_ids=true | all-gather | bytes 278528 | tf_op jit(solution)/shard_map/all_gather | solution.py:108
  264.5 0.2 multiply_reduce_fusion.1
  264.7 0.0 copy-start.10
  264.7 4.6 %fusion.4 = f32[16,1,512]{2,0,1:T(8,128)S(1)} fusion(bf16[16,8192]{1,0:T(8,128)(2,1)S(1)} %all_gather.7, bf16[8192,512]{1,0:T(8,128)(2,1)} %param.30, f32[16]{0:T(128)S(1)} %add_rsqrt_fusion), kind=kOutput, calls=%fused_computation.10 | convolution fusion | flops 134225920 | bytes 8683584 | tf_op jit(solution)/shard_map/dot_general | solution.py:110
  269.3 0.1 fusion.13
  269.4 0.2 fusion.22
  269.6 60.4 %psum.7 = f32[16,544]{1,0:T(8,128)S(1)} all-reduce(f32[16,544]{1,0:T(8,128)S(1)} %fusion.22), channel_id=1, replica_groups=mesh['groups'=2,'src'=2,'chan'=8] {'src','chan'}, use_global_device_ids=true, to_apply=%region_9.10 | all-reduce | flops 8704 | bytes 69632 | tf_op jit(solution)/shard_map/psum | solution.py:120
  330.0 0.1 fusion.36
  330.1 0.1 copy.82
  330.1 0.1 copy.83
  330.2 0.2 fusion.37
  330.4 0.2 multiply_reduce_fusion
  330.6 8.9 %convolution_bitcast_fusion = f32[8192,16]{0,1:T(8,128)} fusion(bf16[512,8192]{1,0:T(8,128)(2,1)} %param.39, bf16[16,8192]{1,0:T(8,128)(2,1)S(1)} %all_gather.7, bf16[8192,512]{1,0:T(8,128)(2,1)} %param.31, f32[16,512]{1,0:T(8,128)S(1)} %get-tuple-element.20, f32[512]{0:T(512)S(1)} %copy-done.10, f32[16]{0:T(128)S(1)} %add_rsqrt_fusion, ...), kind=kOutput, calls=%fused_computation.2 | convolution fusion | flops 268550144 | bytes 17633344 | tf_op jit(solution)/shard_map/dot_general | solution.py:136
  339.6 0.0 reduce-scatter.2.cloned.1.call-update
  339.6 1.1 copy.84
  340.7 0.6 fusion.14
  341.3 51.4 %reduce-scatter.2.cloned.1.call-done = f32[512,16]{0,1:T(8,128)} async-done(((f32[8192,16]{0,1:T(8,128)}), f32[512,16]{0,1:T(8,128)}) %reduce-scatter.2.cloned.1.call-update) | async-done | bytes 32784 | tf_op jit(solution)/shard_map/reduce_scatter | solution.py:135
  392.8 1.4 fusion.15
  (36 shorter events, 0.2 us)
Async XLA Ops:
  7.2 262.2 %copy-start = (bf16[512,544]{0,1:T(8,128)(2,1)S(1)}, bf16[512,544]{0,1:T(8,128)(2,1)}, u32[]{:S(2)}) copy-start(bf16[512,544]{0,1:T(8,128)(2,1)} %param.34) | copy-start | bytes 1671172
  9.3 59.5 %all-to-all-start = ((s32[16,1,1]{2,1,0:T(1,128)}), s32[16,1,1]{2,1,0:T(1,128)S(1)}, u32[]{:S(2)}, u32[]{:S(2)}) async-start(s32[16,1,1]{2,1,0:T(1,128)} %copy.72), calls=%async_computation | async-start | bytes 16384 | tf_op jit(solution)/shard_map/all_to_all | solution.py:90
  16.7 58.5 %copy-start.1 = (f32[1,16,8192]{2,1,0:T(8,128)S(1)}, f32[1,16,8192]{2,1,0:T(8,128)}, u32[]{:S(2)}) copy-start(f32[1,16,8192]{2,1,0:T(8,128)} %param.27) | copy-start | bytes 1572868
  68.9 55.4 %all-to-all-start.2 = ((f32[16,1,1536]{2,1,0:T(1,128)}), f32[16,1,1536]{2,1,0:T(1,128)S(1)}, u32[]{:S(2)}, u32[]{:S(2)}) async-start(f32[16,1,1536]{2,1,0:T(1,128)} %reshape.189), calls=%async_computation.2 | async-start | bytes 196608 | tf_op jit(solution)/shard_map/all_to_all | solution.py:75
  75.2 55.2 %copy-start.3 = (bf16[8,16,2048]{2,1,0:T(8,128)(2,1)S(1)}, bf16[8,16,2048]{2,1,0:T(8,128)(2,1)}, u32[]{:S(2)}) copy-start(bf16[8,16,2048]{2,1,0:T(8,128)(2,1)} %param.23) | copy-start | bytes 1572868
  81.6 49.0 %copy-start.12 = (s32[8]{0:T(128)S(1)}, s32[8]{0:T(128)}, u32[]{:S(2)}) copy-start(s32[8]{0:T(128)} %param.25) | copy-start | bytes 100
  120.0 31.1 %copy-start.4 = (bf16[1,8192]{1,0:T(2,128)(2,1)S(1)}, bf16[1,8192]{1,0:T(2,128)(2,1)}, u32[]{:S(2)}) copy-start(bf16[1,8192]{1,0:T(2,128)(2,1)} %param.21) | copy-start | bytes 49156
  120.0 31.2 %copy-start.5 = (f32[16,512]{1,0:T(8,128)S(1)}, f32[16,512]{1,0:T(8,128)}, u32[]{:S(2)}) copy-start(f32[16,512]{1,0:T(8,128)} %param.37) | copy-start | bytes 98308
  120.0 31.3 %copy-start.13 = (s32[16]{0:T(128)S(1)}, s32[16]{0:T(128)}, u32[]{:S(2)}) copy-start(s32[16]{0:T(128)} %param.24) | copy-start | bytes 196
  120.0 31.9 %copy-start.11 = (bf16[1,2048]{1,0:T(2,128)(2,1)S(1)}, bf16[1,2048]{1,0:T(2,128)(2,1)}, u32[]{:S(2)}) copy-start(bf16[1,2048]{1,0:T(2,128)(2,1)} %param.22) | copy-start | bytes 12292
  124.2 21.9 %all-to-all-start.3 = ((f32[16,1,8192]{2,1,0:T(1,128)}), f32[16,1,8192]{2,1,0:T(1,128)S(1)}, u32[]{:S(2)}, u32[]{:S(2)}) async-start(f32[16,1,8192]{2,1,0:T(1,128)} %reshape.187), calls=%async_computation.3 | async-start | bytes 1048576 | tf_op jit(solution)/shard_map/all_to_all | solution.py:74
  146.2 32.4 %all-to-all-start.1 = ((bf16[16,2,16384]{2,1,0:T(2,128)(2,1)}), bf16[16,2,16384]{2,1,0:T(2,128)(2,1)}, u32[]{:S(2)}, u32[]{:S(2)}) async-start(bf16[16,2,16384]{2,1,0:T(2,128)(2,1)} %reshape.185), calls=%async_computation.1 | async-start | bytes 2097152 | tf_op jit(solution)/shard_map/all_to_all | solution.py:89
  150.5 242.3 %reduce-scatter.2.cloned.1.call-start = ((), (), s32[]{:S(2)}) async-start(), calls=%async_computation.5 | async-start | bytes 557056 | tf_op jit(solution)/shard_map/reduce_scatter | solution.py:135
  178.5 51.5 %copy-start.7 = (bf16[16,512]{1,0:T(8,128)(2,1)S(1)}, bf16[16,512]{1,0:T(8,128)(2,1)}, u32[]{:S(2)}) copy-start(bf16[16,512]{1,0:T(8,128)(2,1)} %param.20) | copy-start | bytes 49156
  234.6 34.7 %copy-start.8 = (f32[4,512]{1,0:T(4,128)S(1)}, f32[4,512]{1,0:T(4,128)}, u32[]{:S(2)}) copy-start(f32[4,512]{1,0:T(4,128)} %param.32) | copy-start | bytes 24580
  264.5 4.9 %copy-start.6 = (f32[512]{0:T(512)S(1)}, f32[512]{0:T(512)}, u32[]{:S(2)}) copy-start(f32[512]{0:T(512)} %param.33) | copy-start | bytes 6148
  264.7 65.5 %copy-start.2 = (bf16[512,512]{1,0:T(8,128)(2,1)S(1)}, bf16[512,512]{1,0:T(8,128)(2,1)}, u32[]{:S(2)}) copy-start(bf16[512,512]{1,0:T(8,128)(2,1)} %param.35) | copy-start | bytes 1572868
  264.7 65.5 %copy-start.9 = (f32[512]{0:T(512)S(1)}, f32[512]{0:T(512)}, u32[]{:S(2)}) copy-start(f32[512]{0:T(512)} %param.36) | copy-start | bytes 6148
  264.7 65.9 %copy-start.10 = (f32[512]{0:T(512)S(1)}, f32[512]{0:T(512)}, u32[]{:S(2)}) copy-start(f32[512]{0:T(512)} %param.38) | copy-start | bytes 6148
Sparse Core Ops, SparseCore 0:
  339.7 53.0 reduce-scatter.1
where the time goes:
time: 408 us; the launch traced here: 401 us
  blocking collectives  126 us (31%)
  other arithmetic  94.8 us (23%)
  waiting for transfers between devices  62.8 us (15%)
  local copies, waits for them, and re-layouts  57.5 us (14%)
  starting transfers between devices  24.7 us (6%)
  matrix products  20.9 us (5%)
  between operations  14.6 us (4%)
    unnamed x3, other arithmetic  76.8 us
    psum x1, blocking collectives, on_device(): lax.psum(jnp.dot(x_low, state_proj, preferred_element_type=jnp.float32),...  60.4 us
    reduce_scatter x1, waiting for transfers between devices, on_device(): lax.psum_scatter(lax.dot_general(mamba_down, gated, (((0,), (1,)), ((), (...  51.4 us
    unnamed x41, local copies, waits for them, and re-layouts  50.1 us
    all_gather x1, blocking collectives, on_device(): lax.all_gather(attended, ('src', 'chan'), axis=0, tiled=True)  35.6 us
    all_gather x1, blocking collectives, on_device(): fragment = lax.all_gather(hidden_mid, ('src', 'chan'), axis=1, tiled=True)  29.9 us
    all_to_all x1, waiting for transfers between devices, on_device(): lax.all_to_all(mamba_state, ('src', 'chan'), split_axis=2, concat_axis=0,...  11.4 us
    dot_general x1, matrix products, on_device(): lax.dot_general(mamba_down, gated, (((0,), (1,)), ((), ())), preferred_el...  8.94 us
  transfers between devices with their start and end apart: 5, of which 2 were waited for; matrix products, arithmetic and copies ran while one was open for 34% of the time, Pallas kernels for 0%

commit v1 on v0

v1 whole, which is shorter than its diff:
```python
import functools
import math

import jax
import jax.numpy as jnp
from jax import lax
from jax.experimental import pallas as pl
from jax.experimental.pallas import tpu as pltpu
from jax.sharding import PartitionSpec as P

D = 8192
NS = 16
DTR = 512
QH = 64
KVH = 8
HD = 128
G = QH // KVH
LANES = 128
NEGATIVE = -1e30
F32 = jnp.float32
BF16 = jnp.bfloat16
VM = pltpu.VMEM


def round_up(value, step):
    return -(-value // step) * step


def vmem(count):
    return [pl.BlockSpec(memory_space=pltpu.VMEM)] * count


def smem(count):
    return [pl.BlockSpec(memory_space=pltpu.SMEM)] * count


def hbm(count):
    return [pl.BlockSpec(memory_space=pl.ANY)] * count


def params(mib):
    return pltpu.CompilerParams(vmem_limit_bytes=mib * 2**20)


def cost(flops, nbytes):
    return pl.CostEstimate(flops=flops, bytes_accessed=nbytes, transcendentals=0)


def swap(x):
    return lax.ppermute(x, "src", [(0, 1), (1, 0)])


def exchange(x):
    return lax.all_to_all(x, "chan", split_axis=0, concat_axis=0, tiled=True)


def pack_kernel(nchan, query_ref, state_ref, conv_ref, out_ref, heads):
    devices = out_ref.shape[0]
    cols = state_ref.shape[2] // devices
    blocks = cols // LANES
    half = QH // 2
    for h in range(QH):
        heads[h : h + 1, :] = query_ref[0:1, h * HD : (h + 1) * HD].astype(F32)
    tail_at = half + NS * blocks
    tail_rows = out_ref.shape[1] - tail_at
    for i in range(devices):
        side = i // nchan
        out_ref[i, 0:half, :] = heads[side * half : (side + 1) * half, :].astype(BF16)
        rows = []
        for b in range(blocks):
            at = i * cols + b * LANES
            out_ref[i, half + b * NS : half + (b + 1) * NS, :] = state_ref[0, :, at : at + LANES].astype(BF16)
            for w in range(conv_ref.shape[0]):
                rows.append(conv_ref[w, 0:1, at : at + LANES])
        rows.append(jnp.zeros((tail_rows - len(rows), LANES), F32))
        out_ref[i, tail_at : tail_at + tail_rows, :] = jnp.concatenate(rows, axis=0).astype(BF16)


def attend_kernel(
    nchan,
    recv_ref,
    pages_ref,
    other_pages_ref,
    newkv_ref,
    other_newkv_ref,
    owner_ref,
    other_owner_ref,
    index_ref,
    other_index_ref,
    lengths_ref,
    out_ref,
    queries,
    result,
    stats,
    ordered,
):
    rows = recv_ref.shape[0]
    held, tokens = pages_ref.shape[0], pages_ref.shape[1]
    c = lax.axis_index("src")
    d = lax.axis_index("chan")
    half_kv = KVH // 2
    scale = 1.0 / math.sqrt(HD)
    count = 2 * held * tokens
    token = lax.broadcasted_iota(jnp.int32, (1, count), 1)
    page = token // tokens
    offset = token % tokens
    owner_of = jnp.full((1, count), -1, jnp.int32)
    for j in range(2 * held):
        owners, indexes = (owner_ref, index_ref) if j < held else (other_owner_ref, other_index_ref)
        owner = owners[j % held]
        left = lengths_ref[owner] - indexes[j % held] * tokens
        owner_of = jnp.where((page == j) & (offset < left), owner, owner_of)
    row_request = lax.broadcasted_iota(jnp.int32, (rows * G, 1), 0) // G
    mask = row_request == owner_of
    lane16 = lax.broadcasted_iota(jnp.int32, (1, 16), 1)
    new_owner = jnp.where(lane16 == 0, c * nchan + d, jnp.where(lane16 == 1, (1 - c) * nchan + d, -1))
    new_mask = row_request == new_owner
    lane = lax.broadcasted_iota(jnp.int32, (1, LANES), 1)
    collected = jnp.zeros((rows * G, LANES), F32)
    queries[...] = recv_ref[:, 0 : QH // 2, :].astype(F32)
    contract = (((1,), (1,)), ((), ()))
    per_chip = (QH // 2) // nchan
    for k in range(half_kv):
        key_at = pl.multiple_of(c * (half_kv * HD) + k * HD, HD)
        value_at = pl.multiple_of(KVH * HD + c * (half_kv * HD) + k * HD, HD)

        def both(at):
            pages = [r[:, :, pl.ds(at, HD)].reshape(held * tokens, HD) for r in (pages_ref, other_pages_ref)]
            fresh = [r[0:1, pl.ds(at, HD)].astype(F32) for r in (newkv_ref, other_newkv_ref)]
            fresh = jnp.concatenate(fresh + [jnp.zeros((14, HD), F32)], axis=0).astype(BF16)
            return jnp.concatenate(pages, axis=0), fresh

        keys, new_keys = both(key_at)
        values, new_values = both(value_at)
        q = queries[:, k * G : (k + 1) * G, :].reshape(rows * G, HD).astype(BF16)
        scores = lax.dot_general(q, keys, contract, preferred_element_type=F32) * scale
        new_scores = lax.dot_general(q, new_keys, contract, preferred_element_type=F32) * scale
        scores = jnp.where(mask, scores, NEGATIVE)
        new_scores = jnp.where(new_mask, new_scores, NEGATIVE)
        peak = jnp.maximum(jnp.max(scores, axis=1, keepdims=True), jnp.max(new_scores, axis=1, keepdims=True))
        weight = jnp.where(mask, jnp.exp(scores - peak), 0.0)
        new_weight = jnp.where(new_mask, jnp.exp(new_scores - peak), 0.0)
        total = jnp.sum(weight, axis=1, keepdims=True) + jnp.sum(new_weight, axis=1, keepdims=True)
        some = total > 0.0
        safe = jnp.where(some, total, 1.0)
        numer = jnp.dot(weight.astype(BF16), values, preferred_element_type=F32)
        numer = numer + jnp.dot(new_weight.astype(BF16), new_values, preferred_element_type=F32)
        collected = jnp.where(lane == k, jnp.where(some, peak + jnp.log(safe), NEGATIVE), collected)
        result[...] = numer / safe
        for g in range(G):
            head = k * G + g
            place = (head % per_chip) * rows
            out_ref[head // per_chip, place : place + rows, :] = result[pl.ds(g, rows, stride=G), :].astype(BF16)
    stats[...] = collected
    for g in range(G):
        ordered[g * rows : (g + 1) * rows, :] = stats[pl.ds(g, rows, stride=G), :]
    turned = ordered[...].T
    pieces = []
    rest = turned[0:8, :]
    for _ in range(3):
        piece = rest.astype(BF16).astype(F32)
        rest = rest - piece
        for k in range(half_kv):
            for j in range(rows * G // LANES):
                pieces.append(piece[k : k + 1, j * LANES : (j + 1) * LANES])
    chunk = per_chip * rows
    stat_rows = out_ref.shape[1] - chunk
    if stat_rows > len(pieces):
        pieces.append(jnp.zeros((stat_rows - len(pieces), LANES), F32))
    packed = jnp.concatenate(pieces, axis=0).astype(BF16)
    for i in range(nchan):
        out_ref[i, chunk : chunk + stat_rows, :] = packed


def combine_kernel(rows, recv_ref, out_ref, pieces, logs, turned):
    nchan = recv_ref.shape[0]
    per_chip = (QH // 2) // nchan
    chunk = per_chip * rows
    stat_rows = recv_ref.shape[1] - chunk
    vectors = (KVH // 2) * rows * G // LANES
    first = lax.axis_index("chan") * chunk
    row = first // LANES
    pieces[...] = recv_ref[:, chunk : chunk + stat_rows, :].astype(F32)
    logs[...] = jnp.zeros_like(logs)
    for s in range(nchan):
        logs[s : s + 1, :] = (
            pieces[s, pl.ds(row, 1), :] + pieces[s, pl.ds(row + vectors, 1), :] + pieces[s, pl.ds(row + 2 * vectors, 1), :]
        )
    found = logs[0:nchan, :]
    weight = jnp.exp(found - jnp.max(found, axis=0, keepdims=True))
    logs[0:nchan, :] = weight / jnp.sum(weight, axis=0, keepdims=True)
    turned[...] = logs[...].T
    mine = turned[pl.ds(pl.multiple_of(first % LANES, chunk), chunk), :]
    total = jnp.zeros((chunk, LANES), F32)
    for s in range(nchan):
        total = total + recv_ref[s, 0:chunk, :].astype(F32) * mine[:, s : s + 1]
    total = total.astype(BF16)
    for i in range(nchan):
        for h in range(per_chip):
            out_ref[i, :, h * HD : (h + 1) * HD] = total[h * rows : (h + 1) * rows, :]


def weight_copies(weight, buffer, sems, nchan):
    c = lax.axis_index("src")
    depth = weight.shape[0] // (2 * nchan)
    copies = []
    for side in range(2):
        for i in range(nchan):
            start = ((c if side == 0 else 1 - c) * nchan + i) * depth
            slot = side * nchan + i
            copies.append(
                pltpu.make_async_copy(
                    weight.at[pl.ds(pl.multiple_of(start, depth), depth), :],
                    buffer.at[pl.ds(slot * depth, depth), :],
                    sems.at[slot],
                )
            )
    return copies


def streamed_dot(copies, own, other, buffer, nchan):
    depth = buffer.shape[0] // (2 * nchan)
    total = None
    for side, ref in ((0, own), (1, other)):
        for i in range(nchan):
            slot = side * nchan + i
            copies[slot].wait()
            part = jnp.dot(ref[i], buffer[slot * depth : (slot + 1) * depth, :], preferred_element_type=F32)
            total = part if total is None else total + part
    return total


def out_kernel(nchan, own, other, residual, weight, out_ref, buffer, sems):
    copies = weight_copies(weight, buffer, sems, nchan)
    for copy in copies:
        copy.start()
    total = streamed_dot(copies, own, other, buffer, nchan)
    hidden = (residual[...].astype(F32) + total).astype(BF16)
    for i in range(nchan):
        out_ref[i] = hidden


def values_kernel(
    nchan, first_row, own, other, arrived, taps, offset, state_proj, weight, conv_out, act_out, rms_out, proj_out, buffer, sems
):
    copies = weight_copies(weight, buffer, sems, nchan)
    for copy in copies:
        copy.start()
    rows, cols = act_out.shape
    squares = jnp.zeros((rows, 1), F32)
    for ref in (own, other):
        for i in range(nchan):
            wide = ref[i].astype(F32)
            squares = squares + jnp.sum(wide * wide, axis=1, keepdims=True)
    inverse = lax.rsqrt(squares / D + 1e-06)
    rms_out[...] = jnp.broadcast_to(inverse, rms_out.shape)
    steps = conv_out.shape[0]
    blocks = cols // LANES
    tail = arrived[:, first_row:, :].astype(F32)
    past = [
        jnp.concatenate([tail[:, b * steps + w, :] for b in range(blocks)], axis=1) for w in range(steps)
    ]
    value = streamed_dot(copies, own, other, buffer, nchan) * inverse
    window = past + [value]
    mixed = jnp.zeros((rows, cols), F32)
    for w in range(steps + 1):
        mixed = mixed + window[w] * taps[w : w + 1, :]
        if w > 0:
            conv_out[w - 1] = window[w]
    mixed = mixed + offset[...]
    act = mixed / (1.0 + jnp.exp(-mixed))
    act_out[...] = act
    part = lax.dot_general(act.astype(BF16), state_proj[...], (((1,), (1,)), ((), ())), preferred_element_type=F32)
    part = part.astype(BF16)
    width = part.shape[1]
    for i in range(nchan):
        proj_out[i] = jnp.zeros(proj_out.shape[1:], BF16)
        proj_out[i, :, 0:width] = part


def gates_kernel(nchan, own, other, rms, weight, out_ref, buffer, sems):
    copies = weight_copies(weight, buffer, sems, nchan)
    for copy in copies:
        copy.start()
    gate = streamed_dot(copies, own, other, buffer, nchan) * rms[:, 0:1]
    out_ref[...] = gate / (1.0 + jnp.exp(-gate))


def down_copies(weight, buffer, sems, half):
    width = weight.shape[1] // 2
    pieces = sems.shape[0]
    step = width // pieces
    copies = []
    for i in range(pieces):
        start = pl.multiple_of(half * width + i * step, step)
        copies.append(
            pltpu.make_async_copy(weight.at[:, pl.ds(start, step)], buffer.at[:, pl.ds(i * step, step)], sems.at[i])
        )
    return copies


def down_product(copies, gated, buffer, out_ref):
    nchan, rows, cols = out_ref.shape
    step = buffer.shape[1] // len(copies)
    for i, copy in enumerate(copies):
        copy.wait()
        part = jnp.dot(gated, buffer[:, i * step : (i + 1) * step], preferred_element_type=F32).astype(BF16)
        for j in range(step // cols):
            out_ref[i * (step // cols) + j] = part[:, j * cols : (j + 1) * cols]


def scan_kernel(
    state_row,
    own,
    other,
    arrived,
    act_ref,
    gate_ref,
    step_proj,
    step_bias,
    decay_log,
    skip_gain,
    weight,
    next_out,
    gated_out,
    send_out,
    turned,
    mixed,
    buffer,
    sems,
):
    copies = down_copies(weight, buffer, sems, 1 - lax.axis_index("src"))
    for copy in copies:
        copy.start()
    nchan, rows = own.shape[0], own.shape[1]
    cols = act_ref.shape[1]
    blocks = cols // LANES
    projected = jnp.zeros(own.shape[1:], F32)
    for ref in (own, other):
        for i in range(nchan):
            projected = projected + ref[i].astype(F32)
    act = act_ref[...]
    raw = jnp.dot(projected[:, 0:DTR].astype(BF16), step_proj[...], preferred_element_type=F32) + step_bias[...]
    step = jnp.maximum(raw, 0.0) + jnp.log1p(jnp.exp(-jnp.abs(raw)))
    turned[...] = jnp.zeros_like(turned)
    turned[0:rows, :] = projected[:, DTR : DTR + LANES]
    mats = turned[...].T
    rate = -jnp.exp(decay_log[...])
    fed = step * act
    for r in range(rows):
        b_col = mats[0:NS, r : r + 1]
        c_col = mats[NS : 2 * NS, r : r + 1]
        for b in range(blocks):
            at = b * LANES
            lanes = slice(at, at + LANES)
            state = arrived[r, state_row + b * NS : state_row + (b + 1) * NS, :].astype(F32)
            after = jnp.exp(step[r : r + 1, lanes] * rate[:, lanes]) * state + fed[r : r + 1, lanes] * b_col
            next_out[r, :, lanes] = after
            mixed[r : r + 1, lanes] = jnp.sum(after * c_col, axis=0, keepdims=True)
    gated = ((mixed[...] + skip_gain[...] * act) * gate_ref[...]).astype(BF16)
    gated_out[...] = gated
    down_product(copies, gated, buffer, send_out)


def down_kernel(gated, weight, out_ref, buffer, sems):
    copies = down_copies(weight, buffer, sems, lax.axis_index("src"))
    for copy in copies:
        copy.start()
    down_product(copies, gated[...], buffer, out_ref)


def on_device(
    residual_input,
    query_heads,
    new_keyval,
    cache_pages,
    prompt_lengths,
    page_owner,
    page_index,
    mamba_state,
    conv_state,
    out_heads,
    in_values,
    in_gates,
    conv_taps,
    conv_offset,
    state_proj,
    step_proj,
    step_bias,
    decay_log,
    skip_gain,
    mamba_down,
):
    nchan = lax.axis_size("chan")
    devices = 2 * nchan
    rows, cols = residual_input.shape
    blocks = cols // LANES
    half = QH // 2
    steps = conv_state.shape[1]
    conv_row = half + NS * blocks
    pack_rows = round_up(conv_row + steps * blocks, 16)
    call = pl.pallas_call
    shape = jax.ShapeDtypeStruct

    other_pages = swap(cache_pages)
    other_newkv = swap(new_keyval)
    other_owner = swap(page_owner)
    other_index = swap(page_index)
    packed = call(
        functools.partial(pack_kernel, nchan),
        out_shape=shape((devices, pack_rows, LANES), BF16),
        in_specs=vmem(3),
        out_specs=vmem(1)[0],
        scratch_shapes=[VM((QH, HD), F32)],
        compiler_params=params(16),
        name="pack",
    )(query_heads, mamba_state, jnp.transpose(conv_state, (1, 0, 2)))
    arrived = lax.all_to_all(packed, ("src", "chan"), split_axis=0, concat_axis=0, tiled=True)

    chunk = (half // nchan) * rows
    stat_rows = round_up(3 * (KVH // 2) * rows * G // LANES, 16)
    partials = call(
        functools.partial(attend_kernel, nchan),
        out_shape=shape((nchan, chunk + stat_rows, LANES), BF16),
        in_specs=vmem(5) + smem(5),
        out_specs=vmem(1)[0],
        scratch_shapes=[
            VM((rows, half, HD), F32),
            VM((rows * G, LANES), F32),
            VM((rows * G, LANES), F32),
            VM((rows * G, LANES), F32),
        ],
        compiler_params=params(32),
        name="attend",
    )(
        arrived,
        cache_pages,
        other_pages,
        new_keyval,
        other_newkv,
        page_owner,
        other_owner,
        page_index,
        other_index,
        prompt_lengths,
    )
    merged = exchange(partials)
    attended = call(
        functools.partial(combine_kernel, rows),
        out_shape=shape((nchan, rows, cols), BF16),
        in_specs=vmem(1),
        out_specs=vmem(1)[0],
        scratch_shapes=[VM((nchan, stat_rows, LANES), F32), VM((LANES, LANES), F32), VM((LANES, LANES), F32)],
        compiler_params=params(16),
        name="combine",
    )(merged)
    att_own = exchange(attended)
    att_other = swap(att_own)

    weight_buffers = [VM((D, cols), BF16), pltpu.SemaphoreType.DMA((devices,))]
    weight_cost = cost(2 * rows * D * cols, 2 * D * cols)
    hidden = call(
        functools.partial(out_kernel, nchan),
        out_shape=shape((nchan, rows, cols), BF16),
        in_specs=vmem(3) + hbm(1),
        out_specs=vmem(1)[0],
        scratch_shapes=weight_buffers,
        compiler_params=params(24),
        cost_estimate=weight_cost,
        name="out",
    )(att_own, att_other, residual_input, out_heads)
    hid_own = exchange(hidden)
    hid_other = swap(hid_own)

    width = round_up(state_proj.shape[1], LANES)
    conv_next, act, rms, part = call(
        functools.partial(values_kernel, nchan, conv_row),
        out_shape=(
            shape((steps, rows, cols), F32),
            shape((rows, cols), F32),
            shape((rows, LANES), F32),
            shape((nchan, rows, width), BF16),
        ),
        in_specs=vmem(6) + hbm(1),
        out_specs=tuple(vmem(4)),
        scratch_shapes=weight_buffers,
        compiler_params=params(24),
        cost_estimate=weight_cost,
        name="values",
    )(hid_own, hid_other, arrived, conv_taps, conv_offset[None, :], state_proj.T, in_values)
    proj_own = exchange(part)
    gate = call(
        functools.partial(gates_kernel, nchan),
        out_shape=shape((rows, cols), F32),
        in_specs=vmem(3) + hbm(1),
        out_specs=vmem(1)[0],
        scratch_shapes=weight_buffers,
        compiler_params=params(24),
        cost_estimate=weight_cost,
        name="gates",
    )(hid_own, hid_other, rms, in_gates)
    proj_other = swap(proj_own)

    pieces = 4
    down_buffers = [VM((cols, D // 2), BF16), pltpu.SemaphoreType.DMA((pieces,))]
    mamba_next, gated, send = call(
        functools.partial(scan_kernel, half),
        out_shape=(
            shape((rows, NS, cols), F32),
            shape((rows, cols), BF16),
            shape((nchan, rows, cols), BF16),
        ),
        in_specs=vmem(9) + hbm(1),
        out_specs=tuple(vmem(3)),
        scratch_shapes=[VM((LANES, LANES), F32), VM((rows, cols), F32)] + down_buffers,
        compiler_params=params(24),
        name="scan",
    )(
        proj_own,
        proj_other,
        arrived,
        act,
        gate,
        step_proj,
        step_bias[None, :],
        decay_log,
        skip_gain[None, :],
        mamba_down,
    )
    taken = swap(send)
    keep = call(
        down_kernel,
        out_shape=shape((nchan, rows, cols), BF16),
        in_specs=vmem(1) + hbm(1),
        out_specs=vmem(1)[0],
        scratch_shapes=down_buffers,
        compiler_params=params(24),
        cost_estimate=cost(rows * D * cols, D * cols),
        name="down",
    )(gated, mamba_down)
    summed = (keep.astype(F32) + taken.astype(F32)).astype(BF16)
    final = exchange(summed)
    down_sum = jnp.sum(final.astype(F32), axis=0)
    hidden_out = (hidden[0].astype(F32) + down_sum).astype(BF16)
    return (hidden_out, mamba_next, jnp.transpose(conv_next, (1, 0, 2)))


def solution(mesh):
    owners = ("groups", "src", "chan")
    channels = ("src", "chan")
    placed = (
        P("groups", channels),
        P(owners, None),
        P(owners, None),
        P(owners, None, None),
        P("groups"),
        P(owners),
        P(owners),
        P(owners, None, None),
        P(owners, None, None),
        P(None, channels),
        P(None, channels),
        P(None, channels),
        P(None, channels),
        P(channels),
        P(channels, None),
        P(None, channels),
        P(channels),
        P(None, channels),
        P(channels),
        P(channels, None),
    )
    return jax.shard_map(
        on_device,
        mesh=mesh,
        in_specs=placed,
        out_specs=(P("groups", channels), P("groups", None, channels), P("groups", None, channels)),
        check_vma=False,
    )
```

time: 408 us -> 106 us (0.26); the launches traced: 401 us -> 105 us
  other arithmetic: 94.8 us -> 0.67 us
  blocking collectives: 126 us -> 50.5 us
  waiting for transfers between devices: 62.8 us -> 16.1 us
  local copies, waits for them, and re-layouts: 57.5 us -> 14.1 us
  matrix products: 20.9 us -> 0 us
  starting transfers between devices: 24.7 us -> 9.02 us
  Pallas kernels: 0 us -> 14.1 us
  between operations: 14.6 us -> 0.86 us
    unnamed x3 -> x2, other arithmetic: 76.8 us -> 0.01 us
    all_gather x2 -> x0, blocking collectives: 65.5 us -> none  [the longest x1 35.6 us: on_device(): lax.all_gather(attended, ('src', 'chan'), axis=0, tiled=True)]
    psum x1 -> x0, blocking collectives: 60.4 us -> none  [on_device(): lax.psum(jnp.dot(x_low, state_proj, preferred_element_type=jnp.float32),...]
    reduce_scatter x1 -> x0, waiting for transfers between devices: 51.4 us -> none  [on_device(): lax.psum_scatter(lax.dot_general(mamba_down, gated, (((0,), (1,)), ((), (...]
    all_to_all x0 -> x5, blocking collectives: none -> 50.5 us  [exchange(): return lax.all_to_all(x, 'chan', split_axis=0, concat_axis=0, tiled=True)]
    unnamed x41 -> x44, local copies, waits for them, and re-layouts: 50.1 us -> 14.1 us
    dot_general x9 -> x0, matrix products: 20.9 us -> none  [the longest x1 8.94 us: on_device(): lax.dot_general(mamba_down, gated, (((0,), (1,)), ((), ())), preferred_el...]
    all_to_all x4 -> x1, starting transfers between devices: 24.1 us -> 7.39 us  [on_device(): lax.all_to_all(packed, ('src', 'chan'), split_axis=0, concat_axis=0, tile...]
  transfers between devices with their start and end apart: 5 -> 9, of which waited for: 2 -> 4; matrix products, arithmetic and copies ran while one was open for 34% -> 0% of each run, Pallas kernels for 0% -> 3%
where the time goes in v1:
time: 106 us; the launch traced here: 105 us
  blocking collectives  50.5 us (48%)
  waiting for transfers between devices  16.1 us (15%)
  local copies, waits for them, and re-layouts  14.1 us (13%)
  Pallas kernels  14.1 us (13%)
  starting transfers between devices  9.02 us (9%)
    all_to_all x5, blocking collectives, exchange(): return lax.all_to_all(x, 'chan', split_axis=0, concat_axis=0, tiled=True)  50.5 us
    unnamed x44, local copies, waits for them, and re-layouts  14.1 us
    all_to_all x1, waiting for transfers between devices, on_device(): lax.all_to_all(packed, ('src', 'chan'), split_axis=0, concat_axis=0, tile...  12.2 us
    all_to_all x1, starting transfers between devices, on_device(): lax.all_to_all(packed, ('src', 'chan'), split_axis=0, concat_axis=0, tile...  7.39 us
    ppermute x8, waiting for transfers between devices, swap(): return lax.ppermute(x, 'src', [(0, 1), (1, 0)])  3.81 us
    pallas_call x1, Pallas kernels, on_device(): call(functools.partial(values_kernel, nchan, conv_row), out_shape=(shape(...  2.81 us
    pallas_call x1, Pallas kernels, on_device(): call(functools.partial(scan_kernel, half), out_shape=(shape((rows, NS, co...  2.64 us
  transfers between devices with their start and end apart: 9, of which 4 were waited for; matrix products, arithmetic and copies ran while one was open for 0% of the time, Pallas kernels for 3%

profile of v1, /device:TPU:0, one launch (start us, length us, event | category | flops | bytes accessed | tf_op | source)
XLA Modules:
  0.0 105.3 jit_solution(13019411135641864798)
XLA Ops:
  0.6 0.0 copy-start.2
  0.6 0.0 copy-start.5
  0.7 1.1 %copy-done.5 = f32[1,16,8192]{2,1,0:T(8,128)S(1)} copy-done((f32[1,16,8192]{2,1,0:T(8,128)S(1)}, f32[1,16,8192]{2,1,0:T(8,128)}, u32[]{:S(2)}) %copy-start.5) | copy-done | bytes 524312
  1.7 0.0 copy-start.6
  1.7 0.9 copy-done.6
  2.6 0.0 copy-start.8
  2.6 0.8 copy-done.8
  3.4 0.0 copy-start.11
  3.4 0.0 copy-start.12
  3.4 0.9 pack.1
  4.3 7.4 %all-to-all-start = ((bf16[16,112,128]{2,1,0:T(8,128)(2,1)}), bf16[16,112,128]{2,1,0:T(8,128)(2,1)S(1)}, u32[]{:S(2)}, u32[]{:S(2)}) async-start(bf16[16,112,128]{2,1,0:T(8,128)(2,1)} %pack.1), calls=%async_computation | async-start | bytes 917504 | tf_op jit(solution)/shard_map/all_to_all | solution.py:418
  11.7 0.4 collective-permute-start
  12.1 0.2 collective-permute-start.1
  12.2 0.3 collective-permute-start.2
  12.6 0.2 collective-permute-start.3
  12.7 1.1 %collective-permute-done.2.other_owner_ref = s32[8]{0:T(128)S(1)} collective-permute-done((s32[8]{0:T(128)}, s32[8]{0:T(128)S(1)}, u32[]{:S(2)}, u32[]{:S(2)}) %collective-permute-start.2) | collective-permute-done | bytes 64 | tf_op jit(solution)/shard_map/ppermute | solution.py:50
  13.8 0.0 collective-permute-done.3.other_index_ref
  13.9 0.0 collective-permute-done.1.other_newkv_ref
  13.9 0.0 collective-permute-done.other_pages_ref
  13.9 12.2 %all-to-all-done.recv_ref.arrived = bf16[16,112,128]{2,1,0:T(8,128)(2,1)S(1)} async-done(((bf16[16,112,128]{2,1,0:T(8,128)(2,1)}), bf16[16,112,128]{2,1,0:T(8,128)(2,1)S(1)}, u32[]{:S(2)}, u32[]{:S(2)}) %all-to-all-start) | async-done | bytes 458784 | tf_op jit(solution)/shard_map/all_to_all | solution.py:418
  26.1 0.0 copy-start.3
  26.1 1.0 copy-done.3
  27.1 0.0 copy-start.10
  27.1 0.7 copy-done.10
  27.8 0.7 copy-done.15
  28.5 0.7 copy-done.16
  29.2 0.7 copy-done.17
  29.8 1.9 %attend.1 = bf16[8,80,128]{2,1,0:T(8,128)(2,1)S(1)} custom-call(bf16[16,112,128]{2,1,0:T(8,128)(2,1)S(1)} %all-to-all-done.recv_ref.arrived, bf16[8,16,2048]{2,1,0:T(8,128)(2,1)S(1)} %copy-done.3, bf16[8,16,2048]{2,1,0:T(8,128)(2,1)S(1)} %collective-permute-done.other_pages_ref, bf16[1,2048]{1,0:T(2,128)(2,1)S(1)} %copy-done.10, ...), custom_call_target="tpu_custom_call" | custom-call | tf_op jit(solution)/shard_map/attend/pallas_call | solution.py:422
  31.7 10.0 %all_to_all.30.recv_ref = bf16[8,80,128]{2,1,0:T(8,128)(2,1)S(1)} all-to-all(bf16[8,80,128]{2,1,0:T(8,128)(2,1)S(1)} %attend.1), channel_id=1, replica_groups=mesh['groups'=2,'src'=2,'chan'=8] {'chan'}, dimensions={0} | all-to-all | bytes 327680 | tf_op jit(solution)/shard_map/all_to_all | solution.py:54
  41.7 0.3 combine.1
  42.0 10.0 %all_to_all.31.own = bf16[8,16,512]{2,1,0:T(8,128)(2,1)S(1)} all-to-all(bf16[8,16,512]{2,1,0:T(8,128)(2,1)S(1)} %combine.1), channel_id=1, replica_groups=mesh['groups'=2,'src'=2,'chan'=8] {'chan'}, dimensions={0} | all-to-all | bytes 262144 | tf_op jit(solution)/shard_map/all_to_all | solution.py:54
  52.0 0.0 collective-permute-start.4
  52.0 1.3 %collective-permute-done.4.other = bf16[8,16,512]{2,1,0:T(8,128)(2,1)S(1)} collective-permute-done((bf16[8,16,512]{2,1,0:T(8,128)(2,1)S(1)}, bf16[8,16,512]{2,1,0:T(8,128)(2,1)S(1)}, u32[]{:S(2)}, u32[]{:S(2)}) %collective-permute-start.4) | collective-permute-done | bytes 131104 | tf_op jit(solution)/shard_map/ppermute | solution.py:50
  53.4 3.4 %copy-done = bf16[8192,512]{1,0:T(8,128)(2,1)S(1)} copy-done((bf16[8192,512]{1,0:T(8,128)(2,1)S(1)}, bf16[8192,512]{1,0:T(8,128)(2,1)}, u32[]{:S(2)}) %copy-start) | copy-done | bytes 8388632
  56.8 0.7 copy-done.9
  57.5 2.0 %out.1 = bf16[8,16,512]{2,1,0:T(8,128)(2,1)S(1)} custom-call(bf16[8,16,512]{2,1,0:T(8,128)(2,1)S(1)} %all_to_all.31.own, bf16[8,16,512]{2,1,0:T(8,128)(2,1)S(1)} %collective-permute-done.4.other, bf16[16,512]{1,0:T(8,128)(2,1)S(1)} %copy-done.9, bf16[8192,512]{1,0:T(8,128)(2,1)S(1)} %copy-done), custom_call_target="tpu_custom_call" | custom-call | flops 134217728 | bytes 8388608 | tf_op jit(solution)/shard_map/out/pallas_call | solution.py:462
  59.5 10.0 %all_to_all.32.own = bf16[8,16,512]{2,1,0:T(8,128)(2,1)S(1)} all-to-all(bf16[8,16,512]{2,1,0:T(8,128)(2,1)S(1)} %out.1), channel_id=1, replica_groups=mesh['groups'=2,'src'=2,'chan'=8] {'chan'}, dimensions={0} | all-to-all | bytes 262144 | tf_op jit(solution)/shard_map/all_to_all | solution.py:54
  69.4 0.0 collective-permute-start.5
  69.4 1.3 %collective-permute-done.5.other = bf16[8,16,512]{2,1,0:T(8,128)(2,1)S(1)} collective-permute-done((bf16[8,16,512]{2,1,0:T(8,128)(2,1)S(1)}, bf16[8,16,512]{2,1,0:T(8,128)(2,1)S(1)}, u32[]{:S(2)}, u32[]{:S(2)}) %collective-permute-start.5) | collective-permute-done | bytes 131104 | tf_op jit(solution)/shard_map/ppermute | solution.py:50
  70.8 0.0 copy-done.2
  70.8 0.0 copy-done.11
  70.8 0.0 copy-done.12
  70.8 0.0 copy-start.1
  70.8 3.5 %copy-done.1 = bf16[8192,512]{1,0:T(8,128)(2,1)S(1)} copy-done((bf16[8192,512]{1,0:T(8,128)(2,1)S(1)}, bf16[8192,512]{1,0:T(8,128)(2,1)}, u32[]{:S(2)}) %copy-start.1) | copy-done | bytes 8388632
  74.4 0.0 copy-start.14
  74.4 2.8 %values.1 = (f32[3,16,512]{2,1,0:T(8,128)}, f32[16,512]{1,0:T(8,128)S(1)}, f32[16,128]{1,0:T(8,128)S(1)}, bf16[8,16,640]{2,1,0:T(8,128)(2,1)S(1)}) custom-call(bf16[8,16,512]{2,1,0:T(8,128)(2,1)S(1)} %all_to_all.32.own, bf16[8,16,512]{2,1,0:T(8,128)(2,1)S(1)} %collective-permute-done.5.other, bf16[16,112,128]{2,1,0:T(8,128)(2,1)S(1)} %all-to-all-done.recv_ref.arrived, ...), custom_call_target="tpu_custom_call" | custom-call | flops 134217728 | bytes 8388608 | tf_op jit(solution)/shard_map/values/pallas_call | solution.py:476
  77.2 10.5 %all_to_all.33.own = bf16[8,16,640]{2,1,0:T(8,128)(2,1)S(1)} all-to-all(bf16[8,16,640]{2,1,0:T(8,128)(2,1)S(1)} %get-tuple-element.10), channel_id=1, replica_groups=mesh['groups'=2,'src'=2,'chan'=8] {'chan'}, dimensions={0} | all-to-all | bytes 327680 | tf_op jit(solution)/shard_map/all_to_all | solution.py:54
  87.6 0.0 collective-permute-start.6
  87.6 0.0 slice-done.2
  87.6 0.0 slice-done.3
  87.7 2.0 %gates.1.gate_ref = f32[16,512]{1,0:T(8,128)S(1)} custom-call(bf16[8,16,512]{2,1,0:T(8,128)(2,1)S(1)} %all_to_all.32.own, bf16[8,16,512]{2,1,0:T(8,128)(2,1)S(1)} %collective-permute-done.5.other, f32[16,128]{1,0:T(8,128)S(1)} %get-tuple-element.12.rms, bf16[8192,512]{1,0:T(8,128)(2,1)S(1)} %bitcast.14), custom_call_target="tpu_custom_call" | custom-call | flops 134217728 | bytes 8388608 | tf_op jit(solution)/shard_map/gates/pallas_call | solution.py:492
  89.7 0.0 collective-permute-done.6.other
  89.7 0.0 slice-done
  89.7 0.0 slice-done.1
  89.7 0.0 copy-done.4
  89.7 0.0 copy-done.7
  89.7 0.0 copy-done.13
  89.8 0.0 copy-done.14
  89.8 2.6 %scan.1 = (f32[16,16,512]{2,1,0:T(8,128)}, bf16[16,512]{1,0:T(8,128)(2,1)S(1)}, bf16[8,16,512]{2,1,0:T(8,128)(2,1)S(1)}) custom-call(bf16[8,16,640]{2,1,0:T(8,128)(2,1)S(1)} %all_to_all.33.own, bf16[8,16,640]{2,1,0:T(8,128)(2,1)S(1)} %collective-permute-done.6.other, bf16[16,112,128]{2,1,0:T(8,128)(2,1)S(1)} %all-to-all-done.recv_ref.arrived, ...), custom_call_target="tpu_custom_call" | custom-call | tf_op jit(solution)/shard_map/scan/pallas_call | solution.py:506
  92.4 0.5 collective-permute-start.7
  93.0 1.6 %down.1 = bf16[8,16,512]{2,1,0:T(8,128)(2,1)S(1)} custom-call(bf16[16,512]{1,0:T(8,128)(2,1)S(1)} %get-tuple-element.13.gated, bf16[512,8192]{1,0:T(8,128)(2,1)S(1)} %bitcast.12), custom_call_target="tpu_custom_call" | custom-call | flops 67108864 | bytes 4194304 | tf_op jit(solution)/shard_map/down/pallas_call | solution.py:531
  94.6 0.0 collective-permute-done.7
  94.6 10.1 %all_to_all.34 = bf16[8,16,512]{2,1,0:T(8,128)(2,1)S(1)} all-to-all(bf16[8,16,512]{2,1,0:T(8,128)(2,1)S(1)} %add_convert_fusion), channel_id=1, replica_groups=mesh['groups'=2,'src'=2,'chan'=8] {'chan'}, dimensions={0} | all-to-all | bytes 262144 | tf_op jit(solution)/shard_map/all_to_all | solution.py:54
  104.7 0.6 fusion
  (16 shorter events, 0.1 us)
Async XLA Ops:
  0.6 70.2 %copy-start.2 = (bf16[512,544]{0,1:T(8,128)(2,1)S(1)}, bf16[512,544]{0,1:T(8,128)(2,1)}, u32[]{:S(2)}) copy-start(bf16[512,544]{0,1:T(8,128)(2,1)} %param.34) | copy-start | bytes 1671172
  0.6 1.1 %copy-start.5 = (f32[1,16,8192]{2,1,0:T(8,128)S(1)}, f32[1,16,8192]{2,1,0:T(8,128)}, u32[]{:S(2)}) copy-start(f32[1,16,8192]{2,1,0:T(8,128)} %state_ref.1) | copy-start | bytes 1572868
  1.7 0.9 copy-start.6
  2.6 0.8 copy-start.8
  3.4 67.4 %copy-start.11 = (f32[4,512]{1,0:T(4,128)S(1)}, f32[4,512]{1,0:T(4,128)}, u32[]{:S(2)}) copy-start(f32[4,512]{1,0:T(4,128)} %taps.1) | copy-start | bytes 24580
  3.4 67.4 %copy-start.12 = (f32[512]{0:T(512)S(1)}, f32[512]{0:T(512)}, u32[]{:S(2)}) copy-start(f32[512]{0:T(512)} %param.33) | copy-start | bytes 6148
  4.3 21.8 %all-to-all-start = ((bf16[16,112,128]{2,1,0:T(8,128)(2,1)}), bf16[16,112,128]{2,1,0:T(8,128)(2,1)S(1)}, u32[]{:S(2)}, u32[]{:S(2)}) async-start(bf16[16,112,128]{2,1,0:T(8,128)(2,1)} %pack.1), calls=%async_computation | async-start | bytes 917504 | tf_op jit(solution)/shard_map/all_to_all | solution.py:418
  11.7 2.2 %collective-permute-start = (bf16[8,16,2048]{2,1,0:T(8,128)(2,1)}, bf16[8,16,2048]{2,1,0:T(8,128)(2,1)S(1)}, u32[]{:S(2)}, u32[]{:S(2)}) collective-permute-start(bf16[8,16,2048]{2,1,0:T(8,128)(2,1)} %pages_ref.1), channel_id=1, source_target_pairs={{0,8},{8,0},{1,9},{9,1},{2,10},{10,2},{3,11},{11,3},{4,12},{12,4},... | collective-permute-start | bytes 1572872 | tf_op jit(solution)/shard_map/ppermute | solution.py:50
  12.1 1.8 %collective-permute-start.1 = (bf16[1,2048]{1,0:T(2,128)(2,1)}, bf16[1,2048]{1,0:T(2,128)(2,1)S(1)}, u32[]{:S(2)}, u32[]{:S(2)}) collective-permute-start(bf16[1,2048]{1,0:T(2,128)(2,1)} %newkv_ref.1), channel_id=1, source_target_pairs={{0,8},{8,0},{1,9},{9,1},{2,10},{10,2},{3,11},{11,3},{4,12},{12,4},... | collective-permute-start | bytes 12296 | tf_op jit(solution)/shard_map/ppermute | solution.py:50
  12.2 1.6 %collective-permute-start.2 = (s32[8]{0:T(128)}, s32[8]{0:T(128)S(1)}, u32[]{:S(2)}, u32[]{:S(2)}) collective-permute-start(s32[8]{0:T(128)} %owner_ref.1), channel_id=1, source_target_pairs={{0,8},{8,0},{1,9},{9,1},{2,10},{10,2},{3,11},{11,3},{4,12},{12,4},... | collective-permute-start | bytes 104 | tf_op jit(solution)/shard_map/ppermute | solution.py:50
  12.6 1.3 %collective-permute-start.3 = (s32[8]{0:T(128)}, s32[8]{0:T(128)S(1)}, u32[]{:S(2)}, u32[]{:S(2)}) collective-permute-start(s32[8]{0:T(128)} %index_ref.1), channel_id=1, source_target_pairs={{0,8},{8,0},{1,9},{9,1},{2,10},{10,2},{3,11},{11,3},{4,12},{12,4},... | collective-permute-start | bytes 104 | tf_op jit(solution)/shard_map/ppermute | solution.py:50
  26.1 1.0 copy-start.3
  27.1 0.7 copy-start.10
  27.8 0.7 copy-start.15
  28.5 0.7 copy-start.16
  29.2 0.7 copy-start.17
  29.8 57.8 %slice-start.2 = ((s8[8388608]{0:T(1024)(128)(4,1)}), s8[4194304]{0:T(1024)(128)(4,1)S(1)}, s32[]{:S(2)}) async-start(s8[8388608]{0:T(1024)(128)(4,1)} %bitcast.13), calls=%async_computation.8 | async-start | bytes 8388608
  52.0 35.6 %slice-start.3 = ((s8[8388608]{0:T(1024)(128)(4,1)}), s8[4194304]{0:T(1024)(128)(4,1)S(1)}, s32[]{:S(2)}) async-start(s8[8388608]{0:T(1024)(128)(4,1)} %bitcast.13), calls=%async_computation.9 | async-start | bytes 8388608
  52.0 1.3 %collective-permute-start.4 = (bf16[8,16,512]{2,1,0:T(8,128)(2,1)S(1)}, bf16[8,16,512]{2,1,0:T(8,128)(2,1)S(1)}, u32[]{:S(2)}, u32[]{:S(2)}) collective-permute-start(bf16[8,16,512]{2,1,0:T(8,128)(2,1)S(1)} %all_to_all.31.own), channel_id=1, source_target_pairs={{0,8},{8,0},{1,9},{9,1},{2,10},{10,2},{3,11},{11,3},{4,12},{12,4},... | collective-permute-start | bytes 393224 | tf_op jit(solution)/shard_map/ppermute | solution.py:50
  53.4 3.4 %copy-start = (bf16[8192,512]{1,0:T(8,128)(2,1)S(1)}, bf16[8192,512]{1,0:T(8,128)(2,1)}, u32[]{:S(2)}) copy-start(bf16[8192,512]{1,0:T(8,128)(2,1)} %weight.5) | copy-start | bytes 25165828
  56.8 0.7 copy-start.9
  69.4 1.3 %collective-permute-start.5 = (bf16[8,16,512]{2,1,0:T(8,128)(2,1)S(1)}, bf16[8,16,512]{2,1,0:T(8,128)(2,1)S(1)}, u32[]{:S(2)}, u32[]{:S(2)}) collective-permute-start(bf16[8,16,512]{2,1,0:T(8,128)(2,1)S(1)} %all_to_all.32.own), channel_id=1, source_target_pairs={{0,8},{8,0},{1,9},{9,1},{2,10},{10,2},{3,11},{11,3},{4,12},{12,4},... | collective-permute-start | bytes 393224 | tf_op jit(solution)/shard_map/ppermute | solution.py:50
  70.8 18.9 %slice-start = ((s8[8388608]{0:T(1024)(128)(4,1)}), s8[4194304]{0:T(1024)(128)(4,1)S(1)}, s32[]{:S(2)}) async-start(s8[8388608]{0:T(1024)(128)(4,1)} %bitcast.11), calls=%async_computation.6 | async-start | bytes 8388608
  70.8 3.5 %copy-start.1 = (bf16[8192,512]{1,0:T(8,128)(2,1)S(1)}, bf16[8192,512]{1,0:T(8,128)(2,1)}, u32[]{:S(2)}) copy-start(bf16[8192,512]{1,0:T(8,128)(2,1)} %weight.6) | copy-start | bytes 25165828
  74.3 15.4 %slice-start.1 = ((s8[8388608]{0:T(1024)(128)(4,1)}), s8[4194304]{0:T(1024)(128)(4,1)S(1)}, s32[]{:S(2)}) async-start(s8[8388608]{0:T(1024)(128)(4,1)} %bitcast.11), calls=%async_computation.7 | async-start | bytes 8388608
  74.3 15.4 %copy-start.4 = (bf16[512,512]{1,0:T(8,128)(2,1)S(1)}, bf16[512,512]{1,0:T(8,128)(2,1)}, u32[]{:S(2)}) copy-start(bf16[512,512]{1,0:T(8,128)(2,1)} %step_proj.1) | copy-start | bytes 1572868
  74.3 15.4 %copy-start.7 = (f32[16,512]{1,0:T(8,128)S(1)}, f32[16,512]{1,0:T(8,128)}, u32[]{:S(2)}) copy-start(f32[16,512]{1,0:T(8,128)} %decay_log.1) | copy-start | bytes 98308
  74.3 15.4 %copy-start.13 = (f32[512]{0:T(512)S(1)}, f32[512]{0:T(512)}, u32[]{:S(2)}) copy-start(f32[512]{0:T(512)} %param.36) | copy-start | bytes 6148
  74.4 15.4 %copy-start.14 = (f32[512]{0:T(512)S(1)}, f32[512]{0:T(512)}, u32[]{:S(2)}) copy-start(f32[512]{0:T(512)} %param.38) | copy-start | bytes 6148
  87.6 2.1 %collective-permute-start.6 = (bf16[8,16,640]{2,1,0:T(8,128)(2,1)S(1)}, bf16[8,16,640]{2,1,0:T(8,128)(2,1)S(1)}, u32[]{:S(2)}, u32[]{:S(2)}) collective-permute-start(bf16[8,16,640]{2,1,0:T(8,128)(2,1)S(1)} %all_to_all.33.own), channel_id=1, source_target_pairs={{0,8},{8,0},{1,9},{9,1},{2,10},{10,2},{3,11},{11,3},{4,12},{12,4},... | collective-permute-start | bytes 491528 | tf_op jit(solution)/shard_map/ppermute | solution.py:50
  92.4 2.2 %collective-permute-start.7 = (bf16[8,16,512]{2,1,0:T(8,128)(2,1)S(1)}, bf16[8,16,512]{2,1,0:T(8,128)(2,1)S(1)}, u32[]{:S(2)}, u32[]{:S(2)}) collective-permute-start(bf16[8,16,512]{2,1,0:T(8,128)(2,1)S(1)} %get-tuple-element.14), channel_id=1, source_target_pairs={{0,8},{8,0},{1,9},{9,1},{2,10},{10,2},{3,11},{11,3},{4,12},{12,4},... | collective-permute-start | bytes 393224 | tf_op jit(solution)/shard_map/ppermute | solution.py:50

commit v2 on v0

v2 whole, which is shorter than its diff:
```python
import functools
import math

import jax
import jax.numpy as jnp
from jax import lax
from jax.experimental import pallas as pl
from jax.experimental.pallas import tpu as pltpu
from jax.sharding import PartitionSpec as P

D = 8192
NS = 16
DTR = 512
QH = 64
KVH = 8
HD = 128
G = QH // KVH
LANES = 128
NEGATIVE = -1e30
LOWEST = -1e20
F32 = jnp.float32
BF16 = jnp.bfloat16
VM = pltpu.VMEM


def round_up(value, step):
    return -(-value // step) * step


def vmem(count):
    return [pl.BlockSpec(memory_space=pltpu.VMEM)] * count


def smem(count):
    return [pl.BlockSpec(memory_space=pltpu.SMEM)] * count


def hbm(count):
    return [pl.BlockSpec(memory_space=pltpu.HBM)] * count


def params(mib):
    return pltpu.CompilerParams(vmem_limit_bytes=mib * 2**20)


def cost(flops, nbytes):
    return pl.CostEstimate(flops=flops, bytes_accessed=nbytes, transcendentals=0)


def swap(x):
    return lax.ppermute(x, "src", [(0, 1), (1, 0)])


def exchange(x):
    return lax.all_to_all(x, "chan", split_axis=0, concat_axis=0, tiled=True)


class Chunk:
    def __init__(self, nchan, held_tokens, blocks, steps):
        self.per = QH // nchan
        self.tokens = held_tokens
        self.owner_rows = held_tokens // LANES
        self.value = held_tokens
        self.misc = 2 * held_tokens
        self.query = self.misc + round_up(2 + self.owner_rows, 16)
        self.state = self.query + round_up(2 * self.per, 16)
        self.conv = NS * blocks
        self.state_rows = self.conv + round_up(steps * blocks, 16)
        self.rows = self.state + 2 * self.state_rows


def pack_kernel(
    nchan,
    lay,
    query_hbm,
    other_query,
    newkv_hbm,
    pages_hbm,
    state_hbm,
    conv_hbm,
    owner_hbm,
    index_hbm,
    lengths_hbm,
    out_ref,
    query,
    newkv,
    pages,
    state,
    conv,
    owners,
    indexes,
    lengths,
    sems,
):
    moves = (
        (pages_hbm, pages),
        (state_hbm, state),
        (conv_hbm, conv),
        (query_hbm, query),
        (newkv_hbm, newkv),
        (owner_hbm, owners),
        (index_hbm, indexes),
        (lengths_hbm, lengths),
    )
    copies = [pltpu.make_async_copy(src, dst, sems.at[i]) for i, (src, dst) in enumerate(moves)]
    for copy in copies:
        copy.start()
    c = lax.axis_index("src")
    held, page_tokens = pages.shape[0], pages.shape[1]
    cols = state.shape[2] // (2 * nchan)
    blocks = cols // LANES
    steps = conv.shape[0]
    rep = nchan // KVH
    for copy in copies[3:]:
        copy.wait()
    lane = lax.broadcasted_iota(jnp.int32, (1, LANES), 1)
    per_row = LANES // page_tokens
    owner_rows = []
    for i in range(lay.owner_rows):
        found = jnp.full((1, LANES), -1, jnp.int32)
        for j in range(per_row):
            owner = owners[i * per_row + j]
            left = lengths[owner] - indexes[i * per_row + j] * page_tokens
            found = jnp.where((lane // page_tokens == j) & (lane % page_tokens < left), owner, found)
        owner_rows.append(found.astype(F32))
    fill = lay.query - lay.misc - 2 - lay.owner_rows
    owner_rows.append(jnp.zeros((fill, LANES), F32))
    for d in range(nchan):
        at = (d // rep) * HD
        fresh = [newkv[0:1, x : x + HD].astype(F32) for x in (at, KVH * HD + at)]
        out_ref[d, lay.misc : lay.query, :] = jnp.concatenate(fresh + owner_rows, axis=0).astype(BF16)
        heads = []
        for ref in (query, other_query):
            for h in range(lay.per):
                place = (d * lay.per + h) * HD
                heads.append(ref[0:1, place : place + HD].astype(F32))
        spare = lay.state - lay.query - len(heads)
        if spare:
            heads.append(jnp.zeros((spare, LANES), F32))
        out_ref[d, lay.query : lay.state, :] = jnp.concatenate(heads, axis=0).astype(BF16)
    copies[0].wait()
    for d in range(nchan):
        at = (d // rep) * HD
        out_ref[d, 0 : lay.tokens, :] = pages[:, :, at : at + HD].reshape(lay.tokens, HD)
        at = KVH * HD + at
        out_ref[d, lay.value : lay.misc, :] = pages[:, :, at : at + HD].reshape(lay.tokens, HD)
    copies[1].wait()
    copies[2].wait()
    for side in range(2):
        first = (c if side == 0 else 1 - c) * (nchan * cols)
        for d in range(nchan):
            base = lay.state + side * lay.state_rows
            rows = []
            for b in range(blocks):
                lanes = pl.ds(pl.multiple_of(first + d * cols + b * LANES, LANES), LANES)
                out_ref[d, base + b * NS : base + (b + 1) * NS, :] = state[0, :, lanes].astype(BF16)
                for w in range(steps):
                    rows.append(conv[w, 0:1, lanes])
            spare = lay.state_rows - lay.conv - len(rows)
            rows.append(jnp.zeros((spare, LANES), F32))
            out_ref[d, base + lay.conv : base + lay.state_rows, :] = jnp.concatenate(rows, axis=0).astype(BF16)


def attend_kernel(lay, recv, out_ref, state_out, queries, scores):
    nchan = recv.shape[0]
    per, tokens = lay.per, lay.tokens
    c = lax.axis_index("src")
    count = nchan * per
    scale = 1.0 / math.sqrt(HD)
    contract = (((1,), (1,)), ((), ()))
    new_keys, new_values, owners = [], [], []
    for s in range(nchan):
        state_out[s] = recv[s, lay.state + lay.state_rows : lay.rows, :]
        heads = recv[s, lay.query : lay.state, :].astype(F32)
        queries[s * per : (s + 1) * per, :] = heads[0:per, :]
        queries[count + s * per : count + (s + 1) * per, :] = heads[per : 2 * per, :]
        misc = recv[s, lay.misc : lay.query, :].astype(F32)
        new_keys.append(misc[0:1, :])
        new_values.append(misc[1:2, :])
        owners.append(jnp.concatenate([misc[2 + i : 3 + i, :] for i in range(lay.owner_rows)], axis=1))
    fill = round_up(nchan, 16) - nchan
    if fill:
        new_keys.append(jnp.zeros((fill, HD), F32))
        new_values.append(jnp.zeros((fill, HD), F32))
    new_keys = jnp.concatenate(new_keys, axis=0).astype(BF16)
    new_values = jnp.concatenate(new_values, axis=0).astype(BF16)
    row = lax.broadcasted_iota(jnp.int32, (2 * count, 1), 0)
    side = jnp.where(row < count, c, 1 - c)
    request = side * nchan + (row % count) // per
    lane = lax.broadcasted_iota(jnp.int32, (1, nchan + fill), 1)
    new_owner = jnp.where(lane < nchan, c * nchan + lane, -1)
    q = queries[...].astype(BF16)
    new_scores = lax.dot_general(q, new_keys, contract, preferred_element_type=F32) * scale
    new_scores = jnp.where(request == new_owner, new_scores, NEGATIVE)
    wide = request.astype(F32)
    highest = None
    for s in range(nchan):
        part = lax.dot_general(q, recv[s, 0:tokens, :], contract, preferred_element_type=F32) * scale
        part = jnp.where(wide == owners[s], part, NEGATIVE)
        scores[:, s * tokens : (s + 1) * tokens] = part
        highest = part if highest is None else jnp.maximum(highest, part)
    peak = jnp.maximum(jnp.max(highest, axis=1, keepdims=True), jnp.max(new_scores, axis=1, keepdims=True))
    peak = jnp.maximum(peak, LOWEST)
    new_weight = jnp.exp(new_scores - peak)
    numer = jnp.dot(new_weight.astype(BF16), new_values, preferred_element_type=F32)
    summed = None
    for s in range(nchan):
        weight = jnp.exp(scores[:, s * tokens : (s + 1) * tokens] - peak)
        summed = weight if summed is None else summed + weight
        numer = numer + jnp.dot(weight.astype(BF16), recv[s, lay.value : lay.misc, :], preferred_element_type=F32)
    total = jnp.sum(summed, axis=1, keepdims=True) + jnp.sum(new_weight, axis=1, keepdims=True)
    out_ref[:, 0:HD] = numer
    lane = lax.broadcasted_iota(jnp.int32, (1, LANES), 1)
    out_ref[:, HD : HD + LANES] = jnp.where(lane == 0, peak, total)


def in_order(own, other, c):
    return jnp.where(c == 0, jnp.concatenate([own, other], axis=0), jnp.concatenate([other, own], axis=0))


def own_first(x, c):
    half = x.shape[0] // 2
    return in_order(x[:half], x[half:], c)


def merge_kernel(lay, own, other, out_ref, result):
    nchan = out_ref.shape[0]
    c = lax.axis_index("src")
    count = nchan * lay.per
    theirs = jnp.concatenate([other[count:, :], other[:count, :]], axis=0)
    ours = own[...]
    top = jnp.maximum(ours[:, HD : HD + 1], theirs[:, HD : HD + 1])
    numer, denom = 0.0, 0.0
    for part in (ours, theirs):
        factor = jnp.exp(part[:, HD : HD + 1] - top)
        numer = numer + factor * part[:, 0:HD]
        denom = denom + factor * part[:, HD + 1 : HD + 2]
    result[...] = numer / denom
    for h in range(lay.per):
        mine = result[pl.ds(h, nchan, stride=lay.per), :]
        rest = result[pl.ds(count + h, nchan, stride=lay.per), :]
        block = in_order(mine, rest, c).astype(BF16)
        for i in range(nchan):
            out_ref[i, :, h * HD : (h + 1) * HD] = block


def out_kernel(lhs, residual, weight, out_ref):
    total = residual[...].astype(F32)
    depth = lhs.shape[2]
    product = None
    for i in range(lhs.shape[0]):
        part = jnp.dot(lhs[i], weight[i * depth : (i + 1) * depth, :], preferred_element_type=F32)
        product = part if product is None else product + part
    hidden = (total + product).astype(BF16)
    for i in range(out_ref.shape[0]):
        out_ref[i] = hidden


def halves_dot(own, other, weight):
    c = lax.axis_index("src")
    nchan, depth = own.shape[0], own.shape[2]
    total = None
    for ref, half in ((own, c), (other, 1 - c)):
        for i in range(nchan):
            rows = pl.ds(pl.multiple_of((half * nchan + i) * depth, depth), depth)
            part = jnp.dot(ref[i], weight[rows, :], preferred_element_type=F32)
            total = part if total is None else total + part
    return total


def values_kernel(
    lay, own, other, arrived, other_state, taps, offset, state_proj, weight, conv_out, act_out, rms_out, proj_out
):
    c = lax.axis_index("src")
    nchan = own.shape[0]
    rows, cols = act_out.shape
    squares = jnp.zeros((rows, own.shape[2]), F32)
    for ref in (own, other):
        for i in range(nchan):
            wide = ref[i].astype(F32)
            squares = squares + wide * wide
    inverse = lax.rsqrt(jnp.sum(squares, axis=1, keepdims=True) / D + 1e-06)
    rms_out[...] = jnp.broadcast_to(inverse, rms_out.shape)
    steps = conv_out.shape[0]
    blocks = cols // LANES
    at = lay.state + lay.conv
    tails = (
        arrived[:, at : lay.state + lay.state_rows, :].astype(F32),
        other_state[:, lay.conv : lay.state_rows, :].astype(F32),
    )
    window = []
    for w in range(steps):
        sides = [jnp.concatenate([t[:, b * steps + w, :] for b in range(blocks)], axis=1) for t in tails]
        window.append(in_order(sides[0], sides[1], c))
    window.append(halves_dot(own, other, weight) * inverse)
    mixed = jnp.zeros((rows, cols), F32)
    for w in range(steps + 1):
        mixed = mixed + window[w] * taps[w : w + 1, :]
        if w > 0:
            conv_out[w - 1] = window[w]
    mixed = mixed + offset[...]
    act = mixed / (1.0 + jnp.exp(-mixed))
    act_out[...] = act
    part = lax.dot_general(act.astype(BF16), state_proj[...], (((1,), (1,)), ((), ())), preferred_element_type=F32)
    part = part.astype(BF16)
    width = part.shape[1]
    for i in range(nchan):
        proj_out[i] = jnp.zeros(proj_out.shape[1:], BF16)
        proj_out[i, :, 0:width] = part


def gates_kernel(own, other, rms, weight, out_ref):
    gate = halves_dot(own, other, weight) * rms[:, 0:1]
    out_ref[...] = gate / (1.0 + jnp.exp(-gate))


def down_product(gated, weight, half, out_ref):
    nchan, rows, cols = out_ref.shape
    step = max(cols, min(1024, nchan * cols))
    for i in range(nchan * cols // step):
        at = pl.multiple_of(half * (nchan * cols) + i * step, step)
        part = jnp.dot(gated, weight[:, pl.ds(at, step)], preferred_element_type=F32).astype(out_ref.dtype)
        for j in range(step // cols):
            out_ref[i * (step // cols) + j] = part[:, j * cols : (j + 1) * cols]


def scan_kernel(
    lay,
    own,
    other,
    arrived,
    other_state,
    act_ref,
    gate_ref,
    step_proj,
    step_bias,
    decay_log,
    skip_gain,
    weight,
    next_out,
    gated_out,
    send_out,
    turned,
    mixed,
):
    c = lax.axis_index("src")
    nchan, rows = own.shape[0], own.shape[1]
    cols = act_ref.shape[1]
    blocks = cols // LANES
    projected = jnp.zeros(own.shape[1:], F32)
    for ref in (own, other):
        for i in range(nchan):
            projected = projected + ref[i].astype(F32)
    act = act_ref[...]
    raw = jnp.dot(projected[:, 0:DTR].astype(BF16), step_proj[...], preferred_element_type=F32) + step_bias[...]
    step = jnp.maximum(raw, 0.0) + jnp.log1p(jnp.exp(-jnp.abs(raw)))
    turned[...] = jnp.zeros_like(turned)
    turned[0:rows, :] = own_first(projected[:, DTR : DTR + LANES], c)
    mats = turned[...].T
    rate = -jnp.exp(decay_log[...])
    fed = own_first(step * act, c)
    step = own_first(step, c)
    for side, states, base in ((0, arrived, lay.state), (1, other_state, 0)):
        for s in range(nchan):
            q = side * nchan + s
            place = (c if side == 0 else 1 - c) * nchan + s
            b_col = mats[0:NS, q : q + 1]
            c_col = mats[NS : 2 * NS, q : q + 1]
            for b in range(blocks):
                lanes = slice(b * LANES, (b + 1) * LANES)
                state = states[s, base + b * NS : base + (b + 1) * NS, :].astype(F32)
                after = jnp.exp(step[q : q + 1, lanes] * rate[:, lanes]) * state + fed[q : q + 1, lanes] * b_col
                next_out[place, :, lanes] = after
                mixed[q : q + 1, lanes] = jnp.sum(after * c_col, axis=0, keepdims=True)
    gated = ((own_first(mixed[...], c) + skip_gain[...] * act) * gate_ref[...]).astype(BF16)
    gated_out[...] = gated
    down_product(gated, weight, 1 - c, send_out)


def down_kernel(gated, weight, out_ref):
    down_product(gated[...], weight, lax.axis_index("src"), out_ref)


def on_device(
    residual_input,
    query_heads,
    new_keyval,
    cache_pages,
    prompt_lengths,
    page_owner,
    page_index,
    mamba_state,
    conv_state,
    out_heads,
    in_values,
    in_gates,
    conv_taps,
    conv_offset,
    state_proj,
    step_proj,
    step_bias,
    decay_log,
    skip_gain,
    mamba_down,
):
    nchan = lax.axis_size("chan")
    rows, cols = residual_input.shape
    steps = conv_state.shape[1]
    held, page_tokens = cache_pages.shape[0], cache_pages.shape[1]
    lay = Chunk(nchan, held * page_tokens, cols // LANES, steps)
    call = pl.pallas_call
    shape = jax.ShapeDtypeStruct

    other_query = swap(query_heads)
    conv_rows = jnp.transpose(conv_state, (1, 0, 2))
    packed = call(
        functools.partial(pack_kernel, nchan, lay),
        out_shape=shape((nchan, lay.rows, LANES), BF16),
        in_specs=hbm(1) + vmem(1) + hbm(7),
        out_specs=vmem(1)[0],
        scratch_shapes=[
            VM(query_heads.shape, BF16),
            VM(new_keyval.shape, BF16),
            VM(cache_pages.shape, BF16),
            VM(mamba_state.shape, F32),
            VM(conv_rows.shape, F32),
            pltpu.SMEM(page_owner.shape, jnp.int32),
            pltpu.SMEM(page_index.shape, jnp.int32),
            pltpu.SMEM(prompt_lengths.shape, jnp.int32),
            pltpu.SemaphoreType.DMA((8,)),
        ],
        compiler_params=params(16 if held < 16 else 40),
        name="pack",
    )(
        query_heads,
        other_query,
        new_keyval,
        cache_pages,
        mamba_state,
        conv_rows,
        page_owner,
        page_index,
        prompt_lengths,
    )
    arrived = exchange(packed)

    pairs = rows * lay.per
    partial, state_send = call(
        functools.partial(attend_kernel, lay),
        out_shape=(shape((pairs, HD + LANES), F32), shape((nchan, lay.state_rows, LANES), BF16)),
        in_specs=vmem(1),
        out_specs=tuple(vmem(2)),
        scratch_shapes=[VM((pairs, HD), F32), VM((pairs, nchan * lay.tokens), F32)],
        compiler_params=params(8 if held < 16 else 48),
        name="attend",
    )(arrived)
    other_partial = swap(partial)
    other_state = swap(state_send)
    attended = call(
        functools.partial(merge_kernel, lay),
        out_shape=shape((nchan, rows, lay.per * HD), BF16),
        in_specs=vmem(2),
        out_specs=vmem(1)[0],
        scratch_shapes=[VM((pairs, HD), F32)],
        compiler_params=params(8),
        name="merge",
    )(partial, other_partial)
    features = exchange(attended)

    weight_cost = cost(2 * rows * D * cols, 2 * D * cols)
    hidden = call(
        out_kernel,
        out_shape=shape((nchan, rows, cols), BF16),
        in_specs=vmem(3),
        out_specs=vmem(1)[0],
        compiler_params=params(16),
        cost_estimate=weight_cost,
        name="out",
    )(features, residual_input, out_heads)
    hid_own = exchange(hidden)
    hid_other = swap(hid_own)

    width = round_up(state_proj.shape[1], LANES)
    conv_next, act, rms, part = call(
        functools.partial(values_kernel, lay),
        out_shape=(
            shape((steps, rows, cols), F32),
            shape((rows, cols), F32),
            shape((rows, LANES), F32),
            shape((nchan, rows, width), BF16),
        ),
        in_specs=vmem(8),
        out_specs=tuple(vmem(4)),
        compiler_params=params(16),
        cost_estimate=weight_cost,
        name="values",
    )(hid_own, hid_other, arrived, other_state, conv_taps, conv_offset[None, :], state_proj.T, in_values)
    proj_own = exchange(part)
    gate = call(
        gates_kernel,
        out_shape=shape((rows, cols), F32),
        in_specs=vmem(4),
        out_specs=vmem(1)[0],
        compiler_params=params(16),
        cost_estimate=weight_cost,
        name="gates",
    )(hid_own, hid_other, rms, in_gates)
    proj_own, gate = lax.optimization_barrier((proj_own, gate))
    proj_other = swap(proj_own)

    mamba_next, gated, send = call(
        functools.partial(scan_kernel, lay),
        out_shape=(
            shape((rows, NS, cols), F32),
            shape((rows, cols), BF16),
            shape((nchan, rows, cols), BF16),
        ),
        in_specs=vmem(11),
        out_specs=tuple(vmem(3)),
        scratch_shapes=[VM((LANES, LANES), F32), VM((rows, cols), F32)],
        compiler_params=params(16),
        name="scan",
    )(
        proj_own,
        proj_other,
        arrived,
        other_state,
        act,
        gate,
        step_proj,
        step_bias[None, :],
        decay_log,
        skip_gain[None, :],
        mamba_down,
    )
    taken = swap(send)
    keep = call(
        down_kernel,
        out_shape=shape((nchan, rows, cols), F32),
        in_specs=vmem(2),
        out_specs=vmem(1)[0],
        compiler_params=params(16),
        cost_estimate=cost(rows * D * cols, D * cols),
        name="down",
    )(gated, mamba_down)
    summed = (keep + taken.astype(F32)).astype(BF16)
    final = exchange(summed)
    down_sum = jnp.sum(final.astype(F32), axis=0)
    hidden_out = (hidden[0].astype(F32) + down_sum).astype(BF16)
    return (hidden_out, mamba_next, jnp.transpose(conv_next, (1, 0, 2)))


def solution(mesh):
    owners = ("groups", "src", "chan")
    channels = ("src", "chan")
    placed = (
        P("groups", channels),
        P(owners, None),
        P(owners, None),
        P(owners, None, None),
        P("groups"),
        P(owners),
        P(owners),
        P(owners, None, None),
        P(owners, None, None),
        P(None, channels),
        P(None, channels),
        P(None, channels),
        P(None, channels),
        P(channels),
        P(channels, None),
        P(None, channels),
        P(channels),
        P(None, channels),
        P(channels),
        P(channels, None),
    )
    return jax.shard_map(
        on_device,
        mesh=mesh,
        in_specs=placed,
        out_specs=(P("groups", channels), P("groups", None, channels), P("groups", None, channels)),
        check_vma=False,
    )
```

time: 408 us -> 113 us (0.28); the launches traced: 401 us -> 112 us
  other arithmetic: 94.8 us -> 1.39 us
  blocking collectives: 126 us -> 53.1 us
  waiting for transfers between devices: 62.8 us -> 15.9 us
  local copies, waits for them, and re-layouts: 57.5 us -> 24 us
  matrix products: 20.9 us -> 0 us
  starting transfers between devices: 24.7 us -> 7.7 us
  between operations: 14.6 us -> 0.78 us
  Pallas kernels: 0 us -> 9.29 us
    unnamed x3 -> x0, other arithmetic: 76.8 us -> none
    all_gather x2 -> x0, blocking collectives: 65.5 us -> none  [the longest x1 35.6 us: on_device(): lax.all_gather(attended, ('src', 'chan'), axis=0, tiled=True)]
    psum x1 -> x0, blocking collectives: 60.4 us -> none  [on_device(): lax.psum(jnp.dot(x_low, state_proj, preferred_element_type=jnp.float32),...]
    all_to_all x0 -> x3, blocking collectives: none -> 53.1 us  [exchange(): return lax.all_to_all(x, 'chan', split_axis=0, concat_axis=0, tiled=True)]
    reduce_scatter x1 -> x0, waiting for transfers between devices: 51.4 us -> none  [on_device(): lax.psum_scatter(lax.dot_general(mamba_down, gated, (((0,), (1,)), ((), (...]
    unnamed x41 -> x42, local copies, waits for them, and re-layouts: 50.1 us -> 24 us
    dot_general x9 -> x0, matrix products: 20.9 us -> none  [the longest x1 8.94 us: on_device(): lax.dot_general(mamba_down, gated, (((0,), (1,)), ((), ())), preferred_el...]
    all_to_all x4 -> x2, starting transfers between devices: 24.1 us -> 6.97 us  [exchange(): return lax.all_to_all(x, 'chan', split_axis=0, concat_axis=0, tiled=True)]
  transfers between devices with their start and end apart: 5 -> 8, of which waited for: 2 -> 6; matrix products, arithmetic and copies ran while one was open for 34% -> 0% of each run, Pallas kernels for 0% -> 2%
where the time goes in v2:
time: 113 us; the launch traced here: 112 us
  blocking collectives  53.1 us (47%)
  local copies, waits for them, and re-layouts  24 us (21%)
  waiting for transfers between devices  15.9 us (14%)
  Pallas kernels  9.29 us (8%)
  starting transfers between devices  7.7 us (7%)
  other arithmetic  1.39 us (1%)
    all_to_all x3, blocking collectives, exchange(): return lax.all_to_all(x, 'chan', split_axis=0, concat_axis=0, tiled=True)  53.1 us
    unnamed x42, local copies, waits for them, and re-layouts  24 us
    all_to_all x2, waiting for transfers between devices, exchange(): return lax.all_to_all(x, 'chan', split_axis=0, concat_axis=0, tiled=True)  10.7 us
    all_to_all x2, starting transfers between devices, exchange(): return lax.all_to_all(x, 'chan', split_axis=0, concat_axis=0, tiled=True)  6.97 us
    ppermute x6, waiting for transfers between devices, swap(): return lax.ppermute(x, 'src', [(0, 1), (1, 0)])  5.14 us
  transfers between devices with their start and end apart: 8, of which 6 were waited for; matrix products, arithmetic and copies ran while one was open for 0% of the time, Pallas kernels for 2%

profile of v2, /device:TPU:0, one launch (start us, length us, event | category | flops | bytes accessed | tf_op | source)
XLA Modules:
  0.0 112.1 jit_solution(6829365013350914126)
XLA Ops:
  0.6 0.0 copy-start.5
  0.6 0.5 collective-permute-start
  1.2 1.1 collective-permute-done.other_query
  2.2 0.0 copy-start.6
  2.2 1.0 copy-done.6
  3.3 0.0 copy-start.7
  3.3 1.0 copy-done.7
  4.3 0.0 copy-start.9
  4.3 0.9 copy-done.9
  5.2 0.0 copy-start.10
  5.2 0.8 copy-done.10
  6.0 0.0 copy-start.13
  6.0 0.7 copy-done.13
  6.7 0.0 copy-start.18
  6.7 0.7 copy-done.18
  7.3 0.0 copy-start.19
  7.3 0.7 copy-done.19
  8.0 0.0 copy-start.20
  8.0 0.7 copy-done.20
  8.6 0.0 copy-start.14
  8.6 0.0 copy-start.15
  8.6 1.2 %pack.1 = bf16[8,448,128]{2,1,0:T(8,128)(2,1)S(1)} custom-call(bf16[1,8192]{1,0:T(2,128)(2,1)S(1)} %copy-done.10, bf16[1,8192]{1,0:T(2,128)(2,1)S(1)} %collective-permute-done.other_query, bf16[1,2048]{1,0:T(2,128)(2,1)S(1)} %copy-done.13, bf16[8,16,2048]{2,1,0:T(8,128)(2,1)S(1)} %copy-done.6, f32[1,16,8192]{2,1,0:T(8,128)S(1)} %copy-done.7, ...), custom_call_target="tpu_custom_call" | custom-call | tf_op jit(solution)/shard_map/pack/pallas_call | solution.py:416
  9.9 30.6 %all_to_all.25.recv.arrived = bf16[8,448,128]{2,1,0:T(8,128)(2,1)S(1)} all-to-all(bf16[8,448,128]{2,1,0:T(8,128)(2,1)S(1)} %pack.1), channel_id=1, replica_groups=mesh['groups'=2,'src'=2,'chan'=8] {'chan'}, dimensions={0} | all-to-all | bytes 1835008 | tf_op jit(solution)/shard_map/all_to_all | solution.py:55
  40.4 0.7 attend.1
  41.2 0.1 collective-permute-start.1
  41.3 1.3 %collective-permute-done.1.other = f32[128,256]{1,0:T(8,128)S(1)} collective-permute-done((f32[128,256]{1,0:T(8,128)S(1)}, f32[128,256]{1,0:T(8,128)S(1)}, u32[]{:S(2)}, u32[]{:S(2)}) %collective-permute-start.1) | collective-permute-done | bytes 131104 | tf_op jit(solution)/shard_map/ppermute | solution.py:51
  42.6 0.3 merge.1
  42.9 12.3 %all_to_all.26.lhs = bf16[8,16,1024]{2,1,0:T(8,128)(2,1)S(1)} all-to-all(bf16[8,16,1024]{2,1,0:T(8,128)(2,1)S(1)} %merge.1), channel_id=1, replica_groups=mesh['groups'=2,'src'=2,'chan'=8] {'chan'}, dimensions={0} | all-to-all | bytes 524288 | tf_op jit(solution)/shard_map/all_to_all | solution.py:55
  55.2 0.0 copy-start.4
  55.2 3.4 %copy-done.4 = bf16[8192,512]{1,0:T(8,128)(2,1)S(1)} copy-done((bf16[8192,512]{1,0:T(8,128)(2,1)S(1)}, bf16[8192,512]{1,0:T(8,128)(2,1)}, u32[]{:S(2)}) %copy-start.4) | copy-done | bytes 8388632
  58.5 0.7 copy-done.12
  59.3 1.9 %out.1 = bf16[8,16,512]{2,1,0:T(8,128)(2,1)} custom-call(bf16[8,16,1024]{2,1,0:T(8,128)(2,1)S(1)} %all_to_all.26.lhs, bf16[16,512]{1,0:T(8,128)(2,1)S(1)} %copy-done.12, bf16[8192,512]{1,0:T(8,128)(2,1)S(1)} %copy-done.4), custom_call_target="tpu_custom_call" | custom-call | flops 134217728 | bytes 8388608 | tf_op jit(solution)/shard_map/out/pallas_call | solution.py:471
  61.1 3.6 %all-to-all-start.2 = ((bf16[8,16,512]{2,1,0:T(8,128)(2,1)}), bf16[8,16,512]{2,1,0:T(8,128)(2,1)S(1)}, u32[]{:S(2)}, u32[]{:S(2)}) async-start(bf16[8,16,512]{2,1,0:T(8,128)(2,1)} %out.1), calls=%async_computation.2 | async-start | bytes 262144 | tf_op jit(solution)/shard_map/all_to_all | solution.py:55
  64.7 0.0 collective-permute-start.3
  64.7 7.3 %all-to-all-done.2.own = bf16[8,16,512]{2,1,0:T(8,128)(2,1)S(1)} async-done(((bf16[8,16,512]{2,1,0:T(8,128)(2,1)}), bf16[8,16,512]{2,1,0:T(8,128)(2,1)S(1)}, u32[]{:S(2)}, u32[]{:S(2)}) %all-to-all-start.2) | async-done | bytes 131104 | tf_op jit(solution)/shard_map/all_to_all | solution.py:55
  72.0 0.0 collective-permute-start.2
  72.1 0.0 collective-permute-done.3.other_state
  72.1 1.3 %collective-permute-done.2.other = bf16[8,16,512]{2,1,0:T(8,128)(2,1)S(1)} collective-permute-done((bf16[8,16,512]{2,1,0:T(8,128)(2,1)S(1)}, bf16[8,16,512]{2,1,0:T(8,128)(2,1)S(1)}, u32[]{:S(2)}, u32[]{:S(2)}) %collective-permute-start.2) | collective-permute-done | bytes 131104 | tf_op jit(solution)/shard_map/ppermute | solution.py:51
  73.4 0.0 copy-done.5
  73.4 0.0 copy-done.14
  73.4 0.0 copy-done.15
  73.4 0.0 copy-start.2
  73.4 3.4 %copy-done.2 = bf16[8192,512]{1,0:T(8,128)(2,1)S(1)} copy-done((bf16[8192,512]{1,0:T(8,128)(2,1)S(1)}, bf16[8192,512]{1,0:T(8,128)(2,1)}, u32[]{:S(2)}) %copy-start.2) | copy-done | bytes 8388632
  76.8 2.1 %values.1 = (f32[3,16,512]{2,1,0:T(8,128)}, f32[16,512]{1,0:T(8,128)S(1)}, f32[16,128]{1,0:T(8,128)S(1)}, bf16[8,16,640]{2,1,0:T(8,128)(2,1)}) custom-call(bf16[8,16,512]{2,1,0:T(8,128)(2,1)S(1)} %all-to-all-done.2.own, bf16[8,16,512]{2,1,0:T(8,128)(2,1)S(1)} %collective-permute-done.2.other, bf16[8,448,128]{2,1,0:T(8,128)(2,1)S(1)} %all_to_all.25.recv.arrived, ...), custom_call_target="tpu_custom_call" | custom-call | flops 134217728 | bytes 8388608 | tf_op jit(solution)/shard_map/values/pallas_call | solution.py:484
  78.9 3.4 %all-to-all-start.3 = ((bf16[8,16,640]{2,1,0:T(8,128)(2,1)}), bf16[8,16,640]{2,1,0:T(8,128)(2,1)S(1)}, u32[]{:S(2)}, u32[]{:S(2)}) async-start(bf16[8,16,640]{2,1,0:T(8,128)(2,1)} %get-tuple-element.16), calls=%async_computation.3 | async-start | bytes 327680 | tf_op jit(solution)/shard_map/all_to_all | solution.py:55
  82.3 0.0 copy-start.3
  82.3 3.4 %copy-done.3 = bf16[8192,512]{1,0:T(8,128)(2,1)S(1)} copy-done((bf16[8192,512]{1,0:T(8,128)(2,1)S(1)}, bf16[8192,512]{1,0:T(8,128)(2,1)}, u32[]{:S(2)}) %copy-start.3) | copy-done | bytes 8388632
  85.7 1.2 %gates.1.gate_ref = f32[16,512]{1,0:T(8,128)S(1)} custom-call(bf16[8,16,512]{2,1,0:T(8,128)(2,1)S(1)} %all-to-all-done.2.own, bf16[8,16,512]{2,1,0:T(8,128)(2,1)S(1)} %collective-permute-done.2.other, f32[16,128]{1,0:T(8,128)S(1)} %get-tuple-element.17.rms, bf16[8192,512]{1,0:T(8,128)(2,1)S(1)} %copy-done.3), custom_call_target="tpu_custom_call" | custom-call | flops 134217728 | bytes 8388608 | tf_op jit(solution)/shard_map/gates/pallas_call | solution.py:499
  86.9 3.4 %all-to-all-done.3.own = bf16[8,16,640]{2,1,0:T(8,128)(2,1)S(1)} async-done(((bf16[8,16,640]{2,1,0:T(8,128)(2,1)}), bf16[8,16,640]{2,1,0:T(8,128)(2,1)S(1)}, u32[]{:S(2)}, u32[]{:S(2)}) %all-to-all-start.3) | async-done | bytes 163872 | tf_op jit(solution)/shard_map/all_to_all | solution.py:55
  90.3 0.0 collective-permute-start.4
  90.3 1.4 %collective-permute-done.4.other = bf16[8,16,640]{2,1,0:T(8,128)(2,1)S(1)} collective-permute-done((bf16[8,16,640]{2,1,0:T(8,128)(2,1)S(1)}, bf16[8,16,640]{2,1,0:T(8,128)(2,1)S(1)}, u32[]{:S(2)}, u32[]{:S(2)}) %collective-permute-start.4) | collective-permute-done | bytes 163872 | tf_op jit(solution)/shard_map/ppermute | solution.py:51
  91.7 0.0 copy-done.8
  91.7 0.0 copy-done.11
  91.7 0.0 copy-done.16
  91.7 0.0 copy-done.17
  91.7 0.0 copy-start
  91.7 3.4 %copy-done = bf16[512,8192]{1,0:T(8,128)(2,1)S(1)} copy-done((bf16[512,8192]{1,0:T(8,128)(2,1)S(1)}, bf16[512,8192]{1,0:T(8,128)(2,1)}, u32[]{:S(2)}) %copy-start) | copy-done | bytes 8388632
  95.1 1.3 %scan.1 = (f32[16,16,512]{2,1,0:T(8,128)}, bf16[16,512]{1,0:T(8,128)(2,1)S(1)}, bf16[8,16,512]{2,1,0:T(8,128)(2,1)S(1)}) custom-call(bf16[8,16,640]{2,1,0:T(8,128)(2,1)S(1)} %all-to-all-done.3.own, bf16[8,16,640]{2,1,0:T(8,128)(2,1)S(1)} %collective-permute-done.4.other, bf16[8,448,128]{2,1,0:T(8,128)(2,1)S(1)} %all_to_all.25.recv.arrived, ...), custom_call_target="tpu_custom_call" | custom-call | tf_op jit(solution)/shard_map/scan/pallas_call | solution.py:511
  96.4 0.1 collective-permute-start.5
  96.5 3.4 %copy-done.1 = bf16[512,8192]{1,0:T(8,128)(2,1)S(1)} copy-done((bf16[512,8192]{1,0:T(8,128)(2,1)S(1)}, bf16[512,8192]{1,0:T(8,128)(2,1)}, u32[]{:S(2)}) %copy-start.1) | copy-done | bytes 8388632
  99.9 0.6 down.1
  100.5 0.0 collective-permute-done.5
  100.6 10.2 %all_to_all.27 = bf16[8,16,512]{2,1,0:T(8,128)(2,1)S(1)} all-to-all(bf16[8,16,512]{2,1,0:T(8,128)(2,1)S(1)} %add_convert_fusion), channel_id=1, replica_groups=mesh['groups'=2,'src'=2,'chan'=8] {'chan'}, dimensions={0} | all-to-all | bytes 262144 | tf_op jit(solution)/shard_map/all_to_all | solution.py:55
  110.8 1.3 %fusion = bf16[16,512]{1,0:T(8,128)(2,1)} fusion(f32[16,512]{1,0:T(8,128)S(1)} %convert_reduce_fusion, bf16[8,16,512]{2,1,0:T(8,128)(2,1)} %out.1), kind=kLoop, calls=%fused_computation.3 | loop fusion | flops 24576 | bytes 65536 | tf_op jit(solution)/shard_map/convert_element_type | solution.py:549
  (8 shorter events, 0.1 us)
Async XLA Ops:
  0.6 72.8 %copy-start.5 = (bf16[512,544]{0,1:T(8,128)(2,1)S(1)}, bf16[512,544]{0,1:T(8,128)(2,1)}, u32[]{:S(2)}) copy-start(bf16[512,544]{0,1:T(8,128)(2,1)} %param.34) | copy-start | bytes 1671172
  0.6 1.6 %collective-permute-start = (bf16[1,8192]{1,0:T(2,128)(2,1)}, bf16[1,8192]{1,0:T(2,128)(2,1)S(1)}, u32[]{:S(2)}, u32[]{:S(2)}) collective-permute-start(bf16[1,8192]{1,0:T(2,128)(2,1)} %query_hbm.1), channel_id=1, source_target_pairs={{0,8},{8,0},{1,9},{9,1},{2,10},{10,2},{3,11},{11,3},{4,12},{12,4},... | collective-permute-start | bytes 49160 | tf_op jit(solution)/shard_map/ppermute | solution.py:51
  2.2 1.0 copy-start.6
  3.3 1.0 copy-start.7
  4.3 0.9 copy-start.9
  5.2 0.8 copy-start.10
  6.0 0.7 copy-start.13
  6.7 0.7 copy-start.18
  7.3 0.7 copy-start.19
  8.0 0.7 copy-start.20
  8.6 64.8 %copy-start.14 = (f32[4,512]{1,0:T(4,128)S(1)}, f32[4,512]{1,0:T(4,128)}, u32[]{:S(2)}) copy-start(f32[4,512]{1,0:T(4,128)} %taps.1) | copy-start | bytes 24580
  8.6 64.8 %copy-start.15 = (f32[512]{0:T(512)S(1)}, f32[512]{0:T(512)}, u32[]{:S(2)}) copy-start(f32[512]{0:T(512)} %param.33) | copy-start | bytes 6148
  41.2 1.4 %collective-permute-start.1 = (f32[128,256]{1,0:T(8,128)S(1)}, f32[128,256]{1,0:T(8,128)S(1)}, u32[]{:S(2)}, u32[]{:S(2)}) collective-permute-start(f32[128,256]{1,0:T(8,128)S(1)} %get-tuple-element.14.own), channel_id=1, source_target_pairs={{0,8},{8,0},{1,9},{9,1},{2,10},{10,2},{3,11},{11,3},{4,12},{12,4},... | collective-permute-start | bytes 393224 | tf_op jit(solution)/shard_map/ppermute | solution.py:51
  55.2 3.4 %copy-start.4 = (bf16[8192,512]{1,0:T(8,128)(2,1)S(1)}, bf16[8192,512]{1,0:T(8,128)(2,1)}, u32[]{:S(2)}) copy-start(bf16[8192,512]{1,0:T(8,128)(2,1)} %weight.5) | copy-start | bytes 25165828
  58.5 0.7 copy-start.12
  61.1 10.9 %all-to-all-start.2 = ((bf16[8,16,512]{2,1,0:T(8,128)(2,1)}), bf16[8,16,512]{2,1,0:T(8,128)(2,1)S(1)}, u32[]{:S(2)}, u32[]{:S(2)}) async-start(bf16[8,16,512]{2,1,0:T(8,128)(2,1)} %out.1), calls=%async_computation.2 | async-start | bytes 262144 | tf_op jit(solution)/shard_map/all_to_all | solution.py:55
  64.7 7.3 %collective-permute-start.3 = (bf16[8,80,128]{2,1,0:T(8,128)(2,1)S(1)}, bf16[8,80,128]{2,1,0:T(8,128)(2,1)S(1)}, u32[]{:S(2)}, u32[]{:S(2)}) collective-permute-start(bf16[8,80,128]{2,1,0:T(8,128)(2,1)S(1)} %get-tuple-element.15), channel_id=1, source_target_pairs={{0,8},{8,0},{1,9},{9,1},{2,10},{10,2},{3,11},{11,3},{4,12},{12,4},... | collective-permute-start | bytes 491528 | tf_op jit(solution)/shard_map/ppermute | solution.py:51
  72.0 1.3 %collective-permute-start.2 = (bf16[8,16,512]{2,1,0:T(8,128)(2,1)S(1)}, bf16[8,16,512]{2,1,0:T(8,128)(2,1)S(1)}, u32[]{:S(2)}, u32[]{:S(2)}) collective-permute-start(bf16[8,16,512]{2,1,0:T(8,128)(2,1)S(1)} %all-to-all-done.2.own), channel_id=1, source_target_pairs={{0,8},{8,0},{1,9},{9,1},{2,10},{10,2},{3,11},{11,3},{4,12},{12,4},... | collective-permute-start | bytes 393224 | tf_op jit(solution)/shard_map/ppermute | solution.py:51
  73.4 3.4 %copy-start.2 = (bf16[8192,512]{1,0:T(8,128)(2,1)S(1)}, bf16[8192,512]{1,0:T(8,128)(2,1)}, u32[]{:S(2)}) copy-start(bf16[8192,512]{1,0:T(8,128)(2,1)} %weight.6) | copy-start | bytes 25165828
  76.8 14.9 %copy-start.8 = (bf16[512,512]{1,0:T(8,128)(2,1)S(1)}, bf16[512,512]{1,0:T(8,128)(2,1)}, u32[]{:S(2)}) copy-start(bf16[512,512]{1,0:T(8,128)(2,1)} %step_proj.1) | copy-start | bytes 1572868
  76.8 14.9 %copy-start.11 = (f32[16,512]{1,0:T(8,128)S(1)}, f32[16,512]{1,0:T(8,128)}, u32[]{:S(2)}) copy-start(f32[16,512]{1,0:T(8,128)} %decay_log.1) | copy-start | bytes 98308
  76.8 14.9 %copy-start.16 = (f32[512]{0:T(512)S(1)}, f32[512]{0:T(512)}, u32[]{:S(2)}) copy-start(f32[512]{0:T(512)} %param.36) | copy-start | bytes 6148
  76.8 14.9 %copy-start.17 = (f32[512]{0:T(512)S(1)}, f32[512]{0:T(512)}, u32[]{:S(2)}) copy-start(f32[512]{0:T(512)} %param.38) | copy-start | bytes 6148
  78.9 11.4 %all-to-all-start.3 = ((bf16[8,16,640]{2,1,0:T(8,128)(2,1)}), bf16[8,16,640]{2,1,0:T(8,128)(2,1)S(1)}, u32[]{:S(2)}, u32[]{:S(2)}) async-start(bf16[8,16,640]{2,1,0:T(8,128)(2,1)} %get-tuple-element.16), calls=%async_computation.3 | async-start | bytes 327680 | tf_op jit(solution)/shard_map/all_to_all | solution.py:55
  82.3 3.4 %copy-start.3 = (bf16[8192,512]{1,0:T(8,128)(2,1)S(1)}, bf16[8192,512]{1,0:T(8,128)(2,1)}, u32[]{:S(2)}) copy-start(bf16[8192,512]{1,0:T(8,128)(2,1)} %weight.7) | copy-start | bytes 25165828
  90.3 1.4 %collective-permute-start.4 = (bf16[8,16,640]{2,1,0:T(8,128)(2,1)S(1)}, bf16[8,16,640]{2,1,0:T(8,128)(2,1)S(1)}, u32[]{:S(2)}, u32[]{:S(2)}) collective-permute-start(bf16[8,16,640]{2,1,0:T(8,128)(2,1)S(1)} %all-to-all-done.3.own), channel_id=1, source_target_pairs={{0,8},{8,0},{1,9},{9,1},{2,10},{10,2},{3,11},{11,3},{4,12},{12,4},... | collective-permute-start | bytes 491528 | tf_op jit(solution)/shard_map/ppermute | solution.py:51
  91.7 3.4 %copy-start = (bf16[512,8192]{1,0:T(8,128)(2,1)S(1)}, bf16[512,8192]{1,0:T(8,128)(2,1)}, u32[]{:S(2)}) copy-start(bf16[512,8192]{1,0:T(8,128)(2,1)} %weight.9) | copy-start | bytes 25165828
  96.4 4.2 %collective-permute-start.5 = (bf16[8,16,512]{2,1,0:T(8,128)(2,1)S(1)}, bf16[8,16,512]{2,1,0:T(8,128)(2,1)S(1)}, u32[]{:S(2)}, u32[]{:S(2)}) collective-permute-start(bf16[8,16,512]{2,1,0:T(8,128)(2,1)S(1)} %get-tuple-element.22), channel_id=1, source_target_pairs={{0,8},{8,0},{1,9},{9,1},{2,10},{10,2},{3,11},{11,3},{4,12},{12,4},... | collective-permute-start | bytes 393224 | tf_op jit(solution)/shard_map/ppermute | solution.py:51
  96.5 3.4 %copy-start.1 = (bf16[512,8192]{1,0:T(8,128)(2,1)S(1)}, bf16[512,8192]{1,0:T(8,128)(2,1)}, u32[]{:S(2)}) copy-start(bf16[512,8192]{1,0:T(8,128)(2,1)} %weight.9) | copy-start | bytes 25165828

commit v3 on v2

--- a/solution.py
+++ b/solution.py
@@ -18,6 +18,8 @@
 LANES = 128
 NEGATIVE = -1e30
 LOWEST = -1e20
+STREAM_MIB = 50
+SHORT = 3 * 10**9
 F32 = jnp.float32
 BF16 = jnp.bfloat16
 VM = pltpu.VMEM
@@ -63,29 +65,27 @@
         self.value = held_tokens
         self.misc = 2 * held_tokens
         self.query = self.misc + round_up(2 + self.owner_rows, 16)
-        self.state = self.query + round_up(2 * self.per, 16)
-        self.conv = NS * blocks
-        self.state_rows = self.conv + round_up(steps * blocks, 16)
-        self.rows = self.state + 2 * self.state_rows
+        self.conv = self.query + round_up(2 * self.per, 16)
+        self.conv_rows = round_up(steps * blocks, 16)
+        self.rows = self.conv + 2 * self.conv_rows
 
 
 def pack_kernel(
     nchan,
     lay,
     query_hbm,
-    other_query,
+    other_hbm,
     newkv_hbm,
     pages_hbm,
-    state_hbm,
     conv_hbm,
     owner_hbm,
     index_hbm,
     lengths_hbm,
     out_ref,
     query,
+    other_query,
     newkv,
     pages,
-    state,
     conv,
     owners,
     indexes,
@@ -94,9 +94,9 @@
 ):
     moves = (
         (pages_hbm, pages),
-        (state_hbm, state),
         (conv_hbm, conv),
         (query_hbm, query),
+        (other_hbm, other_query),
         (newkv_hbm, newkv),
         (owner_hbm, owners),
         (index_hbm, indexes),
@@ -106,12 +106,12 @@
     for copy in copies:
         copy.start()
     c = lax.axis_index("src")
-    held, page_tokens = pages.shape[0], pages.shape[1]
-    cols = state.shape[2] // (2 * nchan)
+    page_tokens = pages.shape[1]
+    cols = conv.shape[2] // (2 * nchan)
     blocks = cols // LANES
     steps = conv.shape[0]
     rep = nchan // KVH
-    for copy in copies[3:]:
+    for copy in copies[1:]:
         copy.wait()
     lane = lax.broadcasted_iota(jnp.int32, (1, LANES), 1)
     per_row = LANES // page_tokens
@@ -134,34 +134,40 @@
             for h in range(lay.per):
                 place = (d * lay.per + h) * HD
                 heads.append(ref[0:1, place : place + HD].astype(F32))
-        spare = lay.state - lay.query - len(heads)
+        spare = lay.conv - lay.query - len(heads)
         if spare:
             heads.append(jnp.zeros((spare, LANES), F32))
-        out_ref[d, lay.query : lay.state, :] = jnp.concatenate(heads, axis=0).astype(BF16)
+        out_ref[d, lay.query : lay.conv, :] = jnp.concatenate(heads, axis=0).astype(BF16)
+    for side in range(2):
+        first = (c if side == 0 else 1 - c) * (nchan * cols)
+        for d in range(nchan):
+            rows = []
+            for b in range(blocks):
+                lanes = pl.ds(pl.multiple_of(first + d * cols + b * LANES, LANES), LANES)
+                for w in range(steps):
+                    rows.append(conv[w, 0:1, lanes])
+            rows.append(jnp.zeros((lay.conv_rows - len(rows), LANES), F32))
+            base = lay.conv + side * lay.conv_rows
+            out_ref[d, base : base + lay.conv_rows, :] = jnp.concatenate(rows, axis=0).astype(BF16)
     copies[0].wait()
     for d in range(nchan):
         at = (d // rep) * HD
         out_ref[d, 0 : lay.tokens, :] = pages[:, :, at : at + HD].reshape(lay.tokens, HD)
         at = KVH * HD + at
         out_ref[d, lay.value : lay.misc, :] = pages[:, :, at : at + HD].reshape(lay.tokens, HD)
-    copies[1].wait()
-    copies[2].wait()
-    for side in range(2):
-        first = (c if side == 0 else 1 - c) * (nchan * cols)
+
+
+def load_kernel(residual, state, residual_out, same, cross):
+    c = lax.axis_index("src")
+    nchan, _, cols = same.shape
+    residual_out[...] = residual[...]
+    for ref, half in ((same, c), (cross, 1 - c)):
         for d in range(nchan):
-            base = lay.state + side * lay.state_rows
-            rows = []
-            for b in range(blocks):
-                lanes = pl.ds(pl.multiple_of(first + d * cols + b * LANES, LANES), LANES)
-                out_ref[d, base + b * NS : base + (b + 1) * NS, :] = state[0, :, lanes].astype(BF16)
-                for w in range(steps):
-                    rows.append(conv[w, 0:1, lanes])
-            spare = lay.state_rows - lay.conv - len(rows)
-            rows.append(jnp.zeros((spare, LANES), F32))
-            out_ref[d, base + lay.conv : base + lay.state_rows, :] = jnp.concatenate(rows, axis=0).astype(BF16)
-
-
-def attend_kernel(lay, recv, out_ref, state_out, queries, scores):
+            lanes = pl.ds(pl.multiple_of((half * nchan + d) * cols, cols), cols)
+            ref[d] = state[0, :, lanes].astype(BF16)
+
+
+def attend_kernel(lay, recv, out_ref, conv_out, queries, scores):
     nchan = recv.shape[0]
     per, tokens = lay.per, lay.tokens
     c = lax.axis_index("src")
@@ -170,8 +176,8 @@
     contract = (((1,), (1,)), ((), ()))
     new_keys, new_values, owners = [], [], []
     for s in range(nchan):
-        state_out[s] = recv[s, lay.state + lay.state_rows : lay.rows, :]
-        heads = recv[s, lay.query : lay.state, :].astype(F32)
+        conv_out[s] = recv[s, lay.conv + lay.conv_rows : lay.rows, :]
+        heads = recv[s, lay.query : lay.conv, :].astype(F32)
         queries[s * per : (s + 1) * per, :] = heads[0:per, :]
         queries[count + s * per : count + (s + 1) * per, :] = heads[per : 2 * per, :]
         misc = recv[s, lay.misc : lay.query, :].astype(F32)
@@ -244,55 +250,79 @@
             out_ref[i, :, h * HD : (h + 1) * HD] = block
 
 
-def out_kernel(lhs, residual, weight, out_ref):
+def stream(weight, buffer, sems, starts):
+    depth = buffer.shape[0] // len(starts)
+    copies = []
+    for i, start in enumerate(starts):
+        rows = pl.ds(pl.multiple_of(start, depth), depth)
+        copies.append(pltpu.make_async_copy(weight.at[rows, :], buffer.at[pl.ds(i * depth, depth), :], sems.at[i]))
+        copies[-1].start()
+    return copies
+
+
+def out_kernel(lhs, residual, cross, weight, hidden_out, out_ref, buffer, sems):
+    blocks = sems.shape[0]
+    depth = buffer.shape[0] // blocks
+    copies = stream(weight, buffer, sems, [i * depth for i in range(blocks)])
+    rows = residual.shape[0]
+    for i in range(out_ref.shape[0]):
+        out_ref[i, rows : rows + NS, :] = cross[i]
     total = residual[...].astype(F32)
-    depth = lhs.shape[2]
+    share = lhs.shape[2] // depth
     product = None
-    for i in range(lhs.shape[0]):
-        part = jnp.dot(lhs[i], weight[i * depth : (i + 1) * depth, :], preferred_element_type=F32)
+    for i, copy in enumerate(copies):
+        at = (i % share) * depth
+        copy.wait()
+        part = jnp.dot(
+            lhs[i // share, :, at : at + depth], buffer[i * depth : (i + 1) * depth, :], preferred_element_type=F32
+        )
         product = part if product is None else product + part
     hidden = (total + product).astype(BF16)
+    hidden_out[...] = hidden
     for i in range(out_ref.shape[0]):
-        out_ref[i] = hidden
-
-
-def halves_dot(own, other, weight):
+        out_ref[i, 0:rows, :] = hidden
+
+
+def half_starts(own):
     c = lax.axis_index("src")
     nchan, depth = own.shape[0], own.shape[2]
+    return [(half * nchan + i) * depth for half in (c, 1 - c) for i in range(nchan)]
+
+
+def halves_dot(copies, own, other, buffer, count):
+    nchan, depth = own.shape[0], own.shape[2]
     total = None
-    for ref, half in ((own, c), (other, 1 - c)):
-        for i in range(nchan):
-            rows = pl.ds(pl.multiple_of((half * nchan + i) * depth, depth), depth)
-            part = jnp.dot(ref[i], weight[rows, :], preferred_element_type=F32)
-            total = part if total is None else total + part
+    for i, copy in enumerate(copies):
+        ref = own if i < nchan else other
+        copy.wait()
+        part = jnp.dot(ref[i % nchan, 0:count, :], buffer[i * depth : (i + 1) * depth, :], preferred_element_type=F32)
+        total = part if total is None else total + part
     return total
 
 
 def values_kernel(
-    lay, own, other, arrived, other_state, taps, offset, state_proj, weight, conv_out, act_out, rms_out, proj_out
+    lay, own, other, arrived, other_conv, taps, offset, state_proj, same, weight, conv_out, act_out, rms_out, proj_out,
+    buffer, sems,
 ):
+    copies = stream(weight, buffer, sems, half_starts(own))
     c = lax.axis_index("src")
     nchan = own.shape[0]
     rows, cols = act_out.shape
     squares = jnp.zeros((rows, own.shape[2]), F32)
     for ref in (own, other):
         for i in range(nchan):
-            wide = ref[i].astype(F32)
+            wide = ref[i, 0:rows, :].astype(F32)
             squares = squares + wide * wide
     inverse = lax.rsqrt(jnp.sum(squares, axis=1, keepdims=True) / D + 1e-06)
     rms_out[...] = jnp.broadcast_to(inverse, rms_out.shape)
     steps = conv_out.shape[0]
     blocks = cols // LANES
-    at = lay.state + lay.conv
-    tails = (
-        arrived[:, at : lay.state + lay.state_rows, :].astype(F32),
-        other_state[:, lay.conv : lay.state_rows, :].astype(F32),
-    )
+    tails = (arrived[:, lay.conv : lay.conv + lay.conv_rows, :].astype(F32), other_conv[...].astype(F32))
     window = []
     for w in range(steps):
         sides = [jnp.concatenate([t[:, b * steps + w, :] for b in range(blocks)], axis=1) for t in tails]
         window.append(in_order(sides[0], sides[1], c))
-    window.append(halves_dot(own, other, weight) * inverse)
+    window.append(halves_dot(copies, own, other, buffer, rows) * inverse)
     mixed = jnp.zeros((rows, cols), F32)
     for w in range(steps + 1):
         mixed = mixed + window[w] * taps[w : w + 1, :]
@@ -302,34 +332,47 @@
     act = mixed / (1.0 + jnp.exp(-mixed))
     act_out[...] = act
     part = lax.dot_general(act.astype(BF16), state_proj[...], (((1,), (1,)), ((), ())), preferred_element_type=F32)
-    part = part.astype(BF16)
-    width = part.shape[1]
+    spare = round_up(part.shape[1], LANES) - part.shape[1]
+    part = jnp.concatenate([part, jnp.zeros((rows, spare), F32)], axis=1).astype(BF16)
+    base = blocks * NS
     for i in range(nchan):
-        proj_out[i] = jnp.zeros(proj_out.shape[1:], BF16)
-        proj_out[i, :, 0:width] = part
-
-
-def gates_kernel(own, other, rms, weight, out_ref):
-    gate = halves_dot(own, other, weight) * rms[:, 0:1]
+        for b in range(blocks):
+            proj_out[i, b * NS : (b + 1) * NS, :] = same[i, :, b * LANES : (b + 1) * LANES]
+        for b in range(part.shape[1] // LANES):
+            proj_out[i, base + b * rows : base + (b + 1) * rows, :] = part[:, b * LANES : (b + 1) * LANES]
+
+
+def gates_kernel(own, other, rms, weight, out_ref, buffer, sems):
+    copies = stream(weight, buffer, sems, half_starts(own))
+    gate = halves_dot(copies, own, other, buffer, out_ref.shape[0]) * rms[:, 0:1]
     out_ref[...] = gate / (1.0 + jnp.exp(-gate))
 
 
-def down_product(gated, weight, half, out_ref):
-    nchan, rows, cols = out_ref.shape
-    step = max(cols, min(1024, nchan * cols))
-    for i in range(nchan * cols // step):
-        at = pl.multiple_of(half * (nchan * cols) + i * step, step)
-        part = jnp.dot(gated, weight[:, pl.ds(at, step)], preferred_element_type=F32).astype(out_ref.dtype)
+def down_stream(weight, buffer, sems, half):
+    width = buffer.shape[1]
+    step = width // sems.shape[0]
+    copies = []
+    for i in range(sems.shape[0]):
+        columns = pl.ds(pl.multiple_of(half * width + i * step, step), step)
+        copies.append(pltpu.make_async_copy(weight.at[:, columns], buffer.at[:, pl.ds(i * step, step)], sems.at[i]))
+        copies[-1].start()
+    return copies
+
+
+def down_product(copies, gated, buffer, out_ref):
+    cols = out_ref.shape[2]
+    step = buffer.shape[1] // len(copies)
+    for i, copy in enumerate(copies):
+        copy.wait()
+        part = jnp.dot(gated, buffer[:, i * step : (i + 1) * step], preferred_element_type=F32).astype(out_ref.dtype)
         for j in range(step // cols):
             out_ref[i * (step // cols) + j] = part[:, j * cols : (j + 1) * cols]
 
 
 def scan_kernel(
-    lay,
     own,
     other,
-    arrived,
-    other_state,
+    hid_other,
     act_ref,
     gate_ref,
     step_proj,
@@ -342,25 +385,31 @@
     send_out,
     turned,
     mixed,
+    buffer,
+    sems,
 ):
     c = lax.axis_index("src")
-    nchan, rows = own.shape[0], own.shape[1]
-    cols = act_ref.shape[1]
+    copies = down_stream(weight, buffer, sems, 1 - c)
+    nchan = own.shape[0]
+    rows, cols = act_ref.shape
     blocks = cols // LANES
-    projected = jnp.zeros(own.shape[1:], F32)
+    base = blocks * NS
+    summed = jnp.zeros((own.shape[1] - base, LANES), F32)
     for ref in (own, other):
         for i in range(nchan):
-            projected = projected + ref[i].astype(F32)
+            summed = summed + ref[i, base:, :].astype(F32)
+    parts = [summed[b * rows : (b + 1) * rows, :] for b in range(summed.shape[0] // rows)]
+    low = jnp.concatenate(parts[: DTR // LANES], axis=1).astype(BF16)
     act = act_ref[...]
-    raw = jnp.dot(projected[:, 0:DTR].astype(BF16), step_proj[...], preferred_element_type=F32) + step_bias[...]
+    raw = jnp.dot(low, step_proj[...], preferred_element_type=F32) + step_bias[...]
     step = jnp.maximum(raw, 0.0) + jnp.log1p(jnp.exp(-jnp.abs(raw)))
     turned[...] = jnp.zeros_like(turned)
-    turned[0:rows, :] = own_first(projected[:, DTR : DTR + LANES], c)
+    turned[0:rows, :] = own_first(parts[DTR // LANES], c)
     mats = turned[...].T
     rate = -jnp.exp(decay_log[...])
     fed = own_first(step * act, c)
     step = own_first(step, c)
-    for side, states, base in ((0, arrived, lay.state), (1, other_state, 0)):
+    for side in range(2):
         for s in range(nchan):
             q = side * nchan + s
             place = (c if side == 0 else 1 - c) * nchan + s
@@ -368,17 +417,29 @@
             c_col = mats[NS : 2 * NS, q : q + 1]
             for b in range(blocks):
                 lanes = slice(b * LANES, (b + 1) * LANES)
-                state = states[s, base + b * NS : base + (b + 1) * NS, :].astype(F32)
+                if side == 0:
+                    state = own[s, b * NS : (b + 1) * NS, :].astype(F32)
+                else:
+                    state = hid_other[s, rows : rows + NS, lanes].astype(F32)
                 after = jnp.exp(step[q : q + 1, lanes] * rate[:, lanes]) * state + fed[q : q + 1, lanes] * b_col
                 next_out[place, :, lanes] = after
                 mixed[q : q + 1, lanes] = jnp.sum(after * c_col, axis=0, keepdims=True)
     gated = ((own_first(mixed[...], c) + skip_gain[...] * act) * gate_ref[...]).astype(BF16)
     gated_out[...] = gated
-    down_product(gated, weight, 1 - c, send_out)
-
-
-def down_kernel(gated, weight, out_ref):
-    down_product(gated[...], weight, lax.axis_index("src"), out_ref)
+    down_product(copies, gated, buffer, send_out)
+
+
+def down_kernel(gated, weight, out_ref, buffer, sems):
+    copies = down_stream(weight, buffer, sems, lax.axis_index("src"))
+    down_product(copies, gated[...], buffer, out_ref)
+
+
+def finish_kernel(final, hidden, out_ref):
+    total = None
+    for i in range(final.shape[0]):
+        part = final[i].astype(F32)
+        total = part if total is None else total + part
+    out_ref[...] = (hidden[...].astype(F32) + total).astype(BF16)
 
 
 def on_device(
@@ -416,115 +477,118 @@
     packed = call(
         functools.partial(pack_kernel, nchan, lay),
         out_shape=shape((nchan, lay.rows, LANES), BF16),
-        in_specs=hbm(1) + vmem(1) + hbm(7),
+        in_specs=hbm(8),
         out_specs=vmem(1)[0],
         scratch_shapes=[
             VM(query_heads.shape, BF16),
+            VM(query_heads.shape, BF16),
             VM(new_keyval.shape, BF16),
             VM(cache_pages.shape, BF16),
-            VM(mamba_state.shape, F32),
             VM(conv_rows.shape, F32),
             pltpu.SMEM(page_owner.shape, jnp.int32),
             pltpu.SMEM(page_index.shape, jnp.int32),
             pltpu.SMEM(prompt_lengths.shape, jnp.int32),
             pltpu.SemaphoreType.DMA((8,)),
         ],
-        compiler_params=params(16 if held < 16 else 40),
+        compiler_params=pltpu.CompilerParams(vmem_limit_bytes=64 * 2**20 - 2**18),
         name="pack",
-    )(
-        query_heads,
-        other_query,
-        new_keyval,
-        cache_pages,
-        mamba_state,
-        conv_rows,
-        page_owner,
-        page_index,
-        prompt_lengths,
-    )
+    )(query_heads, other_query, new_keyval, cache_pages, conv_rows, page_owner, page_index, prompt_lengths)
+    packed, residual_input, mamba_state = lax.optimization_barrier((packed, residual_input, mamba_state))
     arrived = exchange(packed)
+    cut = shape((nchan, NS, cols), BF16)
+    residual, same, cross = call(
+        load_kernel,
+        out_shape=(shape((rows, cols), BF16), cut, cut),
+        in_specs=vmem(2),
+        out_specs=tuple(vmem(3)),
+        compiler_params=params(16),
+        cost_estimate=cost(SHORT, 0),
+        name="load",
+    )(residual_input, mamba_state)
+    arrived, residual, same, cross = lax.optimization_barrier((arrived, residual, same, cross))
 
     pairs = rows * lay.per
-    partial, state_send = call(
+    partial, conv_send = call(
         functools.partial(attend_kernel, lay),
-        out_shape=(shape((pairs, HD + LANES), F32), shape((nchan, lay.state_rows, LANES), BF16)),
+        out_shape=(shape((pairs, HD + LANES), F32), shape((nchan, lay.conv_rows, LANES), BF16)),
         in_specs=vmem(1),
         out_specs=tuple(vmem(2)),
         scratch_shapes=[VM((pairs, HD), F32), VM((pairs, nchan * lay.tokens), F32)],
-        compiler_params=params(8 if held < 16 else 48),
+        compiler_params=params(4 if held < 16 else 40),
         name="attend",
     )(arrived)
     other_partial = swap(partial)
-    other_state = swap(state_send)
+    other_conv = swap(conv_send)
     attended = call(
         functools.partial(merge_kernel, lay),
         out_shape=shape((nchan, rows, lay.per * HD), BF16),
         in_specs=vmem(2),
         out_specs=vmem(1)[0],
         scratch_shapes=[VM((pairs, HD), F32)],
-        compiler_params=params(8),
+        compiler_params=params(4),
         name="merge",
     )(partial, other_partial)
     features = exchange(attended)
 
-    weight_cost = cost(2 * rows * D * cols, 2 * D * cols)
-    hidden = call(
+    streamed = [VM((D, cols), BF16), pltpu.SemaphoreType.DMA((2 * nchan,))]
+    hidden, hid_send = call(
         out_kernel,
-        out_shape=shape((nchan, rows, cols), BF16),
-        in_specs=vmem(3),
-        out_specs=vmem(1)[0],
-        compiler_params=params(16),
-        cost_estimate=weight_cost,
+        out_shape=(shape((rows, cols), BF16), shape((nchan, rows + NS, cols), BF16)),
+        in_specs=vmem(3) + hbm(1),
+        out_specs=tuple(vmem(2)),
+        scratch_shapes=streamed,
+        compiler_params=params(STREAM_MIB),
         name="out",
-    )(features, residual_input, out_heads)
-    hid_own = exchange(hidden)
+    )(features, residual, cross, out_heads)
+    hid_own = exchange(hid_send)
     hid_other = swap(hid_own)
 
-    width = round_up(state_proj.shape[1], LANES)
+    sent_rows = (cols // LANES) * NS + (round_up(state_proj.shape[1], LANES) // LANES) * rows
     conv_next, act, rms, part = call(
         functools.partial(values_kernel, lay),
         out_shape=(
             shape((steps, rows, cols), F32),
             shape((rows, cols), F32),
             shape((rows, LANES), F32),
-            shape((nchan, rows, width), BF16),
+            shape((nchan, sent_rows, LANES), BF16),
         ),
-        in_specs=vmem(8),
+        in_specs=vmem(8) + hbm(1),
         out_specs=tuple(vmem(4)),
-        compiler_params=params(16),
-        cost_estimate=weight_cost,
+        scratch_shapes=streamed,
+        compiler_params=params(STREAM_MIB),
         name="values",
-    )(hid_own, hid_other, arrived, other_state, conv_taps, conv_offset[None, :], state_proj.T, in_values)
+    )(hid_own, hid_other, arrived, other_conv, conv_taps, conv_offset[None, :], state_proj.T, same, in_values)
     proj_own = exchange(part)
     gate = call(
         gates_kernel,
         out_shape=shape((rows, cols), F32),
-        in_specs=vmem(4),
+        in_specs=vmem(3) + hbm(1),
         out_specs=vmem(1)[0],
-        compiler_params=params(16),
-        cost_estimate=weight_cost,
+        scratch_shapes=streamed,
+        compiler_params=params(STREAM_MIB),
+        cost_estimate=cost(SHORT, 0),
         name="gates",
     )(hid_own, hid_other, rms, in_gates)
     proj_own, gate = lax.optimization_barrier((proj_own, gate))
     proj_other = swap(proj_own)
 
+    down_streamed = [VM((cols, D // 2), BF16), pltpu.SemaphoreType.DMA((4,))]
     mamba_next, gated, send = call(
-        functools.partial(scan_kernel, lay),
+        scan_kernel,
         out_shape=(
             shape((rows, NS, cols), F32),
             shape((rows, cols), BF16),
             shape((nchan, rows, cols), BF16),
         ),
-        in_specs=vmem(11),
+        in_specs=vmem(9) + hbm(1),
         out_specs=tuple(vmem(3)),
-        scratch_shapes=[VM((LANES, LANES), F32), VM((rows, cols), F32)],
-        compiler_params=params(16),
+        scratch_shapes=[VM((LANES, LANES), F32), VM((rows, cols), F32)] + down_streamed,
+        compiler_params=params(STREAM_MIB),
         name="scan",
     )(
         proj_own,
         proj_other,
-        arrived,
-        other_state,
+        hid_other,
         act,
         gate,
         step_proj,
@@ -537,16 +601,22 @@
     keep = call(
         down_kernel,
         out_shape=shape((nchan, rows, cols), F32),
-        in_specs=vmem(2),
+        in_specs=vmem(1) + hbm(1),
         out_specs=vmem(1)[0],
-        compiler_params=params(16),
-        cost_estimate=cost(rows * D * cols, D * cols),
+        scratch_shapes=down_streamed,
+        compiler_params=params(STREAM_MIB),
+        cost_estimate=cost(SHORT, 0),
         name="down",
     )(gated, mamba_down)
     summed = (keep + taken.astype(F32)).astype(BF16)
-    final = exchange(summed)
-    down_sum = jnp.sum(final.astype(F32), axis=0)
-    hidden_out = (hidden[0].astype(F32) + down_sum).astype(BF16)
+    hidden_out = call(
+        finish_kernel,
+        out_shape=shape((rows, cols), BF16),
+        in_specs=vmem(2),
+        out_specs=vmem(1)[0],
+        compiler_params=params(4),
+        name="finish",
+    )(exchange(summed), hidden)
     return (hidden_out, mamba_next, jnp.transpose(conv_next, (1, 0, 2)))
 
 

time: 113 us -> 100 us (0.88)
  local copies, waits for them, and re-layouts: 24 us -> 2.41 us
  blocking collectives: 53.1 us -> 35.6 us
  Pallas kernels: 9.29 us -> 21.6 us
  waiting for transfers between devices: 15.9 us -> 27.1 us
  starting transfers between devices: 7.7 us -> 12.2 us
  other arithmetic: 1.39 us -> 0.03 us
    unnamed x42 -> x20, local copies, waits for them, and re-layouts: 24 us -> 2.41 us
    all_to_all x3, blocking collectives: 53.1 us -> 35.6 us  [exchange(): return lax.all_to_all(x, 'chan', split_axis=0, concat_axis=0, tiled=True)]
    all_to_all x2, waiting for transfers between devices: 10.7 us -> 22 us  [exchange(): return lax.all_to_all(x, 'chan', split_axis=0, concat_axis=0, tiled=True)]
    pallas_call x3 -> x5, Pallas kernels: 4.34 us -> 11.2 us  [the longest x1 3.72 us: on_device(): call(gates_kernel, out_shape=shape((rows, cols), F32), in_specs=vmem(3) +...]
    all_to_all x2, starting transfers between devices: 6.97 us -> 10.9 us  [exchange(): return lax.all_to_all(x, 'chan', split_axis=0, concat_axis=0, tiled=True)]
    pallas_call x1, Pallas kernels: 2.1 us -> 4.66 us  [on_device(): call(functools.partial(values_kernel, lay), out_shape=(shape((steps, rows...]
    pallas_call x1, Pallas kernels: 0.65 us -> 2.47 us  [on_device(): call(down_kernel, out_shape=shape((nchan, rows, cols), F32), in_specs=vme...]
    convert_element_type x1 -> x0, other arithmetic: 1.33 us -> none  [on_device(): hidden_out = (hidden[0].astype(F32) + down_sum).astype(BF16)]
  transfers between devices with their start and end apart: 8 -> 8, of which waited for: 6 -> 6; matrix products, arithmetic and copies ran while one was open for 0% -> 0% of each run, Pallas kernels for 2% -> 6%
where the time goes in v3:
time: 100 us; the launch traced here: 99.7 us
  blocking collectives  35.6 us (36%)
  waiting for transfers between devices  27.1 us (27%)
  Pallas kernels  21.6 us (22%)
  starting transfers between devices  12.2 us (12%)
  local copies, waits for them, and re-layouts  2.41 us (2%)
    all_to_all x3, blocking collectives, exchange(): return lax.all_to_all(x, 'chan', split_axis=0, concat_axis=0, tiled=True)  35.6 us
    all_to_all x2, waiting for transfers between devices, exchange(): return lax.all_to_all(x, 'chan', split_axis=0, concat_axis=0, tiled=True)  22 us
    all_to_all x2, starting transfers between devices, exchange(): return lax.all_to_all(x, 'chan', split_axis=0, concat_axis=0, tiled=True)  10.9 us
    ppermute x6, waiting for transfers between devices, swap(): return lax.ppermute(x, 'src', [(0, 1), (1, 0)])  5.06 us
    pallas_call x1, Pallas kernels, on_device(): call(functools.partial(values_kernel, lay), out_shape=(shape((steps, rows...  4.66 us
    pallas_call x1, Pallas kernels, on_device(): call(gates_kernel, out_shape=shape((rows, cols), F32), in_specs=vmem(3) +...  3.72 us
    pallas_call x1, Pallas kernels, on_device(): call(out_kernel, out_shape=(shape((rows, cols), BF16), shape((nchan, rows...  3.71 us
    pallas_call x1, Pallas kernels, on_device(): call(scan_kernel, out_shape=(shape((rows, NS, cols), F32), shape((rows, c...  3.16 us
  transfers between devices with their start and end apart: 8, of which 6 were waited for; matrix products, arithmetic and copies ran while one was open for 0% of the time, Pallas kernels for 6%

profile of v3, /device:TPU:0, one launch (start us, length us, event | category | flops | bytes accessed | tf_op | source)
XLA Modules:
  0.0 99.7 jit_solution(6306280650201261639)
XLA Ops:
  0.6 0.5 collective-permute-start
  1.2 1.1 %collective-permute-done.other_hbm = bf16[1,8192]{1,0:T(2,128)(2,1)S(1)} collective-permute-done((bf16[1,8192]{1,0:T(2,128)(2,1)}, bf16[1,8192]{1,0:T(2,128)(2,1)S(1)}, u32[]{:S(2)}, u32[]{:S(2)}) %collective-permute-start) | collective-permute-done | bytes 16416 | tf_op jit(solution)/shard_map/ppermute | solution.py:53
  2.2 0.0 copy-start.9
  2.2 0.6 copy-done.9
  2.8 2.3 %pack.1 = bf16[8,320,128]{2,1,0:T(8,128)(2,1)} custom-call(bf16[1,8192]{1,0:T(2,128)(2,1)} %query_hbm.1, bf16[1,8192]{1,0:T(2,128)(2,1)} %copy-done.9, bf16[1,2048]{1,0:T(2,128)(2,1)} %newkv_hbm.1, bf16[8,16,2048]{2,1,0:T(8,128)(2,1)} %pages_hbm.1, f32[3,1,8192]{2,1,0:T(1,128)} %bitcast.10, s32[8]{0:T(128)} %owner_hbm.1, s32[8]{0:T(128)} %index_hbm.1, ...), custom_call_target="tpu_custom_call" | custom-call | tf_op jit(solution)/shard_map/pack/pallas_call | solution.py:477
  5.1 7.2 %all-to-all-start = ((bf16[8,320,128]{2,1,0:T(8,128)(2,1)}), bf16[8,320,128]{2,1,0:T(8,128)(2,1)S(1)}, u32[]{:S(2)}, u32[]{:S(2)}) async-start(bf16[8,320,128]{2,1,0:T(8,128)(2,1)} %pack.1), calls=%async_computation | async-start | bytes 1310720 | tf_op jit(solution)/shard_map/all_to_all | solution.py:57
  12.3 0.0 copy-start.7
  12.3 1.0 %copy-done.7 = f32[1,16,8192]{2,1,0:T(8,128)S(1)} copy-done((f32[1,16,8192]{2,1,0:T(8,128)S(1)}, f32[1,16,8192]{2,1,0:T(8,128)}, u32[]{:S(2)}) %copy-start.7) | copy-done | bytes 524312
  13.3 0.0 copy-start.8
  13.3 0.7 copy-done.8
  14.1 0.0 copy-start
  14.1 0.0 copy-start.3
  14.1 0.0 copy-start.4
  14.1 15.8 %all-to-all-done.recv.arrived = bf16[8,320,128]{2,1,0:T(8,128)(2,1)S(1)} async-done(((bf16[8,320,128]{2,1,0:T(8,128)(2,1)}), bf16[8,320,128]{2,1,0:T(8,128)(2,1)S(1)}, u32[]{:S(2)}, u32[]{:S(2)}) %all-to-all-start) | async-done | bytes 655392 | tf_op jit(solution)/shard_map/all_to_all | solution.py:57
  29.9 0.7 attend.1
  30.7 0.1 collective-permute-start.1
  30.7 1.3 %collective-permute-done.1.other = f32[128,256]{1,0:T(8,128)S(1)} collective-permute-done((f32[128,256]{1,0:T(8,128)S(1)}, f32[128,256]{1,0:T(8,128)S(1)}, u32[]{:S(2)}, u32[]{:S(2)}) %collective-permute-start.1) | collective-permute-done | bytes 131104 | tf_op jit(solution)/shard_map/ppermute | solution.py:53
  32.1 0.3 merge.1
  32.3 12.7 %all_to_all.25.lhs = bf16[8,16,1024]{2,1,0:T(8,128)(2,1)S(1)} all-to-all(bf16[8,16,1024]{2,1,0:T(8,128)(2,1)S(1)} %merge.1), channel_id=1, replica_groups=mesh['groups'=2,'src'=2,'chan'=8] {'chan'}, dimensions={0} | all-to-all | bytes 524288 | tf_op jit(solution)/shard_map/all_to_all | solution.py:57
  45.0 3.7 %out.1 = (bf16[16,512]{1,0:T(8,128)(2,1)S(1)}, bf16[8,32,512]{2,1,0:T(8,128)(2,1)S(1)}) custom-call(bf16[8,16,1024]{2,1,0:T(8,128)(2,1)S(1)} %all_to_all.25.lhs, bf16[16,512]{1,0:T(8,128)(2,1)S(1)} %get-tuple-element.34.residual, bf16[8,16,512]{2,1,0:T(8,128)(2,1)S(1)} %get-tuple-element.35.cross, bf16[8192,512]{1,0:T(8,128)(2,1)} %weight.5), custom_call_target="tpu_custom_call" | custom-call | tf_op jit(solution)/shard_map/out/pallas_call | solution.py:534
  48.7 12.0 %all_to_all.26.own = bf16[8,32,512]{2,1,0:T(8,128)(2,1)S(1)} all-to-all(bf16[8,32,512]{2,1,0:T(8,128)(2,1)S(1)} %get-tuple-element.36), channel_id=1, replica_groups=mesh['groups'=2,'src'=2,'chan'=8] {'chan'}, dimensions={0} | all-to-all | bytes 524288 | tf_op jit(solution)/shard_map/all_to_all | solution.py:57
  60.7 0.0 collective-permute-start.2
  60.7 0.5 collective-permute-start.3
  61.2 1.1 %collective-permute-done.3.other_conv = bf16[8,16,128]{2,1,0:T(8,128)(2,1)S(1)} collective-permute-done((bf16[8,16,128]{2,1,0:T(8,128)(2,1)S(1)}, bf16[8,16,128]{2,1,0:T(8,128)(2,1)S(1)}, u32[]{:S(2)}, u32[]{:S(2)}) %collective-permute-start.3) | collective-permute-done | bytes 32800 | tf_op jit(solution)/shard_map/ppermute | solution.py:53
  62.3 0.0 collective-permute-done.2.other.hid_other
  62.3 0.0 copy-done
  62.3 0.0 copy-done.3
  62.3 0.0 copy-done.4
  62.3 4.7 %values.1 = (f32[3,16,512]{2,1,0:T(8,128)}, f32[16,512]{1,0:T(8,128)S(1)}, f32[16,128]{1,0:T(8,128)S(1)}, bf16[8,144,128]{2,1,0:T(8,128)(2,1)}) custom-call(bf16[8,32,512]{2,1,0:T(8,128)(2,1)S(1)} %all_to_all.26.own, bf16[8,32,512]{2,1,0:T(8,128)(2,1)S(1)} %collective-permute-done.2.other.hid_other, bf16[8,320,128]{2,1,0:T(8,128)(2,1)S(1)} %all-to-all-done.recv.arrived, ...), custom_call_target="tpu_custom_call" | custom-call | tf_op jit(solution)/shard_map/values/pallas_call | solution.py:547
  67.0 0.0 copy-start.1
  67.0 0.0 copy-start.2
  67.0 0.0 copy-start.5
  67.0 0.0 copy-start.6
  67.0 3.7 %all-to-all-start.3 = ((bf16[8,144,128]{2,1,0:T(8,128)(2,1)}), bf16[8,144,128]{2,1,0:T(8,128)(2,1)S(1)}, u32[]{:S(2)}, u32[]{:S(2)}) async-start(bf16[8,144,128]{2,1,0:T(8,128)(2,1)} %get-tuple-element.39), calls=%async_computation.3 | async-start | bytes 589824 | tf_op jit(solution)/shard_map/all_to_all | solution.py:57
  70.7 3.7 %gates.1.gate_ref = f32[16,512]{1,0:T(8,128)S(1)} custom-call(bf16[8,32,512]{2,1,0:T(8,128)(2,1)S(1)} %all_to_all.26.own, bf16[8,32,512]{2,1,0:T(8,128)(2,1)S(1)} %collective-permute-done.2.other.hid_other, f32[16,128]{1,0:T(8,128)S(1)} %get-tuple-element.40.rms, bf16[8192,512]{1,0:T(8,128)(2,1)} %weight.7), custom_call_target="tpu_custom_call" | custom-call | flops 3000000000 | tf_op jit(solution)/shard_map/gates/pallas_call | solution.py:562
  74.5 6.2 %all-to-all-done.3.own = bf16[8,144,128]{2,1,0:T(8,128)(2,1)S(1)} async-done(((bf16[8,144,128]{2,1,0:T(8,128)(2,1)}), bf16[8,144,128]{2,1,0:T(8,128)(2,1)S(1)}, u32[]{:S(2)}, u32[]{:S(2)}) %all-to-all-start.3) | async-done | bytes 294944 | tf_op jit(solution)/shard_map/all_to_all | solution.py:57
  80.6 0.0 collective-permute-start.4
  80.6 1.6 %collective-permute-done.4.other = bf16[8,144,128]{2,1,0:T(8,128)(2,1)S(1)} collective-permute-done((bf16[8,144,128]{2,1,0:T(8,128)(2,1)S(1)}, bf16[8,144,128]{2,1,0:T(8,128)(2,1)S(1)}, u32[]{:S(2)}, u32[]{:S(2)}) %collective-permute-start.4) | collective-permute-done | bytes 294944 | tf_op jit(solution)/shard_map/ppermute | solution.py:53
  82.2 0.0 copy-done.1
  82.2 0.0 copy-done.2
  82.2 0.0 copy-done.5
  82.2 0.0 copy-done.6
  82.2 3.2 %scan.1 = (f32[16,16,512]{2,1,0:T(8,128)}, bf16[16,512]{1,0:T(8,128)(2,1)S(1)}, bf16[8,16,512]{2,1,0:T(8,128)(2,1)S(1)}) custom-call(bf16[8,144,128]{2,1,0:T(8,128)(2,1)S(1)} %all-to-all-done.3.own, bf16[8,144,128]{2,1,0:T(8,128)(2,1)S(1)} %collective-permute-done.4.other, bf16[8,32,512]{2,1,0:T(8,128)(2,1)S(1)} %collective-permute-done.2.other.hid_other, ...), custom_call_target="tpu_custom_call" | custom-call | tf_op jit(solution)/shard_map/scan/pallas_call | solution.py:576
  85.4 0.2 collective-permute-start.5
  85.6 2.5 %down.1 = f32[8,16,512]{2,1,0:T(8,128)S(1)} custom-call(bf16[16,512]{1,0:T(8,128)(2,1)S(1)} %get-tuple-element.44.gated, bf16[512,8192]{1,0:T(8,128)(2,1)} %weight.9), custom_call_target="tpu_custom_call" | custom-call | flops 3000000000 | tf_op jit(solution)/shard_map/down/pallas_call | solution.py:601
  88.1 0.0 collective-permute-done.5
  88.1 10.9 %all_to_all.27.final = bf16[8,16,512]{2,1,0:T(8,128)(2,1)S(1)} all-to-all(bf16[8,16,512]{2,1,0:T(8,128)(2,1)S(1)} %add_convert_fusion), channel_id=1, replica_groups=mesh['groups'=2,'src'=2,'chan'=8] {'chan'}, dimensions={0} | all-to-all | bytes 262144 | tf_op jit(solution)/shard_map/all_to_all | solution.py:57
  99.1 0.6 finish.1
  (2 shorter events, 0.1 us)
Async XLA Ops:
  0.6 1.6 %collective-permute-start = (bf16[1,8192]{1,0:T(2,128)(2,1)}, bf16[1,8192]{1,0:T(2,128)(2,1)S(1)}, u32[]{:S(2)}, u32[]{:S(2)}) collective-permute-start(bf16[1,8192]{1,0:T(2,128)(2,1)} %query_hbm.1), channel_id=1, source_target_pairs={{0,8},{8,0},{1,9},{9,1},{2,10},{10,2},{3,11},{11,3},{4,12},{12,4},... | collective-permute-start | bytes 49160 | tf_op jit(solution)/shard_map/ppermute | solution.py:53
  2.2 0.6 copy-start.9
  5.1 24.8 %all-to-all-start = ((bf16[8,320,128]{2,1,0:T(8,128)(2,1)}), bf16[8,320,128]{2,1,0:T(8,128)(2,1)S(1)}, u32[]{:S(2)}, u32[]{:S(2)}) async-start(bf16[8,320,128]{2,1,0:T(8,128)(2,1)} %pack.1), calls=%async_computation | async-start | bytes 1310720 | tf_op jit(solution)/shard_map/all_to_all | solution.py:57
  12.3 1.0 %copy-start.7 = (f32[1,16,8192]{2,1,0:T(8,128)S(1)}, f32[1,16,8192]{2,1,0:T(8,128)}, u32[]{:S(2)}) copy-start(f32[1,16,8192]{2,1,0:T(8,128)} %state) | copy-start | bytes 1572868
  13.3 0.7 copy-start.8
  14.1 48.2 %copy-start = (bf16[512,544]{0,1:T(8,128)(2,1)S(1)}, bf16[512,544]{0,1:T(8,128)(2,1)}, u32[]{:S(2)}) copy-start(bf16[512,544]{0,1:T(8,128)(2,1)} %param.34) | copy-start | bytes 1671172
  14.1 48.2 %copy-start.3 = (f32[4,512]{1,0:T(4,128)S(1)}, f32[4,512]{1,0:T(4,128)}, u32[]{:S(2)}) copy-start(f32[4,512]{1,0:T(4,128)} %taps.1) | copy-start | bytes 24580
  14.1 48.2 %copy-start.4 = (f32[512]{0:T(512)S(1)}, f32[512]{0:T(512)}, u32[]{:S(2)}) copy-start(f32[512]{0:T(512)} %param.33) | copy-start | bytes 6148
  30.7 1.4 %collective-permute-start.1 = (f32[128,256]{1,0:T(8,128)S(1)}, f32[128,256]{1,0:T(8,128)S(1)}, u32[]{:S(2)}, u32[]{:S(2)}) collective-permute-start(f32[128,256]{1,0:T(8,128)S(1)} %get-tuple-element.33.own), channel_id=1, source_target_pairs={{0,8},{8,0},{1,9},{9,1},{2,10},{10,2},{3,11},{11,3},{4,12},{12,4},... | collective-permute-start | bytes 393224 | tf_op jit(solution)/shard_map/ppermute | solution.py:53
  60.7 1.6 %collective-permute-start.2 = (bf16[8,32,512]{2,1,0:T(8,128)(2,1)S(1)}, bf16[8,32,512]{2,1,0:T(8,128)(2,1)S(1)}, u32[]{:S(2)}, u32[]{:S(2)}) collective-permute-start(bf16[8,32,512]{2,1,0:T(8,128)(2,1)S(1)} %all_to_all.26.own), channel_id=1, source_target_pairs={{0,8},{8,0},{1,9},{9,1},{2,10},{10,2},{3,11},{11,3},{4,12},{12,4},... | collective-permute-start | bytes 786440 | tf_op jit(solution)/shard_map/ppermute | solution.py:53
  60.7 1.6 %collective-permute-start.3 = (bf16[8,16,128]{2,1,0:T(8,128)(2,1)S(1)}, bf16[8,16,128]{2,1,0:T(8,128)(2,1)S(1)}, u32[]{:S(2)}, u32[]{:S(2)}) collective-permute-start(bf16[8,16,128]{2,1,0:T(8,128)(2,1)S(1)} %get-tuple-element.37), channel_id=1, source_target_pairs={{0,8},{8,0},{1,9},{9,1},{2,10},{10,2},{3,11},{11,3},{4,12},{12,4},... | collective-permute-start | bytes 98312 | tf_op jit(solution)/shard_map/ppermute | solution.py:53
  67.0 15.3 %copy-start.1 = (bf16[512,512]{1,0:T(8,128)(2,1)S(1)}, bf16[512,512]{1,0:T(8,128)(2,1)}, u32[]{:S(2)}) copy-start(bf16[512,512]{1,0:T(8,128)(2,1)} %step_proj.1) | copy-start | bytes 1572868
  67.0 15.3 %copy-start.2 = (f32[16,512]{1,0:T(8,128)S(1)}, f32[16,512]{1,0:T(8,128)}, u32[]{:S(2)}) copy-start(f32[16,512]{1,0:T(8,128)} %decay_log.1) | copy-start | bytes 98308
  67.0 15.3 %copy-start.5 = (f32[512]{0:T(512)S(1)}, f32[512]{0:T(512)}, u32[]{:S(2)}) copy-start(f32[512]{0:T(512)} %param.36) | copy-start | bytes 6148
  67.0 15.3 %copy-start.6 = (f32[512]{0:T(512)S(1)}, f32[512]{0:T(512)}, u32[]{:S(2)}) copy-start(f32[512]{0:T(512)} %param.38) | copy-start | bytes 6148
  67.0 13.6 %all-to-all-start.3 = ((bf16[8,144,128]{2,1,0:T(8,128)(2,1)}), bf16[8,144,128]{2,1,0:T(8,128)(2,1)S(1)}, u32[]{:S(2)}, u32[]{:S(2)}) async-start(bf16[8,144,128]{2,1,0:T(8,128)(2,1)} %get-tuple-element.39), calls=%async_computation.3 | async-start | bytes 589824 | tf_op jit(solution)/shard_map/all_to_all | solution.py:57
  80.6 1.6 %collective-permute-start.4 = (bf16[8,144,128]{2,1,0:T(8,128)(2,1)S(1)}, bf16[8,144,128]{2,1,0:T(8,128)(2,1)S(1)}, u32[]{:S(2)}, u32[]{:S(2)}) collective-permute-start(bf16[8,144,128]{2,1,0:T(8,128)(2,1)S(1)} %all-to-all-done.3.own), channel_id=1, source_target_pairs={{0,8},{8,0},{1,9},{9,1},{2,10},{10,2},{3,11},{11,3},{4,12},{12,4},... | collective-permute-start | bytes 884744 | tf_op jit(solution)/shard_map/ppermute | solution.py:53
  85.4 2.7 %collective-permute-start.5 = (bf16[8,16,512]{2,1,0:T(8,128)(2,1)S(1)}, bf16[8,16,512]{2,1,0:T(8,128)(2,1)S(1)}, u32[]{:S(2)}, u32[]{:S(2)}) collective-permute-start(bf16[8,16,512]{2,1,0:T(8,128)(2,1)S(1)} %get-tuple-element.45), channel_id=1, source_target_pairs={{0,8},{8,0},{1,9},{9,1},{2,10},{10,2},{3,11},{11,3},{4,12},{12,4},... | collective-permute-start | bytes 393224 | tf_op jit(solution)/shard_map/ppermute | solution.py:53

commit v4 on v3

--- a/solution.py
+++ b/solution.py
@@ -242,9 +242,11 @@
         numer = numer + factor * part[:, 0:HD]
         denom = denom + factor * part[:, HD + 1 : HD + 2]
     result[...] = numer / denom
-    for h in range(lay.per):
-        mine = result[pl.ds(h, nchan, stride=lay.per), :]
-        rest = result[pl.ds(count + h, nchan, stride=lay.per), :]
+    share = lay.per // 2
+    for h in range(share):
+        head = c * share + h
+        mine = result[pl.ds(head, nchan, stride=lay.per), :]
+        rest = result[pl.ds(count + head, nchan, stride=lay.per), :]
         block = in_order(mine, rest, c).astype(BF16)
         for i in range(nchan):
             out_ref[i, :, h * HD : (h + 1) * HD] = block
@@ -258,29 +260,6 @@
         copies.append(pltpu.make_async_copy(weight.at[rows, :], buffer.at[pl.ds(i * depth, depth), :], sems.at[i]))
         copies[-1].start()
     return copies
-
-
-def out_kernel(lhs, residual, cross, weight, hidden_out, out_ref, buffer, sems):
-    blocks = sems.shape[0]
-    depth = buffer.shape[0] // blocks
-    copies = stream(weight, buffer, sems, [i * depth for i in range(blocks)])
-    rows = residual.shape[0]
-    for i in range(out_ref.shape[0]):
-        out_ref[i, rows : rows + NS, :] = cross[i]
-    total = residual[...].astype(F32)
-    share = lhs.shape[2] // depth
-    product = None
-    for i, copy in enumerate(copies):
-        at = (i % share) * depth
-        copy.wait()
-        part = jnp.dot(
-            lhs[i // share, :, at : at + depth], buffer[i * depth : (i + 1) * depth, :], preferred_element_type=F32
-        )
-        product = part if product is None else product + part
-    hidden = (total + product).astype(BF16)
-    hidden_out[...] = hidden
-    for i in range(out_ref.shape[0]):
-        out_ref[i, 0:rows, :] = hidden
 
 
 def half_starts(own):
@@ -298,6 +277,20 @@
         part = jnp.dot(ref[i % nchan, 0:count, :], buffer[i * depth : (i + 1) * depth, :], preferred_element_type=F32)
         total = part if total is None else total + part
     return total
+
+
+def out_kernel(own, other, residual, cross, weight, hidden_out, out_ref, buffer, sems):
+    c = lax.axis_index("src")
+    nchan, rows, depth = own.shape
+    starts = [(2 * i + half) * depth for half in (c, 1 - c) for i in range(nchan)]
+    copies = stream(weight, buffer, sems, starts)
+    for i in range(nchan):
+        out_ref[i, rows : rows + NS, :] = cross[i]
+    product = halves_dot(copies, own, other, buffer, rows)
+    hidden = (residual[...].astype(F32) + product).astype(BF16)
+    hidden_out[...] = hidden
+    for i in range(nchan):
+        out_ref[i, 0:rows, :] = hidden
 
 
 def values_kernel(
@@ -317,6 +310,9 @@
     rms_out[...] = jnp.broadcast_to(inverse, rms_out.shape)
     steps = conv_out.shape[0]
     blocks = cols // LANES
+    for i in range(nchan):
+        for b in range(blocks):
+            proj_out[i, b * NS : (b + 1) * NS, :] = same[i, :, b * LANES : (b + 1) * LANES]
     tails = (arrived[:, lay.conv : lay.conv + lay.conv_rows, :].astype(F32), other_conv[...].astype(F32))
     window = []
     for w in range(steps):
@@ -336,8 +332,6 @@
     part = jnp.concatenate([part, jnp.zeros((rows, spare), F32)], axis=1).astype(BF16)
     base = blocks * NS
     for i in range(nchan):
-        for b in range(blocks):
-            proj_out[i, b * NS : (b + 1) * NS, :] = same[i, :, b * LANES : (b + 1) * LANES]
         for b in range(part.shape[1] // LANES):
             proj_out[i, base + b * rows : base + (b + 1) * rows, :] = part[:, b * LANES : (b + 1) * LANES]
 
@@ -348,23 +342,30 @@
     out_ref[...] = gate / (1.0 + jnp.exp(-gate))
 
 
-def down_stream(weight, buffer, sems, half):
-    width = buffer.shape[1]
-    step = width // sems.shape[0]
+def down_stream(weight, buffer, sems, halves):
+    width = weight.shape[1] // 2
+    pieces = sems.shape[0] // 2
+    step = width // pieces
     copies = []
-    for i in range(sems.shape[0]):
-        columns = pl.ds(pl.multiple_of(half * width + i * step, step), step)
-        copies.append(pltpu.make_async_copy(weight.at[:, columns], buffer.at[:, pl.ds(i * step, step)], sems.at[i]))
-        copies[-1].start()
+    for half in halves:
+        for i in range(pieces):
+            slot = len(copies)
+            columns = pl.ds(pl.multiple_of(half * width + i * step, step), step)
+            target = buffer.at[:, pl.ds(slot * step, step)]
+            copies.append(pltpu.make_async_copy(weight.at[:, columns], target, sems.at[slot]))
+            copies[-1].start()
     return copies
 
 
-def down_product(copies, gated, buffer, out_ref):
-    cols = out_ref.shape[2]
+def down_product(copies, gated, buffer, outs):
+    cols = outs[0].shape[2]
     step = buffer.shape[1] // len(copies)
-    for i, copy in enumerate(copies):
+    pieces = len(copies) // len(outs)
+    for slot, copy in enumerate(copies):
         copy.wait()
-        part = jnp.dot(gated, buffer[:, i * step : (i + 1) * step], preferred_element_type=F32).astype(out_ref.dtype)
+        out_ref, i = outs[slot // pieces], slot % pieces
+        part = jnp.dot(gated, buffer[:, slot * step : (slot + 1) * step], preferred_element_type=F32)
+        part = part.astype(out_ref.dtype)
         for j in range(step // cols):
             out_ref[i * (step // cols) + j] = part[:, j * cols : (j + 1) * cols]
 
@@ -381,15 +382,15 @@
     skip_gain,
     weight,
     next_out,
-    gated_out,
     send_out,
+    keep_out,
     turned,
     mixed,
     buffer,
     sems,
 ):
     c = lax.axis_index("src")
-    copies = down_stream(weight, buffer, sems, 1 - c)
+    copies = down_stream(weight, buffer, sems, (1 - c, c))
     nchan = own.shape[0]
     rows, cols = act_ref.shape
     blocks = cols // LANES
@@ -425,13 +426,7 @@
                 next_out[place, :, lanes] = after
                 mixed[q : q + 1, lanes] = jnp.sum(after * c_col, axis=0, keepdims=True)
     gated = ((own_first(mixed[...], c) + skip_gain[...] * act) * gate_ref[...]).astype(BF16)
-    gated_out[...] = gated
-    down_product(copies, gated, buffer, send_out)
-
-
-def down_kernel(gated, weight, out_ref, buffer, sems):
-    copies = down_stream(weight, buffer, sems, lax.axis_index("src"))
-    down_product(copies, gated[...], buffer, out_ref)
+    down_product(copies, gated, buffer, (send_out, keep_out))
 
 
 def finish_kernel(final, hidden, out_ref):
@@ -519,27 +514,29 @@
     )(arrived)
     other_partial = swap(partial)
     other_conv = swap(conv_send)
+    other_partial, other_conv = lax.optimization_barrier((other_partial, other_conv))
     attended = call(
         functools.partial(merge_kernel, lay),
-        out_shape=shape((nchan, rows, lay.per * HD), BF16),
+        out_shape=shape((nchan, rows, cols), BF16),
         in_specs=vmem(2),
         out_specs=vmem(1)[0],
         scratch_shapes=[VM((pairs, HD), F32)],
         compiler_params=params(4),
         name="merge",
     )(partial, other_partial)
-    features = exchange(attended)
+    att_own = exchange(attended)
+    att_other = swap(att_own)
 
     streamed = [VM((D, cols), BF16), pltpu.SemaphoreType.DMA((2 * nchan,))]
     hidden, hid_send = call(
         out_kernel,
         out_shape=(shape((rows, cols), BF16), shape((nchan, rows + NS, cols), BF16)),
-        in_specs=vmem(3) + hbm(1),
+        in_specs=vmem(4) + hbm(1),
         out_specs=tuple(vmem(2)),
         scratch_shapes=streamed,
         compiler_params=params(STREAM_MIB),
         name="out",
-    )(features, residual, cross, out_heads)
+    )(att_own, att_other, residual, cross, out_heads)
     hid_own = exchange(hid_send)
     hid_other = swap(hid_own)
 
@@ -572,13 +569,13 @@
     proj_own, gate = lax.optimization_barrier((proj_own, gate))
     proj_other = swap(proj_own)
 
-    down_streamed = [VM((cols, D // 2), BF16), pltpu.SemaphoreType.DMA((4,))]
-    mamba_next, gated, send = call(
+    down_streamed = [VM((cols, D), BF16), pltpu.SemaphoreType.DMA((8,))]
+    mamba_next, send, keep = call(
         scan_kernel,
         out_shape=(
             shape((rows, NS, cols), F32),
-            shape((rows, cols), BF16),
             shape((nchan, rows, cols), BF16),
+            shape((nchan, rows, cols), F32),
         ),
         in_specs=vmem(9) + hbm(1),
         out_specs=tuple(vmem(3)),
@@ -598,16 +595,6 @@
         mamba_down,
     )
     taken = swap(send)
-    keep = call(
-        down_kernel,
-        out_shape=shape((nchan, rows, cols), F32),
-        in_specs=vmem(1) + hbm(1),
-        out_specs=vmem(1)[0],
-        scratch_shapes=down_streamed,
-        compiler_params=params(STREAM_MIB),
-        cost_estimate=cost(SHORT, 0),
-        name="down",
-    )(gated, mamba_down)
     summed = (keep + taken.astype(F32)).astype(BF16)
     hidden_out = call(
         finish_kernel,

time: 100 us -> 99.8 us (level)
  waiting for transfers between devices: 27.1 us -> 29.6 us
  blocking collectives: 35.6 us -> 33.6 us
  Pallas kernels: 21.6 us -> 20.6 us
    ppermute x6 -> x7, waiting for transfers between devices: 5.06 us -> 7.63 us  [swap(): return lax.ppermute(x, 'src', [(0, 1), (1, 0)])]
    all_to_all x3, blocking collectives: 35.6 us -> 33.6 us  [exchange(): return lax.all_to_all(x, 'chan', split_axis=0, concat_axis=0, tiled=True)]
    pallas_call x2 -> x1, Pallas kernels: 5.63 us -> 4.66 us  [on_device(): call(scan_kernel, out_shape=(shape((rows, NS, cols), F32), shape((nchan,...]
  transfers between devices with their start and end apart: 8 -> 9, of which waited for: 6 -> 8; matrix products, arithmetic and copies ran while one was open for 0% -> 0% of each run, Pallas kernels for 6% -> 4%
where the time goes in v4:
time: 99.8 us; the launch traced here: 99.3 us
  blocking collectives  33.6 us (34%)
  waiting for transfers between devices  29.6 us (30%)
  Pallas kernels  20.6 us (21%)
  starting transfers between devices  12.2 us (12%)
  local copies, waits for them, and re-layouts  2.41 us (2%)
    all_to_all x3, blocking collectives, exchange(): return lax.all_to_all(x, 'chan', split_axis=0, concat_axis=0, tiled=True)  33.6 us
    all_to_all x2, waiting for transfers between devices, exchange(): return lax.all_to_all(x, 'chan', split_axis=0, concat_axis=0, tiled=True)  22 us
    all_to_all x2, starting transfers between devices, exchange(): return lax.all_to_all(x, 'chan', split_axis=0, concat_axis=0, tiled=True)  10.9 us
    ppermute x7, waiting for transfers between devices, swap(): return lax.ppermute(x, 'src', [(0, 1), (1, 0)])  7.63 us
    pallas_call x1, Pallas kernels, on_device(): call(scan_kernel, out_shape=(shape((rows, NS, cols), F32), shape((nchan,...  4.66 us
    pallas_call x1, Pallas kernels, on_device(): call(functools.partial(values_kernel, lay), out_shape=(shape((steps, rows...  4.66 us
    pallas_call x1, Pallas kernels, on_device(): call(out_kernel, out_shape=(shape((rows, cols), BF16), shape((nchan, rows...  3.72 us
    pallas_call x1, Pallas kernels, on_device(): call(gates_kernel, out_shape=shape((rows, cols), F32), in_specs=vmem(3) +...  3.72 us
  transfers between devices with their start and end apart: 9, of which 8 were waited for; matrix products, arithmetic and copies ran while one was open for 0% of the time, Pallas kernels for 4%

profile of v4, /device:TPU:0, one launch (start us, length us, event | category | flops | bytes accessed | tf_op | source)
XLA Modules:
  0.0 99.3 jit_solution(15122776692525890157)
XLA Ops:
  0.6 0.5 collective-permute-start
  1.2 1.1 %collective-permute-done.other_hbm = bf16[1,8192]{1,0:T(2,128)(2,1)S(1)} collective-permute-done((bf16[1,8192]{1,0:T(2,128)(2,1)}, bf16[1,8192]{1,0:T(2,128)(2,1)S(1)}, u32[]{:S(2)}, u32[]{:S(2)}) %collective-permute-start) | collective-permute-done | bytes 16416 | tf_op jit(solution)/shard_map/ppermute | solution.py:53
  2.2 0.0 copy-start.9
  2.2 0.6 copy-done.9
  2.8 2.3 %pack.1 = bf16[8,320,128]{2,1,0:T(8,128)(2,1)} custom-call(bf16[1,8192]{1,0:T(2,128)(2,1)} %query_hbm.1, bf16[1,8192]{1,0:T(2,128)(2,1)} %copy-done.9, bf16[1,2048]{1,0:T(2,128)(2,1)} %newkv_hbm.1, bf16[8,16,2048]{2,1,0:T(8,128)(2,1)} %pages_hbm.1, f32[3,1,8192]{2,1,0:T(1,128)} %bitcast.10, s32[8]{0:T(128)} %owner_hbm.1, s32[8]{0:T(128)} %index_hbm.1, ...), custom_call_target="tpu_custom_call" | custom-call | tf_op jit(solution)/shard_map/pack/pallas_call | solution.py:472
  5.1 7.2 %all-to-all-start = ((bf16[8,320,128]{2,1,0:T(8,128)(2,1)}), bf16[8,320,128]{2,1,0:T(8,128)(2,1)S(1)}, u32[]{:S(2)}, u32[]{:S(2)}) async-start(bf16[8,320,128]{2,1,0:T(8,128)(2,1)} %pack.1), calls=%async_computation | async-start | bytes 1310720 | tf_op jit(solution)/shard_map/all_to_all | solution.py:57
  12.3 0.0 copy-start.7
  12.3 1.0 %copy-done.7 = f32[1,16,8192]{2,1,0:T(8,128)S(1)} copy-done((f32[1,16,8192]{2,1,0:T(8,128)S(1)}, f32[1,16,8192]{2,1,0:T(8,128)}, u32[]{:S(2)}) %copy-start.7) | copy-done | bytes 524312
  13.3 0.0 copy-start.8
  13.3 0.7 copy-done.8
  14.1 0.0 copy-start
  14.1 0.0 copy-start.3
  14.1 0.0 copy-start.4
  14.1 15.8 %all-to-all-done.recv.arrived = bf16[8,320,128]{2,1,0:T(8,128)(2,1)S(1)} async-done(((bf16[8,320,128]{2,1,0:T(8,128)(2,1)}), bf16[8,320,128]{2,1,0:T(8,128)(2,1)S(1)}, u32[]{:S(2)}, u32[]{:S(2)}) %all-to-all-start) | async-done | bytes 655392 | tf_op jit(solution)/shard_map/all_to_all | solution.py:57
  29.9 0.7 attend.1
  30.7 0.1 collective-permute-start.1
  30.7 0.5 collective-permute-start.2
  31.2 0.9 collective-permute-done.2.other_conv
  32.1 0.0 collective-permute-done.1.other
  32.1 0.2 merge.1
  32.4 10.9 %all_to_all.25.own = bf16[8,16,512]{2,1,0:T(8,128)(2,1)S(1)} all-to-all(bf16[8,16,512]{2,1,0:T(8,128)(2,1)S(1)} %merge.1), channel_id=1, replica_groups=mesh['groups'=2,'src'=2,'chan'=8] {'chan'}, dimensions={0} | all-to-all | bytes 262144 | tf_op jit(solution)/shard_map/all_to_all | solution.py:57
  43.3 0.0 collective-permute-start.3
  43.3 1.3 %collective-permute-done.3.other = bf16[8,16,512]{2,1,0:T(8,128)(2,1)S(1)} collective-permute-done((bf16[8,16,512]{2,1,0:T(8,128)(2,1)S(1)}, bf16[8,16,512]{2,1,0:T(8,128)(2,1)S(1)}, u32[]{:S(2)}, u32[]{:S(2)}) %collective-permute-start.3) | collective-permute-done | bytes 131104 | tf_op jit(solution)/shard_map/ppermute | solution.py:53
  44.6 3.7 %out.1 = (bf16[16,512]{1,0:T(8,128)(2,1)S(1)}, bf16[8,32,512]{2,1,0:T(8,128)(2,1)S(1)}) custom-call(bf16[8,16,512]{2,1,0:T(8,128)(2,1)S(1)} %all_to_all.25.own, bf16[8,16,512]{2,1,0:T(8,128)(2,1)S(1)} %collective-permute-done.3.other, bf16[16,512]{1,0:T(8,128)(2,1)S(1)} %get-tuple-element.38.residual, bf16[8,16,512]{2,1,0:T(8,128)(2,1)S(1)} %get-tuple-element.39.cross, ...), custom_call_target="tpu_custom_call" | custom-call | tf_op jit(solution)/shard_map/out/pallas_call | solution.py:531
  48.3 11.9 %all_to_all.26.own = bf16[8,32,512]{2,1,0:T(8,128)(2,1)S(1)} all-to-all(bf16[8,32,512]{2,1,0:T(8,128)(2,1)S(1)} %get-tuple-element.40), channel_id=1, replica_groups=mesh['groups'=2,'src'=2,'chan'=8] {'chan'}, dimensions={0} | all-to-all | bytes 524288 | tf_op jit(solution)/shard_map/all_to_all | solution.py:57
  60.3 0.0 collective-permute-start.4
  60.3 1.5 %collective-permute-done.4.other.hid_other = bf16[8,32,512]{2,1,0:T(8,128)(2,1)S(1)} collective-permute-done((bf16[8,32,512]{2,1,0:T(8,128)(2,1)S(1)}, bf16[8,32,512]{2,1,0:T(8,128)(2,1)S(1)}, u32[]{:S(2)}, u32[]{:S(2)}) %collective-permute-start.4) | collective-permute-done | bytes 262176 | tf_op jit(solution)/shard_map/ppermute | solution.py:53
  61.8 0.0 copy-done
  61.8 0.0 copy-done.3
  61.8 0.0 copy-done.4
  61.8 4.7 %values.1 = (f32[3,16,512]{2,1,0:T(8,128)}, f32[16,512]{1,0:T(8,128)S(1)}, f32[16,128]{1,0:T(8,128)S(1)}, bf16[8,144,128]{2,1,0:T(8,128)(2,1)}) custom-call(bf16[8,32,512]{2,1,0:T(8,128)(2,1)S(1)} %all_to_all.26.own, bf16[8,32,512]{2,1,0:T(8,128)(2,1)S(1)} %collective-permute-done.4.other.hid_other, bf16[8,320,128]{2,1,0:T(8,128)(2,1)S(1)} %all-to-all-done.recv.arrived, ...), custom_call_target="tpu_custom_call" | custom-call | tf_op jit(solution)/shard_map/values/pallas_call | solution.py:544
  66.5 0.0 copy-start.1
  66.5 0.0 copy-start.2
  66.5 0.0 copy-start.5
  66.5 0.0 copy-start.6
  66.5 3.7 %all-to-all-start.3 = ((bf16[8,144,128]{2,1,0:T(8,128)(2,1)}), bf16[8,144,128]{2,1,0:T(8,128)(2,1)S(1)}, u32[]{:S(2)}, u32[]{:S(2)}) async-start(bf16[8,144,128]{2,1,0:T(8,128)(2,1)} %get-tuple-element.43), calls=%async_computation.3 | async-start | bytes 589824 | tf_op jit(solution)/shard_map/all_to_all | solution.py:57
  70.2 3.7 %gates.1.gate_ref = f32[16,512]{1,0:T(8,128)S(1)} custom-call(bf16[8,32,512]{2,1,0:T(8,128)(2,1)S(1)} %all_to_all.26.own, bf16[8,32,512]{2,1,0:T(8,128)(2,1)S(1)} %collective-permute-done.4.other.hid_other, f32[16,128]{1,0:T(8,128)S(1)} %get-tuple-element.44.rms, bf16[8192,512]{1,0:T(8,128)(2,1)} %weight.6), custom_call_target="tpu_custom_call" | custom-call | flops 3000000000 | tf_op jit(solution)/shard_map/gates/pallas_call | solution.py:559
  74.0 6.2 %all-to-all-done.3.own = bf16[8,144,128]{2,1,0:T(8,128)(2,1)S(1)} async-done(((bf16[8,144,128]{2,1,0:T(8,128)(2,1)}), bf16[8,144,128]{2,1,0:T(8,128)(2,1)S(1)}, u32[]{:S(2)}, u32[]{:S(2)}) %all-to-all-start.3) | async-done | bytes 294944 | tf_op jit(solution)/shard_map/all_to_all | solution.py:57
  80.2 0.0 collective-permute-start.5
  80.2 1.6 %collective-permute-done.5.other = bf16[8,144,128]{2,1,0:T(8,128)(2,1)S(1)} collective-permute-done((bf16[8,144,128]{2,1,0:T(8,128)(2,1)S(1)}, bf16[8,144,128]{2,1,0:T(8,128)(2,1)S(1)}, u32[]{:S(2)}, u32[]{:S(2)}) %collective-permute-start.5) | collective-permute-done | bytes 294944 | tf_op jit(solution)/shard_map/ppermute | solution.py:53
  81.8 0.0 copy-done.1
  81.8 0.0 copy-done.2
  81.8 0.0 copy-done.5
  81.8 0.0 copy-done.6
  81.8 4.7 %scan.1 = (f32[16,16,512]{2,1,0:T(8,128)}, bf16[8,16,512]{2,1,0:T(8,128)(2,1)S(1)}, f32[8,16,512]{2,1,0:T(8,128)S(1)}) custom-call(bf16[8,144,128]{2,1,0:T(8,128)(2,1)S(1)} %all-to-all-done.3.own, bf16[8,144,128]{2,1,0:T(8,128)(2,1)S(1)} %collective-permute-done.5.other, bf16[8,32,512]{2,1,0:T(8,128)(2,1)S(1)} %collective-permute-done.4.other.hid_other, ...), custom_call_target="tpu_custom_call" | custom-call | tf_op jit(solution)/shard_map/scan/pallas_call | solution.py:573
  86.4 0.2 collective-permute-start.6
  86.6 1.2 %collective-permute-done.6 = bf16[8,16,512]{2,1,0:T(8,128)(2,1)S(1)} collective-permute-done((bf16[8,16,512]{2,1,0:T(8,128)(2,1)S(1)}, bf16[8,16,512]{2,1,0:T(8,128)(2,1)S(1)}, u32[]{:S(2)}, u32[]{:S(2)}) %collective-permute-start.6) | collective-permute-done | bytes 131104 | tf_op jit(solution)/shard_map/ppermute | solution.py:53
  87.9 10.8 %all_to_all.27.final = bf16[8,16,512]{2,1,0:T(8,128)(2,1)S(1)} all-to-all(bf16[8,16,512]{2,1,0:T(8,128)(2,1)S(1)} %add_convert_fusion), channel_id=1, replica_groups=mesh['groups'=2,'src'=2,'chan'=8] {'chan'}, dimensions={0} | all-to-all | bytes 262144 | tf_op jit(solution)/shard_map/all_to_all | solution.py:57
  98.7 0.6 finish.1
  (2 shorter events, 0.1 us)
Async XLA Ops:
  0.6 1.6 %collective-permute-start = (bf16[1,8192]{1,0:T(2,128)(2,1)}, bf16[1,8192]{1,0:T(2,128)(2,1)S(1)}, u32[]{:S(2)}, u32[]{:S(2)}) collective-permute-start(bf16[1,8192]{1,0:T(2,128)(2,1)} %query_hbm.1), channel_id=1, source_target_pairs={{0,8},{8,0},{1,9},{9,1},{2,10},{10,2},{3,11},{11,3},{4,12},{12,4},... | collective-permute-start | bytes 49160 | tf_op jit(solution)/shard_map/ppermute | solution.py:53
  2.2 0.6 copy-start.9
  5.1 24.8 %all-to-all-start = ((bf16[8,320,128]{2,1,0:T(8,128)(2,1)}), bf16[8,320,128]{2,1,0:T(8,128)(2,1)S(1)}, u32[]{:S(2)}, u32[]{:S(2)}) async-start(bf16[8,320,128]{2,1,0:T(8,128)(2,1)} %pack.1), calls=%async_computation | async-start | bytes 1310720 | tf_op jit(solution)/shard_map/all_to_all | solution.py:57
  12.3 1.0 %copy-start.7 = (f32[1,16,8192]{2,1,0:T(8,128)S(1)}, f32[1,16,8192]{2,1,0:T(8,128)}, u32[]{:S(2)}) copy-start(f32[1,16,8192]{2,1,0:T(8,128)} %state) | copy-start | bytes 1572868
  13.3 0.7 copy-start.8
  14.1 47.7 %copy-start = (bf16[512,544]{0,1:T(8,128)(2,1)S(1)}, bf16[512,544]{0,1:T(8,128)(2,1)}, u32[]{:S(2)}) copy-start(bf16[512,544]{0,1:T(8,128)(2,1)} %param.34) | copy-start | bytes 1671172
  14.1 47.7 %copy-start.3 = (f32[4,512]{1,0:T(4,128)S(1)}, f32[4,512]{1,0:T(4,128)}, u32[]{:S(2)}) copy-start(f32[4,512]{1,0:T(4,128)} %taps.1) | copy-start | bytes 24580
  14.1 47.7 %copy-start.4 = (f32[512]{0:T(512)S(1)}, f32[512]{0:T(512)}, u32[]{:S(2)}) copy-start(f32[512]{0:T(512)} %param.33) | copy-start | bytes 6148
  30.7 1.5 %collective-permute-start.1 = (f32[128,256]{1,0:T(8,128)S(1)}, f32[128,256]{1,0:T(8,128)S(1)}, u32[]{:S(2)}, u32[]{:S(2)}) collective-permute-start(f32[128,256]{1,0:T(8,128)S(1)} %get-tuple-element.35.own), channel_id=1, source_target_pairs={{0,8},{8,0},{1,9},{9,1},{2,10},{10,2},{3,11},{11,3},{4,12},{12,4},... | collective-permute-start | bytes 393224 | tf_op jit(solution)/shard_map/ppermute | solution.py:53
  30.7 1.4 %collective-permute-start.2 = (bf16[8,16,128]{2,1,0:T(8,128)(2,1)S(1)}, bf16[8,16,128]{2,1,0:T(8,128)(2,1)S(1)}, u32[]{:S(2)}, u32[]{:S(2)}) collective-permute-start(bf16[8,16,128]{2,1,0:T(8,128)(2,1)S(1)} %get-tuple-element.36), channel_id=1, source_target_pairs={{0,8},{8,0},{1,9},{9,1},{2,10},{10,2},{3,11},{11,3},{4,12},{12,4},... | collective-permute-start | bytes 98312 | tf_op jit(solution)/shard_map/ppermute | solution.py:53
  43.3 1.3 %collective-permute-start.3 = (bf16[8,16,512]{2,1,0:T(8,128)(2,1)S(1)}, bf16[8,16,512]{2,1,0:T(8,128)(2,1)S(1)}, u32[]{:S(2)}, u32[]{:S(2)}) collective-permute-start(bf16[8,16,512]{2,1,0:T(8,128)(2,1)S(1)} %all_to_all.25.own), channel_id=1, source_target_pairs={{0,8},{8,0},{1,9},{9,1},{2,10},{10,2},{3,11},{11,3},{4,12},{12,4},... | collective-permute-start | bytes 393224 | tf_op jit(solution)/shard_map/ppermute | solution.py:53
  60.3 1.5 %collective-permute-start.4 = (bf16[8,32,512]{2,1,0:T(8,128)(2,1)S(1)}, bf16[8,32,512]{2,1,0:T(8,128)(2,1)S(1)}, u32[]{:S(2)}, u32[]{:S(2)}) collective-permute-start(bf16[8,32,512]{2,1,0:T(8,128)(2,1)S(1)} %all_to_all.26.own), channel_id=1, source_target_pairs={{0,8},{8,0},{1,9},{9,1},{2,10},{10,2},{3,11},{11,3},{4,12},{12,4},... | collective-permute-start | bytes 786440 | tf_op jit(solution)/shard_map/ppermute | solution.py:53
  66.5 15.3 %copy-start.1 = (bf16[512,512]{1,0:T(8,128)(2,1)S(1)}, bf16[512,512]{1,0:T(8,128)(2,1)}, u32[]{:S(2)}) copy-start(bf16[512,512]{1,0:T(8,128)(2,1)} %step_proj.1) | copy-start | bytes 1572868
  66.5 15.3 %copy-start.2 = (f32[16,512]{1,0:T(8,128)S(1)}, f32[16,512]{1,0:T(8,128)}, u32[]{:S(2)}) copy-start(f32[16,512]{1,0:T(8,128)} %decay_log.1) | copy-start | bytes 98308
  66.5 15.3 %copy-start.5 = (f32[512]{0:T(512)S(1)}, f32[512]{0:T(512)}, u32[]{:S(2)}) copy-start(f32[512]{0:T(512)} %param.36) | copy-start | bytes 6148
  66.5 15.2 %copy-start.6 = (f32[512]{0:T(512)S(1)}, f32[512]{0:T(512)}, u32[]{:S(2)}) copy-start(f32[512]{0:T(512)} %param.38) | copy-start | bytes 6148
  66.5 13.6 %all-to-all-start.3 = ((bf16[8,144,128]{2,1,0:T(8,128)(2,1)}), bf16[8,144,128]{2,1,0:T(8,128)(2,1)S(1)}, u32[]{:S(2)}, u32[]{:S(2)}) async-start(bf16[8,144,128]{2,1,0:T(8,128)(2,1)} %get-tuple-element.43), calls=%async_computation.3 | async-start | bytes 589824 | tf_op jit(solution)/shard_map/all_to_all | solution.py:57
  80.2 1.6 %collective-permute-start.5 = (bf16[8,144,128]{2,1,0:T(8,128)(2,1)S(1)}, bf16[8,144,128]{2,1,0:T(8,128)(2,1)S(1)}, u32[]{:S(2)}, u32[]{:S(2)}) collective-permute-start(bf16[8,144,128]{2,1,0:T(8,128)(2,1)S(1)} %all-to-all-done.3.own), channel_id=1, source_target_pairs={{0,8},{8,0},{1,9},{9,1},{2,10},{10,2},{3,11},{11,3},{4,12},{12,4},... | collective-permute-start | bytes 884744 | tf_op jit(solution)/shard_map/ppermute | solution.py:53
  86.4 1.4 %collective-permute-start.6 = (bf16[8,16,512]{2,1,0:T(8,128)(2,1)S(1)}, bf16[8,16,512]{2,1,0:T(8,128)(2,1)S(1)}, u32[]{:S(2)}, u32[]{:S(2)}) collective-permute-start(bf16[8,16,512]{2,1,0:T(8,128)(2,1)S(1)} %get-tuple-element.49), channel_id=1, source_target_pairs={{0,8},{8,0},{1,9},{9,1},{2,10},{10,2},{3,11},{11,3},{4,12},{12,4},... | collective-permute-start | bytes 393224 | tf_op jit(solution)/shard_map/ppermute | solution.py:53

commit v5 on v4

--- a/solution.py
+++ b/solution.py
@@ -19,6 +19,7 @@
 NEGATIVE = -1e30
 LOWEST = -1e20
 STREAM_MIB = 50
+DOWN_READY = 1
 SHORT = 3 * 10**9
 F32 = jnp.float32
 BF16 = jnp.bfloat16
@@ -167,7 +168,7 @@
             ref[d] = state[0, :, lanes].astype(BF16)
 
 
-def attend_kernel(lay, recv, out_ref, conv_out, queries, scores):
+def attend_kernel(lay, recv, out_ref, conv_own, conv_out, queries, scores):
     nchan = recv.shape[0]
     per, tokens = lay.per, lay.tokens
     c = lax.axis_index("src")
@@ -176,6 +177,7 @@
     contract = (((1,), (1,)), ((), ()))
     new_keys, new_values, owners = [], [], []
     for s in range(nchan):
+        conv_own[s] = recv[s, lay.conv : lay.conv + lay.conv_rows, :]
         conv_out[s] = recv[s, lay.conv + lay.conv_rows : lay.rows, :]
         heads = recv[s, lay.query : lay.conv, :].astype(F32)
         queries[s * per : (s + 1) * per, :] = heads[0:per, :]
@@ -262,10 +264,66 @@
     return copies
 
 
-def half_starts(own):
+def row_starts(nchan, depth, by_chip, own):
     c = lax.axis_index("src")
-    nchan, depth = own.shape[0], own.shape[2]
-    return [(half * nchan + i) * depth for half in (c, 1 - c) for i in range(nchan)]
+    half = c if own else 1 - c
+    return [((2 * i + half) if by_chip else (half * nchan + i)) * depth for i in range(nchan)]
+
+
+def fetch_kernel(nchan, by_chip, weight, out_ref, sems):
+    depth = weight.shape[0] // (2 * nchan)
+    starts = row_starts(nchan, depth, by_chip, False)[: out_ref.shape[0] // depth]
+    for copy in stream(weight, out_ref, sems, starts):
+        copy.wait()
+
+
+def exchange_and_fetch(x, weight, by_chip, share, name):
+    x, weight = lax.optimization_barrier((x, weight))
+    received = exchange(x)
+    nchan = x.shape[0]
+    fetched = pl.pallas_call(
+        functools.partial(fetch_kernel, nchan, by_chip),
+        out_shape=jax.ShapeDtypeStruct((weight.shape[0] // share, weight.shape[1]), weight.dtype),
+        in_specs=hbm(1),
+        out_specs=vmem(1)[0],
+        scratch_shapes=[pltpu.SemaphoreType.DMA((2 * nchan // share,))],
+        compiler_params=params(STREAM_MIB),
+        cost_estimate=cost(SHORT, 0),
+        name=name,
+    )(weight)
+    return lax.optimization_barrier((received, fetched))
+
+
+def own_kernel(by_chip, lhs, weight, out_ref, buffer, sems):
+    nchan, depth = lhs.shape[0], lhs.shape[2]
+    copies = stream(weight, buffer, sems, row_starts(nchan, depth, by_chip, True))
+    total = None
+    for i, copy in enumerate(copies):
+        copy.wait()
+        part = jnp.dot(
+            lhs[i, 0 : out_ref.shape[0], :], buffer[i * depth : (i + 1) * depth, :], preferred_element_type=F32
+        )
+        total = part if total is None else total + part
+    out_ref[...] = total
+
+
+def rest_start(by_chip, lhs, fetched, weight, buffer, sems):
+    nchan, depth = lhs.shape[0], lhs.shape[2]
+    ready = fetched.shape[0] // depth
+    return stream(weight, buffer, sems, row_starts(nchan, depth, by_chip, False)[ready:])
+
+
+def rest_dot(copies, lhs, total, fetched, buffer):
+    depth, rows = lhs.shape[2], total.shape[0]
+    ready = fetched.shape[0] // depth
+    for i in range(lhs.shape[0]):
+        if i < ready:
+            block = fetched[i * depth : (i + 1) * depth, :]
+        else:
+            copies[i - ready].wait()
+            block = buffer[(i - ready) * depth : (i - ready + 1) * depth, :]
+        total = total + jnp.dot(lhs[i, 0:rows, :], block, preferred_element_type=F32)
+    return total
 
 
 def halves_dot(copies, own, other, buffer, count):
@@ -279,14 +337,12 @@
     return total
 
 
-def out_kernel(own, other, residual, cross, weight, hidden_out, out_ref, buffer, sems):
-    c = lax.axis_index("src")
-    nchan, rows, depth = own.shape
-    starts = [(2 * i + half) * depth for half in (c, 1 - c) for i in range(nchan)]
-    copies = stream(weight, buffer, sems, starts)
+def out_kernel(lhs, partial, residual, cross, fetched, weight, hidden_out, out_ref, buffer, sems):
+    copies = rest_start(True, lhs, fetched, weight, buffer, sems)
+    nchan, rows, _ = lhs.shape
     for i in range(nchan):
         out_ref[i, rows : rows + NS, :] = cross[i]
-    product = halves_dot(copies, own, other, buffer, rows)
+    product = rest_dot(copies, lhs, partial[...], fetched, buffer)
     hidden = (residual[...].astype(F32) + product).astype(BF16)
     hidden_out[...] = hidden
     for i in range(nchan):
@@ -294,10 +350,10 @@
 
 
 def values_kernel(
-    lay, own, other, arrived, other_conv, taps, offset, state_proj, same, weight, conv_out, act_out, rms_out, proj_out,
-    buffer, sems,
+    lay, own, other, own_conv, other_conv, taps, offset, state_proj, same, partial, fetched, weight,
+    conv_out, act_out, rms_out, proj_out, buffer, sems,
 ):
-    copies = stream(weight, buffer, sems, half_starts(own))
+    copies = rest_start(False, other, fetched, weight, buffer, sems)
     c = lax.axis_index("src")
     nchan = own.shape[0]
     rows, cols = act_out.shape
@@ -313,12 +369,12 @@
     for i in range(nchan):
         for b in range(blocks):
             proj_out[i, b * NS : (b + 1) * NS, :] = same[i, :, b * LANES : (b + 1) * LANES]
-    tails = (arrived[:, lay.conv : lay.conv + lay.conv_rows, :].astype(F32), other_conv[...].astype(F32))
+    tails = (own_conv[...].astype(F32), other_conv[...].astype(F32))
     window = []
     for w in range(steps):
         sides = [jnp.concatenate([t[:, b * steps + w, :] for b in range(blocks)], axis=1) for t in tails]
         window.append(in_order(sides[0], sides[1], c))
-    window.append(halves_dot(copies, own, other, buffer, rows) * inverse)
+    window.append(rest_dot(copies, other, partial[...], fetched, buffer) * inverse)
     mixed = jnp.zeros((rows, cols), F32)
     for w in range(steps + 1):
         mixed = mixed + window[w] * taps[w : w + 1, :]
@@ -336,36 +392,48 @@
             proj_out[i, base + b * rows : base + (b + 1) * rows, :] = part[:, b * LANES : (b + 1) * LANES]
 
 
-def gates_kernel(own, other, rms, weight, out_ref, buffer, sems):
-    copies = stream(weight, buffer, sems, half_starts(own))
+def gates_kernel(own, other, rms, weight, down_hbm, out_ref, down_out, buffer, sems, down_sems):
+    nchan, depth = own.shape[0], own.shape[2]
+    copies = stream(
+        weight,
+        buffer,
+        sems,
+        row_starts(nchan, depth, False, True) + row_starts(nchan, depth, False, False),
+    )
+    part_down = down_stream(down_hbm, down_out, down_sems, (1 - lax.axis_index("src"),), 0)
     gate = halves_dot(copies, own, other, buffer, out_ref.shape[0]) * rms[:, 0:1]
     out_ref[...] = gate / (1.0 + jnp.exp(-gate))
-
-
-def down_stream(weight, buffer, sems, halves):
+    for copy in part_down:
+        copy.wait()
+
+
+def down_stream(weight, buffer, sems, halves, first):
     width = weight.shape[1] // 2
-    pieces = sems.shape[0] // 2
-    step = width // pieces
+    step = buffer.shape[1] // sems.shape[0]
+    blocks = [(half, i) for half in halves for i in range(width // step)]
     copies = []
-    for half in halves:
-        for i in range(pieces):
-            slot = len(copies)
-            columns = pl.ds(pl.multiple_of(half * width + i * step, step), step)
-            target = buffer.at[:, pl.ds(slot * step, step)]
-            copies.append(pltpu.make_async_copy(weight.at[:, columns], target, sems.at[slot]))
-            copies[-1].start()
+    for half, i in blocks[first : first + sems.shape[0]]:
+        slot = len(copies)
+        columns = pl.ds(pl.multiple_of(half * width + i * step, step), step)
+        target = buffer.at[:, pl.ds(slot * step, step)]
+        copies.append(pltpu.make_async_copy(weight.at[:, columns], target, sems.at[slot]))
+        copies[-1].start()
     return copies
 
 
-def down_product(copies, gated, buffer, outs):
+def down_product(copies, gated, fetched, buffer, outs):
     cols = outs[0].shape[2]
     step = buffer.shape[1] // len(copies)
-    pieces = len(copies) // len(outs)
-    for slot, copy in enumerate(copies):
-        copy.wait()
+    ready = fetched.shape[1] // step
+    pieces = (ready + len(copies)) // len(outs)
+    for slot in range(ready + len(copies)):
+        if slot < ready:
+            block = fetched[:, slot * step : (slot + 1) * step]
+        else:
+            copies[slot - ready].wait()
+            block = buffer[:, (slot - ready) * step : (slot - ready + 1) * step]
         out_ref, i = outs[slot // pieces], slot % pieces
-        part = jnp.dot(gated, buffer[:, slot * step : (slot + 1) * step], preferred_element_type=F32)
-        part = part.astype(out_ref.dtype)
+        part = jnp.dot(gated, block, preferred_element_type=F32).astype(out_ref.dtype)
         for j in range(step // cols):
             out_ref[i * (step // cols) + j] = part[:, j * cols : (j + 1) * cols]
 
@@ -380,17 +448,20 @@
     step_bias,
     decay_log,
     skip_gain,
+    fetched,
     weight,
-    next_out,
+    next_hbm,
     send_out,
     keep_out,
     turned,
     mixed,
+    next_out,
     buffer,
     sems,
+    save_sem,
 ):
     c = lax.axis_index("src")
-    copies = down_stream(weight, buffer, sems, (1 - c, c))
+    copies = down_stream(weight, buffer, sems, (1 - c, c), DOWN_READY)
     nchan = own.shape[0]
     rows, cols = act_ref.shape
     blocks = cols // LANES
@@ -425,8 +496,11 @@
                 after = jnp.exp(step[q : q + 1, lanes] * rate[:, lanes]) * state + fed[q : q + 1, lanes] * b_col
                 next_out[place, :, lanes] = after
                 mixed[q : q + 1, lanes] = jnp.sum(after * c_col, axis=0, keepdims=True)
+    save = pltpu.make_async_copy(next_out, next_hbm, save_sem)
+    save.start()
     gated = ((own_first(mixed[...], c) + skip_gain[...] * act) * gate_ref[...]).astype(BF16)
-    down_product(copies, gated, buffer, (send_out, keep_out))
+    down_product(copies, gated, fetched, buffer, (send_out, keep_out))
+    save.wait()
 
 
 def finish_kernel(final, hidden, out_ref):
@@ -503,11 +577,12 @@
     arrived, residual, same, cross = lax.optimization_barrier((arrived, residual, same, cross))
 
     pairs = rows * lay.per
-    partial, conv_send = call(
+    conv_cut = shape((nchan, lay.conv_rows, LANES), BF16)
+    partial, conv_own, conv_send = call(
         functools.partial(attend_kernel, lay),
-        out_shape=(shape((pairs, HD + LANES), F32), shape((nchan, lay.conv_rows, LANES), BF16)),
+        out_shape=(shape((pairs, HD + LANES), F32), conv_cut, conv_cut),
         in_specs=vmem(1),
-        out_specs=tuple(vmem(2)),
+        out_specs=tuple(vmem(3)),
         scratch_shapes=[VM((pairs, HD), F32), VM((pairs, nchan * lay.tokens), F32)],
         compiler_params=params(4 if held < 16 else 40),
         name="attend",
@@ -524,21 +599,38 @@
         compiler_params=params(4),
         name="merge",
     )(partial, other_partial)
-    att_own = exchange(attended)
+    att_own, out_fetched = exchange_and_fetch(attended, out_heads, True, 4, "fetch_out")
     att_other = swap(att_own)
+    half_streamed = [VM((D // 2, cols), BF16), pltpu.SemaphoreType.DMA((nchan,))]
+    rest_streamed = [VM((D // 4, cols), BF16), pltpu.SemaphoreType.DMA((nchan // 2,))]
+
+    def own_product(x, weight, by_chip, name):
+        return call(
+            functools.partial(own_kernel, by_chip),
+            out_shape=shape((rows, cols), F32),
+            in_specs=vmem(1) + hbm(1),
+            out_specs=vmem(1)[0],
+            scratch_shapes=half_streamed,
+            compiler_params=params(STREAM_MIB),
+            cost_estimate=cost(SHORT, 0),
+            name=name,
+        )(x, weight)
+
+    out_partial = own_product(att_own, out_heads, True, "out_own")
 
     streamed = [VM((D, cols), BF16), pltpu.SemaphoreType.DMA((2 * nchan,))]
     hidden, hid_send = call(
         out_kernel,
         out_shape=(shape((rows, cols), BF16), shape((nchan, rows + NS, cols), BF16)),
-        in_specs=vmem(4) + hbm(1),
+        in_specs=vmem(5) + hbm(1),
         out_specs=tuple(vmem(2)),
-        scratch_shapes=streamed,
+        scratch_shapes=rest_streamed,
         compiler_params=params(STREAM_MIB),
         name="out",
-    )(att_own, att_other, residual, cross, out_heads)
-    hid_own = exchange(hid_send)
+    )(att_other, out_partial, residual, cross, out_fetched, out_heads)
+    hid_own, values_fetched = exchange_and_fetch(hid_send, in_values, False, 4, "fetch_values")
     hid_other = swap(hid_own)
+    values_partial = own_product(hid_own, in_values, False, "values_own")
 
     sent_rows = (cols // LANES) * NS + (round_up(state_proj.shape[1], LANES) // LANES) * rows
     conv_next, act, rms, part = call(
@@ -549,27 +641,35 @@
             shape((rows, LANES), F32),
             shape((nchan, sent_rows, LANES), BF16),
         ),
-        in_specs=vmem(8) + hbm(1),
+        in_specs=vmem(10) + hbm(1),
         out_specs=tuple(vmem(4)),
-        scratch_shapes=streamed,
+        scratch_shapes=[VM((D // 2 - D // 4, cols), BF16), pltpu.SemaphoreType.DMA((nchan - 2 * nchan // 4,))],
         compiler_params=params(STREAM_MIB),
         name="values",
-    )(hid_own, hid_other, arrived, other_conv, conv_taps, conv_offset[None, :], state_proj.T, same, in_values)
+    )(hid_own, hid_other, conv_own, other_conv, conv_taps, conv_offset[None, :], state_proj.T, same, values_partial, values_fetched, in_values)
+    part, down_weight = lax.optimization_barrier((part, mamba_down))
     proj_own = exchange(part)
-    gate = call(
+    pieces = 8
+    piece = D // pieces
+    gate, down_fetched = call(
         gates_kernel,
-        out_shape=shape((rows, cols), F32),
-        in_specs=vmem(3) + hbm(1),
-        out_specs=vmem(1)[0],
-        scratch_shapes=streamed,
+        out_shape=(shape((rows, cols), F32), shape((cols, DOWN_READY * piece), BF16)),
+        in_specs=vmem(3) + hbm(2),
+        out_specs=tuple(vmem(2)),
+        scratch_shapes=streamed + [pltpu.SemaphoreType.DMA((DOWN_READY,))],
         compiler_params=params(STREAM_MIB),
         cost_estimate=cost(SHORT, 0),
         name="gates",
-    )(hid_own, hid_other, rms, in_gates)
-    proj_own, gate = lax.optimization_barrier((proj_own, gate))
+    )(hid_own, hid_other, rms, in_gates, down_weight)
+    proj_own, gate, down_fetched = lax.optimization_barrier((proj_own, gate, down_fetched))
     proj_other = swap(proj_own)
 
-    down_streamed = [VM((cols, D), BF16), pltpu.SemaphoreType.DMA((8,))]
+    down_streamed = [
+        VM((rows, NS, cols), F32),
+        VM((cols, D - DOWN_READY * piece), BF16),
+        pltpu.SemaphoreType.DMA((pieces - DOWN_READY,)),
+        pltpu.SemaphoreType.DMA,
+    ]
     mamba_next, send, keep = call(
         scan_kernel,
         out_shape=(
@@ -577,8 +677,8 @@
             shape((nchan, rows, cols), BF16),
             shape((nchan, rows, cols), F32),
         ),
-        in_specs=vmem(9) + hbm(1),
-        out_specs=tuple(vmem(3)),
+        in_specs=vmem(10) + hbm(1),
+        out_specs=tuple(hbm(1) + vmem(2)),
         scratch_shapes=[VM((LANES, LANES), F32), VM((rows, cols), F32)] + down_streamed,
         compiler_params=params(STREAM_MIB),
         name="scan",
@@ -592,6 +692,7 @@
         step_bias[None, :],
         decay_log,
         skip_gain[None, :],
+        down_fetched,
         mamba_down,
     )
     taken = swap(send)

time: 99.8 us -> 101 us (1.012)
  blocking collectives: 33.6 us -> 10.8 us
  waiting for transfers between devices: 29.6 us -> 40.9 us
  starting transfers between devices: 12.2 us -> 19.2 us
  Pallas kernels: 20.6 us -> 26.1 us
    all_to_all x3 -> x1, blocking collectives: 33.6 us -> 10.8 us  [exchange(): return lax.all_to_all(x, 'chan', split_axis=0, concat_axis=0, tiled=True)]
    all_to_all x2 -> x4, waiting for transfers between devices: 22 us -> 36.2 us  [exchange(): return lax.all_to_all(x, 'chan', split_axis=0, concat_axis=0, tiled=True)]
    pallas_call x1 -> x5, Pallas kernels: 3.72 us -> 11.9 us  [the longest x2 4.79 us: own_product(): call(functools.partial(own_kernel, by_chip), out_shape=shape((rows, cols)...]
    all_to_all x2 -> x4, starting transfers between devices: 10.9 us -> 17.9 us  [exchange(): return lax.all_to_all(x, 'chan', split_axis=0, concat_axis=0, tiled=True)]
    ppermute x7, waiting for transfers between devices: 7.63 us -> 4.76 us  [swap(): return lax.ppermute(x, 'src', [(0, 1), (1, 0)])]
    pallas_call x1, Pallas kernels: 4.66 us -> 2.89 us  [on_device(): call(functools.partial(values_kernel, lay), out_shape=(shape((steps, rows...]
    pallas_call x1, Pallas kernels: 3.72 us -> 2.65 us  [on_device(): call(out_kernel, out_shape=(shape((rows, cols), BF16), shape((nchan, rows...]
  transfers between devices with their start and end apart: 9 -> 11, of which waited for: 8 -> 8; matrix products, arithmetic and copies ran while one was open for 0% -> 0% of each run, Pallas kernels for 4% -> 12%
where the time goes in v5:
time: 101 us; the launch traced here: 100 us
  waiting for transfers between devices  40.9 us (40%)
  Pallas kernels  26.1 us (26%)
  starting transfers between devices  19.2 us (19%)
  blocking collectives  10.8 us (11%)
  local copies, waits for them, and re-layouts  2.41 us (2%)
    all_to_all x4, waiting for transfers between devices, exchange(): return lax.all_to_all(x, 'chan', split_axis=0, concat_axis=0, tiled=True)  36.2 us
    all_to_all x4, starting transfers between devices, exchange(): return lax.all_to_all(x, 'chan', split_axis=0, concat_axis=0, tiled=True)  17.9 us
    all_to_all x1, blocking collectives, exchange(): return lax.all_to_all(x, 'chan', split_axis=0, concat_axis=0, tiled=True)  10.8 us
    pallas_call x2, Pallas kernels, own_product(): call(functools.partial(own_kernel, by_chip), out_shape=shape((rows, cols)...  4.79 us
    ppermute x7, waiting for transfers between devices, swap(): return lax.ppermute(x, 'src', [(0, 1), (1, 0)])  4.76 us
    pallas_call x1, Pallas kernels, on_device(): call(scan_kernel, out_shape=(shape((rows, NS, cols), F32), shape((nchan,...  4.14 us
    pallas_call x1, Pallas kernels, on_device(): call(gates_kernel, out_shape=(shape((rows, cols), F32), shape((cols, DOWN...  3.91 us
    pallas_call x2, Pallas kernels, exchange_and_fetch(): pl.pallas_call(functools.partial(fetch_kernel, nchan, by_chip), out_shape...  3.16 us
  transfers between devices with their start and end apart: 11, of which 8 were waited for; matrix products, arithmetic and copies ran while one was open for 0% of the time, Pallas kernels for 12%

profile of v5, /device:TPU:0, one launch (start us, length us, event | category | flops | bytes accessed | tf_op | source)
XLA Modules:
  0.0 100.2 jit_solution(17650826150085968459)
XLA Ops:
  0.6 0.5 collective-permute-start
  1.2 1.1 %collective-permute-done.other_hbm = bf16[1,8192]{1,0:T(2,128)(2,1)S(1)} collective-permute-done((bf16[1,8192]{1,0:T(2,128)(2,1)}, bf16[1,8192]{1,0:T(2,128)(2,1)S(1)}, u32[]{:S(2)}, u32[]{:S(2)}) %collective-permute-start) | collective-permute-done | bytes 16416 | tf_op jit(solution)/shard_map/ppermute | solution.py:54
  2.2 0.0 copy-start.9
  2.2 0.6 copy-done.9
  2.8 2.2 %pack.1 = bf16[8,320,128]{2,1,0:T(8,128)(2,1)} custom-call(bf16[1,8192]{1,0:T(2,128)(2,1)} %query_hbm.1, bf16[1,8192]{1,0:T(2,128)(2,1)} %copy-done.9, bf16[1,2048]{1,0:T(2,128)(2,1)} %newkv_hbm.1, bf16[8,16,2048]{2,1,0:T(8,128)(2,1)} %pages_hbm.1, f32[3,1,8192]{2,1,0:T(1,128)} %bitcast.10, s32[8]{0:T(128)} %owner_hbm.1, s32[8]{0:T(128)} %index_hbm.1, ...), custom_call_target="tpu_custom_call" | custom-call | tf_op jit(solution)/shard_map/pack/pallas_call | solution.py:546
  5.1 7.2 %all-to-all-start = ((bf16[8,320,128]{2,1,0:T(8,128)(2,1)}), bf16[8,320,128]{2,1,0:T(8,128)(2,1)S(1)}, u32[]{:S(2)}, u32[]{:S(2)}) async-start(bf16[8,320,128]{2,1,0:T(8,128)(2,1)} %pack.1), calls=%async_computation | async-start | bytes 1310720 | tf_op jit(solution)/shard_map/all_to_all | solution.py:58
  12.3 0.0 copy-start.7
  12.3 1.0 %copy-done.7 = f32[1,16,8192]{2,1,0:T(8,128)S(1)} copy-done((f32[1,16,8192]{2,1,0:T(8,128)S(1)}, f32[1,16,8192]{2,1,0:T(8,128)}, u32[]{:S(2)}) %copy-start.7) | copy-done | bytes 524312
  13.3 0.0 copy-start.8
  13.3 0.7 copy-done.8
  14.1 15.8 %all-to-all-done.recv = bf16[8,320,128]{2,1,0:T(8,128)(2,1)S(1)} async-done(((bf16[8,320,128]{2,1,0:T(8,128)(2,1)}), bf16[8,320,128]{2,1,0:T(8,128)(2,1)S(1)}, u32[]{:S(2)}, u32[]{:S(2)}) %all-to-all-start) | async-done | bytes 655392 | tf_op jit(solution)/shard_map/all_to_all | solution.py:58
  29.9 0.7 attend.1
  30.6 0.1 collective-permute-start.1
  30.7 0.5 collective-permute-start.2
  31.2 0.9 collective-permute-done.2.other_conv
  32.1 0.0 collective-permute-done.1.other
  32.1 0.9 merge.1
  33.0 3.6 %all-to-all-start.1 = ((bf16[8,16,512]{2,1,0:T(8,128)(2,1)}), bf16[8,16,512]{2,1,0:T(8,128)(2,1)S(1)}, u32[]{:S(2)}, u32[]{:S(2)}) async-start(bf16[8,16,512]{2,1,0:T(8,128)(2,1)} %merge.1), calls=%async_computation.1 | async-start | bytes 262144 | tf_op jit(solution)/shard_map/all_to_all | solution.py:58
  36.6 1.5 %fetch_out.1.fetched = bf16[2048,512]{1,0:T(8,128)(2,1)S(1)} custom-call(bf16[8192,512]{1,0:T(8,128)(2,1)} %weight.8), custom_call_target="tpu_custom_call" | custom-call | flops 3000000000 | tf_op jit(solution)/shard_map/fetch_out/pallas_call | solution.py:284
  38.2 5.9 %all-to-all-done.1.lhs = bf16[8,16,512]{2,1,0:T(8,128)(2,1)S(1)} async-done(((bf16[8,16,512]{2,1,0:T(8,128)(2,1)}), bf16[8,16,512]{2,1,0:T(8,128)(2,1)S(1)}, u32[]{:S(2)}, u32[]{:S(2)}) %all-to-all-start.1) | async-done | bytes 131104 | tf_op jit(solution)/shard_map/all_to_all | solution.py:58
  44.1 0.0 collective-permute-start.3
  44.1 2.4 %out_own.1.partial = f32[16,512]{1,0:T(8,128)S(1)} custom-call(bf16[8,16,512]{2,1,0:T(8,128)(2,1)S(1)} %all-to-all-done.1.lhs, bf16[8192,512]{1,0:T(8,128)(2,1)} %weight.8), custom_call_target="tpu_custom_call" | custom-call | flops 3000000000 | tf_op jit(solution)/shard_map/out_own/pallas_call | solution.py:608
  46.5 0.0 collective-permute-done.3.lhs
  46.5 2.7 %out.1 = (bf16[16,512]{1,0:T(8,128)(2,1)S(1)}, bf16[8,32,512]{2,1,0:T(8,128)(2,1)}) custom-call(bf16[8,16,512]{2,1,0:T(8,128)(2,1)S(1)} %collective-permute-done.3.lhs, f32[16,512]{1,0:T(8,128)S(1)} %out_own.1.partial, bf16[16,512]{1,0:T(8,128)(2,1)S(1)} %get-tuple-element.55.residual, bf16[8,16,512]{2,1,0:T(8,128)(2,1)S(1)} %get-tuple-element.56.cross, ...), custom_call_target="tpu_custom_call" | custom-call | tf_op jit(solution)/shard_map/out/pallas_call | solution.py:622
  49.2 3.4 %all-to-all-start.2 = ((bf16[8,32,512]{2,1,0:T(8,128)(2,1)}), bf16[8,32,512]{2,1,0:T(8,128)(2,1)S(1)}, u32[]{:S(2)}, u32[]{:S(2)}) async-start(bf16[8,32,512]{2,1,0:T(8,128)(2,1)} %get-tuple-element.59), calls=%async_computation.2 | async-start | bytes 524288 | tf_op jit(solution)/shard_map/all_to_all | solution.py:58
  52.6 0.0 copy-start
  52.6 0.0 copy-start.3
  52.6 0.0 copy-start.6
  52.7 1.6 %fetch_values.1.fetched = bf16[2048,512]{1,0:T(8,128)(2,1)S(1)} custom-call(bf16[8192,512]{1,0:T(8,128)(2,1)} %weight.11), custom_call_target="tpu_custom_call" | custom-call | flops 3000000000 | tf_op jit(solution)/shard_map/fetch_values/pallas_call | solution.py:284
  54.3 8.1 %all-to-all-done.2.lhs.own = bf16[8,32,512]{2,1,0:T(8,128)(2,1)S(1)} async-done(((bf16[8,32,512]{2,1,0:T(8,128)(2,1)}), bf16[8,32,512]{2,1,0:T(8,128)(2,1)S(1)}, u32[]{:S(2)}, u32[]{:S(2)}) %all-to-all-start.2) | async-done | bytes 262176 | tf_op jit(solution)/shard_map/all_to_all | solution.py:58
  62.4 0.0 collective-permute-start.4
  62.4 2.4 %values_own.1.partial = f32[16,512]{1,0:T(8,128)S(1)} custom-call(bf16[8,32,512]{2,1,0:T(8,128)(2,1)S(1)} %all-to-all-done.2.lhs.own, bf16[8192,512]{1,0:T(8,128)(2,1)} %weight.11), custom_call_target="tpu_custom_call" | custom-call | flops 3000000000 | tf_op jit(solution)/shard_map/values_own/pallas_call | solution.py:608
  64.8 0.0 collective-permute-done.4.other.hid_other
  64.8 0.0 copy-done
  64.9 0.0 copy-done.3
  64.9 0.0 copy-done.6
  64.9 2.9 %values.1 = (f32[3,16,512]{2,1,0:T(8,128)}, f32[16,512]{1,0:T(8,128)S(1)}, f32[16,128]{1,0:T(8,128)S(1)}, bf16[8,144,128]{2,1,0:T(8,128)(2,1)}) custom-call(bf16[8,32,512]{2,1,0:T(8,128)(2,1)S(1)} %all-to-all-done.2.lhs.own, bf16[8,32,512]{2,1,0:T(8,128)(2,1)S(1)} %collective-permute-done.4.other.hid_other, ...), custom_call_target="tpu_custom_call" | custom-call | tf_op jit(solution)/shard_map/values/pallas_call | solution.py:636
  67.8 3.6 %all-to-all-start.3 = ((bf16[8,144,128]{2,1,0:T(8,128)(2,1)}), bf16[8,144,128]{2,1,0:T(8,128)(2,1)S(1)}, u32[]{:S(2)}, u32[]{:S(2)}) async-start(bf16[8,144,128]{2,1,0:T(8,128)(2,1)} %get-tuple-element.67), calls=%async_computation.3 | async-start | bytes 589824 | tf_op jit(solution)/shard_map/all_to_all | solution.py:58
  71.4 0.0 copy-start.1
  71.4 0.0 copy-start.2
  71.4 0.0 copy-start.4
  71.4 0.0 copy-start.5
  71.4 3.9 %gates.1 = (f32[16,512]{1,0:T(8,128)S(1)}, bf16[512,1024]{1,0:T(8,128)(2,1)S(1)}) custom-call(bf16[8,32,512]{2,1,0:T(8,128)(2,1)S(1)} %all-to-all-done.2.lhs.own, bf16[8,32,512]{2,1,0:T(8,128)(2,1)S(1)} %collective-permute-done.4.other.hid_other, f32[16,128]{1,0:T(8,128)S(1)} %get-tuple-element.68.rms, bf16[8192,512]{1,0:T(8,128)(2,1)} %weight.12, ...), custom_call_target="tpu_custom_call" | custom-call | flops 3000000000 | tf_op jit(solution)/shard_map/gates/pallas_call | solution.py:654
  75.4 6.3 %all-to-all-done.3.own = bf16[8,144,128]{2,1,0:T(8,128)(2,1)S(1)} async-done(((bf16[8,144,128]{2,1,0:T(8,128)(2,1)}), bf16[8,144,128]{2,1,0:T(8,128)(2,1)S(1)}, u32[]{:S(2)}, u32[]{:S(2)}) %all-to-all-start.3) | async-done | bytes 294944 | tf_op jit(solution)/shard_map/all_to_all | solution.py:58
  81.7 0.0 collective-permute-start.5
  81.7 1.6 %collective-permute-done.5.other = bf16[8,144,128]{2,1,0:T(8,128)(2,1)S(1)} collective-permute-done((bf16[8,144,128]{2,1,0:T(8,128)(2,1)S(1)}, bf16[8,144,128]{2,1,0:T(8,128)(2,1)S(1)}, u32[]{:S(2)}, u32[]{:S(2)}) %collective-permute-start.5) | collective-permute-done | bytes 294944 | tf_op jit(solution)/shard_map/ppermute | solution.py:54
  83.2 0.0 copy-done.1
  83.2 0.0 copy-done.2
  83.2 0.0 copy-done.4
  83.2 0.0 copy-done.5
  83.3 4.1 %scan.1 = (f32[16,16,512]{2,1,0:T(8,128)}, bf16[8,16,512]{2,1,0:T(8,128)(2,1)S(1)}, f32[8,16,512]{2,1,0:T(8,128)S(1)}) custom-call(bf16[8,144,128]{2,1,0:T(8,128)(2,1)S(1)} %all-to-all-done.3.own, bf16[8,144,128]{2,1,0:T(8,128)(2,1)S(1)} %collective-permute-done.5.other, bf16[8,32,512]{2,1,0:T(8,128)(2,1)S(1)} %collective-permute-done.4.other.hid_other, ...), custom_call_target="tpu_custom_call" | custom-call | tf_op jit(solution)/shard_map/scan/pallas_call | solution.py:673
  87.4 0.2 collective-permute-start.6
  87.6 1.2 %collective-permute-done.6 = bf16[8,16,512]{2,1,0:T(8,128)(2,1)S(1)} collective-permute-done((bf16[8,16,512]{2,1,0:T(8,128)(2,1)S(1)}, bf16[8,16,512]{2,1,0:T(8,128)(2,1)S(1)}, u32[]{:S(2)}, u32[]{:S(2)}) %collective-permute-start.6) | collective-permute-done | bytes 131104 | tf_op jit(solution)/shard_map/ppermute | solution.py:54
  88.8 10.8 %all_to_all.25.final = bf16[8,16,512]{2,1,0:T(8,128)(2,1)S(1)} all-to-all(bf16[8,16,512]{2,1,0:T(8,128)(2,1)S(1)} %add_convert_fusion), channel_id=1, replica_groups=mesh['groups'=2,'src'=2,'chan'=8] {'chan'}, dimensions={0} | all-to-all | bytes 262144 | tf_op jit(solution)/shard_map/all_to_all | solution.py:58
  99.6 0.6 finish.1
  (2 shorter events, 0.1 us)
Async XLA Ops:
  0.6 1.6 %collective-permute-start = (bf16[1,8192]{1,0:T(2,128)(2,1)}, bf16[1,8192]{1,0:T(2,128)(2,1)S(1)}, u32[]{:S(2)}, u32[]{:S(2)}) collective-permute-start(bf16[1,8192]{1,0:T(2,128)(2,1)} %query_hbm.1), channel_id=1, source_target_pairs={{0,8},{8,0},{1,9},{9,1},{2,10},{10,2},{3,11},{11,3},{4,12},{12,4},... | collective-permute-start | bytes 49160 | tf_op jit(solution)/shard_map/ppermute | solution.py:54
  2.2 0.6 copy-start.9
  5.1 24.8 %all-to-all-start = ((bf16[8,320,128]{2,1,0:T(8,128)(2,1)}), bf16[8,320,128]{2,1,0:T(8,128)(2,1)S(1)}, u32[]{:S(2)}, u32[]{:S(2)}) async-start(bf16[8,320,128]{2,1,0:T(8,128)(2,1)} %pack.1), calls=%async_computation | async-start | bytes 1310720 | tf_op jit(solution)/shard_map/all_to_all | solution.py:58
  12.3 1.0 %copy-start.7 = (f32[1,16,8192]{2,1,0:T(8,128)S(1)}, f32[1,16,8192]{2,1,0:T(8,128)}, u32[]{:S(2)}) copy-start(f32[1,16,8192]{2,1,0:T(8,128)} %state) | copy-start | bytes 1572868
  13.3 0.7 copy-start.8
  30.6 1.5 %collective-permute-start.1 = (f32[128,256]{1,0:T(8,128)S(1)}, f32[128,256]{1,0:T(8,128)S(1)}, u32[]{:S(2)}, u32[]{:S(2)}) collective-permute-start(f32[128,256]{1,0:T(8,128)S(1)} %get-tuple-element.49.own), channel_id=1, source_target_pairs={{0,8},{8,0},{1,9},{9,1},{2,10},{10,2},{3,11},{11,3},{4,12},{12,4},... | collective-permute-start | bytes 393224 | tf_op jit(solution)/shard_map/ppermute | solution.py:54
  30.7 1.4 %collective-permute-start.2 = (bf16[8,16,128]{2,1,0:T(8,128)(2,1)S(1)}, bf16[8,16,128]{2,1,0:T(8,128)(2,1)S(1)}, u32[]{:S(2)}, u32[]{:S(2)}) collective-permute-start(bf16[8,16,128]{2,1,0:T(8,128)(2,1)S(1)} %get-tuple-element.50), channel_id=1, source_target_pairs={{0,8},{8,0},{1,9},{9,1},{2,10},{10,2},{3,11},{11,3},{4,12},{12,4},... | collective-permute-start | bytes 98312 | tf_op jit(solution)/shard_map/ppermute | solution.py:54
  33.0 11.1 %all-to-all-start.1 = ((bf16[8,16,512]{2,1,0:T(8,128)(2,1)}), bf16[8,16,512]{2,1,0:T(8,128)(2,1)S(1)}, u32[]{:S(2)}, u32[]{:S(2)}) async-start(bf16[8,16,512]{2,1,0:T(8,128)(2,1)} %merge.1), calls=%async_computation.1 | async-start | bytes 262144 | tf_op jit(solution)/shard_map/all_to_all | solution.py:58
  44.1 2.4 %collective-permute-start.3 = (bf16[8,16,512]{2,1,0:T(8,128)(2,1)S(1)}, bf16[8,16,512]{2,1,0:T(8,128)(2,1)S(1)}, u32[]{:S(2)}, u32[]{:S(2)}) collective-permute-start(bf16[8,16,512]{2,1,0:T(8,128)(2,1)S(1)} %all-to-all-done.1.lhs), channel_id=1, source_target_pairs={{0,8},{8,0},{1,9},{9,1},{2,10},{10,2},{3,11},{11,3},{4,12},{12,4},... | collective-permute-start | bytes 393224 | tf_op jit(solution)/shard_map/ppermute | solution.py:54
  49.2 13.2 %all-to-all-start.2 = ((bf16[8,32,512]{2,1,0:T(8,128)(2,1)}), bf16[8,32,512]{2,1,0:T(8,128)(2,1)S(1)}, u32[]{:S(2)}, u32[]{:S(2)}) async-start(bf16[8,32,512]{2,1,0:T(8,128)(2,1)} %get-tuple-element.59), calls=%async_computation.2 | async-start | bytes 524288 | tf_op jit(solution)/shard_map/all_to_all | solution.py:58
  52.6 12.2 %copy-start = (bf16[512,544]{0,1:T(8,128)(2,1)S(1)}, bf16[512,544]{0,1:T(8,128)(2,1)}, u32[]{:S(2)}) copy-start(bf16[512,544]{0,1:T(8,128)(2,1)} %param.34) | copy-start | bytes 1671172
  52.6 12.2 %copy-start.3 = (f32[4,512]{1,0:T(4,128)S(1)}, f32[4,512]{1,0:T(4,128)}, u32[]{:S(2)}) copy-start(f32[4,512]{1,0:T(4,128)} %taps.1) | copy-start | bytes 24580
  52.6 12.2 %copy-start.6 = (f32[512]{0:T(512)S(1)}, f32[512]{0:T(512)}, u32[]{:S(2)}) copy-start(f32[512]{0:T(512)} %param.33) | copy-start | bytes 6148
  62.4 2.4 %collective-permute-start.4 = (bf16[8,32,512]{2,1,0:T(8,128)(2,1)S(1)}, bf16[8,32,512]{2,1,0:T(8,128)(2,1)S(1)}, u32[]{:S(2)}, u32[]{:S(2)}) collective-permute-start(bf16[8,32,512]{2,1,0:T(8,128)(2,1)S(1)} %all-to-all-done.2.lhs.own), channel_id=1, source_target_pairs={{0,8},{8,0},{1,9},{9,1},{2,10},{10,2},{3,11},{11,3},{4,12},{12,4},... | collective-permute-start | bytes 786440 | tf_op jit(solution)/shard_map/ppermute | solution.py:54
  67.8 13.9 %all-to-all-start.3 = ((bf16[8,144,128]{2,1,0:T(8,128)(2,1)}), bf16[8,144,128]{2,1,0:T(8,128)(2,1)S(1)}, u32[]{:S(2)}, u32[]{:S(2)}) async-start(bf16[8,144,128]{2,1,0:T(8,128)(2,1)} %get-tuple-element.67), calls=%async_computation.3 | async-start | bytes 589824 | tf_op jit(solution)/shard_map/all_to_all | solution.py:58
  71.4 11.8 %copy-start.1 = (bf16[512,512]{1,0:T(8,128)(2,1)S(1)}, bf16[512,512]{1,0:T(8,128)(2,1)}, u32[]{:S(2)}) copy-start(bf16[512,512]{1,0:T(8,128)(2,1)} %step_proj.1) | copy-start | bytes 1572868
  71.4 11.8 %copy-start.2 = (f32[16,512]{1,0:T(8,128)S(1)}, f32[16,512]{1,0:T(8,128)}, u32[]{:S(2)}) copy-start(f32[16,512]{1,0:T(8,128)} %decay_log.1) | copy-start | bytes 98308
  71.4 11.8 %copy-start.4 = (f32[512]{0:T(512)S(1)}, f32[512]{0:T(512)}, u32[]{:S(2)}) copy-start(f32[512]{0:T(512)} %param.36) | copy-start | bytes 6148
  71.4 11.8 %copy-start.5 = (f32[512]{0:T(512)S(1)}, f32[512]{0:T(512)}, u32[]{:S(2)}) copy-start(f32[512]{0:T(512)} %param.38) | copy-start | bytes 6148
  81.7 1.6 %collective-permute-start.5 = (bf16[8,144,128]{2,1,0:T(8,128)(2,1)S(1)}, bf16[8,144,128]{2,1,0:T(8,128)(2,1)S(1)}, u32[]{:S(2)}, u32[]{:S(2)}) collective-permute-start(bf16[8,144,128]{2,1,0:T(8,128)(2,1)S(1)} %all-to-all-done.3.own), channel_id=1, source_target_pairs={{0,8},{8,0},{1,9},{9,1},{2,10},{10,2},{3,11},{11,3},{4,12},{12,4},... | collective-permute-start | bytes 884744 | tf_op jit(solution)/shard_map/ppermute | solution.py:54
  87.4 1.4 %collective-permute-start.6 = (bf16[8,16,512]{2,1,0:T(8,128)(2,1)S(1)}, bf16[8,16,512]{2,1,0:T(8,128)(2,1)S(1)}, u32[]{:S(2)}, u32[]{:S(2)}) collective-permute-start(bf16[8,16,512]{2,1,0:T(8,128)(2,1)S(1)} %get-tuple-element.77), channel_id=1, source_target_pairs={{0,8},{8,0},{1,9},{9,1},{2,10},{10,2},{3,11},{11,3},{4,12},{12,4},... | collective-permute-start | bytes 393224 | tf_op jit(solution)/shard_map/ppermute | solution.py:54

commit v6 on v5

--- a/solution.py
+++ b/solution.py
@@ -270,60 +270,20 @@
     return [((2 * i + half) if by_chip else (half * nchan + i)) * depth for i in range(nchan)]
 
 
-def fetch_kernel(nchan, by_chip, weight, out_ref, sems):
-    depth = weight.shape[0] // (2 * nchan)
-    starts = row_starts(nchan, depth, by_chip, False)[: out_ref.shape[0] // depth]
-    for copy in stream(weight, out_ref, sems, starts):
+def half_dot(copies, lhs, total, buffer, rows):
+    depth = lhs.shape[2]
+    for i, copy in enumerate(copies):
         copy.wait()
-
-
-def exchange_and_fetch(x, weight, by_chip, share, name):
-    x, weight = lax.optimization_barrier((x, weight))
-    received = exchange(x)
-    nchan = x.shape[0]
-    fetched = pl.pallas_call(
-        functools.partial(fetch_kernel, nchan, by_chip),
-        out_shape=jax.ShapeDtypeStruct((weight.shape[0] // share, weight.shape[1]), weight.dtype),
-        in_specs=hbm(1),
-        out_specs=vmem(1)[0],
-        scratch_shapes=[pltpu.SemaphoreType.DMA((2 * nchan // share,))],
-        compiler_params=params(STREAM_MIB),
-        cost_estimate=cost(SHORT, 0),
-        name=name,
-    )(weight)
-    return lax.optimization_barrier((received, fetched))
+        block = buffer[i * depth : (i + 1) * depth, :]
+        part = jnp.dot(lhs[i, 0:rows, :], block, preferred_element_type=F32)
+        total = part if total is None else total + part
+    return total
 
 
 def own_kernel(by_chip, lhs, weight, out_ref, buffer, sems):
     nchan, depth = lhs.shape[0], lhs.shape[2]
     copies = stream(weight, buffer, sems, row_starts(nchan, depth, by_chip, True))
-    total = None
-    for i, copy in enumerate(copies):
-        copy.wait()
-        part = jnp.dot(
-            lhs[i, 0 : out_ref.shape[0], :], buffer[i * depth : (i + 1) * depth, :], preferred_element_type=F32
-        )
-        total = part if total is None else total + part
-    out_ref[...] = total
-
-
-def rest_start(by_chip, lhs, fetched, weight, buffer, sems):
-    nchan, depth = lhs.shape[0], lhs.shape[2]
-    ready = fetched.shape[0] // depth
-    return stream(weight, buffer, sems, row_starts(nchan, depth, by_chip, False)[ready:])
-
-
-def rest_dot(copies, lhs, total, fetched, buffer):
-    depth, rows = lhs.shape[2], total.shape[0]
-    ready = fetched.shape[0] // depth
-    for i in range(lhs.shape[0]):
-        if i < ready:
-            block = fetched[i * depth : (i + 1) * depth, :]
-        else:
-            copies[i - ready].wait()
-            block = buffer[(i - ready) * depth : (i - ready + 1) * depth, :]
-        total = total + jnp.dot(lhs[i, 0:rows, :], block, preferred_element_type=F32)
-    return total
+    out_ref[...] = half_dot(copies, lhs, None, buffer, out_ref.shape[0])
 
 
 def halves_dot(copies, own, other, buffer, count):
@@ -337,12 +297,12 @@
     return total
 
 
-def out_kernel(lhs, partial, residual, cross, fetched, weight, hidden_out, out_ref, buffer, sems):
-    copies = rest_start(True, lhs, fetched, weight, buffer, sems)
-    nchan, rows, _ = lhs.shape
+def out_kernel(lhs, partial, residual, cross, weight, hidden_out, out_ref, buffer, sems):
+    nchan, rows, depth = lhs.shape
+    copies = stream(weight, buffer, sems, row_starts(nchan, depth, True, False))
     for i in range(nchan):
         out_ref[i, rows : rows + NS, :] = cross[i]
-    product = rest_dot(copies, lhs, partial[...], fetched, buffer)
+    product = half_dot(copies, lhs, partial[...], buffer, rows)
     hidden = (residual[...].astype(F32) + product).astype(BF16)
     hidden_out[...] = hidden
     for i in range(nchan):
@@ -350,10 +310,10 @@
 
 
 def values_kernel(
-    lay, own, other, own_conv, other_conv, taps, offset, state_proj, same, partial, fetched, weight,
+    lay, own, other, own_conv, other_conv, taps, offset, state_proj, same, partial, weight,
     conv_out, act_out, rms_out, proj_out, buffer, sems,
 ):
-    copies = rest_start(False, other, fetched, weight, buffer, sems)
+    copies = stream(weight, buffer, sems, row_starts(own.shape[0], own.shape[2], False, False))
     c = lax.axis_index("src")
     nchan = own.shape[0]
     rows, cols = act_out.shape
@@ -374,7 +334,7 @@
     for w in range(steps):
         sides = [jnp.concatenate([t[:, b * steps + w, :] for b in range(blocks)], axis=1) for t in tails]
         window.append(in_order(sides[0], sides[1], c))
-    window.append(rest_dot(copies, other, partial[...], fetched, buffer) * inverse)
+    window.append(half_dot(copies, other, partial[...], buffer, rows) * inverse)
     mixed = jnp.zeros((rows, cols), F32)
     for w in range(steps + 1):
         mixed = mixed + window[w] * taps[w : w + 1, :]
@@ -421,21 +381,20 @@
     return copies
 
 
-def down_product(copies, gated, fetched, buffer, outs):
-    cols = outs[0].shape[2]
+def down_product(copies, gated, fetched, buffer, out_ref):
+    cols = out_ref.shape[2]
     step = buffer.shape[1] // len(copies)
-    ready = fetched.shape[1] // step
-    pieces = (ready + len(copies)) // len(outs)
+    ready = 0 if fetched is None else fetched.shape[1] // step
+    each = step // cols
     for slot in range(ready + len(copies)):
         if slot < ready:
             block = fetched[:, slot * step : (slot + 1) * step]
         else:
             copies[slot - ready].wait()
             block = buffer[:, (slot - ready) * step : (slot - ready + 1) * step]
-        out_ref, i = outs[slot // pieces], slot % pieces
         part = jnp.dot(gated, block, preferred_element_type=F32).astype(out_ref.dtype)
-        for j in range(step // cols):
-            out_ref[i * (step // cols) + j] = part[:, j * cols : (j + 1) * cols]
+        for j in range(each):
+            out_ref[slot * each + j] = part[:, j * cols : (j + 1) * cols]
 
 
 def scan_kernel(
@@ -451,8 +410,8 @@
     fetched,
     weight,
     next_hbm,
+    gated_out,
     send_out,
-    keep_out,
     turned,
     mixed,
     next_out,
@@ -461,7 +420,7 @@
     save_sem,
 ):
     c = lax.axis_index("src")
-    copies = down_stream(weight, buffer, sems, (1 - c, c), DOWN_READY)
+    copies = down_stream(weight, buffer, sems, (1 - c,), DOWN_READY)
     nchan = own.shape[0]
     rows, cols = act_ref.shape
     blocks = cols // LANES
@@ -499,8 +458,14 @@
     save = pltpu.make_async_copy(next_out, next_hbm, save_sem)
     save.start()
     gated = ((own_first(mixed[...], c) + skip_gain[...] * act) * gate_ref[...]).astype(BF16)
-    down_product(copies, gated, fetched, buffer, (send_out, keep_out))
+    gated_out[...] = gated
+    down_product(copies, gated, fetched, buffer, send_out)
     save.wait()
+
+
+def down_kernel(gated, weight, out_ref, buffer, sems):
+    copies = down_stream(weight, buffer, sems, (lax.axis_index("src"),), 0)
+    down_product(copies, gated[...], None, buffer, out_ref)
 
 
 def finish_kernel(final, hidden, out_ref):
@@ -599,10 +564,9 @@
         compiler_params=params(4),
         name="merge",
     )(partial, other_partial)
-    att_own, out_fetched = exchange_and_fetch(attended, out_heads, True, 4, "fetch_out")
+    att_own = exchange(attended)
     att_other = swap(att_own)
     half_streamed = [VM((D // 2, cols), BF16), pltpu.SemaphoreType.DMA((nchan,))]
-    rest_streamed = [VM((D // 4, cols), BF16), pltpu.SemaphoreType.DMA((nchan // 2,))]
 
     def own_product(x, weight, by_chip, name):
         return call(
@@ -622,13 +586,13 @@
     hidden, hid_send = call(
         out_kernel,
         out_shape=(shape((rows, cols), BF16), shape((nchan, rows + NS, cols), BF16)),
-        in_specs=vmem(5) + hbm(1),
+        in_specs=vmem(4) + hbm(1),
         out_specs=tuple(vmem(2)),
-        scratch_shapes=rest_streamed,
+        scratch_shapes=half_streamed,
         compiler_params=params(STREAM_MIB),
         name="out",
-    )(att_other, out_partial, residual, cross, out_fetched, out_heads)
-    hid_own, values_fetched = exchange_and_fetch(hid_send, in_values, False, 4, "fetch_values")
+    )(att_other, out_partial, residual, cross, out_heads)
+    hid_own = exchange(hid_send)
     hid_other = swap(hid_own)
     values_partial = own_product(hid_own, in_values, False, "values_own")
 
@@ -641,12 +605,12 @@
             shape((rows, LANES), F32),
             shape((nchan, sent_rows, LANES), BF16),
         ),
-        in_specs=vmem(10) + hbm(1),
+        in_specs=vmem(9) + hbm(1),
         out_specs=tuple(vmem(4)),
-        scratch_shapes=[VM((D // 2 - D // 4, cols), BF16), pltpu.SemaphoreType.DMA((nchan - 2 * nchan // 4,))],
+        scratch_shapes=half_streamed,
         compiler_params=params(STREAM_MIB),
         name="values",
-    )(hid_own, hid_other, conv_own, other_conv, conv_taps, conv_offset[None, :], state_proj.T, same, values_partial, values_fetched, in_values)
+    )(hid_own, hid_other, conv_own, other_conv, conv_taps, conv_offset[None, :], state_proj.T, same, values_partial, in_values)
     part, down_weight = lax.optimization_barrier((part, mamba_down))
     proj_own = exchange(part)
     pieces = 8
@@ -666,16 +630,16 @@
 
     down_streamed = [
         VM((rows, NS, cols), F32),
-        VM((cols, D - DOWN_READY * piece), BF16),
-        pltpu.SemaphoreType.DMA((pieces - DOWN_READY,)),
+        VM((cols, D // 2 - DOWN_READY * piece), BF16),
+        pltpu.SemaphoreType.DMA((pieces // 2 - DOWN_READY,)),
         pltpu.SemaphoreType.DMA,
     ]
-    mamba_next, send, keep = call(
+    mamba_next, gated, send = call(
         scan_kernel,
         out_shape=(
             shape((rows, NS, cols), F32),
+            shape((rows, cols), BF16),
             shape((nchan, rows, cols), BF16),
-            shape((nchan, rows, cols), F32),
         ),
         in_specs=vmem(10) + hbm(1),
         out_specs=tuple(hbm(1) + vmem(2)),
@@ -696,6 +660,16 @@
         mamba_down,
     )
     taken = swap(send)
+    keep = call(
+        down_kernel,
+        out_shape=shape((nchan, rows, cols), F32),
+        in_specs=vmem(1) + hbm(1),
+        out_specs=vmem(1)[0],
+        scratch_shapes=[VM((cols, D // 2), BF16), pltpu.SemaphoreType.DMA((pieces // 2,))],
+        compiler_params=params(STREAM_MIB),
+        cost_estimate=cost(SHORT, 0),
+        name="down",
+    )(gated, mamba_down)
     summed = (keep + taken.astype(F32)).astype(BF16)
     hidden_out = call(
         finish_kernel,

time: 101 us -> 99.3 us (0.983)
  blocking collectives: 10.8 us -> 34.2 us
  waiting for transfers between devices: 40.9 us -> 25.7 us
  starting transfers between devices: 19.2 us -> 12.1 us
  Pallas kernels: 26.1 us -> 23.4 us
    all_to_all x1 -> x3, blocking collectives: 10.8 us -> 34.2 us  [exchange(): return lax.all_to_all(x, 'chan', split_axis=0, concat_axis=0, tiled=True)]
    all_to_all x4 -> x2, waiting for transfers between devices: 36.2 us -> 22.1 us  [exchange(): return lax.all_to_all(x, 'chan', split_axis=0, concat_axis=0, tiled=True)]
    all_to_all x4 -> x2, starting transfers between devices: 17.9 us -> 10.8 us  [exchange(): return lax.all_to_all(x, 'chan', split_axis=0, concat_axis=0, tiled=True)]
    pallas_call x3 -> x2, Pallas kernels: 7.3 us -> 5.02 us  [the longest x1 2.55 us: on_device(): call(scan_kernel, out_shape=(shape((rows, NS, cols), F32), shape((rows, c...]
    ppermute x7, waiting for transfers between devices: 4.76 us -> 3.54 us  [swap(): return lax.ppermute(x, 'src', [(0, 1), (1, 0)])]
  transfers between devices with their start and end apart: 11 -> 9, of which waited for: 8 -> 5; matrix products, arithmetic and copies ran while one was open for 0% -> 0% of each run, Pallas kernels for 12% -> 11%
where the time goes in v6:
time: 99.3 us; the launch traced here: 98.7 us
  blocking collectives  34.2 us (34%)
  waiting for transfers between devices  25.7 us (26%)
  Pallas kernels  23.4 us (24%)
  starting transfers between devices  12.1 us (12%)
  local copies, waits for them, and re-layouts  2.41 us (2%)
    all_to_all x3, blocking collectives, exchange(): return lax.all_to_all(x, 'chan', split_axis=0, concat_axis=0, tiled=True)  34.2 us
    all_to_all x2, waiting for transfers between devices, exchange(): return lax.all_to_all(x, 'chan', split_axis=0, concat_axis=0, tiled=True)  22.1 us
    all_to_all x2, starting transfers between devices, exchange(): return lax.all_to_all(x, 'chan', split_axis=0, concat_axis=0, tiled=True)  10.8 us
    pallas_call x2, Pallas kernels, own_product(): call(functools.partial(own_kernel, by_chip), out_shape=shape((rows, cols)...  4.8 us
    pallas_call x1, Pallas kernels, on_device(): call(gates_kernel, out_shape=(shape((rows, cols), F32), shape((cols, DOWN...  3.91 us
    ppermute x7, waiting for transfers between devices, swap(): return lax.ppermute(x, 'src', [(0, 1), (1, 0)])  3.54 us
    pallas_call x1, Pallas kernels, on_device(): call(functools.partial(values_kernel, lay), out_shape=(shape((steps, rows...  3.36 us
    pallas_call x1, Pallas kernels, on_device(): call(scan_kernel, out_shape=(shape((rows, NS, cols), F32), shape((rows, c...  2.55 us
  transfers between devices with their start and end apart: 9, of which 5 were waited for; matrix products, arithmetic and copies ran while one was open for 0% of the time, Pallas kernels for 11%

profile of v6, /device:TPU:0, one launch (start us, length us, event | category | flops | bytes accessed | tf_op | source)
XLA Modules:
  0.0 98.7 jit_solution(12502107937389378757)
XLA Ops:
  0.6 0.5 collective-permute-start
  1.2 1.1 %collective-permute-done.other_hbm = bf16[1,8192]{1,0:T(2,128)(2,1)S(1)} collective-permute-done((bf16[1,8192]{1,0:T(2,128)(2,1)}, bf16[1,8192]{1,0:T(2,128)(2,1)S(1)}, u32[]{:S(2)}, u32[]{:S(2)}) %collective-permute-start) | collective-permute-done | bytes 16416 | tf_op jit(solution)/shard_map/ppermute | solution.py:54
  2.2 0.0 copy-start.9
  2.2 0.6 copy-done.9
  2.8 2.3 %pack.1 = bf16[8,320,128]{2,1,0:T(8,128)(2,1)} custom-call(bf16[1,8192]{1,0:T(2,128)(2,1)} %query_hbm.1, bf16[1,8192]{1,0:T(2,128)(2,1)} %copy-done.9, bf16[1,2048]{1,0:T(2,128)(2,1)} %newkv_hbm.1, bf16[8,16,2048]{2,1,0:T(8,128)(2,1)} %pages_hbm.1, f32[3,1,8192]{2,1,0:T(1,128)} %bitcast.10, s32[8]{0:T(128)} %owner_hbm.1, s32[8]{0:T(128)} %index_hbm.1, ...), custom_call_target="tpu_custom_call" | custom-call | tf_op jit(solution)/shard_map/pack/pallas_call | solution.py:511
  5.1 7.2 %all-to-all-start = ((bf16[8,320,128]{2,1,0:T(8,128)(2,1)}), bf16[8,320,128]{2,1,0:T(8,128)(2,1)S(1)}, u32[]{:S(2)}, u32[]{:S(2)}) async-start(bf16[8,320,128]{2,1,0:T(8,128)(2,1)} %pack.1), calls=%async_computation | async-start | bytes 1310720 | tf_op jit(solution)/shard_map/all_to_all | solution.py:58
  12.3 0.0 copy-start.7
  12.3 1.0 %copy-done.7 = f32[1,16,8192]{2,1,0:T(8,128)S(1)} copy-done((f32[1,16,8192]{2,1,0:T(8,128)S(1)}, f32[1,16,8192]{2,1,0:T(8,128)}, u32[]{:S(2)}) %copy-start.7) | copy-done | bytes 524312
  13.3 0.0 copy-start.8
  13.3 0.7 copy-done.8
  14.1 15.8 %all-to-all-done.recv = bf16[8,320,128]{2,1,0:T(8,128)(2,1)S(1)} async-done(((bf16[8,320,128]{2,1,0:T(8,128)(2,1)}), bf16[8,320,128]{2,1,0:T(8,128)(2,1)S(1)}, u32[]{:S(2)}, u32[]{:S(2)}) %all-to-all-start) | async-done | bytes 655392 | tf_op jit(solution)/shard_map/all_to_all | solution.py:58
  29.9 0.7 attend.1
  30.7 0.1 collective-permute-start.1
  30.7 0.5 collective-permute-start.2
  31.2 0.9 collective-permute-done.2.other_conv
  32.1 0.0 collective-permute-done.1.other
  32.1 0.2 merge.1
  32.4 10.9 %all_to_all.25.lhs = bf16[8,16,512]{2,1,0:T(8,128)(2,1)S(1)} all-to-all(bf16[8,16,512]{2,1,0:T(8,128)(2,1)S(1)} %merge.1), channel_id=1, replica_groups=mesh['groups'=2,'src'=2,'chan'=8] {'chan'}, dimensions={0} | all-to-all | bytes 262144 | tf_op jit(solution)/shard_map/all_to_all | solution.py:58
  43.3 0.0 collective-permute-start.3
  43.3 2.4 %out_own.1.partial = f32[16,512]{1,0:T(8,128)S(1)} custom-call(bf16[8,16,512]{2,1,0:T(8,128)(2,1)S(1)} %all_to_all.25.lhs, bf16[8192,512]{1,0:T(8,128)(2,1)} %weight.8), custom_call_target="tpu_custom_call" | custom-call | flops 3000000000 | tf_op jit(solution)/shard_map/out_own/pallas_call | solution.py:572
  45.7 0.0 copy-start
  45.7 0.0 copy-start.3
  45.7 0.0 copy-start.4
  45.7 0.0 collective-permute-done.3.lhs
  45.7 2.5 %out.1 = (bf16[16,512]{1,0:T(8,128)(2,1)S(1)}, bf16[8,32,512]{2,1,0:T(8,128)(2,1)S(1)}) custom-call(bf16[8,16,512]{2,1,0:T(8,128)(2,1)S(1)} %collective-permute-done.3.lhs, f32[16,512]{1,0:T(8,128)S(1)} %out_own.1.partial, bf16[16,512]{1,0:T(8,128)(2,1)S(1)} %get-tuple-element.44.residual, bf16[8,16,512]{2,1,0:T(8,128)(2,1)S(1)} %get-tuple-element.45.cross, ...), custom_call_target="tpu_custom_call" | custom-call | tf_op jit(solution)/shard_map/out/pallas_call | solution.py:586
  48.2 12.3 %all_to_all.26.lhs.own = bf16[8,32,512]{2,1,0:T(8,128)(2,1)S(1)} all-to-all(bf16[8,32,512]{2,1,0:T(8,128)(2,1)S(1)} %get-tuple-element.46), channel_id=1, replica_groups=mesh['groups'=2,'src'=2,'chan'=8] {'chan'}, dimensions={0} | all-to-all | bytes 524288 | tf_op jit(solution)/shard_map/all_to_all | solution.py:58
  60.5 0.0 collective-permute-start.4
  60.5 2.4 %values_own.1.partial = f32[16,512]{1,0:T(8,128)S(1)} custom-call(bf16[8,32,512]{2,1,0:T(8,128)(2,1)S(1)} %all_to_all.26.lhs.own, bf16[8192,512]{1,0:T(8,128)(2,1)} %weight.10), custom_call_target="tpu_custom_call" | custom-call | flops 3000000000 | tf_op jit(solution)/shard_map/values_own/pallas_call | solution.py:572
  62.9 0.0 collective-permute-done.4.other.hid_other
  62.9 0.0 copy-done
  62.9 0.0 copy-done.3
  62.9 0.0 copy-done.4
  63.0 3.4 %values.1 = (f32[3,16,512]{2,1,0:T(8,128)}, f32[16,512]{1,0:T(8,128)S(1)}, f32[16,128]{1,0:T(8,128)S(1)}, bf16[8,144,128]{2,1,0:T(8,128)(2,1)}) custom-call(bf16[8,32,512]{2,1,0:T(8,128)(2,1)S(1)} %all_to_all.26.lhs.own, bf16[8,32,512]{2,1,0:T(8,128)(2,1)S(1)} %collective-permute-done.4.other.hid_other, bf16[8,16,128]{2,1,0:T(8,128)(2,1)S(1)} %get-tuple-element.47.own_conv, ...), custom_call_target="tpu_custom_call" | custom-call | tf_op jit(solution)/shard_map/values/pallas_call | solution.py:600
  66.3 3.6 %all-to-all-start.3 = ((bf16[8,144,128]{2,1,0:T(8,128)(2,1)}), bf16[8,144,128]{2,1,0:T(8,128)(2,1)S(1)}, u32[]{:S(2)}, u32[]{:S(2)}) async-start(bf16[8,144,128]{2,1,0:T(8,128)(2,1)} %get-tuple-element.51), calls=%async_computation.3 | async-start | bytes 589824 | tf_op jit(solution)/shard_map/all_to_all | solution.py:58
  69.9 0.0 copy-start.1
  70.0 0.0 copy-start.2
  70.0 0.0 copy-start.5
  70.0 0.0 copy-start.6
  70.0 3.9 %gates.1 = (f32[16,512]{1,0:T(8,128)S(1)}, bf16[512,1024]{1,0:T(8,128)(2,1)S(1)}) custom-call(bf16[8,32,512]{2,1,0:T(8,128)(2,1)S(1)} %all_to_all.26.lhs.own, bf16[8,32,512]{2,1,0:T(8,128)(2,1)S(1)} %collective-permute-done.4.other.hid_other, f32[16,128]{1,0:T(8,128)S(1)} %get-tuple-element.52.rms, bf16[8192,512]{1,0:T(8,128)(2,1)} %weight.11, ...), custom_call_target="tpu_custom_call" | custom-call | flops 3000000000 | tf_op jit(solution)/shard_map/gates/pallas_call | solution.py:618
  73.9 6.3 %all-to-all-done.3.own = bf16[8,144,128]{2,1,0:T(8,128)(2,1)S(1)} async-done(((bf16[8,144,128]{2,1,0:T(8,128)(2,1)}), bf16[8,144,128]{2,1,0:T(8,128)(2,1)S(1)}, u32[]{:S(2)}, u32[]{:S(2)}) %all-to-all-start.3) | async-done | bytes 294944 | tf_op jit(solution)/shard_map/all_to_all | solution.py:58
  80.2 0.0 collective-permute-start.5
  80.2 1.6 %collective-permute-done.5.other = bf16[8,144,128]{2,1,0:T(8,128)(2,1)S(1)} collective-permute-done((bf16[8,144,128]{2,1,0:T(8,128)(2,1)S(1)}, bf16[8,144,128]{2,1,0:T(8,128)(2,1)S(1)}, u32[]{:S(2)}, u32[]{:S(2)}) %collective-permute-start.5) | collective-permute-done | bytes 294944 | tf_op jit(solution)/shard_map/ppermute | solution.py:54
  81.8 0.0 copy-done.1
  81.8 0.0 copy-done.2
  81.8 0.0 copy-done.5
  81.8 0.0 copy-done.6
  81.8 2.5 %scan.1 = (f32[16,16,512]{2,1,0:T(8,128)}, bf16[16,512]{1,0:T(8,128)(2,1)S(1)}, bf16[8,16,512]{2,1,0:T(8,128)(2,1)S(1)}) custom-call(bf16[8,144,128]{2,1,0:T(8,128)(2,1)S(1)} %all-to-all-done.3.own, bf16[8,144,128]{2,1,0:T(8,128)(2,1)S(1)} %collective-permute-done.5.other, bf16[8,32,512]{2,1,0:T(8,128)(2,1)S(1)} %collective-permute-done.4.other.hid_other, ...), custom_call_target="tpu_custom_call" | custom-call | tf_op jit(solution)/shard_map/scan/pallas_call | solution.py:637
  84.4 0.2 collective-permute-start.6
  84.6 2.5 %down.1 = f32[8,16,512]{2,1,0:T(8,128)S(1)} custom-call(bf16[16,512]{1,0:T(8,128)(2,1)S(1)} %get-tuple-element.60.gated, bf16[512,8192]{1,0:T(8,128)(2,1)} %weight.13), custom_call_target="tpu_custom_call" | custom-call | flops 3000000000 | tf_op jit(solution)/shard_map/down/pallas_call | solution.py:663
  87.0 0.0 collective-permute-done.6
  87.1 10.9 %all_to_all.27.final = bf16[8,16,512]{2,1,0:T(8,128)(2,1)S(1)} all-to-all(bf16[8,16,512]{2,1,0:T(8,128)(2,1)S(1)} %add_convert_fusion), channel_id=1, replica_groups=mesh['groups'=2,'src'=2,'chan'=8] {'chan'}, dimensions={0} | all-to-all | bytes 262144 | tf_op jit(solution)/shard_map/all_to_all | solution.py:58
  98.0 0.6 finish.1
  (2 shorter events, 0.1 us)
Async XLA Ops:
  0.6 1.6 %collective-permute-start = (bf16[1,8192]{1,0:T(2,128)(2,1)}, bf16[1,8192]{1,0:T(2,128)(2,1)S(1)}, u32[]{:S(2)}, u32[]{:S(2)}) collective-permute-start(bf16[1,8192]{1,0:T(2,128)(2,1)} %query_hbm.1), channel_id=1, source_target_pairs={{0,8},{8,0},{1,9},{9,1},{2,10},{10,2},{3,11},{11,3},{4,12},{12,4},... | collective-permute-start | bytes 49160 | tf_op jit(solution)/shard_map/ppermute | solution.py:54
  2.2 0.6 copy-start.9
  5.1 24.8 %all-to-all-start = ((bf16[8,320,128]{2,1,0:T(8,128)(2,1)}), bf16[8,320,128]{2,1,0:T(8,128)(2,1)S(1)}, u32[]{:S(2)}, u32[]{:S(2)}) async-start(bf16[8,320,128]{2,1,0:T(8,128)(2,1)} %pack.1), calls=%async_computation | async-start | bytes 1310720 | tf_op jit(solution)/shard_map/all_to_all | solution.py:58
  12.3 1.0 %copy-start.7 = (f32[1,16,8192]{2,1,0:T(8,128)S(1)}, f32[1,16,8192]{2,1,0:T(8,128)}, u32[]{:S(2)}) copy-start(f32[1,16,8192]{2,1,0:T(8,128)} %state) | copy-start | bytes 1572868
  13.3 0.7 copy-start.8
  30.7 1.5 %collective-permute-start.1 = (f32[128,256]{1,0:T(8,128)S(1)}, f32[128,256]{1,0:T(8,128)S(1)}, u32[]{:S(2)}, u32[]{:S(2)}) collective-permute-start(f32[128,256]{1,0:T(8,128)S(1)} %get-tuple-element.41.own), channel_id=1, source_target_pairs={{0,8},{8,0},{1,9},{9,1},{2,10},{10,2},{3,11},{11,3},{4,12},{12,4},... | collective-permute-start | bytes 393224 | tf_op jit(solution)/shard_map/ppermute | solution.py:54
  30.7 1.4 %collective-permute-start.2 = (bf16[8,16,128]{2,1,0:T(8,128)(2,1)S(1)}, bf16[8,16,128]{2,1,0:T(8,128)(2,1)S(1)}, u32[]{:S(2)}, u32[]{:S(2)}) collective-permute-start(bf16[8,16,128]{2,1,0:T(8,128)(2,1)S(1)} %get-tuple-element.42), channel_id=1, source_target_pairs={{0,8},{8,0},{1,9},{9,1},{2,10},{10,2},{3,11},{11,3},{4,12},{12,4},... | collective-permute-start | bytes 98312 | tf_op jit(solution)/shard_map/ppermute | solution.py:54
  43.3 2.4 %collective-permute-start.3 = (bf16[8,16,512]{2,1,0:T(8,128)(2,1)S(1)}, bf16[8,16,512]{2,1,0:T(8,128)(2,1)S(1)}, u32[]{:S(2)}, u32[]{:S(2)}) collective-permute-start(bf16[8,16,512]{2,1,0:T(8,128)(2,1)S(1)} %all_to_all.25.lhs), channel_id=1, source_target_pairs={{0,8},{8,0},{1,9},{9,1},{2,10},{10,2},{3,11},{11,3},{4,12},{12,4},... | collective-permute-start | bytes 393224 | tf_op jit(solution)/shard_map/ppermute | solution.py:54
  45.7 17.3 %copy-start = (bf16[512,544]{0,1:T(8,128)(2,1)S(1)}, bf16[512,544]{0,1:T(8,128)(2,1)}, u32[]{:S(2)}) copy-start(bf16[512,544]{0,1:T(8,128)(2,1)} %param.34) | copy-start | bytes 1671172
  45.7 17.3 %copy-start.3 = (f32[4,512]{1,0:T(4,128)S(1)}, f32[4,512]{1,0:T(4,128)}, u32[]{:S(2)}) copy-start(f32[4,512]{1,0:T(4,128)} %taps.1) | copy-start | bytes 24580
  45.7 17.2 %copy-start.4 = (f32[512]{0:T(512)S(1)}, f32[512]{0:T(512)}, u32[]{:S(2)}) copy-start(f32[512]{0:T(512)} %param.33) | copy-start | bytes 6148
  60.5 2.4 %collective-permute-start.4 = (bf16[8,32,512]{2,1,0:T(8,128)(2,1)S(1)}, bf16[8,32,512]{2,1,0:T(8,128)(2,1)S(1)}, u32[]{:S(2)}, u32[]{:S(2)}) collective-permute-start(bf16[8,32,512]{2,1,0:T(8,128)(2,1)S(1)} %all_to_all.26.lhs.own), channel_id=1, source_target_pairs={{0,8},{8,0},{1,9},{9,1},{2,10},{10,2},{3,11},{11,3},{4,12},{12,4},... | collective-permute-start | bytes 786440 | tf_op jit(solution)/shard_map/ppermute | solution.py:54
  66.3 13.9 %all-to-all-start.3 = ((bf16[8,144,128]{2,1,0:T(8,128)(2,1)}), bf16[8,144,128]{2,1,0:T(8,128)(2,1)S(1)}, u32[]{:S(2)}, u32[]{:S(2)}) async-start(bf16[8,144,128]{2,1,0:T(8,128)(2,1)} %get-tuple-element.51), calls=%async_computation.3 | async-start | bytes 589824 | tf_op jit(solution)/shard_map/all_to_all | solution.py:58
  69.9 11.8 %copy-start.1 = (bf16[512,512]{1,0:T(8,128)(2,1)S(1)}, bf16[512,512]{1,0:T(8,128)(2,1)}, u32[]{:S(2)}) copy-start(bf16[512,512]{1,0:T(8,128)(2,1)} %step_proj.1) | copy-start | bytes 1572868
  70.0 11.8 %copy-start.2 = (f32[16,512]{1,0:T(8,128)S(1)}, f32[16,512]{1,0:T(8,128)}, u32[]{:S(2)}) copy-start(f32[16,512]{1,0:T(8,128)} %decay_log.1) | copy-start | bytes 98308
  70.0 11.8 %copy-start.5 = (f32[512]{0:T(512)S(1)}, f32[512]{0:T(512)}, u32[]{:S(2)}) copy-start(f32[512]{0:T(512)} %param.36) | copy-start | bytes 6148
  70.0 11.8 %copy-start.6 = (f32[512]{0:T(512)S(1)}, f32[512]{0:T(512)}, u32[]{:S(2)}) copy-start(f32[512]{0:T(512)} %param.38) | copy-start | bytes 6148
  80.2 1.6 %collective-permute-start.5 = (bf16[8,144,128]{2,1,0:T(8,128)(2,1)S(1)}, bf16[8,144,128]{2,1,0:T(8,128)(2,1)S(1)}, u32[]{:S(2)}, u32[]{:S(2)}) collective-permute-start(bf16[8,144,128]{2,1,0:T(8,128)(2,1)S(1)} %all-to-all-done.3.own), channel_id=1, source_target_pairs={{0,8},{8,0},{1,9},{9,1},{2,10},{10,2},{3,11},{11,3},{4,12},{12,4},... | collective-permute-start | bytes 884744 | tf_op jit(solution)/shard_map/ppermute | solution.py:54
  84.4 2.7 %collective-permute-start.6 = (bf16[8,16,512]{2,1,0:T(8,128)(2,1)S(1)}, bf16[8,16,512]{2,1,0:T(8,128)(2,1)S(1)}, u32[]{:S(2)}, u32[]{:S(2)}) collective-permute-start(bf16[8,16,512]{2,1,0:T(8,128)(2,1)S(1)} %get-tuple-element.61), channel_id=1, source_target_pairs={{0,8},{8,0},{1,9},{9,1},{2,10},{10,2},{3,11},{11,3},{4,12},{12,4},... | collective-permute-start | bytes 393224 | tf_op jit(solution)/shard_map/ppermute | solution.py:54

commit v7 on v6

--- a/solution.py
+++ b/solution.py
@@ -17,7 +17,6 @@
 G = QH // KVH
 LANES = 128
 NEGATIVE = -1e30
-LOWEST = -1e20
 STREAM_MIB = 50
 DOWN_READY = 1
 SHORT = 3 * 10**9
@@ -64,18 +63,18 @@
         self.tokens = held_tokens
         self.owner_rows = held_tokens // LANES
         self.value = held_tokens
-        self.misc = 2 * held_tokens
-        self.query = self.misc + round_up(2 + self.owner_rows, 16)
-        self.conv = self.query + round_up(2 * self.per, 16)
-        self.conv_rows = round_up(steps * blocks, 16)
-        self.rows = self.conv + 2 * self.conv_rows
+        self.small = 2 * held_tokens
+        self.query = 2 + self.owner_rows
+        self.conv = self.query + self.per
+        self.conv_rows = steps * blocks
+        self.small_rows = round_up(self.conv + 2 * self.conv_rows, 16)
+        self.rows = self.small + self.small_rows
 
 
 def pack_kernel(
     nchan,
     lay,
     query_hbm,
-    other_hbm,
     newkv_hbm,
     pages_hbm,
     conv_hbm,
@@ -84,7 +83,6 @@
     lengths_hbm,
     out_ref,
     query,
-    other_query,
     newkv,
     pages,
     conv,
@@ -97,7 +95,6 @@
         (pages_hbm, pages),
         (conv_hbm, conv),
         (query_hbm, query),
-        (other_hbm, other_query),
         (newkv_hbm, newkv),
         (owner_hbm, owners),
         (index_hbm, indexes),
@@ -124,38 +121,27 @@
             left = lengths[owner] - indexes[i * per_row + j] * page_tokens
             found = jnp.where((lane // page_tokens == j) & (lane % page_tokens < left), owner, found)
         owner_rows.append(found.astype(F32))
-    fill = lay.query - lay.misc - 2 - lay.owner_rows
-    owner_rows.append(jnp.zeros((fill, LANES), F32))
     for d in range(nchan):
         at = (d // rep) * HD
-        fresh = [newkv[0:1, x : x + HD].astype(F32) for x in (at, KVH * HD + at)]
-        out_ref[d, lay.misc : lay.query, :] = jnp.concatenate(fresh + owner_rows, axis=0).astype(BF16)
-        heads = []
-        for ref in (query, other_query):
-            for h in range(lay.per):
-                place = (d * lay.per + h) * HD
-                heads.append(ref[0:1, place : place + HD].astype(F32))
-        spare = lay.conv - lay.query - len(heads)
-        if spare:
-            heads.append(jnp.zeros((spare, LANES), F32))
-        out_ref[d, lay.query : lay.conv, :] = jnp.concatenate(heads, axis=0).astype(BF16)
-    for side in range(2):
-        first = (c if side == 0 else 1 - c) * (nchan * cols)
-        for d in range(nchan):
-            rows = []
+        small = [newkv[0:1, x : x + HD].astype(F32) for x in (at, KVH * HD + at)] + owner_rows
+        for h in range(lay.per):
+            place = (d * lay.per + h) * HD
+            small.append(query[0:1, place : place + HD].astype(F32))
+        for half in (c, 1 - c):
+            first = (half * nchan + d) * cols
             for b in range(blocks):
-                lanes = pl.ds(pl.multiple_of(first + d * cols + b * LANES, LANES), LANES)
+                lanes = pl.ds(pl.multiple_of(first + b * LANES, LANES), LANES)
                 for w in range(steps):
-                    rows.append(conv[w, 0:1, lanes])
-            rows.append(jnp.zeros((lay.conv_rows - len(rows), LANES), F32))
-            base = lay.conv + side * lay.conv_rows
-            out_ref[d, base : base + lay.conv_rows, :] = jnp.concatenate(rows, axis=0).astype(BF16)
+                    small.append(conv[w, 0:1, lanes])
+        if lay.small_rows > len(small):
+            small.append(jnp.zeros((lay.small_rows - len(small), LANES), F32))
+        out_ref[d, lay.small : lay.rows, :] = jnp.concatenate(small, axis=0).astype(BF16)
     copies[0].wait()
     for d in range(nchan):
         at = (d // rep) * HD
         out_ref[d, 0 : lay.tokens, :] = pages[:, :, at : at + HD].reshape(lay.tokens, HD)
         at = KVH * HD + at
-        out_ref[d, lay.value : lay.misc, :] = pages[:, :, at : at + HD].reshape(lay.tokens, HD)
+        out_ref[d, lay.value : lay.small, :] = pages[:, :, at : at + HD].reshape(lay.tokens, HD)
 
 
 def load_kernel(residual, state, residual_out, same, cross):
@@ -168,7 +154,7 @@
             ref[d] = state[0, :, lanes].astype(BF16)
 
 
-def attend_kernel(lay, recv, out_ref, conv_own, conv_out, queries, scores):
+def attend_kernel(lay, recv, other, out_ref, conv_own, conv_other, queries, scores, result):
     nchan = recv.shape[0]
     per, tokens = lay.per, lay.tokens
     c = lax.axis_index("src")
@@ -176,50 +162,50 @@
     scale = 1.0 / math.sqrt(HD)
     contract = (((1,), (1,)), ((), ()))
     new_keys, new_values, owners = [], [], []
-    for s in range(nchan):
-        conv_own[s] = recv[s, lay.conv : lay.conv + lay.conv_rows, :]
-        conv_out[s] = recv[s, lay.conv + lay.conv_rows : lay.rows, :]
-        heads = recv[s, lay.query : lay.conv, :].astype(F32)
-        queries[s * per : (s + 1) * per, :] = heads[0:per, :]
-        queries[count + s * per : count + (s + 1) * per, :] = heads[per : 2 * per, :]
-        misc = recv[s, lay.misc : lay.query, :].astype(F32)
-        new_keys.append(misc[0:1, :])
-        new_values.append(misc[1:2, :])
-        owners.append(jnp.concatenate([misc[2 + i : 3 + i, :] for i in range(lay.owner_rows)], axis=1))
+    spare = conv_own.shape[1] - lay.conv_rows
+    for ref, conv_out, at in ((recv, conv_own, lay.conv), (other, conv_other, lay.conv + lay.conv_rows)):
+        for s in range(nchan):
+            small = ref[s, lay.small : lay.rows, :].astype(F32)
+            conv = small[at : at + lay.conv_rows, :]
+            conv_out[s] = jnp.concatenate([conv, jnp.zeros((spare, LANES), F32)], axis=0) if spare else conv
+            owners.append(jnp.concatenate([small[2 + i : 3 + i, :] for i in range(lay.owner_rows)], axis=1))
+            if ref is recv:
+                queries[s * per : (s + 1) * per, :] = small[lay.query : lay.query + per, :]
+                new_keys.append(small[0:1, :])
+                new_values.append(small[1:2, :])
     fill = round_up(nchan, 16) - nchan
     if fill:
         new_keys.append(jnp.zeros((fill, HD), F32))
         new_values.append(jnp.zeros((fill, HD), F32))
     new_keys = jnp.concatenate(new_keys, axis=0).astype(BF16)
     new_values = jnp.concatenate(new_values, axis=0).astype(BF16)
-    row = lax.broadcasted_iota(jnp.int32, (2 * count, 1), 0)
-    side = jnp.where(row < count, c, 1 - c)
-    request = side * nchan + (row % count) // per
+    place = lax.broadcasted_iota(jnp.int32, (count, 1), 0) // per
     lane = lax.broadcasted_iota(jnp.int32, (1, nchan + fill), 1)
-    new_owner = jnp.where(lane < nchan, c * nchan + lane, -1)
     q = queries[...].astype(BF16)
     new_scores = lax.dot_general(q, new_keys, contract, preferred_element_type=F32) * scale
-    new_scores = jnp.where(request == new_owner, new_scores, NEGATIVE)
-    wide = request.astype(F32)
+    new_scores = jnp.where(place == lane, new_scores, NEGATIVE)
+    wide = (c * nchan + place).astype(F32)
+    sources = [(ref, s) for ref in (recv, other) for s in range(nchan)]
     highest = None
-    for s in range(nchan):
-        part = lax.dot_general(q, recv[s, 0:tokens, :], contract, preferred_element_type=F32) * scale
-        part = jnp.where(wide == owners[s], part, NEGATIVE)
-        scores[:, s * tokens : (s + 1) * tokens] = part
+    for i, (ref, s) in enumerate(sources):
+        part = lax.dot_general(q, ref[s, 0:tokens, :], contract, preferred_element_type=F32) * scale
+        part = jnp.where(wide == owners[i], part, NEGATIVE)
+        scores[:, i * tokens : (i + 1) * tokens] = part
         highest = part if highest is None else jnp.maximum(highest, part)
     peak = jnp.maximum(jnp.max(highest, axis=1, keepdims=True), jnp.max(new_scores, axis=1, keepdims=True))
-    peak = jnp.maximum(peak, LOWEST)
     new_weight = jnp.exp(new_scores - peak)
     numer = jnp.dot(new_weight.astype(BF16), new_values, preferred_element_type=F32)
     summed = None
-    for s in range(nchan):
-        weight = jnp.exp(scores[:, s * tokens : (s + 1) * tokens] - peak)
+    for i, (ref, s) in enumerate(sources):
+        weight = jnp.exp(scores[:, i * tokens : (i + 1) * tokens] - peak)
         summed = weight if summed is None else summed + weight
-        numer = numer + jnp.dot(weight.astype(BF16), recv[s, lay.value : lay.misc, :], preferred_element_type=F32)
+        numer = numer + jnp.dot(weight.astype(BF16), ref[s, lay.value : lay.small, :], preferred_element_type=F32)
     total = jnp.sum(summed, axis=1, keepdims=True) + jnp.sum(new_weight, axis=1, keepdims=True)
-    out_ref[:, 0:HD] = numer
-    lane = lax.broadcasted_iota(jnp.int32, (1, LANES), 1)
-    out_ref[:, HD : HD + LANES] = jnp.where(lane == 0, peak, total)
+    result[...] = numer / total
+    heads = [result[pl.ds(h, nchan, stride=per), :] for h in range(per)]
+    block = jnp.concatenate(heads, axis=0).astype(BF16)
+    for i in range(nchan):
+        out_ref[i] = block
 
 
 def in_order(own, other, c):
@@ -229,29 +215,6 @@
 def own_first(x, c):
     half = x.shape[0] // 2
     return in_order(x[:half], x[half:], c)
-
-
-def merge_kernel(lay, own, other, out_ref, result):
-    nchan = out_ref.shape[0]
-    c = lax.axis_index("src")
-    count = nchan * lay.per
-    theirs = jnp.concatenate([other[count:, :], other[:count, :]], axis=0)
-    ours = own[...]
-    top = jnp.maximum(ours[:, HD : HD + 1], theirs[:, HD : HD + 1])
-    numer, denom = 0.0, 0.0
-    for part in (ours, theirs):
-        factor = jnp.exp(part[:, HD : HD + 1] - top)
-        numer = numer + factor * part[:, 0:HD]
-        denom = denom + factor * part[:, HD + 1 : HD + 2]
-    result[...] = numer / denom
-    share = lay.per // 2
-    for h in range(share):
-        head = c * share + h
-        mine = result[pl.ds(head, nchan, stride=lay.per), :]
-        rest = result[pl.ds(count + head, nchan, stride=lay.per), :]
-        block = in_order(mine, rest, c).astype(BF16)
-        for i in range(nchan):
-            out_ref[i, :, h * HD : (h + 1) * HD] = block
 
 
 def stream(weight, buffer, sems, starts):
@@ -264,10 +227,10 @@
     return copies
 
 
-def row_starts(nchan, depth, by_chip, own):
+def row_starts(nchan, depth, own):
     c = lax.axis_index("src")
     half = c if own else 1 - c
-    return [((2 * i + half) if by_chip else (half * nchan + i)) * depth for i in range(nchan)]
+    return [(half * nchan + i) * depth for i in range(nchan)]
 
 
 def half_dot(copies, lhs, total, buffer, rows):
@@ -280,9 +243,9 @@
     return total
 
 
-def own_kernel(by_chip, lhs, weight, out_ref, buffer, sems):
+def own_kernel(lhs, weight, out_ref, buffer, sems):
     nchan, depth = lhs.shape[0], lhs.shape[2]
-    copies = stream(weight, buffer, sems, row_starts(nchan, depth, by_chip, True))
+    copies = stream(weight, buffer, sems, row_starts(nchan, depth, True))
     out_ref[...] = half_dot(copies, lhs, None, buffer, out_ref.shape[0])
 
 
@@ -297,13 +260,32 @@
     return total
 
 
-def out_kernel(lhs, partial, residual, cross, weight, hidden_out, out_ref, buffer, sems):
-    nchan, rows, depth = lhs.shape
-    copies = stream(weight, buffer, sems, row_starts(nchan, depth, True, False))
+def fetch_kernel(weight, out_ref, sems):
+    depth = out_ref.shape[0] // sems.shape[0]
+    for copy in stream(weight, out_ref, sems, [i * depth for i in range(sems.shape[0])]):
+        copy.wait()
+
+
+def out_kernel(lay, own, other, residual, cross, fetched, weight, hidden_out, out_ref, buffer, sems):
+    c = lax.axis_index("src")
+    nchan, rows = own.shape[0], residual.shape[0]
+    depth = lay.per * HD
+    ready = fetched.shape[0] // depth
+    copies = stream(weight, buffer, sems, [i * depth for i in range(ready, nchan)])
     for i in range(nchan):
         out_ref[i, rows : rows + NS, :] = cross[i]
-    product = half_dot(copies, lhs, partial[...], buffer, rows)
-    hidden = (residual[...].astype(F32) + product).astype(BF16)
+    product = residual[...].astype(F32)
+    for i in range(nchan):
+        mine, rest = own[i].astype(F32), other[i].astype(F32)
+        heads = [slice(h * nchan, (h + 1) * nchan) for h in range(lay.per)]
+        lhs = jnp.concatenate([in_order(mine[h], rest[h], c) for h in heads], axis=1).astype(BF16)
+        if i < ready:
+            block = fetched[i * depth : (i + 1) * depth, :]
+        else:
+            copies[i - ready].wait()
+            block = buffer[(i - ready) * depth : (i - ready + 1) * depth, :]
+        product = product + jnp.dot(lhs, block, preferred_element_type=F32)
+    hidden = product.astype(BF16)
     hidden_out[...] = hidden
     for i in range(nchan):
         out_ref[i, 0:rows, :] = hidden
@@ -313,7 +295,7 @@
     lay, own, other, own_conv, other_conv, taps, offset, state_proj, same, partial, weight,
     conv_out, act_out, rms_out, proj_out, buffer, sems,
 ):
-    copies = stream(weight, buffer, sems, row_starts(own.shape[0], own.shape[2], False, False))
+    copies = stream(weight, buffer, sems, row_starts(own.shape[0], own.shape[2], False))
     c = lax.axis_index("src")
     nchan = own.shape[0]
     rows, cols = act_out.shape
@@ -329,7 +311,7 @@
     for i in range(nchan):
         for b in range(blocks):
             proj_out[i, b * NS : (b + 1) * NS, :] = same[i, :, b * LANES : (b + 1) * LANES]
-    tails = (own_conv[...].astype(F32), other_conv[...].astype(F32))
+    tails = (own_conv[...], other_conv[...])
     window = []
     for w in range(steps):
         sides = [jnp.concatenate([t[:, b * steps + w, :] for b in range(blocks)], axis=1) for t in tails]
@@ -358,7 +340,7 @@
         weight,
         buffer,
         sems,
-        row_starts(nchan, depth, False, True) + row_starts(nchan, depth, False, False),
+        row_starts(nchan, depth, True) + row_starts(nchan, depth, False),
     )
     part_down = down_stream(down_hbm, down_out, down_sems, (1 - lax.axis_index("src"),), 0)
     gate = halves_dot(copies, own, other, buffer, out_ref.shape[0]) * rms[:, 0:1]
@@ -506,15 +488,13 @@
     call = pl.pallas_call
     shape = jax.ShapeDtypeStruct
 
-    other_query = swap(query_heads)
     conv_rows = jnp.transpose(conv_state, (1, 0, 2))
     packed = call(
         functools.partial(pack_kernel, nchan, lay),
         out_shape=shape((nchan, lay.rows, LANES), BF16),
-        in_specs=hbm(8),
+        in_specs=hbm(7),
         out_specs=vmem(1)[0],
         scratch_shapes=[
-            VM(query_heads.shape, BF16),
             VM(query_heads.shape, BF16),
             VM(new_keyval.shape, BF16),
             VM(cache_pages.shape, BF16),
@@ -522,11 +502,11 @@
             pltpu.SMEM(page_owner.shape, jnp.int32),
             pltpu.SMEM(page_index.shape, jnp.int32),
             pltpu.SMEM(prompt_lengths.shape, jnp.int32),
-            pltpu.SemaphoreType.DMA((8,)),
+            pltpu.SemaphoreType.DMA((7,)),
         ],
         compiler_params=pltpu.CompilerParams(vmem_limit_bytes=64 * 2**20 - 2**18),
         name="pack",
-    )(query_heads, other_query, new_keyval, cache_pages, conv_rows, page_owner, page_index, prompt_lengths)
+    )(query_heads, new_keyval, cache_pages, conv_rows, page_owner, page_index, prompt_lengths)
     packed, residual_input, mamba_state = lax.optimization_barrier((packed, residual_input, mamba_state))
     arrived = exchange(packed)
     cut = shape((nchan, NS, cols), BF16)
@@ -541,60 +521,57 @@
     )(residual_input, mamba_state)
     arrived, residual, same, cross = lax.optimization_barrier((arrived, residual, same, cross))
 
-    pairs = rows * lay.per
-    conv_cut = shape((nchan, lay.conv_rows, LANES), BF16)
-    partial, conv_own, conv_send = call(
+    other_arrived = swap(arrived)
+    pairs = nchan * lay.per
+    conv_cut = shape((nchan, round_up(lay.conv_rows, 8), LANES), F32)
+    attended, conv_own, conv_other = call(
         functools.partial(attend_kernel, lay),
-        out_shape=(shape((pairs, HD + LANES), F32), conv_cut, conv_cut),
-        in_specs=vmem(1),
+        out_shape=(shape((nchan, pairs, LANES), BF16), conv_cut, conv_cut),
+        in_specs=vmem(2),
         out_specs=tuple(vmem(3)),
-        scratch_shapes=[VM((pairs, HD), F32), VM((pairs, nchan * lay.tokens), F32)],
-        compiler_params=params(4 if held < 16 else 40),
+        scratch_shapes=[VM((pairs, HD), F32), VM((pairs, 2 * nchan * lay.tokens), F32), VM((pairs, HD), F32)],
+        compiler_params=params(4 if held < 16 else 44),
         name="attend",
-    )(arrived)
-    other_partial = swap(partial)
-    other_conv = swap(conv_send)
-    other_partial, other_conv = lax.optimization_barrier((other_partial, other_conv))
-    attended = call(
-        functools.partial(merge_kernel, lay),
-        out_shape=shape((nchan, rows, cols), BF16),
-        in_specs=vmem(2),
+    )(arrived, other_arrived)
+    att_own, out_weight = lax.optimization_barrier((exchange(attended), out_heads))
+    att_other = swap(att_own)
+    fetched_rows = D // 4
+    out_fetched = call(
+        fetch_kernel,
+        out_shape=shape((fetched_rows, cols), BF16),
+        in_specs=hbm(1),
         out_specs=vmem(1)[0],
-        scratch_shapes=[VM((pairs, HD), F32)],
-        compiler_params=params(4),
-        name="merge",
-    )(partial, other_partial)
-    att_own = exchange(attended)
-    att_other = swap(att_own)
+        scratch_shapes=[pltpu.SemaphoreType.DMA((4,))],
+        compiler_params=params(STREAM_MIB),
+        cost_estimate=cost(SHORT, 0),
+        name="fetch",
+    )(out_weight)
+    hidden, hid_send = call(
+        functools.partial(out_kernel, lay),
+        out_shape=(shape((rows, cols), BF16), shape((nchan, rows + NS, cols), BF16)),
+        in_specs=vmem(5) + hbm(1),
+        out_specs=tuple(vmem(2)),
+        scratch_shapes=[
+            VM((D - fetched_rows, cols), BF16),
+            pltpu.SemaphoreType.DMA(((D - fetched_rows) // (lay.per * HD),)),
+        ],
+        compiler_params=params(STREAM_MIB),
+        name="out",
+    )(att_own, att_other, residual, cross, out_fetched, out_heads)
     half_streamed = [VM((D // 2, cols), BF16), pltpu.SemaphoreType.DMA((nchan,))]
-
-    def own_product(x, weight, by_chip, name):
-        return call(
-            functools.partial(own_kernel, by_chip),
-            out_shape=shape((rows, cols), F32),
-            in_specs=vmem(1) + hbm(1),
-            out_specs=vmem(1)[0],
-            scratch_shapes=half_streamed,
-            compiler_params=params(STREAM_MIB),
-            cost_estimate=cost(SHORT, 0),
-            name=name,
-        )(x, weight)
-
-    out_partial = own_product(att_own, out_heads, True, "out_own")
-
     streamed = [VM((D, cols), BF16), pltpu.SemaphoreType.DMA((2 * nchan,))]
-    hidden, hid_send = call(
-        out_kernel,
-        out_shape=(shape((rows, cols), BF16), shape((nchan, rows + NS, cols), BF16)),
-        in_specs=vmem(4) + hbm(1),
-        out_specs=tuple(vmem(2)),
+    hid_own = exchange(hid_send)
+    hid_other = swap(hid_own)
+    values_partial = call(
+        own_kernel,
+        out_shape=shape((rows, cols), F32),
+        in_specs=vmem(1) + hbm(1),
+        out_specs=vmem(1)[0],
         scratch_shapes=half_streamed,
         compiler_params=params(STREAM_MIB),
-        name="out",
-    )(att_other, out_partial, residual, cross, out_heads)
-    hid_own = exchange(hid_send)
-    hid_other = swap(hid_own)
-    values_partial = own_product(hid_own, in_values, False, "values_own")
+        cost_estimate=cost(SHORT, 0),
+        name="values_own",
+    )(hid_own, in_values)
 
     sent_rows = (cols // LANES) * NS + (round_up(state_proj.shape[1], LANES) // LANES) * rows
     conv_next, act, rms, part = call(
@@ -610,7 +587,7 @@
         scratch_shapes=half_streamed,
         compiler_params=params(STREAM_MIB),
         name="values",
-    )(hid_own, hid_other, conv_own, other_conv, conv_taps, conv_offset[None, :], state_proj.T, same, values_partial, in_values)
+    )(hid_own, hid_other, conv_own, conv_other, conv_taps, conv_offset[None, :], state_proj.T, same, values_partial, in_values)
     part, down_weight = lax.optimization_barrier((part, mamba_down))
     proj_own = exchange(part)
     pieces = 8

time: 99.3 us -> 96.6 us (0.973)
  starting transfers between devices: 12.1 us -> 11.1 us
  waiting for transfers between devices: 25.7 us -> 24.7 us
    ppermute x7 -> x5, starting transfers between devices: 1.29 us -> 0.21 us  [swap(): return lax.ppermute(x, 'src', [(0, 1), (1, 0)])]
    all_to_all x2, waiting for transfers between devices: 22.1 us -> 21.1 us  [exchange(): return lax.all_to_all(x, 'chan', split_axis=0, concat_axis=0, tiled=True)]
    unnamed x20 -> x18, local copies, waits for them, and re-layouts: 2.41 us -> 1.8 us
    ppermute x7 -> x5, waiting for transfers between devices: 3.54 us -> 3.64 us  [swap(): return lax.ppermute(x, 'src', [(0, 1), (1, 0)])]
    pallas_call x5 -> x4, Pallas kernels: 8.23 us -> 8.17 us  [the longest x1 3.13 us: on_device(): call(functools.partial(out_kernel, lay), out_shape=(shape((rows, cols), B...]
  transfers between devices with their start and end apart: 9 -> 7, of which waited for: 5 -> 4; matrix products, arithmetic and copies ran while one was open for 0% -> 0% of each run, Pallas kernels for 11% -> 11%
where the time goes in v7:
time: 96.6 us; the launch traced here: 96 us
  blocking collectives  34.1 us (35%)
  waiting for transfers between devices  24.7 us (26%)
  Pallas kernels  23.3 us (24%)
  starting transfers between devices  11.1 us (11%)
  local copies, waits for them, and re-layouts  1.8 us (2%)
    all_to_all x3, blocking collectives, exchange(): return lax.all_to_all(x, 'chan', split_axis=0, concat_axis=0, tiled=True)  34.1 us
    all_to_all x2, waiting for transfers between devices, exchange(): return lax.all_to_all(x, 'chan', split_axis=0, concat_axis=0, tiled=True)  21.1 us
    all_to_all x2, starting transfers between devices, exchange(): return lax.all_to_all(x, 'chan', split_axis=0, concat_axis=0, tiled=True)  10.9 us
    pallas_call x1, Pallas kernels, on_device(): call(gates_kernel, out_shape=(shape((rows, cols), F32), shape((cols, DOWN...  3.91 us
    ppermute x5, waiting for transfers between devices, swap(): return lax.ppermute(x, 'src', [(0, 1), (1, 0)])  3.64 us
    pallas_call x1, Pallas kernels, on_device(): call(functools.partial(values_kernel, lay), out_shape=(shape((steps, rows...  3.36 us
    pallas_call x1, Pallas kernels, on_device(): call(functools.partial(out_kernel, lay), out_shape=(shape((rows, cols), B...  3.13 us
    pallas_call x1, Pallas kernels, on_device(): call(scan_kernel, out_shape=(shape((rows, NS, cols), F32), shape((rows, c...  2.55 us
  transfers between devices with their start and end apart: 7, of which 4 were waited for; matrix products, arithmetic and copies ran while one was open for 0% of the time, Pallas kernels for 11%

profile of v7, /device:TPU:0, one launch (start us, length us, event | category | flops | bytes accessed | tf_op | source)
XLA Modules:
  0.0 96.0 jit_solution(2472085073658852920)
XLA Ops:
  0.6 2.2 %pack.1 = bf16[8,304,128]{2,1,0:T(8,128)(2,1)} custom-call(bf16[1,8192]{1,0:T(2,128)(2,1)} %query_hbm.1, bf16[1,2048]{1,0:T(2,128)(2,1)} %newkv_hbm.1, bf16[8,16,2048]{2,1,0:T(8,128)(2,1)} %pages_hbm.1, f32[3,1,8192]{2,1,0:T(1,128)} %bitcast.10, s32[8]{0:T(128)} %owner_hbm.1, s32[8]{0:T(128)} %index_hbm.1, s32[16]{0:T(128)} %lengths_hbm.1), custom_call_target="tpu_custom_call" | custom-call | tf_op jit(solution)/shard_map/pack/pallas_call | solution.py:492
  2.8 7.3 %all-to-all-start = ((bf16[8,304,128]{2,1,0:T(8,128)(2,1)}), bf16[8,304,128]{2,1,0:T(8,128)(2,1)S(1)}, u32[]{:S(2)}, u32[]{:S(2)}) async-start(bf16[8,304,128]{2,1,0:T(8,128)(2,1)} %pack.1), calls=%async_computation | async-start | bytes 1245184 | tf_op jit(solution)/shard_map/all_to_all | solution.py:57
  10.1 0.0 copy-start.7
  10.1 1.0 %copy-done.7 = f32[1,16,8192]{2,1,0:T(8,128)S(1)} copy-done((f32[1,16,8192]{2,1,0:T(8,128)S(1)}, f32[1,16,8192]{2,1,0:T(8,128)}, u32[]{:S(2)}) %copy-start.7) | copy-done | bytes 524312
  11.2 0.0 copy-start.8
  11.2 0.7 copy-done.8
  11.9 14.8 %all-to-all-done.recv = bf16[8,304,128]{2,1,0:T(8,128)(2,1)S(1)} async-done(((bf16[8,304,128]{2,1,0:T(8,128)(2,1)}), bf16[8,304,128]{2,1,0:T(8,128)(2,1)S(1)}, u32[]{:S(2)}, u32[]{:S(2)}) %all-to-all-start) | async-done | bytes 622624 | tf_op jit(solution)/shard_map/all_to_all | solution.py:57
  26.7 0.0 collective-permute-start
  26.7 2.0 %collective-permute-done.other = bf16[8,304,128]{2,1,0:T(8,128)(2,1)S(1)} collective-permute-done((bf16[8,304,128]{2,1,0:T(8,128)(2,1)S(1)}, bf16[8,304,128]{2,1,0:T(8,128)(2,1)S(1)}, u32[]{:S(2)}, u32[]{:S(2)}) %collective-permute-start) | collective-permute-done | bytes 622624 | tf_op jit(solution)/shard_map/ppermute | solution.py:53
  28.8 1.1 %attend.1 = (bf16[8,64,128]{2,1,0:T(8,128)(2,1)S(1)}, f32[8,16,128]{2,1,0:T(8,128)S(1)}, f32[8,16,128]{2,1,0:T(8,128)S(1)}) custom-call(bf16[8,304,128]{2,1,0:T(8,128)(2,1)S(1)} %all-to-all-done.recv, bf16[8,304,128]{2,1,0:T(8,128)(2,1)S(1)} %collective-permute-done.other), custom_call_target="tpu_custom_call" | custom-call | tf_op jit(solution)/shard_map/attend/pallas_call | solution.py:527
  29.9 10.8 %all_to_all.25.own = bf16[8,64,128]{2,1,0:T(8,128)(2,1)S(1)} all-to-all(bf16[8,64,128]{2,1,0:T(8,128)(2,1)S(1)} %get-tuple-element.41), channel_id=1, replica_groups=mesh['groups'=2,'src'=2,'chan'=8] {'chan'}, dimensions={0} | all-to-all | bytes 262144 | tf_op jit(solution)/shard_map/all_to_all | solution.py:57
  40.7 0.0 collective-permute-start.1
  40.7 1.5 %fetch.1.fetched = bf16[2048,512]{1,0:T(8,128)(2,1)S(1)} custom-call(bf16[8192,512]{1,0:T(8,128)(2,1)} %weight.7), custom_call_target="tpu_custom_call" | custom-call | flops 3000000000 | tf_op jit(solution)/shard_map/fetch/pallas_call | solution.py:539
  42.2 0.0 collective-permute-done.1.other
  42.2 3.1 %out.1 = (bf16[16,512]{1,0:T(8,128)(2,1)S(1)}, bf16[8,32,512]{2,1,0:T(8,128)(2,1)S(1)}) custom-call(bf16[8,64,128]{2,1,0:T(8,128)(2,1)S(1)} %all_to_all.25.own, bf16[8,64,128]{2,1,0:T(8,128)(2,1)S(1)} %collective-permute-done.1.other, bf16[16,512]{1,0:T(8,128)(2,1)S(1)} %get-tuple-element.43.residual, bf16[8,16,512]{2,1,0:T(8,128)(2,1)S(1)} %get-tuple-element.44.cross, ...), custom_call_target="tpu_custom_call" | custom-call | tf_op jit(solution)/shard_map/out/pallas_call | solution.py:549
  45.4 0.0 copy-start
  45.4 0.0 copy-start.3
  45.4 0.0 copy-start.4
  45.4 12.4 %all_to_all.26.lhs.own = bf16[8,32,512]{2,1,0:T(8,128)(2,1)S(1)} all-to-all(bf16[8,32,512]{2,1,0:T(8,128)(2,1)S(1)} %get-tuple-element.46), channel_id=1, replica_groups=mesh['groups'=2,'src'=2,'chan'=8] {'chan'}, dimensions={0} | all-to-all | bytes 524288 | tf_op jit(solution)/shard_map/all_to_all | solution.py:57
  57.8 0.0 collective-permute-start.2
  57.8 2.4 %values_own.1.partial = f32[16,512]{1,0:T(8,128)S(1)} custom-call(bf16[8,32,512]{2,1,0:T(8,128)(2,1)S(1)} %all_to_all.26.lhs.own, bf16[8192,512]{1,0:T(8,128)(2,1)} %weight.9), custom_call_target="tpu_custom_call" | custom-call | flops 3000000000 | tf_op jit(solution)/shard_map/values_own/pallas_call | solution.py:565
  60.2 0.0 collective-permute-done.2.other.hid_other
  60.2 0.0 copy-done
  60.2 0.0 copy-done.3
  60.3 0.0 copy-done.4
  60.3 3.4 %values.1 = (f32[3,16,512]{2,1,0:T(8,128)}, f32[16,512]{1,0:T(8,128)S(1)}, f32[16,128]{1,0:T(8,128)S(1)}, bf16[8,144,128]{2,1,0:T(8,128)(2,1)}) custom-call(bf16[8,32,512]{2,1,0:T(8,128)(2,1)S(1)} %all_to_all.26.lhs.own, bf16[8,32,512]{2,1,0:T(8,128)(2,1)S(1)} %collective-permute-done.2.other.hid_other, f32[8,16,128]{2,1,0:T(8,128)S(1)} %get-tuple-element.47.own_conv, ...), custom_call_target="tpu_custom_call" | custom-call | tf_op jit(solution)/shard_map/values/pallas_call | solution.py:577
  63.6 3.6 %all-to-all-start.3 = ((bf16[8,144,128]{2,1,0:T(8,128)(2,1)}), bf16[8,144,128]{2,1,0:T(8,128)(2,1)S(1)}, u32[]{:S(2)}, u32[]{:S(2)}) async-start(bf16[8,144,128]{2,1,0:T(8,128)(2,1)} %get-tuple-element.51), calls=%async_computation.3 | async-start | bytes 589824 | tf_op jit(solution)/shard_map/all_to_all | solution.py:57
  67.3 0.0 copy-start.1
  67.3 0.0 copy-start.2
  67.3 0.0 copy-start.5
  67.3 0.0 copy-start.6
  67.3 3.9 %gates.1 = (f32[16,512]{1,0:T(8,128)S(1)}, bf16[512,1024]{1,0:T(8,128)(2,1)S(1)}) custom-call(bf16[8,32,512]{2,1,0:T(8,128)(2,1)S(1)} %all_to_all.26.lhs.own, bf16[8,32,512]{2,1,0:T(8,128)(2,1)S(1)} %collective-permute-done.2.other.hid_other, f32[16,128]{1,0:T(8,128)S(1)} %get-tuple-element.52.rms, bf16[8192,512]{1,0:T(8,128)(2,1)} %weight.10, ...), custom_call_target="tpu_custom_call" | custom-call | flops 3000000000 | tf_op jit(solution)/shard_map/gates/pallas_call | solution.py:595
  71.2 6.3 %all-to-all-done.3.own = bf16[8,144,128]{2,1,0:T(8,128)(2,1)S(1)} async-done(((bf16[8,144,128]{2,1,0:T(8,128)(2,1)}), bf16[8,144,128]{2,1,0:T(8,128)(2,1)S(1)}, u32[]{:S(2)}, u32[]{:S(2)}) %all-to-all-start.3) | async-done | bytes 294944 | tf_op jit(solution)/shard_map/all_to_all | solution.py:57
  77.5 0.0 collective-permute-start.3
  77.5 1.6 %collective-permute-done.3.other = bf16[8,144,128]{2,1,0:T(8,128)(2,1)S(1)} collective-permute-done((bf16[8,144,128]{2,1,0:T(8,128)(2,1)S(1)}, bf16[8,144,128]{2,1,0:T(8,128)(2,1)S(1)}, u32[]{:S(2)}, u32[]{:S(2)}) %collective-permute-start.3) | collective-permute-done | bytes 294944 | tf_op jit(solution)/shard_map/ppermute | solution.py:53
  79.1 0.0 copy-done.1
  79.1 0.0 copy-done.2
  79.1 0.0 copy-done.5
  79.1 0.0 copy-done.6
  79.1 2.5 %scan.1 = (f32[16,16,512]{2,1,0:T(8,128)}, bf16[16,512]{1,0:T(8,128)(2,1)S(1)}, bf16[8,16,512]{2,1,0:T(8,128)(2,1)S(1)}) custom-call(bf16[8,144,128]{2,1,0:T(8,128)(2,1)S(1)} %all-to-all-done.3.own, bf16[8,144,128]{2,1,0:T(8,128)(2,1)S(1)} %collective-permute-done.3.other, bf16[8,32,512]{2,1,0:T(8,128)(2,1)S(1)} %collective-permute-done.2.other.hid_other, ...), custom_call_target="tpu_custom_call" | custom-call | tf_op jit(solution)/shard_map/scan/pallas_call | solution.py:614
  81.7 0.2 collective-permute-start.4
  81.9 2.5 %down.1 = f32[8,16,512]{2,1,0:T(8,128)S(1)} custom-call(bf16[16,512]{1,0:T(8,128)(2,1)S(1)} %get-tuple-element.60.gated, bf16[512,8192]{1,0:T(8,128)(2,1)} %weight.12), custom_call_target="tpu_custom_call" | custom-call | flops 3000000000 | tf_op jit(solution)/shard_map/down/pallas_call | solution.py:640
  84.4 0.0 collective-permute-done.4
  84.4 10.9 %all_to_all.27.final = bf16[8,16,512]{2,1,0:T(8,128)(2,1)S(1)} all-to-all(bf16[8,16,512]{2,1,0:T(8,128)(2,1)S(1)} %add_convert_fusion), channel_id=1, replica_groups=mesh['groups'=2,'src'=2,'chan'=8] {'chan'}, dimensions={0} | all-to-all | bytes 262144 | tf_op jit(solution)/shard_map/all_to_all | solution.py:57
  95.3 0.6 finish.1
  (2 shorter events, 0.1 us)
Async XLA Ops:
  2.8 23.9 %all-to-all-start = ((bf16[8,304,128]{2,1,0:T(8,128)(2,1)}), bf16[8,304,128]{2,1,0:T(8,128)(2,1)S(1)}, u32[]{:S(2)}, u32[]{:S(2)}) async-start(bf16[8,304,128]{2,1,0:T(8,128)(2,1)} %pack.1), calls=%async_computation | async-start | bytes 1245184 | tf_op jit(solution)/shard_map/all_to_all | solution.py:57
  10.1 1.0 %copy-start.7 = (f32[1,16,8192]{2,1,0:T(8,128)S(1)}, f32[1,16,8192]{2,1,0:T(8,128)}, u32[]{:S(2)}) copy-start(f32[1,16,8192]{2,1,0:T(8,128)} %state) | copy-start | bytes 1572868
  11.2 0.7 copy-start.8
  26.7 2.1 %collective-permute-start = (bf16[8,304,128]{2,1,0:T(8,128)(2,1)S(1)}, bf16[8,304,128]{2,1,0:T(8,128)(2,1)S(1)}, u32[]{:S(2)}, u32[]{:S(2)}) collective-permute-start(bf16[8,304,128]{2,1,0:T(8,128)(2,1)S(1)} %all-to-all-done.recv), channel_id=1, source_target_pairs={{0,8},{8,0},{1,9},{9,1},{2,10},{10,2},{3,11},{11,3},{4,12},{12,4},... | collective-permute-start | bytes 1867784 | tf_op jit(solution)/shard_map/ppermute | solution.py:53
  40.7 1.6 %collective-permute-start.1 = (bf16[8,64,128]{2,1,0:T(8,128)(2,1)S(1)}, bf16[8,64,128]{2,1,0:T(8,128)(2,1)S(1)}, u32[]{:S(2)}, u32[]{:S(2)}) collective-permute-start(bf16[8,64,128]{2,1,0:T(8,128)(2,1)S(1)} %all_to_all.25.own), channel_id=1, source_target_pairs={{0,8},{8,0},{1,9},{9,1},{2,10},{10,2},{3,11},{11,3},{4,12},{12,4},... | collective-permute-start | bytes 393224 | tf_op jit(solution)/shard_map/ppermute | solution.py:53
  45.4 14.9 %copy-start = (bf16[512,544]{0,1:T(8,128)(2,1)S(1)}, bf16[512,544]{0,1:T(8,128)(2,1)}, u32[]{:S(2)}) copy-start(bf16[512,544]{0,1:T(8,128)(2,1)} %param.34) | copy-start | bytes 1671172
  45.4 14.9 %copy-start.3 = (f32[4,512]{1,0:T(4,128)S(1)}, f32[4,512]{1,0:T(4,128)}, u32[]{:S(2)}) copy-start(f32[4,512]{1,0:T(4,128)} %taps.1) | copy-start | bytes 24580
  45.4 14.9 %copy-start.4 = (f32[512]{0:T(512)S(1)}, f32[512]{0:T(512)}, u32[]{:S(2)}) copy-start(f32[512]{0:T(512)} %param.33) | copy-start | bytes 6148
  57.8 2.4 %collective-permute-start.2 = (bf16[8,32,512]{2,1,0:T(8,128)(2,1)S(1)}, bf16[8,32,512]{2,1,0:T(8,128)(2,1)S(1)}, u32[]{:S(2)}, u32[]{:S(2)}) collective-permute-start(bf16[8,32,512]{2,1,0:T(8,128)(2,1)S(1)} %all_to_all.26.lhs.own), channel_id=1, source_target_pairs={{0,8},{8,0},{1,9},{9,1},{2,10},{10,2},{3,11},{11,3},{4,12},{12,4},... | collective-permute-start | bytes 786440 | tf_op jit(solution)/shard_map/ppermute | solution.py:53
  63.6 13.9 %all-to-all-start.3 = ((bf16[8,144,128]{2,1,0:T(8,128)(2,1)}), bf16[8,144,128]{2,1,0:T(8,128)(2,1)S(1)}, u32[]{:S(2)}, u32[]{:S(2)}) async-start(bf16[8,144,128]{2,1,0:T(8,128)(2,1)} %get-tuple-element.51), calls=%async_computation.3 | async-start | bytes 589824 | tf_op jit(solution)/shard_map/all_to_all | solution.py:57
  67.3 11.8 %copy-start.1 = (bf16[512,512]{1,0:T(8,128)(2,1)S(1)}, bf16[512,512]{1,0:T(8,128)(2,1)}, u32[]{:S(2)}) copy-start(bf16[512,512]{1,0:T(8,128)(2,1)} %step_proj.1) | copy-start | bytes 1572868
  67.3 11.8 %copy-start.2 = (f32[16,512]{1,0:T(8,128)S(1)}, f32[16,512]{1,0:T(8,128)}, u32[]{:S(2)}) copy-start(f32[16,512]{1,0:T(8,128)} %decay_log.1) | copy-start | bytes 98308
  67.3 11.8 %copy-start.5 = (f32[512]{0:T(512)S(1)}, f32[512]{0:T(512)}, u32[]{:S(2)}) copy-start(f32[512]{0:T(512)} %param.36) | copy-start | bytes 6148
  67.3 11.8 %copy-start.6 = (f32[512]{0:T(512)S(1)}, f32[512]{0:T(512)}, u32[]{:S(2)}) copy-start(f32[512]{0:T(512)} %param.38) | copy-start | bytes 6148
  77.5 1.6 %collective-permute-start.3 = (bf16[8,144,128]{2,1,0:T(8,128)(2,1)S(1)}, bf16[8,144,128]{2,1,0:T(8,128)(2,1)S(1)}, u32[]{:S(2)}, u32[]{:S(2)}) collective-permute-start(bf16[8,144,128]{2,1,0:T(8,128)(2,1)S(1)} %all-to-all-done.3.own), channel_id=1, source_target_pairs={{0,8},{8,0},{1,9},{9,1},{2,10},{10,2},{3,11},{11,3},{4,12},{12,4},... | collective-permute-start | bytes 884744 | tf_op jit(solution)/shard_map/ppermute | solution.py:53
  81.7 2.7 %collective-permute-start.4 = (bf16[8,16,512]{2,1,0:T(8,128)(2,1)S(1)}, bf16[8,16,512]{2,1,0:T(8,128)(2,1)S(1)}, u32[]{:S(2)}, u32[]{:S(2)}) collective-permute-start(bf16[8,16,512]{2,1,0:T(8,128)(2,1)S(1)} %get-tuple-element.61), channel_id=1, source_target_pairs={{0,8},{8,0},{1,9},{9,1},{2,10},{10,2},{3,11},{11,3},{4,12},{12,4},... | collective-permute-start | bytes 393224 | tf_op jit(solution)/shard_map/ppermute | solution.py:53

commit v8 on v7

--- a/solution.py
+++ b/solution.py
@@ -81,16 +81,9 @@
     owner_hbm,
     index_hbm,
     lengths_hbm,
-    out_ref,
-    query,
-    newkv,
-    pages,
-    conv,
-    owners,
-    indexes,
-    lengths,
-    sems,
+    *refs,
 ):
+    outs, (query, newkv, pages, conv, owners, indexes, lengths, sems) = refs[:nchan], refs[nchan:]
     moves = (
         (pages_hbm, pages),
         (conv_hbm, conv),
@@ -121,12 +114,13 @@
             left = lengths[owner] - indexes[i * per_row + j] * page_tokens
             found = jnp.where((lane // page_tokens == j) & (lane % page_tokens < left), owner, found)
         owner_rows.append(found.astype(F32))
-    for d in range(nchan):
-        at = (d // rep) * HD
-        small = [newkv[0:1, x : x + HD].astype(F32) for x in (at, KVH * HD + at)] + owner_rows
+    targets = [jnp.bitwise_xor(lax.axis_index("chan"), k) for k in range(nchan)]
+    for d, out_ref in zip(targets, outs):
+        at = lax.div(d, rep) * HD
+        small = [newkv[0:1, pl.ds(pl.multiple_of(x, HD), HD)].astype(F32) for x in (at, KVH * HD + at)] + owner_rows
         for h in range(lay.per):
-            place = (d * lay.per + h) * HD
-            small.append(query[0:1, place : place + HD].astype(F32))
+            place = pl.multiple_of((d * lay.per + h) * HD, HD)
+            small.append(query[0:1, pl.ds(place, HD)].astype(F32))
         for half in (c, 1 - c):
             first = (half * nchan + d) * cols
             for b in range(blocks):
@@ -135,13 +129,14 @@
                     small.append(conv[w, 0:1, lanes])
         if lay.small_rows > len(small):
             small.append(jnp.zeros((lay.small_rows - len(small), LANES), F32))
-        out_ref[d, lay.small : lay.rows, :] = jnp.concatenate(small, axis=0).astype(BF16)
+        out_ref[lay.small : lay.rows, :] = jnp.concatenate(small, axis=0).astype(BF16)
     copies[0].wait()
-    for d in range(nchan):
-        at = (d // rep) * HD
-        out_ref[d, 0 : lay.tokens, :] = pages[:, :, at : at + HD].reshape(lay.tokens, HD)
-        at = KVH * HD + at
-        out_ref[d, lay.value : lay.small, :] = pages[:, :, at : at + HD].reshape(lay.tokens, HD)
+    for d, out_ref in zip(targets, outs):
+        at = lax.div(d, rep) * HD
+        keys = pl.ds(pl.multiple_of(at, HD), HD)
+        values = pl.ds(pl.multiple_of(KVH * HD + at, HD), HD)
+        out_ref[0 : lay.tokens, :] = pages[:, :, keys].reshape(lay.tokens, HD)
+        out_ref[lay.value : lay.small, :] = pages[:, :, values].reshape(lay.tokens, HD)
 
 
 def load_kernel(residual, state, residual_out, same, cross):
@@ -154,8 +149,10 @@
             ref[d] = state[0, :, lanes].astype(BF16)
 
 
-def attend_kernel(lay, recv, other, out_ref, conv_own, conv_other, queries, scores, result):
-    nchan = recv.shape[0]
+def attend_kernel(lay, nchan, *refs):
+    recv, other = refs[:nchan], refs[nchan : 2 * nchan]
+    out_ref, conv_own, conv_other, queries, scores, result = refs[2 * nchan :]
+    d = lax.axis_index("chan")
     per, tokens = lay.per, lay.tokens
     c = lax.axis_index("src")
     count = nchan * per
@@ -163,14 +160,15 @@
     contract = (((1,), (1,)), ((), ()))
     new_keys, new_values, owners = [], [], []
     spare = conv_own.shape[1] - lay.conv_rows
-    for ref, conv_out, at in ((recv, conv_own, lay.conv), (other, conv_other, lay.conv + lay.conv_rows)):
-        for s in range(nchan):
-            small = ref[s, lay.small : lay.rows, :].astype(F32)
+    for blocks, conv_out, at in ((recv, conv_own, lay.conv), (other, conv_other, lay.conv + lay.conv_rows)):
+        for k, ref in enumerate(blocks):
+            s = jnp.bitwise_xor(d, k)
+            small = ref[lay.small : lay.rows, :].astype(F32)
             conv = small[at : at + lay.conv_rows, :]
             conv_out[s] = jnp.concatenate([conv, jnp.zeros((spare, LANES), F32)], axis=0) if spare else conv
             owners.append(jnp.concatenate([small[2 + i : 3 + i, :] for i in range(lay.owner_rows)], axis=1))
-            if ref is recv:
-                queries[s * per : (s + 1) * per, :] = small[lay.query : lay.query + per, :]
+            if blocks is recv:
+                queries[pl.ds(pl.multiple_of(s * per, per), per), :] = small[lay.query : lay.query + per, :]
                 new_keys.append(small[0:1, :])
                 new_values.append(small[1:2, :])
     fill = round_up(nchan, 16) - nchan
@@ -183,12 +181,12 @@
     lane = lax.broadcasted_iota(jnp.int32, (1, nchan + fill), 1)
     q = queries[...].astype(BF16)
     new_scores = lax.dot_general(q, new_keys, contract, preferred_element_type=F32) * scale
-    new_scores = jnp.where(place == lane, new_scores, NEGATIVE)
+    new_scores = jnp.where(jnp.bitwise_xor(place, d) == lane, new_scores, NEGATIVE)
     wide = (c * nchan + place).astype(F32)
-    sources = [(ref, s) for ref in (recv, other) for s in range(nchan)]
+    sources = list(recv) + list(other)
     highest = None
-    for i, (ref, s) in enumerate(sources):
-        part = lax.dot_general(q, ref[s, 0:tokens, :], contract, preferred_element_type=F32) * scale
+    for i, ref in enumerate(sources):
+        part = lax.dot_general(q, ref[0:tokens, :], contract, preferred_element_type=F32) * scale
         part = jnp.where(wide == owners[i], part, NEGATIVE)
         scores[:, i * tokens : (i + 1) * tokens] = part
         highest = part if highest is None else jnp.maximum(highest, part)
@@ -196,10 +194,10 @@
     new_weight = jnp.exp(new_scores - peak)
     numer = jnp.dot(new_weight.astype(BF16), new_values, preferred_element_type=F32)
     summed = None
-    for i, (ref, s) in enumerate(sources):
+    for i, ref in enumerate(sources):
         weight = jnp.exp(scores[:, i * tokens : (i + 1) * tokens] - peak)
         summed = weight if summed is None else summed + weight
-        numer = numer + jnp.dot(weight.astype(BF16), ref[s, lay.value : lay.small, :], preferred_element_type=F32)
+        numer = numer + jnp.dot(weight.astype(BF16), ref[lay.value : lay.small, :], preferred_element_type=F32)
     total = jnp.sum(summed, axis=1, keepdims=True) + jnp.sum(new_weight, axis=1, keepdims=True)
     result[...] = numer / total
     heads = [result[pl.ds(h, nchan, stride=per), :] for h in range(per)]
@@ -489,11 +487,12 @@
     shape = jax.ShapeDtypeStruct
 
     conv_rows = jnp.transpose(conv_state, (1, 0, 2))
+    chunk = shape((lay.rows, LANES), BF16)
     packed = call(
         functools.partial(pack_kernel, nchan, lay),
-        out_shape=shape((nchan, lay.rows, LANES), BF16),
+        out_shape=(chunk,) * nchan,
         in_specs=hbm(7),
-        out_specs=vmem(1)[0],
+        out_specs=tuple(vmem(nchan)),
         scratch_shapes=[
             VM(query_heads.shape, BF16),
             VM(new_keyval.shape, BF16),
@@ -507,8 +506,10 @@
         compiler_params=pltpu.CompilerParams(vmem_limit_bytes=64 * 2**20 - 2**18),
         name="pack",
     )(query_heads, new_keyval, cache_pages, conv_rows, page_owner, page_index, prompt_lengths)
-    packed, residual_input, mamba_state = lax.optimization_barrier((packed, residual_input, mamba_state))
-    arrived = exchange(packed)
+    *packed, residual_input, mamba_state = lax.optimization_barrier((*packed, residual_input, mamba_state))
+    arrived = [packed[0]]
+    for k in range(1, nchan):
+        arrived.append(lax.ppermute(packed[k], "chan", [(i, i ^ k) for i in range(nchan)]))
     cut = shape((nchan, NS, cols), BF16)
     residual, same, cross = call(
         load_kernel,
@@ -519,20 +520,21 @@
         cost_estimate=cost(SHORT, 0),
         name="load",
     )(residual_input, mamba_state)
-    arrived, residual, same, cross = lax.optimization_barrier((arrived, residual, same, cross))
-
-    other_arrived = swap(arrived)
+
+    early = nchan // 4
+    arrived[early], residual, same, cross = lax.optimization_barrier((arrived[early], residual, same, cross))
+    other_arrived = [swap(block) for block in arrived]
     pairs = nchan * lay.per
     conv_cut = shape((nchan, round_up(lay.conv_rows, 8), LANES), F32)
     attended, conv_own, conv_other = call(
-        functools.partial(attend_kernel, lay),
+        functools.partial(attend_kernel, lay, nchan),
         out_shape=(shape((nchan, pairs, LANES), BF16), conv_cut, conv_cut),
-        in_specs=vmem(2),
+        in_specs=vmem(2 * nchan),
         out_specs=tuple(vmem(3)),
         scratch_shapes=[VM((pairs, HD), F32), VM((pairs, 2 * nchan * lay.tokens), F32), VM((pairs, HD), F32)],
         compiler_params=params(4 if held < 16 else 44),
         name="attend",
-    )(arrived, other_arrived)
+    )(*arrived, *other_arrived)
     att_own, out_weight = lax.optimization_barrier((exchange(attended), out_heads))
     att_other = swap(att_own)
     fetched_rows = D // 4

time: 96.6 us -> 96 us (level)
  waiting for transfers between devices: 24.7 us -> 16.2 us
  starting transfers between devices: 11.1 us -> 18.5 us
    all_to_all x2 -> x1, waiting for transfers between devices: 21.1 us -> 6.29 us  [exchange(): return lax.all_to_all(x, 'chan', split_axis=0, concat_axis=0, tiled=True)]
    ppermute x0 -> x7, starting transfers between devices: none -> 12.5 us  [on_device(): lax.ppermute(packed[k], 'chan', [(i, i ^ k) for i in range(nchan)])]
    ppermute x0 -> x7, waiting for transfers between devices: none -> 7.36 us  [on_device(): lax.ppermute(packed[k], 'chan', [(i, i ^ k) for i in range(nchan)])]
    all_to_all x2 -> x1, starting transfers between devices: 10.9 us -> 3.63 us  [exchange(): return lax.all_to_all(x, 'chan', split_axis=0, concat_axis=0, tiled=True)]
    ppermute x5 -> x12, starting transfers between devices: 0.21 us -> 2.35 us  [swap(): return lax.ppermute(x, 'src', [(0, 1), (1, 0)])]
    ppermute x5 -> x12, waiting for transfers between devices: 3.64 us -> 2.51 us  [swap(): return lax.ppermute(x, 'src', [(0, 1), (1, 0)])]
  transfers between devices with their start and end apart: 7 -> 20, of which waited for: 4 -> 7; matrix products, arithmetic and copies ran while one was open for 0% -> 0% of each run, Pallas kernels for 11% -> 11%
where the time goes in v8:
time: 96 us; the launch traced here: 95.4 us
  blocking collectives  34.7 us (36%)
  Pallas kernels  23.4 us (24%)
  starting transfers between devices  18.5 us (19%)
  waiting for transfers between devices  16.2 us (17%)
  local copies, waits for them, and re-layouts  1.81 us (2%)
    all_to_all x3, blocking collectives, exchange(): return lax.all_to_all(x, 'chan', split_axis=0, concat_axis=0, tiled=True)  34.7 us
    ppermute x7, starting transfers between devices, on_device(): lax.ppermute(packed[k], 'chan', [(i, i ^ k) for i in range(nchan)])  12.5 us
    ppermute x7, waiting for transfers between devices, on_device(): lax.ppermute(packed[k], 'chan', [(i, i ^ k) for i in range(nchan)])  7.36 us
    all_to_all x1, waiting for transfers between devices, exchange(): return lax.all_to_all(x, 'chan', split_axis=0, concat_axis=0, tiled=True)  6.29 us
    pallas_call x1, Pallas kernels, on_device(): call(gates_kernel, out_shape=(shape((rows, cols), F32), shape((cols, DOWN...  3.91 us
    all_to_all x1, starting transfers between devices, exchange(): return lax.all_to_all(x, 'chan', split_axis=0, concat_axis=0, tiled=True)  3.63 us
    pallas_call x1, Pallas kernels, on_device(): call(functools.partial(values_kernel, lay), out_shape=(shape((steps, rows...  3.36 us
    pallas_call x1, Pallas kernels, on_device(): call(functools.partial(out_kernel, lay), out_shape=(shape((rows, cols), B...  3.13 us
  transfers between devices with their start and end apart: 20, of which 7 were waited for; matrix products, arithmetic and copies ran while one was open for 0% of the time, Pallas kernels for 11%

profile of v8, /device:TPU:0, one launch (start us, length us, event | category | flops | bytes accessed | tf_op | source)
XLA Modules:
  0.0 95.4 jit_solution(3181574371826075718)
XLA Ops:
  0.6 2.3 %pack.1 = (bf16[304,128]{1,0:T(8,128)(2,1)}, bf16[304,128]{1,0:T(8,128)(2,1)}, bf16[304,128]{1,0:T(8,128)(2,1)}, bf16[304,128]{1,0:T(8,128)(2,1)}, bf16[304,128]...) custom-call(bf16[1,8192]{1,0:T(2,128)(2,1)} %query_hbm.1, ...), custom_call_target="tpu_custom_call" | custom-call | tf_op jit(solution)/shard_map/pack/pallas_call | solution.py:491
  2.9 0.0 copy-start.2
  2.9 3.0 %collective-permute-start = (bf16[304,128]{1,0:T(8,128)(2,1)}, bf16[304,128]{1,0:T(8,128)(2,1)S(1)}, u32[]{:S(2)}, u32[]{:S(2)}) collective-permute-start(bf16[304,128]{1,0:T(8,128)(2,1)} %get-tuple-element.58), channel_id=1, source_target_pairs={{0,1},{1,0},{2,3},{3,2},{4,5},{5,4},{6,7},{7,6},{8,9},{9,8},{10,11... | collective-permute-start | bytes 233480 | tf_op jit(solution)/shard_map/ppermute | solution.py:512
  5.9 1.6 %collective-permute-start.1 = (bf16[304,128]{1,0:T(8,128)(2,1)}, bf16[304,128]{1,0:T(8,128)(2,1)S(1)}, u32[]{:S(2)}, u32[]{:S(2)}) collective-permute-start(bf16[304,128]{1,0:T(8,128)(2,1)} %get-tuple-element.59), channel_id=1, source_target_pairs={{0,2},{1,3},{2,0},{3,1},{4,6},{5,7},{6,4},{7,5},{8,10},{9,11},{10,... | collective-permute-start | bytes 233480 | tf_op jit(solution)/shard_map/ppermute | solution.py:512
  7.5 0.0 collective-permute-start.2
  7.5 3.0 %collective-permute-start.3 = (bf16[304,128]{1,0:T(8,128)(2,1)}, bf16[304,128]{1,0:T(8,128)(2,1)S(1)}, u32[]{:S(2)}, u32[]{:S(2)}) collective-permute-start(bf16[304,128]{1,0:T(8,128)(2,1)} %get-tuple-element.67), channel_id=1, source_target_pairs={{0,4},{1,5},{2,6},{3,7},{4,0},{5,1},{6,2},{7,3},{8,12},{9,13},{10,... | collective-permute-start | bytes 233480 | tf_op jit(solution)/shard_map/ppermute | solution.py:512
  10.5 1.3 %collective-permute-start.4 = (bf16[304,128]{1,0:T(8,128)(2,1)}, bf16[304,128]{1,0:T(8,128)(2,1)S(1)}, u32[]{:S(2)}, u32[]{:S(2)}) collective-permute-start(bf16[304,128]{1,0:T(8,128)(2,1)} %get-tuple-element.68), channel_id=1, source_target_pairs={{0,5},{1,4},{2,7},{3,6},{4,1},{5,0},{6,3},{7,2},{8,13},{9,12},{10,... | collective-permute-start | bytes 233480 | tf_op jit(solution)/shard_map/ppermute | solution.py:512
  11.8 0.0 collective-permute-done.refs_1_
  11.8 3.6 %collective-permute-start.5 = (bf16[304,128]{1,0:T(8,128)(2,1)}, bf16[304,128]{1,0:T(8,128)(2,1)S(1)}, u32[]{:S(2)}, u32[]{:S(2)}) collective-permute-start(bf16[304,128]{1,0:T(8,128)(2,1)} %get-tuple-element.69), channel_id=1, source_target_pairs={{0,6},{1,7},{2,4},{3,5},{4,2},{5,3},{6,0},{7,1},{8,14},{9,15},{10,... | collective-permute-start | bytes 233480 | tf_op jit(solution)/shard_map/ppermute | solution.py:512
  15.4 0.0 collective-permute-done.1.refs_2_
  15.4 0.0 collective-permute-start.6
  15.4 0.0 collective-permute-done.2.refs_3_
  15.4 0.1 collective-permute-start.7
  15.5 0.0 collective-permute-done.3.refs_4_
  15.5 0.5 collective-permute-start.8
  16.0 7.3 %collective-permute-done.4.refs_5_ = bf16[304,128]{1,0:T(8,128)(2,1)S(1)} collective-permute-done((bf16[304,128]{1,0:T(8,128)(2,1)}, bf16[304,128]{1,0:T(8,128)(2,1)S(1)}, u32[]{:S(2)}, u32[]{:S(2)}) %collective-permute-start.4) | collective-permute-done | bytes 77856 | tf_op jit(solution)/shard_map/ppermute | solution.py:512
  23.3 0.0 collective-permute-start.10
  23.3 1.0 %copy-done.8 = f32[1,16,8192]{2,1,0:T(8,128)S(1)} copy-done((f32[1,16,8192]{2,1,0:T(8,128)S(1)}, f32[1,16,8192]{2,1,0:T(8,128)}, u32[]{:S(2)}) %copy-start.8) | copy-done | bytes 524312
  24.4 0.7 copy-done.9
  25.1 0.0 collective-permute-done.5.refs_6_
  25.1 0.6 collective-permute-start.11
  25.7 0.0 collective-permute-done.6.refs_7_
  25.7 0.1 collective-permute-start.12
  25.8 0.0 collective-permute-done.7.refs_8_
  25.8 0.4 collective-permute-start.13
  26.2 0.0 collective-permute-done.8.refs_9_
  26.2 0.1 collective-permute-start.14
  26.3 0.0 collective-permute-done.10.refs_11_
  26.3 0.4 collective-permute-start.9
  26.7 0.0 collective-permute-done.11.refs_12_
  26.8 0.2 collective-permute-done.12.refs_13_
  27.0 0.2 collective-permute-done.13.refs_14_
  27.1 0.4 collective-permute-done.14.refs_15_
  27.5 0.2 collective-permute-done.9.refs_10_
  27.7 0.0 copy-done.2
  27.7 1.1 %attend.1 = (bf16[8,64,128]{2,1,0:T(8,128)(2,1)S(1)}, f32[8,16,128]{2,1,0:T(8,128)S(1)}, f32[8,16,128]{2,1,0:T(8,128)S(1)}) custom-call(bf16[304,128]{1,0:T(8,128)(2,1)S(1)} %copy-done.2, bf16[304,128]{1,0:T(8,128)(2,1)S(1)} %collective-permute-done.refs_1_, bf16[304,128]{1,0:T(8,128)(2,1)S(1)} %collective-permute-done.1.refs_2_, ...), custom_call_target="tpu_custom_call" | custom-call | tf_op jit(solution)/shard_map/attend/pallas_call | solution.py:529
  28.8 11.3 %all_to_all.20.own = bf16[8,64,128]{2,1,0:T(8,128)(2,1)S(1)} all-to-all(bf16[8,64,128]{2,1,0:T(8,128)(2,1)S(1)} %get-tuple-element.71), channel_id=1, replica_groups=mesh['groups'=2,'src'=2,'chan'=8] {'chan'}, dimensions={0} | all-to-all | bytes 262144 | tf_op jit(solution)/shard_map/all_to_all | solution.py:57
  40.1 0.0 collective-permute-start.15
  40.1 1.5 %fetch.1.fetched = bf16[2048,512]{1,0:T(8,128)(2,1)S(1)} custom-call(bf16[8192,512]{1,0:T(8,128)(2,1)} %weight.7), custom_call_target="tpu_custom_call" | custom-call | flops 3000000000 | tf_op jit(solution)/shard_map/fetch/pallas_call | solution.py:541
  41.7 0.0 collective-permute-done.15.other
  41.7 3.1 %out.1 = (bf16[16,512]{1,0:T(8,128)(2,1)S(1)}, bf16[8,32,512]{2,1,0:T(8,128)(2,1)S(1)}) custom-call(bf16[8,64,128]{2,1,0:T(8,128)(2,1)S(1)} %all_to_all.20.own, bf16[8,64,128]{2,1,0:T(8,128)(2,1)S(1)} %collective-permute-done.15.other, bf16[16,512]{1,0:T(8,128)(2,1)S(1)} %get-tuple-element.73.residual, bf16[8,16,512]{2,1,0:T(8,128)(2,1)S(1)} %get-tuple-element.74.cross, ...), custom_call_target="tpu_custom_call" | custom-call | tf_op jit(solution)/shard_map/out/pallas_call | solution.py:551
  44.8 0.0 copy-start
  44.8 0.0 copy-start.4
  44.8 0.0 copy-start.5
  44.8 12.4 %all_to_all.21.lhs.own = bf16[8,32,512]{2,1,0:T(8,128)(2,1)S(1)} all-to-all(bf16[8,32,512]{2,1,0:T(8,128)(2,1)S(1)} %get-tuple-element.76), channel_id=1, replica_groups=mesh['groups'=2,'src'=2,'chan'=8] {'chan'}, dimensions={0} | all-to-all | bytes 524288 | tf_op jit(solution)/shard_map/all_to_all | solution.py:57
  57.3 0.0 collective-permute-start.16
  57.3 2.4 %values_own.1.partial = f32[16,512]{1,0:T(8,128)S(1)} custom-call(bf16[8,32,512]{2,1,0:T(8,128)(2,1)S(1)} %all_to_all.21.lhs.own, bf16[8192,512]{1,0:T(8,128)(2,1)} %weight.9), custom_call_target="tpu_custom_call" | custom-call | flops 3000000000 | tf_op jit(solution)/shard_map/values_own/pallas_call | solution.py:567
  59.7 0.0 collective-permute-done.16.other.hid_other
  59.7 3.4 %values.1 = (f32[3,16,512]{2,1,0:T(8,128)}, f32[16,512]{1,0:T(8,128)S(1)}, f32[16,128]{1,0:T(8,128)S(1)}, bf16[8,144,128]{2,1,0:T(8,128)(2,1)}) custom-call(bf16[8,32,512]{2,1,0:T(8,128)(2,1)S(1)} %all_to_all.21.lhs.own, bf16[8,32,512]{2,1,0:T(8,128)(2,1)S(1)} %collective-permute-done.16.other.hid_other, f32[8,16,128]{2,1,0:T(8,128)S(1)} %get-tuple-element.77.own_conv, ...), custom_call_target="tpu_custom_call" | custom-call | tf_op jit(solution)/shard_map/values/pallas_call | solution.py:579
  63.1 3.6 %all-to-all-start.2 = ((bf16[8,144,128]{2,1,0:T(8,128)(2,1)}), bf16[8,144,128]{2,1,0:T(8,128)(2,1)S(1)}, u32[]{:S(2)}, u32[]{:S(2)}) async-start(bf16[8,144,128]{2,1,0:T(8,128)(2,1)} %get-tuple-element.81), calls=%async_computation.2 | async-start | bytes 589824 | tf_op jit(solution)/shard_map/all_to_all | solution.py:57
  66.7 0.0 copy-start.3
  66.7 0.0 copy-start.6
  66.8 0.0 copy-start.7
  66.8 3.9 %gates.1 = (f32[16,512]{1,0:T(8,128)S(1)}, bf16[512,1024]{1,0:T(8,128)(2,1)S(1)}) custom-call(bf16[8,32,512]{2,1,0:T(8,128)(2,1)S(1)} %all_to_all.21.lhs.own, bf16[8,32,512]{2,1,0:T(8,128)(2,1)S(1)} %collective-permute-done.16.other.hid_other, f32[16,128]{1,0:T(8,128)S(1)} %get-tuple-element.82.rms, bf16[8192,512]{1,0:T(8,128)(2,1)} %weight.10, ...), custom_call_target="tpu_custom_call" | custom-call | flops 3000000000 | tf_op jit(solution)/shard_map/gates/pallas_call | solution.py:597
  70.7 6.3 %all-to-all-done.2.own = bf16[8,144,128]{2,1,0:T(8,128)(2,1)S(1)} async-done(((bf16[8,144,128]{2,1,0:T(8,128)(2,1)}), bf16[8,144,128]{2,1,0:T(8,128)(2,1)S(1)}, u32[]{:S(2)}, u32[]{:S(2)}) %all-to-all-start.2) | async-done | bytes 294944 | tf_op jit(solution)/shard_map/all_to_all | solution.py:57
  77.0 0.0 collective-permute-start.17
  77.0 1.6 %collective-permute-done.17.other = bf16[8,144,128]{2,1,0:T(8,128)(2,1)S(1)} collective-permute-done((bf16[8,144,128]{2,1,0:T(8,128)(2,1)S(1)}, bf16[8,144,128]{2,1,0:T(8,128)(2,1)S(1)}, u32[]{:S(2)}, u32[]{:S(2)}) %collective-permute-start.17) | collective-permute-done | bytes 294944 | tf_op jit(solution)/shard_map/ppermute | solution.py:53
  78.6 0.0 copy-done.7
  78.6 2.5 %scan.1 = (f32[16,16,512]{2,1,0:T(8,128)}, bf16[16,512]{1,0:T(8,128)(2,1)S(1)}, bf16[8,16,512]{2,1,0:T(8,128)(2,1)S(1)}) custom-call(bf16[8,144,128]{2,1,0:T(8,128)(2,1)S(1)} %all-to-all-done.2.own, bf16[8,144,128]{2,1,0:T(8,128)(2,1)S(1)} %collective-permute-done.17.other, bf16[8,32,512]{2,1,0:T(8,128)(2,1)S(1)} %collective-permute-done.16.other.hid_other, ...), custom_call_target="tpu_custom_call" | custom-call | tf_op jit(solution)/shard_map/scan/pallas_call | solution.py:616
  81.1 0.2 collective-permute-start.18
  81.3 2.5 %down.1 = f32[8,16,512]{2,1,0:T(8,128)S(1)} custom-call(bf16[16,512]{1,0:T(8,128)(2,1)S(1)} %get-tuple-element.90.gated, bf16[512,8192]{1,0:T(8,128)(2,1)} %weight.12), custom_call_target="tpu_custom_call" | custom-call | flops 3000000000 | tf_op jit(solution)/shard_map/down/pallas_call | solution.py:642
  83.8 0.0 collective-permute-done.18
  83.9 10.9 %all_to_all.22.final = bf16[8,16,512]{2,1,0:T(8,128)(2,1)S(1)} all-to-all(bf16[8,16,512]{2,1,0:T(8,128)(2,1)S(1)} %add_convert_fusion), channel_id=1, replica_groups=mesh['groups'=2,'src'=2,'chan'=8] {'chan'}, dimensions={0} | all-to-all | bytes 262144 | tf_op jit(solution)/shard_map/all_to_all | solution.py:57
  94.8 0.6 finish.1
  (11 shorter events, 0.1 us)
Async XLA Ops:
  2.9 24.8 %copy-start.2 = (bf16[304,128]{1,0:T(8,128)(2,1)S(1)}, bf16[304,128]{1,0:T(8,128)(2,1)}, u32[]{:S(2)}) copy-start(bf16[304,128]{1,0:T(8,128)(2,1)} %get-tuple-element.57.refs_0_) | copy-start | bytes 233476
  2.9 8.9 %collective-permute-start = (bf16[304,128]{1,0:T(8,128)(2,1)}, bf16[304,128]{1,0:T(8,128)(2,1)S(1)}, u32[]{:S(2)}, u32[]{:S(2)}) collective-permute-start(bf16[304,128]{1,0:T(8,128)(2,1)} %get-tuple-element.58), channel_id=1, source_target_pairs={{0,1},{1,0},{2,3},{3,2},{4,5},{5,4},{6,7},{7,6},{8,9},{9,8},{10,11... | collective-permute-start | bytes 233480 | tf_op jit(solution)/shard_map/ppermute | solution.py:512
  5.9 9.5 %collective-permute-start.1 = (bf16[304,128]{1,0:T(8,128)(2,1)}, bf16[304,128]{1,0:T(8,128)(2,1)S(1)}, u32[]{:S(2)}, u32[]{:S(2)}) collective-permute-start(bf16[304,128]{1,0:T(8,128)(2,1)} %get-tuple-element.59), channel_id=1, source_target_pairs={{0,2},{1,3},{2,0},{3,1},{4,6},{5,7},{6,4},{7,5},{8,10},{9,11},{10,... | collective-permute-start | bytes 233480 | tf_op jit(solution)/shard_map/ppermute | solution.py:512
  7.5 7.9 %collective-permute-start.2 = (bf16[304,128]{1,0:T(8,128)(2,1)}, bf16[304,128]{1,0:T(8,128)(2,1)S(1)}, u32[]{:S(2)}, u32[]{:S(2)}) collective-permute-start(bf16[304,128]{1,0:T(8,128)(2,1)} %get-tuple-element.66), channel_id=1, source_target_pairs={{0,3},{1,2},{2,1},{3,0},{4,7},{5,6},{6,5},{7,4},{8,11},{9,10},{10,... | collective-permute-start | bytes 233480 | tf_op jit(solution)/shard_map/ppermute | solution.py:512
  7.5 8.0 %collective-permute-start.3 = (bf16[304,128]{1,0:T(8,128)(2,1)}, bf16[304,128]{1,0:T(8,128)(2,1)S(1)}, u32[]{:S(2)}, u32[]{:S(2)}) collective-permute-start(bf16[304,128]{1,0:T(8,128)(2,1)} %get-tuple-element.67), channel_id=1, source_target_pairs={{0,4},{1,5},{2,6},{3,7},{4,0},{5,1},{6,2},{7,3},{8,12},{9,13},{10,... | collective-permute-start | bytes 233480 | tf_op jit(solution)/shard_map/ppermute | solution.py:512
  10.5 12.8 %collective-permute-start.4 = (bf16[304,128]{1,0:T(8,128)(2,1)}, bf16[304,128]{1,0:T(8,128)(2,1)S(1)}, u32[]{:S(2)}, u32[]{:S(2)}) collective-permute-start(bf16[304,128]{1,0:T(8,128)(2,1)} %get-tuple-element.68), channel_id=1, source_target_pairs={{0,5},{1,4},{2,7},{3,6},{4,1},{5,0},{6,3},{7,2},{8,13},{9,12},{10,... | collective-permute-start | bytes 233480 | tf_op jit(solution)/shard_map/ppermute | solution.py:512
  11.8 13.3 %collective-permute-start.5 = (bf16[304,128]{1,0:T(8,128)(2,1)}, bf16[304,128]{1,0:T(8,128)(2,1)S(1)}, u32[]{:S(2)}, u32[]{:S(2)}) collective-permute-start(bf16[304,128]{1,0:T(8,128)(2,1)} %get-tuple-element.69), channel_id=1, source_target_pairs={{0,6},{1,7},{2,4},{3,5},{4,2},{5,3},{6,0},{7,1},{8,14},{9,15},{10,... | collective-permute-start | bytes 233480 | tf_op jit(solution)/shard_map/ppermute | solution.py:512
  15.4 10.3 %collective-permute-start.6 = (bf16[304,128]{1,0:T(8,128)(2,1)}, bf16[304,128]{1,0:T(8,128)(2,1)S(1)}, u32[]{:S(2)}, u32[]{:S(2)}) collective-permute-start(bf16[304,128]{1,0:T(8,128)(2,1)} %get-tuple-element.70), channel_id=1, source_target_pairs={{0,7},{1,6},{2,5},{3,4},{4,3},{5,2},{6,1},{7,0},{8,15},{9,14},{10,... | collective-permute-start | bytes 233480 | tf_op jit(solution)/shard_map/ppermute | solution.py:512
  15.4 10.4 %collective-permute-start.7 = (bf16[304,128]{1,0:T(8,128)(2,1)}, bf16[304,128]{1,0:T(8,128)(2,1)S(1)}, u32[]{:S(2)}, u32[]{:S(2)}) collective-permute-start(bf16[304,128]{1,0:T(8,128)(2,1)} %get-tuple-element.57.refs_0_), channel_id=1, source_target_pairs={{0,8},{8,0},{1,9},{9,1},{2,10},{10,2},{3,11},{11,3},{4,12},{12,4},... | collective-permute-start | bytes 233480 | tf_op jit(solution)/shard_map/ppermute | solution.py:53
  15.5 10.7 %collective-permute-start.8 = (bf16[304,128]{1,0:T(8,128)(2,1)S(1)}, bf16[304,128]{1,0:T(8,128)(2,1)S(1)}, u32[]{:S(2)}, u32[]{:S(2)}) collective-permute-start(bf16[304,128]{1,0:T(8,128)(2,1)S(1)} %collective-permute-done.refs_1_), channel_id=1, source_target_pairs={{0,8},{8,0},{1,9},{9,1},{2,10},{10,2},{3,11},{11,3},{4,12},{12,4},... | collective-permute-start | bytes 233480 | tf_op jit(solution)/shard_map/ppermute | solution.py:53
  23.3 3.0 %collective-permute-start.10 = (bf16[304,128]{1,0:T(8,128)(2,1)S(1)}, bf16[304,128]{1,0:T(8,128)(2,1)S(1)}, u32[]{:S(2)}, u32[]{:S(2)}) collective-permute-start(bf16[304,128]{1,0:T(8,128)(2,1)S(1)} %collective-permute-done.2.refs_3_), channel_id=1, source_target_pairs={{0,8},{8,0},{1,9},{9,1},{2,10},{10,2},{3,11},{11,3},{4,12},{12,4},... | collective-permute-start | bytes 233480 | tf_op jit(solution)/shard_map/ppermute | solution.py:53
  23.3 1.0 %copy-start.8 = (f32[1,16,8192]{2,1,0:T(8,128)S(1)}, f32[1,16,8192]{2,1,0:T(8,128)}, u32[]{:S(2)}) copy-start(f32[1,16,8192]{2,1,0:T(8,128)} %state) | copy-start | bytes 1572868
  24.4 0.7 copy-start.9
  25.1 1.6 %collective-permute-start.11 = (bf16[304,128]{1,0:T(8,128)(2,1)S(1)}, bf16[304,128]{1,0:T(8,128)(2,1)S(1)}, u32[]{:S(2)}, u32[]{:S(2)}) collective-permute-start(bf16[304,128]{1,0:T(8,128)(2,1)S(1)} %collective-permute-done.3.refs_4_), channel_id=1, source_target_pairs={{0,8},{8,0},{1,9},{9,1},{2,10},{10,2},{3,11},{11,3},{4,12},{12,4},... | collective-permute-start | bytes 233480 | tf_op jit(solution)/shard_map/ppermute | solution.py:53
  25.7 1.3 %collective-permute-start.12 = (bf16[304,128]{1,0:T(8,128)(2,1)S(1)}, bf16[304,128]{1,0:T(8,128)(2,1)S(1)}, u32[]{:S(2)}, u32[]{:S(2)}) collective-permute-start(bf16[304,128]{1,0:T(8,128)(2,1)S(1)} %collective-permute-done.4.refs_5_), channel_id=1, source_target_pairs={{0,8},{8,0},{1,9},{9,1},{2,10},{10,2},{3,11},{11,3},{4,12},{12,4},... | collective-permute-start | bytes 233480 | tf_op jit(solution)/shard_map/ppermute | solution.py:53
  25.8 1.3 %collective-permute-start.13 = (bf16[304,128]{1,0:T(8,128)(2,1)S(1)}, bf16[304,128]{1,0:T(8,128)(2,1)S(1)}, u32[]{:S(2)}, u32[]{:S(2)}) collective-permute-start(bf16[304,128]{1,0:T(8,128)(2,1)S(1)} %collective-permute-done.5.refs_6_), channel_id=1, source_target_pairs={{0,8},{8,0},{1,9},{9,1},{2,10},{10,2},{3,11},{11,3},{4,12},{12,4},... | collective-permute-start | bytes 233480 | tf_op jit(solution)/shard_map/ppermute | solution.py:53
  26.2 1.3 %collective-permute-start.14 = (bf16[304,128]{1,0:T(8,128)(2,1)S(1)}, bf16[304,128]{1,0:T(8,128)(2,1)S(1)}, u32[]{:S(2)}, u32[]{:S(2)}) collective-permute-start(bf16[304,128]{1,0:T(8,128)(2,1)S(1)} %collective-permute-done.6.refs_7_), channel_id=1, source_target_pairs={{0,8},{8,0},{1,9},{9,1},{2,10},{10,2},{3,11},{11,3},{4,12},{12,4},... | collective-permute-start | bytes 233480 | tf_op jit(solution)/shard_map/ppermute | solution.py:53
  26.3 1.3 %collective-permute-start.9 = (bf16[304,128]{1,0:T(8,128)(2,1)S(1)}, bf16[304,128]{1,0:T(8,128)(2,1)S(1)}, u32[]{:S(2)}, u32[]{:S(2)}) collective-permute-start(bf16[304,128]{1,0:T(8,128)(2,1)S(1)} %collective-permute-done.1.refs_2_), channel_id=1, source_target_pairs={{0,8},{8,0},{1,9},{9,1},{2,10},{10,2},{3,11},{11,3},{4,12},{12,4},... | collective-permute-start | bytes 233480 | tf_op jit(solution)/shard_map/ppermute | solution.py:53
  40.1 1.6 %collective-permute-start.15 = (bf16[8,64,128]{2,1,0:T(8,128)(2,1)S(1)}, bf16[8,64,128]{2,1,0:T(8,128)(2,1)S(1)}, u32[]{:S(2)}, u32[]{:S(2)}) collective-permute-start(bf16[8,64,128]{2,1,0:T(8,128)(2,1)S(1)} %all_to_all.20.own), channel_id=1, source_target_pairs={{0,8},{8,0},{1,9},{9,1},{2,10},{10,2},{3,11},{11,3},{4,12},{12,4},... | collective-permute-start | bytes 393224 | tf_op jit(solution)/shard_map/ppermute | solution.py:53
  44.8 14.9 %copy-start = (bf16[512,544]{0,1:T(8,128)(2,1)S(1)}, bf16[512,544]{0,1:T(8,128)(2,1)}, u32[]{:S(2)}) copy-start(bf16[512,544]{0,1:T(8,128)(2,1)} %param.34) | copy-start | bytes 1671172
  44.8 14.9 %copy-start.4 = (f32[4,512]{1,0:T(4,128)S(1)}, f32[4,512]{1,0:T(4,128)}, u32[]{:S(2)}) copy-start(f32[4,512]{1,0:T(4,128)} %taps.1) | copy-start | bytes 24580
  44.8 14.9 %copy-start.5 = (f32[512]{0:T(512)S(1)}, f32[512]{0:T(512)}, u32[]{:S(2)}) copy-start(f32[512]{0:T(512)} %param.33) | copy-start | bytes 6148
  57.3 2.4 %collective-permute-start.16 = (bf16[8,32,512]{2,1,0:T(8,128)(2,1)S(1)}, bf16[8,32,512]{2,1,0:T(8,128)(2,1)S(1)}, u32[]{:S(2)}, u32[]{:S(2)}) collective-permute-start(bf16[8,32,512]{2,1,0:T(8,128)(2,1)S(1)} %all_to_all.21.lhs.own), channel_id=1, source_target_pairs={{0,8},{8,0},{1,9},{9,1},{2,10},{10,2},{3,11},{11,3},{4,12},{12,4},... | collective-permute-start | bytes 786440 | tf_op jit(solution)/shard_map/ppermute | solution.py:53
  63.1 13.9 %all-to-all-start.2 = ((bf16[8,144,128]{2,1,0:T(8,128)(2,1)}), bf16[8,144,128]{2,1,0:T(8,128)(2,1)S(1)}, u32[]{:S(2)}, u32[]{:S(2)}) async-start(bf16[8,144,128]{2,1,0:T(8,128)(2,1)} %get-tuple-element.81), calls=%async_computation.2 | async-start | bytes 589824 | tf_op jit(solution)/shard_map/all_to_all | solution.py:57
  66.7 11.8 %copy-start.1 = (bf16[512,512]{1,0:T(8,128)(2,1)S(1)}, bf16[512,512]{1,0:T(8,128)(2,1)}, u32[]{:S(2)}) copy-start(bf16[512,512]{1,0:T(8,128)(2,1)} %step_proj.1) | copy-start | bytes 1572868
  66.7 11.8 %copy-start.3 = (f32[16,512]{1,0:T(8,128)S(1)}, f32[16,512]{1,0:T(8,128)}, u32[]{:S(2)}) copy-start(f32[16,512]{1,0:T(8,128)} %decay_log.1) | copy-start | bytes 98308
  66.7 11.8 %copy-start.6 = (f32[512]{0:T(512)S(1)}, f32[512]{0:T(512)}, u32[]{:S(2)}) copy-start(f32[512]{0:T(512)} %param.36) | copy-start | bytes 6148
  66.8 11.8 %copy-start.7 = (f32[512]{0:T(512)S(1)}, f32[512]{0:T(512)}, u32[]{:S(2)}) copy-start(f32[512]{0:T(512)} %param.38) | copy-start | bytes 6148
  77.0 1.6 %collective-permute-start.17 = (bf16[8,144,128]{2,1,0:T(8,128)(2,1)S(1)}, bf16[8,144,128]{2,1,0:T(8,128)(2,1)S(1)}, u32[]{:S(2)}, u32[]{:S(2)}) collective-permute-start(bf16[8,144,128]{2,1,0:T(8,128)(2,1)S(1)} %all-to-all-done.2.own), channel_id=1, source_target_pairs={{0,8},{8,0},{1,9},{9,1},{2,10},{10,2},{3,11},{11,3},{4,12},{12,4},... | collective-permute-start | bytes 884744 | tf_op jit(solution)/shard_map/ppermute | solution.py:53
  81.1 2.7 %collective-permute-start.18 = (bf16[8,16,512]{2,1,0:T(8,128)(2,1)S(1)}, bf16[8,16,512]{2,1,0:T(8,128)(2,1)S(1)}, u32[]{:S(2)}, u32[]{:S(2)}) collective-permute-start(bf16[8,16,512]{2,1,0:T(8,128)(2,1)S(1)} %get-tuple-element.91), channel_id=1, source_target_pairs={{0,8},{8,0},{1,9},{9,1},{2,10},{10,2},{3,11},{11,3},{4,12},{12,4},... | collective-permute-start | bytes 393224 | tf_op jit(solution)/shard_map/ppermute | solution.py:53

commit v9 on v8

--- a/solution.py
+++ b/solution.py
@@ -81,9 +81,11 @@
     owner_hbm,
     index_hbm,
     lengths_hbm,
+    state_hbm,
     *refs,
 ):
-    outs, (query, newkv, pages, conv, owners, indexes, lengths, sems) = refs[:nchan], refs[nchan:]
+    outs, (same, cross) = refs[:nchan], refs[nchan : nchan + 2]
+    query, newkv, pages, conv, owners, indexes, lengths, state, sems = refs[nchan + 2 :]
     moves = (
         (pages_hbm, pages),
         (conv_hbm, conv),
@@ -92,6 +94,7 @@
         (owner_hbm, owners),
         (index_hbm, indexes),
         (lengths_hbm, lengths),
+        (state_hbm, state),
     )
     copies = [pltpu.make_async_copy(src, dst, sems.at[i]) for i, (src, dst) in enumerate(moves)]
     for copy in copies:
@@ -102,7 +105,7 @@
     blocks = cols // LANES
     steps = conv.shape[0]
     rep = nchan // KVH
-    for copy in copies[1:]:
+    for copy in copies[1:-1]:
         copy.wait()
     lane = lax.broadcasted_iota(jnp.int32, (1, LANES), 1)
     per_row = LANES // page_tokens
@@ -137,12 +140,7 @@
         values = pl.ds(pl.multiple_of(KVH * HD + at, HD), HD)
         out_ref[0 : lay.tokens, :] = pages[:, :, keys].reshape(lay.tokens, HD)
         out_ref[lay.value : lay.small, :] = pages[:, :, values].reshape(lay.tokens, HD)
-
-
-def load_kernel(residual, state, residual_out, same, cross):
-    c = lax.axis_index("src")
-    nchan, _, cols = same.shape
-    residual_out[...] = residual[...]
+    copies[-1].wait()
     for ref, half in ((same, c), (cross, 1 - c)):
         for d in range(nchan):
             lanes = pl.ds(pl.multiple_of((half * nchan + d) * cols, cols), cols)
@@ -488,11 +486,12 @@
 
     conv_rows = jnp.transpose(conv_state, (1, 0, 2))
     chunk = shape((lay.rows, LANES), BF16)
-    packed = call(
+    cut = shape((nchan, NS, cols), BF16)
+    *packed, same, cross = call(
         functools.partial(pack_kernel, nchan, lay),
-        out_shape=(chunk,) * nchan,
-        in_specs=hbm(7),
-        out_specs=tuple(vmem(nchan)),
+        out_shape=(chunk,) * nchan + (cut, cut),
+        in_specs=hbm(8),
+        out_specs=tuple(vmem(nchan + 2)),
         scratch_shapes=[
             VM(query_heads.shape, BF16),
             VM(new_keyval.shape, BF16),
@@ -501,28 +500,15 @@
             pltpu.SMEM(page_owner.shape, jnp.int32),
             pltpu.SMEM(page_index.shape, jnp.int32),
             pltpu.SMEM(prompt_lengths.shape, jnp.int32),
-            pltpu.SemaphoreType.DMA((7,)),
+            VM(mamba_state.shape, F32),
+            pltpu.SemaphoreType.DMA((8,)),
         ],
         compiler_params=pltpu.CompilerParams(vmem_limit_bytes=64 * 2**20 - 2**18),
         name="pack",
-    )(query_heads, new_keyval, cache_pages, conv_rows, page_owner, page_index, prompt_lengths)
-    *packed, residual_input, mamba_state = lax.optimization_barrier((*packed, residual_input, mamba_state))
+    )(query_heads, new_keyval, cache_pages, conv_rows, page_owner, page_index, prompt_lengths, mamba_state)
     arrived = [packed[0]]
     for k in range(1, nchan):
         arrived.append(lax.ppermute(packed[k], "chan", [(i, i ^ k) for i in range(nchan)]))
-    cut = shape((nchan, NS, cols), BF16)
-    residual, same, cross = call(
-        load_kernel,
-        out_shape=(shape((rows, cols), BF16), cut, cut),
-        in_specs=vmem(2),
-        out_specs=tuple(vmem(3)),
-        compiler_params=params(16),
-        cost_estimate=cost(SHORT, 0),
-        name="load",
-    )(residual_input, mamba_state)
-
-    early = nchan // 4
-    arrived[early], residual, same, cross = lax.optimization_barrier((arrived[early], residual, same, cross))
     other_arrived = [swap(block) for block in arrived]
     pairs = nchan * lay.per
     conv_cut = shape((nchan, round_up(lay.conv_rows, 8), LANES), F32)
@@ -559,7 +545,7 @@
         ],
         compiler_params=params(STREAM_MIB),
         name="out",
-    )(att_own, att_other, residual, cross, out_fetched, out_heads)
+    )(att_own, att_other, residual_input, cross, out_fetched, out_heads)
     half_streamed = [VM((D // 2, cols), BF16), pltpu.SemaphoreType.DMA((nchan,))]
     streamed = [VM((D, cols), BF16), pltpu.SemaphoreType.DMA((2 * nchan,))]
     hid_own = exchange(hid_send)

time: 96 us -> 96.1 us (level)
  transfers between devices with their start and end apart: 20 -> 20, of which waited for: 7 -> 8; matrix products, arithmetic and copies ran while one was open for 0% -> 0% of each run, Pallas kernels for 11% -> 11%
where the time goes in v9:
time: 96.1 us; the launch traced here: 95.6 us
  blocking collectives  35.5 us (37%)
  Pallas kernels  23.5 us (24%)
  starting transfers between devices  18.2 us (19%)
  waiting for transfers between devices  16.4 us (17%)
    all_to_all x3, blocking collectives, exchange(): return lax.all_to_all(x, 'chan', split_axis=0, concat_axis=0, tiled=True)  35.5 us
    ppermute x7, starting transfers between devices, on_device(): lax.ppermute(packed[k], 'chan', [(i, i ^ k) for i in range(nchan)])  12.5 us
    ppermute x7, waiting for transfers between devices, on_device(): lax.ppermute(packed[k], 'chan', [(i, i ^ k) for i in range(nchan)])  7.36 us
    all_to_all x1, waiting for transfers between devices, exchange(): return lax.all_to_all(x, 'chan', split_axis=0, concat_axis=0, tiled=True)  6.29 us
    pallas_call x1, Pallas kernels, on_device(): call(gates_kernel, out_shape=(shape((rows, cols), F32), shape((cols, DOWN...  3.91 us
    all_to_all x1, starting transfers between devices, exchange(): return lax.all_to_all(x, 'chan', split_axis=0, concat_axis=0, tiled=True)  3.63 us
    pallas_call x1, Pallas kernels, on_device(): call(functools.partial(values_kernel, lay), out_shape=(shape((steps, rows...  3.36 us
    pallas_call x1, Pallas kernels, on_device(): call(functools.partial(out_kernel, lay), out_shape=(shape((rows, cols), B...  3.13 us
  transfers between devices with their start and end apart: 20, of which 8 were waited for; matrix products, arithmetic and copies ran while one was open for 0% of the time, Pallas kernels for 11%

profile of v9, /device:TPU:0, one launch (start us, length us, event | category | flops | bytes accessed | tf_op | source)
XLA Modules:
  0.0 95.6 jit_solution(11861017075359326878)
XLA Ops:
  0.6 0.0 copy-start.6
  0.6 2.4 %pack.1 = (bf16[304,128]{1,0:T(8,128)(2,1)}, bf16[304,128]{1,0:T(8,128)(2,1)}, bf16[304,128]{1,0:T(8,128)(2,1)}, bf16[304,128]{1,0:T(8,128)(2,1)}, bf16[304,128]...) custom-call(bf16[1,8192]{1,0:T(2,128)(2,1)} %query_hbm.1, ...), custom_call_target="tpu_custom_call" | custom-call | tf_op jit(solution)/shard_map/pack/pallas_call | solution.py:490
  3.1 0.0 copy-start.3
  3.1 3.0 %collective-permute-start = (bf16[304,128]{1,0:T(8,128)(2,1)}, bf16[304,128]{1,0:T(8,128)(2,1)S(1)}, u32[]{:S(2)}, u32[]{:S(2)}) collective-permute-start(bf16[304,128]{1,0:T(8,128)(2,1)} %get-tuple-element.35), channel_id=1, source_target_pairs={{0,1},{1,0},{2,3},{3,2},{4,5},{5,4},{6,7},{7,6},{8,9},{9,8},{10,11... | collective-permute-start | bytes 233480 | tf_op jit(solution)/shard_map/ppermute | solution.py:511
  6.1 1.6 %collective-permute-start.1 = (bf16[304,128]{1,0:T(8,128)(2,1)}, bf16[304,128]{1,0:T(8,128)(2,1)S(1)}, u32[]{:S(2)}, u32[]{:S(2)}) collective-permute-start(bf16[304,128]{1,0:T(8,128)(2,1)} %get-tuple-element.36), channel_id=1, source_target_pairs={{0,2},{1,3},{2,0},{3,1},{4,6},{5,7},{6,4},{7,5},{8,10},{9,11},{10,... | collective-permute-start | bytes 233480 | tf_op jit(solution)/shard_map/ppermute | solution.py:511
  7.7 0.0 collective-permute-start.2
  7.7 3.0 %collective-permute-start.3 = (bf16[304,128]{1,0:T(8,128)(2,1)}, bf16[304,128]{1,0:T(8,128)(2,1)S(1)}, u32[]{:S(2)}, u32[]{:S(2)}) collective-permute-start(bf16[304,128]{1,0:T(8,128)(2,1)} %get-tuple-element.38), channel_id=1, source_target_pairs={{0,4},{1,5},{2,6},{3,7},{4,0},{5,1},{6,2},{7,3},{8,12},{9,13},{10,... | collective-permute-start | bytes 233480 | tf_op jit(solution)/shard_map/ppermute | solution.py:511
  10.7 1.3 %collective-permute-start.4 = (bf16[304,128]{1,0:T(8,128)(2,1)}, bf16[304,128]{1,0:T(8,128)(2,1)S(1)}, u32[]{:S(2)}, u32[]{:S(2)}) collective-permute-start(bf16[304,128]{1,0:T(8,128)(2,1)} %get-tuple-element.39), channel_id=1, source_target_pairs={{0,5},{1,4},{2,7},{3,6},{4,1},{5,0},{6,3},{7,2},{8,13},{9,12},{10,... | collective-permute-start | bytes 233480 | tf_op jit(solution)/shard_map/ppermute | solution.py:511
  11.9 0.0 collective-permute-done.refs_1_
  11.9 3.6 %collective-permute-start.5 = (bf16[304,128]{1,0:T(8,128)(2,1)}, bf16[304,128]{1,0:T(8,128)(2,1)S(1)}, u32[]{:S(2)}, u32[]{:S(2)}) collective-permute-start(bf16[304,128]{1,0:T(8,128)(2,1)} %get-tuple-element.40), channel_id=1, source_target_pairs={{0,6},{1,7},{2,4},{3,5},{4,2},{5,3},{6,0},{7,1},{8,14},{9,15},{10,... | collective-permute-start | bytes 233480 | tf_op jit(solution)/shard_map/ppermute | solution.py:511
  15.6 0.0 collective-permute-done.1.refs_2_
  15.6 0.0 collective-permute-start.6
  15.6 0.0 collective-permute-done.2.refs_3_
  15.6 0.1 collective-permute-start.7
  15.6 0.0 collective-permute-done.3.refs_4_
  15.7 0.5 collective-permute-start.8
  16.1 7.3 %collective-permute-done.4.refs_5_ = bf16[304,128]{1,0:T(8,128)(2,1)S(1)} collective-permute-done((bf16[304,128]{1,0:T(8,128)(2,1)}, bf16[304,128]{1,0:T(8,128)(2,1)S(1)}, u32[]{:S(2)}, u32[]{:S(2)}) %collective-permute-start.4) | collective-permute-done | bytes 77856 | tf_op jit(solution)/shard_map/ppermute | solution.py:511
  23.5 0.0 collective-permute-start.9
  23.5 0.0 collective-permute-done.5.refs_6_
  23.5 0.5 collective-permute-start.10
  24.0 0.0 collective-permute-done.6.refs_7_
  24.0 0.1 collective-permute-start.11
  24.1 0.0 collective-permute-done.7.refs_8_
  24.1 0.4 collective-permute-start.12
  24.5 0.0 collective-permute-done.8.refs_9_
  24.5 0.1 collective-permute-start.13
  24.6 0.2 collective-permute-done.9.refs_10_
  24.8 0.3 collective-permute-start.14
  25.0 0.0 collective-permute-done.10.refs_11_
  25.0 0.2 collective-permute-done.11.refs_12_
  25.3 0.2 collective-permute-done.12.refs_13_
  25.4 0.4 collective-permute-done.13.refs_14_
  25.8 0.2 collective-permute-done.14.refs_15_
  26.0 0.9 copy-done.4
  26.9 1.1 %attend.1 = (bf16[8,64,128]{2,1,0:T(8,128)(2,1)S(1)}, f32[8,16,128]{2,1,0:T(8,128)S(1)}, f32[8,16,128]{2,1,0:T(8,128)S(1)}) custom-call(bf16[304,128]{1,0:T(8,128)(2,1)S(1)} %copy-done.4, bf16[304,128]{1,0:T(8,128)(2,1)S(1)} %collective-permute-done.refs_1_, bf16[304,128]{1,0:T(8,128)(2,1)S(1)} %collective-permute-done.1.refs_2_, ...), custom_call_target="tpu_custom_call" | custom-call | tf_op jit(solution)/shard_map/attend/pallas_call | solution.py:515
  28.0 12.2 %all_to_all.20.own = bf16[8,64,128]{2,1,0:T(8,128)(2,1)S(1)} all-to-all(bf16[8,64,128]{2,1,0:T(8,128)(2,1)S(1)} %get-tuple-element.42), channel_id=1, replica_groups=mesh['groups'=2,'src'=2,'chan'=8] {'chan'}, dimensions={0} | all-to-all | bytes 262144 | tf_op jit(solution)/shard_map/all_to_all | solution.py:57
  40.2 0.0 collective-permute-start.15
  40.2 1.5 %fetch.1.fetched = bf16[2048,512]{1,0:T(8,128)(2,1)S(1)} custom-call(bf16[8192,512]{1,0:T(8,128)(2,1)} %weight.7), custom_call_target="tpu_custom_call" | custom-call | flops 3000000000 | tf_op jit(solution)/shard_map/fetch/pallas_call | solution.py:527
  41.8 0.0 collective-permute-done.15.other
  41.8 3.1 %out.1 = (bf16[16,512]{1,0:T(8,128)(2,1)S(1)}, bf16[8,32,512]{2,1,0:T(8,128)(2,1)S(1)}) custom-call(bf16[8,64,128]{2,1,0:T(8,128)(2,1)S(1)} %all_to_all.20.own, bf16[8,64,128]{2,1,0:T(8,128)(2,1)S(1)} %collective-permute-done.15.other, bf16[16,512]{1,0:T(8,128)(2,1)S(1)} %copy-done.6, bf16[8,16,512]{2,1,0:T(8,128)(2,1)S(1)} %copy-done.3, ...), custom_call_target="tpu_custom_call" | custom-call | tf_op jit(solution)/shard_map/out/pallas_call | solution.py:537
  44.9 0.0 copy-start
  44.9 0.0 copy-start.2
  45.0 0.0 copy-start.7
  45.0 0.0 copy-start.8
  45.0 12.4 %all_to_all.21.lhs.own = bf16[8,32,512]{2,1,0:T(8,128)(2,1)S(1)} all-to-all(bf16[8,32,512]{2,1,0:T(8,128)(2,1)S(1)} %get-tuple-element.46), channel_id=1, replica_groups=mesh['groups'=2,'src'=2,'chan'=8] {'chan'}, dimensions={0} | all-to-all | bytes 524288 | tf_op jit(solution)/shard_map/all_to_all | solution.py:57
  57.4 0.0 collective-permute-start.16
  57.4 2.4 %values_own.1.partial = f32[16,512]{1,0:T(8,128)S(1)} custom-call(bf16[8,32,512]{2,1,0:T(8,128)(2,1)S(1)} %all_to_all.21.lhs.own, bf16[8192,512]{1,0:T(8,128)(2,1)} %weight.9), custom_call_target="tpu_custom_call" | custom-call | flops 3000000000 | tf_op jit(solution)/shard_map/values_own/pallas_call | solution.py:553
  59.8 0.0 collective-permute-done.16.other.hid_other
  59.9 3.4 %values.1 = (f32[3,16,512]{2,1,0:T(8,128)}, f32[16,512]{1,0:T(8,128)S(1)}, f32[16,128]{1,0:T(8,128)S(1)}, bf16[8,144,128]{2,1,0:T(8,128)(2,1)}) custom-call(bf16[8,32,512]{2,1,0:T(8,128)(2,1)S(1)} %all_to_all.21.lhs.own, bf16[8,32,512]{2,1,0:T(8,128)(2,1)S(1)} %collective-permute-done.16.other.hid_other, f32[8,16,128]{2,1,0:T(8,128)S(1)} %get-tuple-element.47.own_conv, ...), custom_call_target="tpu_custom_call" | custom-call | tf_op jit(solution)/shard_map/values/pallas_call | solution.py:565
  63.2 3.6 %all-to-all-start.2 = ((bf16[8,144,128]{2,1,0:T(8,128)(2,1)}), bf16[8,144,128]{2,1,0:T(8,128)(2,1)S(1)}, u32[]{:S(2)}, u32[]{:S(2)}) async-start(bf16[8,144,128]{2,1,0:T(8,128)(2,1)} %get-tuple-element.51), calls=%async_computation.2 | async-start | bytes 589824 | tf_op jit(solution)/shard_map/all_to_all | solution.py:57
  66.9 0.0 copy-start.5
  66.9 0.0 copy-start.9
  66.9 0.0 copy-start.10
  66.9 3.9 %gates.1 = (f32[16,512]{1,0:T(8,128)S(1)}, bf16[512,1024]{1,0:T(8,128)(2,1)S(1)}) custom-call(bf16[8,32,512]{2,1,0:T(8,128)(2,1)S(1)} %all_to_all.21.lhs.own, bf16[8,32,512]{2,1,0:T(8,128)(2,1)S(1)} %collective-permute-done.16.other.hid_other, f32[16,128]{1,0:T(8,128)S(1)} %get-tuple-element.52.rms, bf16[8192,512]{1,0:T(8,128)(2,1)} %weight.10, ...), custom_call_target="tpu_custom_call" | custom-call | flops 3000000000 | tf_op jit(solution)/shard_map/gates/pallas_call | solution.py:583
  70.8 6.3 %all-to-all-done.2.own = bf16[8,144,128]{2,1,0:T(8,128)(2,1)S(1)} async-done(((bf16[8,144,128]{2,1,0:T(8,128)(2,1)}), bf16[8,144,128]{2,1,0:T(8,128)(2,1)S(1)}, u32[]{:S(2)}, u32[]{:S(2)}) %all-to-all-start.2) | async-done | bytes 294944 | tf_op jit(solution)/shard_map/all_to_all | solution.py:57
  77.1 0.0 collective-permute-start.17
  77.1 1.6 %collective-permute-done.17.other = bf16[8,144,128]{2,1,0:T(8,128)(2,1)S(1)} collective-permute-done((bf16[8,144,128]{2,1,0:T(8,128)(2,1)S(1)}, bf16[8,144,128]{2,1,0:T(8,128)(2,1)S(1)}, u32[]{:S(2)}, u32[]{:S(2)}) %collective-permute-start.17) | collective-permute-done | bytes 294944 | tf_op jit(solution)/shard_map/ppermute | solution.py:53
  78.7 0.0 copy-done.10
  78.7 2.5 %scan.1 = (f32[16,16,512]{2,1,0:T(8,128)}, bf16[16,512]{1,0:T(8,128)(2,1)S(1)}, bf16[8,16,512]{2,1,0:T(8,128)(2,1)S(1)}) custom-call(bf16[8,144,128]{2,1,0:T(8,128)(2,1)S(1)} %all-to-all-done.2.own, bf16[8,144,128]{2,1,0:T(8,128)(2,1)S(1)} %collective-permute-done.17.other, bf16[8,32,512]{2,1,0:T(8,128)(2,1)S(1)} %collective-permute-done.16.other.hid_other, ...), custom_call_target="tpu_custom_call" | custom-call | tf_op jit(solution)/shard_map/scan/pallas_call | solution.py:602
  81.3 0.2 collective-permute-start.18
  81.5 2.5 %down.1 = f32[8,16,512]{2,1,0:T(8,128)S(1)} custom-call(bf16[16,512]{1,0:T(8,128)(2,1)S(1)} %get-tuple-element.60.gated, bf16[512,8192]{1,0:T(8,128)(2,1)} %weight.12), custom_call_target="tpu_custom_call" | custom-call | flops 3000000000 | tf_op jit(solution)/shard_map/down/pallas_call | solution.py:628
  84.0 0.0 collective-permute-done.18
  84.0 10.9 %all_to_all.22.final = bf16[8,16,512]{2,1,0:T(8,128)(2,1)S(1)} all-to-all(bf16[8,16,512]{2,1,0:T(8,128)(2,1)S(1)} %add_convert_fusion), channel_id=1, replica_groups=mesh['groups'=2,'src'=2,'chan'=8] {'chan'}, dimensions={0} | all-to-all | bytes 262144 | tf_op jit(solution)/shard_map/all_to_all | solution.py:57
  94.9 0.6 finish.1
  (12 shorter events, 0.1 us)
Async XLA Ops:
  0.6 41.1 %copy-start.6 = (bf16[16,512]{1,0:T(8,128)(2,1)S(1)}, bf16[16,512]{1,0:T(8,128)(2,1)}, u32[]{:S(2)}) copy-start(bf16[16,512]{1,0:T(8,128)(2,1)} %residual.1) | copy-start | bytes 49156
  3.1 38.7 %copy-start.3 = (bf16[8,16,512]{2,1,0:T(8,128)(2,1)S(1)}, bf16[8,16,512]{2,1,0:T(8,128)(2,1)}, u32[]{:S(2)}) copy-start(bf16[8,16,512]{2,1,0:T(8,128)(2,1)} %get-tuple-element.44.cross) | copy-start | bytes 393220
  3.1 8.9 %collective-permute-start = (bf16[304,128]{1,0:T(8,128)(2,1)}, bf16[304,128]{1,0:T(8,128)(2,1)S(1)}, u32[]{:S(2)}, u32[]{:S(2)}) collective-permute-start(bf16[304,128]{1,0:T(8,128)(2,1)} %get-tuple-element.35), channel_id=1, source_target_pairs={{0,1},{1,0},{2,3},{3,2},{4,5},{5,4},{6,7},{7,6},{8,9},{9,8},{10,11... | collective-permute-start | bytes 233480 | tf_op jit(solution)/shard_map/ppermute | solution.py:511
  6.1 9.5 %collective-permute-start.1 = (bf16[304,128]{1,0:T(8,128)(2,1)}, bf16[304,128]{1,0:T(8,128)(2,1)S(1)}, u32[]{:S(2)}, u32[]{:S(2)}) collective-permute-start(bf16[304,128]{1,0:T(8,128)(2,1)} %get-tuple-element.36), channel_id=1, source_target_pairs={{0,2},{1,3},{2,0},{3,1},{4,6},{5,7},{6,4},{7,5},{8,10},{9,11},{10,... | collective-permute-start | bytes 233480 | tf_op jit(solution)/shard_map/ppermute | solution.py:511
  7.7 7.9 %collective-permute-start.2 = (bf16[304,128]{1,0:T(8,128)(2,1)}, bf16[304,128]{1,0:T(8,128)(2,1)S(1)}, u32[]{:S(2)}, u32[]{:S(2)}) collective-permute-start(bf16[304,128]{1,0:T(8,128)(2,1)} %get-tuple-element.37), channel_id=1, source_target_pairs={{0,3},{1,2},{2,1},{3,0},{4,7},{5,6},{6,5},{7,4},{8,11},{9,10},{10,... | collective-permute-start | bytes 233480 | tf_op jit(solution)/shard_map/ppermute | solution.py:511
  7.7 8.0 %collective-permute-start.3 = (bf16[304,128]{1,0:T(8,128)(2,1)}, bf16[304,128]{1,0:T(8,128)(2,1)S(1)}, u32[]{:S(2)}, u32[]{:S(2)}) collective-permute-start(bf16[304,128]{1,0:T(8,128)(2,1)} %get-tuple-element.38), channel_id=1, source_target_pairs={{0,4},{1,5},{2,6},{3,7},{4,0},{5,1},{6,2},{7,3},{8,12},{9,13},{10,... | collective-permute-start | bytes 233480 | tf_op jit(solution)/shard_map/ppermute | solution.py:511
  10.7 12.8 %collective-permute-start.4 = (bf16[304,128]{1,0:T(8,128)(2,1)}, bf16[304,128]{1,0:T(8,128)(2,1)S(1)}, u32[]{:S(2)}, u32[]{:S(2)}) collective-permute-start(bf16[304,128]{1,0:T(8,128)(2,1)} %get-tuple-element.39), channel_id=1, source_target_pairs={{0,5},{1,4},{2,7},{3,6},{4,1},{5,0},{6,3},{7,2},{8,13},{9,12},{10,... | collective-permute-start | bytes 233480 | tf_op jit(solution)/shard_map/ppermute | solution.py:511
  11.9 11.5 %collective-permute-start.5 = (bf16[304,128]{1,0:T(8,128)(2,1)}, bf16[304,128]{1,0:T(8,128)(2,1)S(1)}, u32[]{:S(2)}, u32[]{:S(2)}) collective-permute-start(bf16[304,128]{1,0:T(8,128)(2,1)} %get-tuple-element.40), channel_id=1, source_target_pairs={{0,6},{1,7},{2,4},{3,5},{4,2},{5,3},{6,0},{7,1},{8,14},{9,15},{10,... | collective-permute-start | bytes 233480 | tf_op jit(solution)/shard_map/ppermute | solution.py:511
  15.6 8.4 %collective-permute-start.6 = (bf16[304,128]{1,0:T(8,128)(2,1)}, bf16[304,128]{1,0:T(8,128)(2,1)S(1)}, u32[]{:S(2)}, u32[]{:S(2)}) collective-permute-start(bf16[304,128]{1,0:T(8,128)(2,1)} %get-tuple-element.41), channel_id=1, source_target_pairs={{0,7},{1,6},{2,5},{3,4},{4,3},{5,2},{6,1},{7,0},{8,15},{9,14},{10,... | collective-permute-start | bytes 233480 | tf_op jit(solution)/shard_map/ppermute | solution.py:511
  15.6 8.5 %collective-permute-start.7 = (bf16[304,128]{1,0:T(8,128)(2,1)}, bf16[304,128]{1,0:T(8,128)(2,1)S(1)}, u32[]{:S(2)}, u32[]{:S(2)}) collective-permute-start(bf16[304,128]{1,0:T(8,128)(2,1)} %get-tuple-element.34.refs_0_), channel_id=1, source_target_pairs={{0,8},{8,0},{1,9},{9,1},{2,10},{10,2},{3,11},{11,3},{4,12},{12,4},... | collective-permute-start | bytes 233480 | tf_op jit(solution)/shard_map/ppermute | solution.py:53
  15.7 8.9 %collective-permute-start.8 = (bf16[304,128]{1,0:T(8,128)(2,1)S(1)}, bf16[304,128]{1,0:T(8,128)(2,1)S(1)}, u32[]{:S(2)}, u32[]{:S(2)}) collective-permute-start(bf16[304,128]{1,0:T(8,128)(2,1)S(1)} %collective-permute-done.refs_1_), channel_id=1, source_target_pairs={{0,8},{8,0},{1,9},{9,1},{2,10},{10,2},{3,11},{11,3},{4,12},{12,4},... | collective-permute-start | bytes 233480 | tf_op jit(solution)/shard_map/ppermute | solution.py:53
  23.5 1.3 %collective-permute-start.9 = (bf16[304,128]{1,0:T(8,128)(2,1)S(1)}, bf16[304,128]{1,0:T(8,128)(2,1)S(1)}, u32[]{:S(2)}, u32[]{:S(2)}) collective-permute-start(bf16[304,128]{1,0:T(8,128)(2,1)S(1)} %collective-permute-done.1.refs_2_), channel_id=1, source_target_pairs={{0,8},{8,0},{1,9},{9,1},{2,10},{10,2},{3,11},{11,3},{4,12},{12,4},... | collective-permute-start | bytes 233480 | tf_op jit(solution)/shard_map/ppermute | solution.py:53
  23.5 1.5 %collective-permute-start.10 = (bf16[304,128]{1,0:T(8,128)(2,1)S(1)}, bf16[304,128]{1,0:T(8,128)(2,1)S(1)}, u32[]{:S(2)}, u32[]{:S(2)}) collective-permute-start(bf16[304,128]{1,0:T(8,128)(2,1)S(1)} %collective-permute-done.2.refs_3_), channel_id=1, source_target_pairs={{0,8},{8,0},{1,9},{9,1},{2,10},{10,2},{3,11},{11,3},{4,12},{12,4},... | collective-permute-start | bytes 233480 | tf_op jit(solution)/shard_map/ppermute | solution.py:53
  24.0 1.3 %collective-permute-start.11 = (bf16[304,128]{1,0:T(8,128)(2,1)S(1)}, bf16[304,128]{1,0:T(8,128)(2,1)S(1)}, u32[]{:S(2)}, u32[]{:S(2)}) collective-permute-start(bf16[304,128]{1,0:T(8,128)(2,1)S(1)} %collective-permute-done.3.refs_4_), channel_id=1, source_target_pairs={{0,8},{8,0},{1,9},{9,1},{2,10},{10,2},{3,11},{11,3},{4,12},{12,4},... | collective-permute-start | bytes 233480 | tf_op jit(solution)/shard_map/ppermute | solution.py:53
  24.1 1.4 %collective-permute-start.12 = (bf16[304,128]{1,0:T(8,128)(2,1)S(1)}, bf16[304,128]{1,0:T(8,128)(2,1)S(1)}, u32[]{:S(2)}, u32[]{:S(2)}) collective-permute-start(bf16[304,128]{1,0:T(8,128)(2,1)S(1)} %collective-permute-done.4.refs_5_), channel_id=1, source_target_pairs={{0,8},{8,0},{1,9},{9,1},{2,10},{10,2},{3,11},{11,3},{4,12},{12,4},... | collective-permute-start | bytes 233480 | tf_op jit(solution)/shard_map/ppermute | solution.py:53
  24.5 1.3 %collective-permute-start.13 = (bf16[304,128]{1,0:T(8,128)(2,1)S(1)}, bf16[304,128]{1,0:T(8,128)(2,1)S(1)}, u32[]{:S(2)}, u32[]{:S(2)}) collective-permute-start(bf16[304,128]{1,0:T(8,128)(2,1)S(1)} %collective-permute-done.5.refs_6_), channel_id=1, source_target_pairs={{0,8},{8,0},{1,9},{9,1},{2,10},{10,2},{3,11},{11,3},{4,12},{12,4},... | collective-permute-start | bytes 233480 | tf_op jit(solution)/shard_map/ppermute | solution.py:53
  24.8 1.3 %collective-permute-start.14 = (bf16[304,128]{1,0:T(8,128)(2,1)S(1)}, bf16[304,128]{1,0:T(8,128)(2,1)S(1)}, u32[]{:S(2)}, u32[]{:S(2)}) collective-permute-start(bf16[304,128]{1,0:T(8,128)(2,1)S(1)} %collective-permute-done.6.refs_7_), channel_id=1, source_target_pairs={{0,8},{8,0},{1,9},{9,1},{2,10},{10,2},{3,11},{11,3},{4,12},{12,4},... | collective-permute-start | bytes 233480 | tf_op jit(solution)/shard_map/ppermute | solution.py:53
  26.0 0.9 copy-start.4
  40.2 1.6 %collective-permute-start.15 = (bf16[8,64,128]{2,1,0:T(8,128)(2,1)S(1)}, bf16[8,64,128]{2,1,0:T(8,128)(2,1)S(1)}, u32[]{:S(2)}, u32[]{:S(2)}) collective-permute-start(bf16[8,64,128]{2,1,0:T(8,128)(2,1)S(1)} %all_to_all.20.own), channel_id=1, source_target_pairs={{0,8},{8,0},{1,9},{9,1},{2,10},{10,2},{3,11},{11,3},{4,12},{12,4},... | collective-permute-start | bytes 393224 | tf_op jit(solution)/shard_map/ppermute | solution.py:53
  44.9 14.9 %copy-start = (bf16[512,544]{0,1:T(8,128)(2,1)S(1)}, bf16[512,544]{0,1:T(8,128)(2,1)}, u32[]{:S(2)}) copy-start(bf16[512,544]{0,1:T(8,128)(2,1)} %param.34) | copy-start | bytes 1671172
  44.9 14.9 %copy-start.2 = (bf16[8,16,512]{2,1,0:T(8,128)(2,1)S(1)}, bf16[8,16,512]{2,1,0:T(8,128)(2,1)}, u32[]{:S(2)}) copy-start(bf16[8,16,512]{2,1,0:T(8,128)(2,1)} %get-tuple-element.49.same) | copy-start | bytes 393220
  45.0 14.9 %copy-start.7 = (f32[4,512]{1,0:T(4,128)S(1)}, f32[4,512]{1,0:T(4,128)}, u32[]{:S(2)}) copy-start(f32[4,512]{1,0:T(4,128)} %taps.1) | copy-start | bytes 24580
  45.0 14.9 %copy-start.8 = (f32[512]{0:T(512)S(1)}, f32[512]{0:T(512)}, u32[]{:S(2)}) copy-start(f32[512]{0:T(512)} %param.33) | copy-start | bytes 6148
  57.4 2.4 %collective-permute-start.16 = (bf16[8,32,512]{2,1,0:T(8,128)(2,1)S(1)}, bf16[8,32,512]{2,1,0:T(8,128)(2,1)S(1)}, u32[]{:S(2)}, u32[]{:S(2)}) collective-permute-start(bf16[8,32,512]{2,1,0:T(8,128)(2,1)S(1)} %all_to_all.21.lhs.own), channel_id=1, source_target_pairs={{0,8},{8,0},{1,9},{9,1},{2,10},{10,2},{3,11},{11,3},{4,12},{12,4},... | collective-permute-start | bytes 786440 | tf_op jit(solution)/shard_map/ppermute | solution.py:53
  63.2 13.9 %all-to-all-start.2 = ((bf16[8,144,128]{2,1,0:T(8,128)(2,1)}), bf16[8,144,128]{2,1,0:T(8,128)(2,1)S(1)}, u32[]{:S(2)}, u32[]{:S(2)}) async-start(bf16[8,144,128]{2,1,0:T(8,128)(2,1)} %get-tuple-element.51), calls=%async_computation.2 | async-start | bytes 589824 | tf_op jit(solution)/shard_map/all_to_all | solution.py:57
  66.9 11.8 %copy-start.1 = (bf16[512,512]{1,0:T(8,128)(2,1)S(1)}, bf16[512,512]{1,0:T(8,128)(2,1)}, u32[]{:S(2)}) copy-start(bf16[512,512]{1,0:T(8,128)(2,1)} %step_proj.1) | copy-start | bytes 1572868
  66.9 11.8 %copy-start.5 = (f32[16,512]{1,0:T(8,128)S(1)}, f32[16,512]{1,0:T(8,128)}, u32[]{:S(2)}) copy-start(f32[16,512]{1,0:T(8,128)} %decay_log.1) | copy-start | bytes 98308
  66.9 11.8 %copy-start.9 = (f32[512]{0:T(512)S(1)}, f32[512]{0:T(512)}, u32[]{:S(2)}) copy-start(f32[512]{0:T(512)} %param.36) | copy-start | bytes 6148
  66.9 11.8 %copy-start.10 = (f32[512]{0:T(512)S(1)}, f32[512]{0:T(512)}, u32[]{:S(2)}) copy-start(f32[512]{0:T(512)} %param.38) | copy-start | bytes 6148
  77.1 1.6 %collective-permute-start.17 = (bf16[8,144,128]{2,1,0:T(8,128)(2,1)S(1)}, bf16[8,144,128]{2,1,0:T(8,128)(2,1)S(1)}, u32[]{:S(2)}, u32[]{:S(2)}) collective-permute-start(bf16[8,144,128]{2,1,0:T(8,128)(2,1)S(1)} %all-to-all-done.2.own), channel_id=1, source_target_pairs={{0,8},{8,0},{1,9},{9,1},{2,10},{10,2},{3,11},{11,3},{4,12},{12,4},... | collective-permute-start | bytes 884744 | tf_op jit(solution)/shard_map/ppermute | solution.py:53
  81.3 2.7 %collective-permute-start.18 = (bf16[8,16,512]{2,1,0:T(8,128)(2,1)S(1)}, bf16[8,16,512]{2,1,0:T(8,128)(2,1)S(1)}, u32[]{:S(2)}, u32[]{:S(2)}) collective-permute-start(bf16[8,16,512]{2,1,0:T(8,128)(2,1)S(1)} %get-tuple-element.61), channel_id=1, source_target_pairs={{0,8},{8,0},{1,9},{9,1},{2,10},{10,2},{3,11},{11,3},{4,12},{12,4},... | collective-permute-start | bytes 393224 | tf_op jit(solution)/shard_map/ppermute | solution.py:53

commit v10 on v9

--- a/solution.py
+++ b/solution.py
@@ -510,6 +510,7 @@
     for k in range(1, nchan):
         arrived.append(lax.ppermute(packed[k], "chan", [(i, i ^ k) for i in range(nchan)]))
     other_arrived = [swap(block) for block in arrived]
+    arrived[0] = swap(other_arrived[0])
     pairs = nchan * lay.per
     conv_cut = shape((nchan, round_up(lay.conv_rows, 8), LANES), F32)
     attended, conv_own, conv_other = call(

time: 96.1 us -> 95.9 us (level)
    ppermute x12 -> x13, starting transfers between devices: 2.13 us -> 2.64 us  [swap(): return lax.ppermute(x, 'src', [(0, 1), (1, 0)])]
    ppermute x12 -> x13, waiting for transfers between devices: 2.75 us -> 2.75 us  [swap(): return lax.ppermute(x, 'src', [(0, 1), (1, 0)])]
  transfers between devices with their start and end apart: 20 -> 21, of which waited for: 8 -> 8; matrix products, arithmetic and copies ran while one was open for 0% -> 0% of each run, Pallas kernels for 11% -> 11%
where the time goes in v10:
time: 95.9 us; the launch traced here: 95.4 us
  blocking collectives  36.3 us (38%)
  Pallas kernels  23.5 us (25%)
  starting transfers between devices  18.3 us (19%)
  waiting for transfers between devices  16.3 us (17%)
    all_to_all x3, blocking collectives, exchange(): return lax.all_to_all(x, 'chan', split_axis=0, concat_axis=0, tiled=True)  36.3 us
    ppermute x7, starting transfers between devices, on_device(): lax.ppermute(packed[k], 'chan', [(i, i ^ k) for i in range(nchan)])  12.1 us
    ppermute x7, waiting for transfers between devices, on_device(): lax.ppermute(packed[k], 'chan', [(i, i ^ k) for i in range(nchan)])  7.22 us
    all_to_all x1, waiting for transfers between devices, exchange(): return lax.all_to_all(x, 'chan', split_axis=0, concat_axis=0, tiled=True)  6.29 us
    pallas_call x1, Pallas kernels, on_device(): call(gates_kernel, out_shape=(shape((rows, cols), F32), shape((cols, DOWN...  3.91 us
    all_to_all x1, starting transfers between devices, exchange(): return lax.all_to_all(x, 'chan', split_axis=0, concat_axis=0, tiled=True)  3.63 us
    pallas_call x1, Pallas kernels, on_device(): call(functools.partial(values_kernel, lay), out_shape=(shape((steps, rows...  3.36 us
    pallas_call x1, Pallas kernels, on_device(): call(functools.partial(out_kernel, lay), out_shape=(shape((rows, cols), B...  3.13 us
  transfers between devices with their start and end apart: 21, of which 8 were waited for; matrix products, arithmetic and copies ran while one was open for 0% of the time, Pallas kernels for 11%

profile of v10, /device:TPU:0, one launch (start us, length us, event | category | flops | bytes accessed | tf_op | source)
XLA Modules:
  0.0 95.4 jit_solution(3480730989007842227)
XLA Ops:
  0.6 2.4 %pack.1 = (bf16[304,128]{1,0:T(8,128)(2,1)}, bf16[304,128]{1,0:T(8,128)(2,1)}, bf16[304,128]{1,0:T(8,128)(2,1)}, bf16[304,128]{1,0:T(8,128)(2,1)}, bf16[304,128]...) custom-call(bf16[1,8192]{1,0:T(2,128)(2,1)} %query_hbm.1, ...), custom_call_target="tpu_custom_call" | custom-call | tf_op jit(solution)/shard_map/pack/pallas_call | solution.py:490
  3.1 0.5 collective-permute-start
  3.6 2.6 %collective-permute-start.2 = (bf16[304,128]{1,0:T(8,128)(2,1)}, bf16[304,128]{1,0:T(8,128)(2,1)S(1)}, u32[]{:S(2)}, u32[]{:S(2)}) collective-permute-start(bf16[304,128]{1,0:T(8,128)(2,1)} %get-tuple-element.35), channel_id=1, source_target_pairs={{0,1},{1,0},{2,3},{3,2},{4,5},{5,4},{6,7},{7,6},{8,9},{9,8},{10,11... | collective-permute-start | bytes 233480 | tf_op jit(solution)/shard_map/ppermute | solution.py:511
  6.2 1.6 %collective-permute-start.3 = (bf16[304,128]{1,0:T(8,128)(2,1)}, bf16[304,128]{1,0:T(8,128)(2,1)S(1)}, u32[]{:S(2)}, u32[]{:S(2)}) collective-permute-start(bf16[304,128]{1,0:T(8,128)(2,1)} %get-tuple-element.36), channel_id=1, source_target_pairs={{0,2},{1,3},{2,0},{3,1},{4,6},{5,7},{6,4},{7,5},{8,10},{9,11},{10,... | collective-permute-start | bytes 233480 | tf_op jit(solution)/shard_map/ppermute | solution.py:511
  7.8 0.0 collective-permute-start.4
  7.8 3.0 %collective-permute-start.5 = (bf16[304,128]{1,0:T(8,128)(2,1)}, bf16[304,128]{1,0:T(8,128)(2,1)S(1)}, u32[]{:S(2)}, u32[]{:S(2)}) collective-permute-start(bf16[304,128]{1,0:T(8,128)(2,1)} %get-tuple-element.38), channel_id=1, source_target_pairs={{0,4},{1,5},{2,6},{3,7},{4,0},{5,1},{6,2},{7,3},{8,12},{9,13},{10,... | collective-permute-start | bytes 233480 | tf_op jit(solution)/shard_map/ppermute | solution.py:511
  10.7 0.0 collective-permute-done.refs_8_
  10.7 1.3 %collective-permute-start.6 = (bf16[304,128]{1,0:T(8,128)(2,1)}, bf16[304,128]{1,0:T(8,128)(2,1)S(1)}, u32[]{:S(2)}, u32[]{:S(2)}) collective-permute-start(bf16[304,128]{1,0:T(8,128)(2,1)} %get-tuple-element.39), channel_id=1, source_target_pairs={{0,5},{1,4},{2,7},{3,6},{4,1},{5,0},{6,3},{7,2},{8,13},{9,12},{10,... | collective-permute-start | bytes 233480 | tf_op jit(solution)/shard_map/ppermute | solution.py:511
  12.0 0.0 collective-permute-done.2.refs_1_
  12.0 3.6 %collective-permute-start.7 = (bf16[304,128]{1,0:T(8,128)(2,1)}, bf16[304,128]{1,0:T(8,128)(2,1)S(1)}, u32[]{:S(2)}, u32[]{:S(2)}) collective-permute-start(bf16[304,128]{1,0:T(8,128)(2,1)} %get-tuple-element.40), channel_id=1, source_target_pairs={{0,6},{1,7},{2,4},{3,5},{4,2},{5,3},{6,0},{7,1},{8,14},{9,15},{10,... | collective-permute-start | bytes 233480 | tf_op jit(solution)/shard_map/ppermute | solution.py:511
  15.6 0.0 collective-permute-done.3.refs_2_
  15.6 0.0 collective-permute-start.8
  15.7 0.0 collective-permute-done.4.refs_3_
  15.7 0.1 collective-permute-start.1
  15.7 0.0 collective-permute-done.5.refs_4_
  15.7 0.5 collective-permute-start.9
  16.2 7.2 %collective-permute-done.6.refs_5_ = bf16[304,128]{1,0:T(8,128)(2,1)S(1)} collective-permute-done((bf16[304,128]{1,0:T(8,128)(2,1)}, bf16[304,128]{1,0:T(8,128)(2,1)S(1)}, u32[]{:S(2)}, u32[]{:S(2)}) %collective-permute-start.6) | collective-permute-done | bytes 77856 | tf_op jit(solution)/shard_map/ppermute | solution.py:511
  23.4 0.0 collective-permute-start.10
  23.4 0.0 collective-permute-done.7.refs_6_
  23.4 0.5 collective-permute-start.11
  23.9 0.0 collective-permute-done.8.refs_7_
  24.0 0.1 collective-permute-start.12
  24.0 0.0 collective-permute-done.1.refs_0_
  24.0 0.4 collective-permute-start.13
  24.5 0.0 collective-permute-done.9.refs_9_
  24.5 0.1 collective-permute-start.14
  24.5 0.2 collective-permute-done.10.refs_10_
  24.7 0.3 collective-permute-start.15
  25.0 0.0 collective-permute-done.11.refs_11_
  25.0 0.2 collective-permute-done.12.refs_12_
  25.2 0.2 collective-permute-done.13.refs_13_
  25.4 0.4 collective-permute-done.14.refs_14_
  25.7 0.2 collective-permute-done.15.refs_15_
  26.0 1.1 %attend.1 = (bf16[8,64,128]{2,1,0:T(8,128)(2,1)S(1)}, f32[8,16,128]{2,1,0:T(8,128)S(1)}, f32[8,16,128]{2,1,0:T(8,128)S(1)}) custom-call(bf16[304,128]{1,0:T(8,128)(2,1)S(1)} %collective-permute-done.1.refs_0_, bf16[304,128]{1,0:T(8,128)(2,1)S(1)} %collective-permute-done.2.refs_1_, bf16[304,128]{1,0:T(8,128)(2,1)S(1)} %collective-permute-done.3.refs_2_, ...), custom_call_target="tpu_custom_call" | custom-call | tf_op jit(solution)/shard_map/attend/pallas_call | solution.py:516
  27.1 12.9 %all_to_all.20.own = bf16[8,64,128]{2,1,0:T(8,128)(2,1)S(1)} all-to-all(bf16[8,64,128]{2,1,0:T(8,128)(2,1)S(1)} %get-tuple-element.42), channel_id=1, replica_groups=mesh['groups'=2,'src'=2,'chan'=8] {'chan'}, dimensions={0} | all-to-all | bytes 262144 | tf_op jit(solution)/shard_map/all_to_all | solution.py:57
  40.0 0.0 collective-permute-start.16
  40.0 1.5 %fetch.1.fetched = bf16[2048,512]{1,0:T(8,128)(2,1)S(1)} custom-call(bf16[8192,512]{1,0:T(8,128)(2,1)} %weight.7), custom_call_target="tpu_custom_call" | custom-call | flops 3000000000 | tf_op jit(solution)/shard_map/fetch/pallas_call | solution.py:528
  41.6 0.0 collective-permute-done.16.other
  41.6 3.1 %out.1 = (bf16[16,512]{1,0:T(8,128)(2,1)S(1)}, bf16[8,32,512]{2,1,0:T(8,128)(2,1)S(1)}) custom-call(bf16[8,64,128]{2,1,0:T(8,128)(2,1)S(1)} %all_to_all.20.own, bf16[8,64,128]{2,1,0:T(8,128)(2,1)S(1)} %collective-permute-done.16.other, bf16[16,512]{1,0:T(8,128)(2,1)S(1)} %copy-done.5, bf16[8,16,512]{2,1,0:T(8,128)(2,1)S(1)} %copy-done.3, ...), custom_call_target="tpu_custom_call" | custom-call | tf_op jit(solution)/shard_map/out/pallas_call | solution.py:538
  44.8 0.0 copy-start
  44.8 0.0 copy-start.2
  44.8 0.0 copy-start.6
  44.8 0.0 copy-start.7
  44.8 12.4 %all_to_all.21.lhs.own = bf16[8,32,512]{2,1,0:T(8,128)(2,1)S(1)} all-to-all(bf16[8,32,512]{2,1,0:T(8,128)(2,1)S(1)} %get-tuple-element.46), channel_id=1, replica_groups=mesh['groups'=2,'src'=2,'chan'=8] {'chan'}, dimensions={0} | all-to-all | bytes 524288 | tf_op jit(solution)/shard_map/all_to_all | solution.py:57
  57.2 0.0 collective-permute-start.17
  57.2 2.4 %values_own.1.partial = f32[16,512]{1,0:T(8,128)S(1)} custom-call(bf16[8,32,512]{2,1,0:T(8,128)(2,1)S(1)} %all_to_all.21.lhs.own, bf16[8192,512]{1,0:T(8,128)(2,1)} %weight.9), custom_call_target="tpu_custom_call" | custom-call | flops 3000000000 | tf_op jit(solution)/shard_map/values_own/pallas_call | solution.py:554
  59.7 0.0 collective-permute-done.17.other.hid_other
  59.7 3.4 %values.1 = (f32[3,16,512]{2,1,0:T(8,128)}, f32[16,512]{1,0:T(8,128)S(1)}, f32[16,128]{1,0:T(8,128)S(1)}, bf16[8,144,128]{2,1,0:T(8,128)(2,1)}) custom-call(bf16[8,32,512]{2,1,0:T(8,128)(2,1)S(1)} %all_to_all.21.lhs.own, bf16[8,32,512]{2,1,0:T(8,128)(2,1)S(1)} %collective-permute-done.17.other.hid_other, f32[8,16,128]{2,1,0:T(8,128)S(1)} %get-tuple-element.47.own_conv, ...), custom_call_target="tpu_custom_call" | custom-call | tf_op jit(solution)/shard_map/values/pallas_call | solution.py:566
  63.1 3.6 %all-to-all-start.2 = ((bf16[8,144,128]{2,1,0:T(8,128)(2,1)}), bf16[8,144,128]{2,1,0:T(8,128)(2,1)S(1)}, u32[]{:S(2)}, u32[]{:S(2)}) async-start(bf16[8,144,128]{2,1,0:T(8,128)(2,1)} %get-tuple-element.51), calls=%async_computation.2 | async-start | bytes 589824 | tf_op jit(solution)/shard_map/all_to_all | solution.py:57
  66.7 0.0 copy-start.4
  66.7 0.0 copy-start.8
  66.7 0.0 copy-start.9
  66.7 3.9 %gates.1 = (f32[16,512]{1,0:T(8,128)S(1)}, bf16[512,1024]{1,0:T(8,128)(2,1)S(1)}) custom-call(bf16[8,32,512]{2,1,0:T(8,128)(2,1)S(1)} %all_to_all.21.lhs.own, bf16[8,32,512]{2,1,0:T(8,128)(2,1)S(1)} %collective-permute-done.17.other.hid_other, f32[16,128]{1,0:T(8,128)S(1)} %get-tuple-element.52.rms, bf16[8192,512]{1,0:T(8,128)(2,1)} %weight.10, ...), custom_call_target="tpu_custom_call" | custom-call | flops 3000000000 | tf_op jit(solution)/shard_map/gates/pallas_call | solution.py:584
  70.7 6.3 %all-to-all-done.2.own = bf16[8,144,128]{2,1,0:T(8,128)(2,1)S(1)} async-done(((bf16[8,144,128]{2,1,0:T(8,128)(2,1)}), bf16[8,144,128]{2,1,0:T(8,128)(2,1)S(1)}, u32[]{:S(2)}, u32[]{:S(2)}) %all-to-all-start.2) | async-done | bytes 294944 | tf_op jit(solution)/shard_map/all_to_all | solution.py:57
  77.0 0.0 collective-permute-start.18
  77.0 1.6 %collective-permute-done.18.other = bf16[8,144,128]{2,1,0:T(8,128)(2,1)S(1)} collective-permute-done((bf16[8,144,128]{2,1,0:T(8,128)(2,1)S(1)}, bf16[8,144,128]{2,1,0:T(8,128)(2,1)S(1)}, u32[]{:S(2)}, u32[]{:S(2)}) %collective-permute-start.18) | collective-permute-done | bytes 294944 | tf_op jit(solution)/shard_map/ppermute | solution.py:53
  78.5 0.0 copy-done.1
  78.5 0.0 copy-done.8
  78.6 2.5 %scan.1 = (f32[16,16,512]{2,1,0:T(8,128)}, bf16[16,512]{1,0:T(8,128)(2,1)S(1)}, bf16[8,16,512]{2,1,0:T(8,128)(2,1)S(1)}) custom-call(bf16[8,144,128]{2,1,0:T(8,128)(2,1)S(1)} %all-to-all-done.2.own, bf16[8,144,128]{2,1,0:T(8,128)(2,1)S(1)} %collective-permute-done.18.other, bf16[8,32,512]{2,1,0:T(8,128)(2,1)S(1)} %collective-permute-done.17.other.hid_other, ...), custom_call_target="tpu_custom_call" | custom-call | tf_op jit(solution)/shard_map/scan/pallas_call | solution.py:603
  81.1 0.2 collective-permute-start.19
  81.3 2.5 %down.1 = f32[8,16,512]{2,1,0:T(8,128)S(1)} custom-call(bf16[16,512]{1,0:T(8,128)(2,1)S(1)} %get-tuple-element.60.gated, bf16[512,8192]{1,0:T(8,128)(2,1)} %weight.12), custom_call_target="tpu_custom_call" | custom-call | flops 3000000000 | tf_op jit(solution)/shard_map/down/pallas_call | solution.py:629
  83.8 0.0 collective-permute-done.19
  83.8 10.9 %all_to_all.22.final = bf16[8,16,512]{2,1,0:T(8,128)(2,1)S(1)} all-to-all(bf16[8,16,512]{2,1,0:T(8,128)(2,1)S(1)} %add_convert_fusion), channel_id=1, replica_groups=mesh['groups'=2,'src'=2,'chan'=8] {'chan'}, dimensions={0} | all-to-all | bytes 262144 | tf_op jit(solution)/shard_map/all_to_all | solution.py:57
  94.8 0.6 finish.1
  (12 shorter events, 0.1 us)
Async XLA Ops:
  0.6 41.0 %copy-start.5 = (bf16[16,512]{1,0:T(8,128)(2,1)S(1)}, bf16[16,512]{1,0:T(8,128)(2,1)}, u32[]{:S(2)}) copy-start(bf16[16,512]{1,0:T(8,128)(2,1)} %residual.1) | copy-start | bytes 49156
  3.1 38.6 %copy-start.3 = (bf16[8,16,512]{2,1,0:T(8,128)(2,1)S(1)}, bf16[8,16,512]{2,1,0:T(8,128)(2,1)}, u32[]{:S(2)}) copy-start(bf16[8,16,512]{2,1,0:T(8,128)(2,1)} %get-tuple-element.44.cross) | copy-start | bytes 393220
  3.1 7.7 %collective-permute-start = (bf16[304,128]{1,0:T(8,128)(2,1)}, bf16[304,128]{1,0:T(8,128)(2,1)S(1)}, u32[]{:S(2)}, u32[]{:S(2)}) collective-permute-start(bf16[304,128]{1,0:T(8,128)(2,1)} %get-tuple-element.34), channel_id=1, source_target_pairs={{0,8},{8,0},{1,9},{9,1},{2,10},{10,2},{3,11},{11,3},{4,12},{12,4},... | collective-permute-start | bytes 233480 | tf_op jit(solution)/shard_map/ppermute | solution.py:53
  3.6 8.5 %collective-permute-start.2 = (bf16[304,128]{1,0:T(8,128)(2,1)}, bf16[304,128]{1,0:T(8,128)(2,1)S(1)}, u32[]{:S(2)}, u32[]{:S(2)}) collective-permute-start(bf16[304,128]{1,0:T(8,128)(2,1)} %get-tuple-element.35), channel_id=1, source_target_pairs={{0,1},{1,0},{2,3},{3,2},{4,5},{5,4},{6,7},{7,6},{8,9},{9,8},{10,11... | collective-permute-start | bytes 233480 | tf_op jit(solution)/shard_map/ppermute | solution.py:511
  6.2 9.5 %collective-permute-start.3 = (bf16[304,128]{1,0:T(8,128)(2,1)}, bf16[304,128]{1,0:T(8,128)(2,1)S(1)}, u32[]{:S(2)}, u32[]{:S(2)}) collective-permute-start(bf16[304,128]{1,0:T(8,128)(2,1)} %get-tuple-element.36), channel_id=1, source_target_pairs={{0,2},{1,3},{2,0},{3,1},{4,6},{5,7},{6,4},{7,5},{8,10},{9,11},{10,... | collective-permute-start | bytes 233480 | tf_op jit(solution)/shard_map/ppermute | solution.py:511
  7.8 7.9 %collective-permute-start.4 = (bf16[304,128]{1,0:T(8,128)(2,1)}, bf16[304,128]{1,0:T(8,128)(2,1)S(1)}, u32[]{:S(2)}, u32[]{:S(2)}) collective-permute-start(bf16[304,128]{1,0:T(8,128)(2,1)} %get-tuple-element.37), channel_id=1, source_target_pairs={{0,3},{1,2},{2,1},{3,0},{4,7},{5,6},{6,5},{7,4},{8,11},{9,10},{10,... | collective-permute-start | bytes 233480 | tf_op jit(solution)/shard_map/ppermute | solution.py:511
  7.8 8.0 %collective-permute-start.5 = (bf16[304,128]{1,0:T(8,128)(2,1)}, bf16[304,128]{1,0:T(8,128)(2,1)S(1)}, u32[]{:S(2)}, u32[]{:S(2)}) collective-permute-start(bf16[304,128]{1,0:T(8,128)(2,1)} %get-tuple-element.38), channel_id=1, source_target_pairs={{0,4},{1,5},{2,6},{3,7},{4,0},{5,1},{6,2},{7,3},{8,12},{9,13},{10,... | collective-permute-start | bytes 233480 | tf_op jit(solution)/shard_map/ppermute | solution.py:511
  10.7 12.7 %collective-permute-start.6 = (bf16[304,128]{1,0:T(8,128)(2,1)}, bf16[304,128]{1,0:T(8,128)(2,1)S(1)}, u32[]{:S(2)}, u32[]{:S(2)}) collective-permute-start(bf16[304,128]{1,0:T(8,128)(2,1)} %get-tuple-element.39), channel_id=1, source_target_pairs={{0,5},{1,4},{2,7},{3,6},{4,1},{5,0},{6,3},{7,2},{8,13},{9,12},{10,... | collective-permute-start | bytes 233480 | tf_op jit(solution)/shard_map/ppermute | solution.py:511
  12.0 11.4 %collective-permute-start.7 = (bf16[304,128]{1,0:T(8,128)(2,1)}, bf16[304,128]{1,0:T(8,128)(2,1)S(1)}, u32[]{:S(2)}, u32[]{:S(2)}) collective-permute-start(bf16[304,128]{1,0:T(8,128)(2,1)} %get-tuple-element.40), channel_id=1, source_target_pairs={{0,6},{1,7},{2,4},{3,5},{4,2},{5,3},{6,0},{7,1},{8,14},{9,15},{10,... | collective-permute-start | bytes 233480 | tf_op jit(solution)/shard_map/ppermute | solution.py:511
  15.6 8.3 %collective-permute-start.8 = (bf16[304,128]{1,0:T(8,128)(2,1)}, bf16[304,128]{1,0:T(8,128)(2,1)S(1)}, u32[]{:S(2)}, u32[]{:S(2)}) collective-permute-start(bf16[304,128]{1,0:T(8,128)(2,1)} %get-tuple-element.41), channel_id=1, source_target_pairs={{0,7},{1,6},{2,5},{3,4},{4,3},{5,2},{6,1},{7,0},{8,15},{9,14},{10,... | collective-permute-start | bytes 233480 | tf_op jit(solution)/shard_map/ppermute | solution.py:511
  15.7 8.4 %collective-permute-start.1 = (bf16[304,128]{1,0:T(8,128)(2,1)S(1)}, bf16[304,128]{1,0:T(8,128)(2,1)S(1)}, u32[]{:S(2)}, u32[]{:S(2)}) collective-permute-start(bf16[304,128]{1,0:T(8,128)(2,1)S(1)} %collective-permute-done.refs_8_), channel_id=1, source_target_pairs={{0,8},{8,0},{1,9},{9,1},{2,10},{10,2},{3,11},{11,3},{4,12},{12,4},... | collective-permute-start | bytes 233480 | tf_op jit(solution)/shard_map/ppermute | solution.py:53
  15.7 8.7 %collective-permute-start.9 = (bf16[304,128]{1,0:T(8,128)(2,1)S(1)}, bf16[304,128]{1,0:T(8,128)(2,1)S(1)}, u32[]{:S(2)}, u32[]{:S(2)}) collective-permute-start(bf16[304,128]{1,0:T(8,128)(2,1)S(1)} %collective-permute-done.2.refs_1_), channel_id=1, source_target_pairs={{0,8},{8,0},{1,9},{9,1},{2,10},{10,2},{3,11},{11,3},{4,12},{12,4},... | collective-permute-start | bytes 233480 | tf_op jit(solution)/shard_map/ppermute | solution.py:53
  23.4 1.3 %collective-permute-start.10 = (bf16[304,128]{1,0:T(8,128)(2,1)S(1)}, bf16[304,128]{1,0:T(8,128)(2,1)S(1)}, u32[]{:S(2)}, u32[]{:S(2)}) collective-permute-start(bf16[304,128]{1,0:T(8,128)(2,1)S(1)} %collective-permute-done.3.refs_2_), channel_id=1, source_target_pairs={{0,8},{8,0},{1,9},{9,1},{2,10},{10,2},{3,11},{11,3},{4,12},{12,4},... | collective-permute-start | bytes 233480 | tf_op jit(solution)/shard_map/ppermute | solution.py:53
  23.4 1.5 %collective-permute-start.11 = (bf16[304,128]{1,0:T(8,128)(2,1)S(1)}, bf16[304,128]{1,0:T(8,128)(2,1)S(1)}, u32[]{:S(2)}, u32[]{:S(2)}) collective-permute-start(bf16[304,128]{1,0:T(8,128)(2,1)S(1)} %collective-permute-done.4.refs_3_), channel_id=1, source_target_pairs={{0,8},{8,0},{1,9},{9,1},{2,10},{10,2},{3,11},{11,3},{4,12},{12,4},... | collective-permute-start | bytes 233480 | tf_op jit(solution)/shard_map/ppermute | solution.py:53
  24.0 1.3 %collective-permute-start.12 = (bf16[304,128]{1,0:T(8,128)(2,1)S(1)}, bf16[304,128]{1,0:T(8,128)(2,1)S(1)}, u32[]{:S(2)}, u32[]{:S(2)}) collective-permute-start(bf16[304,128]{1,0:T(8,128)(2,1)S(1)} %collective-permute-done.5.refs_4_), channel_id=1, source_target_pairs={{0,8},{8,0},{1,9},{9,1},{2,10},{10,2},{3,11},{11,3},{4,12},{12,4},... | collective-permute-start | bytes 233480 | tf_op jit(solution)/shard_map/ppermute | solution.py:53
  24.0 1.4 %collective-permute-start.13 = (bf16[304,128]{1,0:T(8,128)(2,1)S(1)}, bf16[304,128]{1,0:T(8,128)(2,1)S(1)}, u32[]{:S(2)}, u32[]{:S(2)}) collective-permute-start(bf16[304,128]{1,0:T(8,128)(2,1)S(1)} %collective-permute-done.6.refs_5_), channel_id=1, source_target_pairs={{0,8},{8,0},{1,9},{9,1},{2,10},{10,2},{3,11},{11,3},{4,12},{12,4},... | collective-permute-start | bytes 233480 | tf_op jit(solution)/shard_map/ppermute | solution.py:53
  24.5 1.3 %collective-permute-start.14 = (bf16[304,128]{1,0:T(8,128)(2,1)S(1)}, bf16[304,128]{1,0:T(8,128)(2,1)S(1)}, u32[]{:S(2)}, u32[]{:S(2)}) collective-permute-start(bf16[304,128]{1,0:T(8,128)(2,1)S(1)} %collective-permute-done.7.refs_6_), channel_id=1, source_target_pairs={{0,8},{8,0},{1,9},{9,1},{2,10},{10,2},{3,11},{11,3},{4,12},{12,4},... | collective-permute-start | bytes 233480 | tf_op jit(solution)/shard_map/ppermute | solution.py:53
  24.7 1.3 %collective-permute-start.15 = (bf16[304,128]{1,0:T(8,128)(2,1)S(1)}, bf16[304,128]{1,0:T(8,128)(2,1)S(1)}, u32[]{:S(2)}, u32[]{:S(2)}) collective-permute-start(bf16[304,128]{1,0:T(8,128)(2,1)S(1)} %collective-permute-done.8.refs_7_), channel_id=1, source_target_pairs={{0,8},{8,0},{1,9},{9,1},{2,10},{10,2},{3,11},{11,3},{4,12},{12,4},... | collective-permute-start | bytes 233480 | tf_op jit(solution)/shard_map/ppermute | solution.py:53
  40.0 1.6 %collective-permute-start.16 = (bf16[8,64,128]{2,1,0:T(8,128)(2,1)S(1)}, bf16[8,64,128]{2,1,0:T(8,128)(2,1)S(1)}, u32[]{:S(2)}, u32[]{:S(2)}) collective-permute-start(bf16[8,64,128]{2,1,0:T(8,128)(2,1)S(1)} %all_to_all.20.own), channel_id=1, source_target_pairs={{0,8},{8,0},{1,9},{9,1},{2,10},{10,2},{3,11},{11,3},{4,12},{12,4},... | collective-permute-start | bytes 393224 | tf_op jit(solution)/shard_map/ppermute | solution.py:53
  44.8 14.9 %copy-start = (bf16[512,544]{0,1:T(8,128)(2,1)S(1)}, bf16[512,544]{0,1:T(8,128)(2,1)}, u32[]{:S(2)}) copy-start(bf16[512,544]{0,1:T(8,128)(2,1)} %param.34) | copy-start | bytes 1671172
  44.8 14.9 %copy-start.2 = (bf16[8,16,512]{2,1,0:T(8,128)(2,1)S(1)}, bf16[8,16,512]{2,1,0:T(8,128)(2,1)}, u32[]{:S(2)}) copy-start(bf16[8,16,512]{2,1,0:T(8,128)(2,1)} %get-tuple-element.49.same) | copy-start | bytes 393220
  44.8 14.9 %copy-start.6 = (f32[4,512]{1,0:T(4,128)S(1)}, f32[4,512]{1,0:T(4,128)}, u32[]{:S(2)}) copy-start(f32[4,512]{1,0:T(4,128)} %taps.1) | copy-start | bytes 24580
  44.8 14.9 %copy-start.7 = (f32[512]{0:T(512)S(1)}, f32[512]{0:T(512)}, u32[]{:S(2)}) copy-start(f32[512]{0:T(512)} %param.33) | copy-start | bytes 6148
  57.2 2.4 %collective-permute-start.17 = (bf16[8,32,512]{2,1,0:T(8,128)(2,1)S(1)}, bf16[8,32,512]{2,1,0:T(8,128)(2,1)S(1)}, u32[]{:S(2)}, u32[]{:S(2)}) collective-permute-start(bf16[8,32,512]{2,1,0:T(8,128)(2,1)S(1)} %all_to_all.21.lhs.own), channel_id=1, source_target_pairs={{0,8},{8,0},{1,9},{9,1},{2,10},{10,2},{3,11},{11,3},{4,12},{12,4},... | collective-permute-start | bytes 786440 | tf_op jit(solution)/shard_map/ppermute | solution.py:53
  63.1 13.9 %all-to-all-start.2 = ((bf16[8,144,128]{2,1,0:T(8,128)(2,1)}), bf16[8,144,128]{2,1,0:T(8,128)(2,1)S(1)}, u32[]{:S(2)}, u32[]{:S(2)}) async-start(bf16[8,144,128]{2,1,0:T(8,128)(2,1)} %get-tuple-element.51), calls=%async_computation.2 | async-start | bytes 589824 | tf_op jit(solution)/shard_map/all_to_all | solution.py:57
  66.7 11.8 %copy-start.1 = (bf16[512,512]{1,0:T(8,128)(2,1)S(1)}, bf16[512,512]{1,0:T(8,128)(2,1)}, u32[]{:S(2)}) copy-start(bf16[512,512]{1,0:T(8,128)(2,1)} %step_proj.1) | copy-start | bytes 1572868
  66.7 11.8 %copy-start.4 = (f32[16,512]{1,0:T(8,128)S(1)}, f32[16,512]{1,0:T(8,128)}, u32[]{:S(2)}) copy-start(f32[16,512]{1,0:T(8,128)} %decay_log.1) | copy-start | bytes 98308
  66.7 11.8 %copy-start.8 = (f32[512]{0:T(512)S(1)}, f32[512]{0:T(512)}, u32[]{:S(2)}) copy-start(f32[512]{0:T(512)} %param.36) | copy-start | bytes 6148
  66.7 11.8 %copy-start.9 = (f32[512]{0:T(512)S(1)}, f32[512]{0:T(512)}, u32[]{:S(2)}) copy-start(f32[512]{0:T(512)} %param.38) | copy-start | bytes 6148
  77.0 1.6 %collective-permute-start.18 = (bf16[8,144,128]{2,1,0:T(8,128)(2,1)S(1)}, bf16[8,144,128]{2,1,0:T(8,128)(2,1)S(1)}, u32[]{:S(2)}, u32[]{:S(2)}) collective-permute-start(bf16[8,144,128]{2,1,0:T(8,128)(2,1)S(1)} %all-to-all-done.2.own), channel_id=1, source_target_pairs={{0,8},{8,0},{1,9},{9,1},{2,10},{10,2},{3,11},{11,3},{4,12},{12,4},... | collective-permute-start | bytes 884744 | tf_op jit(solution)/shard_map/ppermute | solution.py:53
  81.1 2.7 %collective-permute-start.19 = (bf16[8,16,512]{2,1,0:T(8,128)(2,1)S(1)}, bf16[8,16,512]{2,1,0:T(8,128)(2,1)S(1)}, u32[]{:S(2)}, u32[]{:S(2)}) collective-permute-start(bf16[8,16,512]{2,1,0:T(8,128)(2,1)S(1)} %get-tuple-element.61), channel_id=1, source_target_pairs={{0,8},{8,0},{1,9},{9,1},{2,10},{10,2},{3,11},{11,3},{4,12},{12,4},... | collective-permute-start | bytes 393224 | tf_op jit(solution)/shard_map/ppermute | solution.py:53

commit v11 on v8

--- a/solution.py
+++ b/solution.py
@@ -521,8 +521,7 @@
         name="load",
     )(residual_input, mamba_state)
 
-    early = nchan // 4
-    arrived[early], residual, same, cross = lax.optimization_barrier((arrived[early], residual, same, cross))
+    arrived[0], residual, same, cross = lax.optimization_barrier((arrived[0], residual, same, cross))
     other_arrived = [swap(block) for block in arrived]
     pairs = nchan * lay.per
     conv_cut = shape((nchan, round_up(lay.conv_rows, 8), LANES), F32)

time: 96 us -> 95.1 us (level)
  waiting for transfers between devices: 16.2 us -> 14.9 us
    ppermute x7, waiting for transfers between devices: 7.36 us -> 6.09 us  [on_device(): lax.ppermute(packed[k], 'chan', [(i, i ^ k) for i in range(nchan)])]
    unnamed x20 -> x24, local copies, waits for them, and re-layouts: 1.81 us -> 2.65 us
  transfers between devices with their start and end apart: 20 -> 20, of which waited for: 7 -> 8; matrix products, arithmetic and copies ran while one was open for 0% -> 0% of each run, Pallas kernels for 11% -> 11%
where the time goes in v11:
time: 95.1 us; the launch traced here: 94.5 us
  blocking collectives  34.2 us (36%)
  Pallas kernels  23.4 us (25%)
  starting transfers between devices  18.4 us (19%)
  waiting for transfers between devices  14.9 us (16%)
  local copies, waits for them, and re-layouts  2.65 us (3%)
    all_to_all x3, blocking collectives, exchange(): return lax.all_to_all(x, 'chan', split_axis=0, concat_axis=0, tiled=True)  34.2 us
    ppermute x7, starting transfers between devices, on_device(): lax.ppermute(packed[k], 'chan', [(i, i ^ k) for i in range(nchan)])  12.5 us
    all_to_all x1, waiting for transfers between devices, exchange(): return lax.all_to_all(x, 'chan', split_axis=0, concat_axis=0, tiled=True)  6.29 us
    ppermute x7, waiting for transfers between devices, on_device(): lax.ppermute(packed[k], 'chan', [(i, i ^ k) for i in range(nchan)])  6.09 us
    pallas_call x1, Pallas kernels, on_device(): call(gates_kernel, out_shape=(shape((rows, cols), F32), shape((cols, DOWN...  3.91 us
    all_to_all x1, starting transfers between devices, exchange(): return lax.all_to_all(x, 'chan', split_axis=0, concat_axis=0, tiled=True)  3.63 us
    pallas_call x1, Pallas kernels, on_device(): call(functools.partial(values_kernel, lay), out_shape=(shape((steps, rows...  3.36 us
    pallas_call x1, Pallas kernels, on_device(): call(functools.partial(out_kernel, lay), out_shape=(shape((rows, cols), B...  3.13 us
  transfers between devices with their start and end apart: 20, of which 8 were waited for; matrix products, arithmetic and copies ran while one was open for 0% of the time, Pallas kernels for 11%

profile of v11, /device:TPU:0, one launch (start us, length us, event | category | flops | bytes accessed | tf_op | source)
XLA Modules:
  0.0 94.5 jit_solution(16771837853809151086)
XLA Ops:
  0.6 2.3 %pack.1 = (bf16[304,128]{1,0:T(8,128)(2,1)}, bf16[304,128]{1,0:T(8,128)(2,1)}, bf16[304,128]{1,0:T(8,128)(2,1)}, bf16[304,128]{1,0:T(8,128)(2,1)}, bf16[304,128]...) custom-call(bf16[1,8192]{1,0:T(2,128)(2,1)} %query_hbm.1, ...), custom_call_target="tpu_custom_call" | custom-call | tf_op jit(solution)/shard_map/pack/pallas_call | solution.py:491
  2.9 0.0 copy-start.2
  2.9 3.0 %collective-permute-start = (bf16[304,128]{1,0:T(8,128)(2,1)}, bf16[304,128]{1,0:T(8,128)(2,1)S(1)}, u32[]{:S(2)}, u32[]{:S(2)}) collective-permute-start(bf16[304,128]{1,0:T(8,128)(2,1)} %get-tuple-element.64), channel_id=1, source_target_pairs={{0,1},{1,0},{2,3},{3,2},{4,5},{5,4},{6,7},{7,6},{8,9},{9,8},{10,11... | collective-permute-start | bytes 233480 | tf_op jit(solution)/shard_map/ppermute | solution.py:512
  5.9 1.6 %collective-permute-start.1 = (bf16[304,128]{1,0:T(8,128)(2,1)}, bf16[304,128]{1,0:T(8,128)(2,1)S(1)}, u32[]{:S(2)}, u32[]{:S(2)}) collective-permute-start(bf16[304,128]{1,0:T(8,128)(2,1)} %get-tuple-element.65), channel_id=1, source_target_pairs={{0,2},{1,3},{2,0},{3,1},{4,6},{5,7},{6,4},{7,5},{8,10},{9,11},{10,... | collective-permute-start | bytes 233480 | tf_op jit(solution)/shard_map/ppermute | solution.py:512
  7.5 0.0 collective-permute-start.2
  7.5 3.0 %collective-permute-start.3 = (bf16[304,128]{1,0:T(8,128)(2,1)}, bf16[304,128]{1,0:T(8,128)(2,1)S(1)}, u32[]{:S(2)}, u32[]{:S(2)}) collective-permute-start(bf16[304,128]{1,0:T(8,128)(2,1)} %get-tuple-element.67), channel_id=1, source_target_pairs={{0,4},{1,5},{2,6},{3,7},{4,0},{5,1},{6,2},{7,3},{8,12},{9,13},{10,... | collective-permute-start | bytes 233480 | tf_op jit(solution)/shard_map/ppermute | solution.py:512
  10.5 1.3 %collective-permute-start.4 = (bf16[304,128]{1,0:T(8,128)(2,1)}, bf16[304,128]{1,0:T(8,128)(2,1)S(1)}, u32[]{:S(2)}, u32[]{:S(2)}) collective-permute-start(bf16[304,128]{1,0:T(8,128)(2,1)} %get-tuple-element.68), channel_id=1, source_target_pairs={{0,5},{1,4},{2,7},{3,6},{4,1},{5,0},{6,3},{7,2},{8,13},{9,12},{10,... | collective-permute-start | bytes 233480 | tf_op jit(solution)/shard_map/ppermute | solution.py:512
  11.8 1.0 %copy-done.8 = f32[1,16,8192]{2,1,0:T(8,128)S(1)} copy-done((f32[1,16,8192]{2,1,0:T(8,128)S(1)}, f32[1,16,8192]{2,1,0:T(8,128)}, u32[]{:S(2)}) %copy-start.8) | copy-done | bytes 524312
  12.8 0.7 copy-done.9
  13.6 0.0 collective-permute-done.refs_1_
  13.6 0.8 copy-done.11
  14.4 3.6 %collective-permute-start.5 = (bf16[304,128]{1,0:T(8,128)(2,1)S(1)}, bf16[304,128]{1,0:T(8,128)(2,1)S(1)}, u32[]{:S(2)}, u32[]{:S(2)}) collective-permute-start(bf16[304,128]{1,0:T(8,128)(2,1)S(1)} %copy-done.11), channel_id=1, source_target_pairs={{0,6},{1,7},{2,4},{3,5},{4,2},{5,3},{6,0},{7,1},{8,14},{9,15},{10,... | collective-permute-start | bytes 233480 | tf_op jit(solution)/shard_map/ppermute | solution.py:512
  18.0 0.0 collective-permute-done.1.refs_2_
  18.1 0.0 collective-permute-start.6
  18.1 0.0 collective-permute-done.2.refs_3_
  18.1 0.0 copy-done.2
  18.1 0.1 collective-permute-start.7
  18.2 0.0 collective-permute-done.3.refs_4_
  18.2 0.5 collective-permute-start.8
  18.7 3.8 %collective-permute-done.4.refs_5_ = bf16[304,128]{1,0:T(8,128)(2,1)S(1)} collective-permute-done((bf16[304,128]{1,0:T(8,128)(2,1)}, bf16[304,128]{1,0:T(8,128)(2,1)S(1)}, u32[]{:S(2)}, u32[]{:S(2)}) %collective-permute-start.4) | collective-permute-done | bytes 77856 | tf_op jit(solution)/shard_map/ppermute | solution.py:512
  22.5 0.0 collective-permute-start.9
  22.5 0.0 collective-permute-done.5.refs_6_
  22.5 0.5 collective-permute-start.10
  23.0 2.2 %collective-permute-done.6.refs_7_ = bf16[304,128]{1,0:T(8,128)(2,1)S(1)} collective-permute-done((bf16[304,128]{1,0:T(8,128)(2,1)S(1)}, bf16[304,128]{1,0:T(8,128)(2,1)S(1)}, u32[]{:S(2)}, u32[]{:S(2)}) %collective-permute-start.6) | collective-permute-done | bytes 77856 | tf_op jit(solution)/shard_map/ppermute | solution.py:512
  25.2 0.0 collective-permute-start.11
  25.3 0.0 collective-permute-done.7.refs_8_
  25.3 0.5 collective-permute-start.12
  25.8 0.0 collective-permute-done.8.refs_9_
  25.8 0.1 collective-permute-start.13
  25.8 0.0 collective-permute-done.9.refs_10_
  25.8 0.4 collective-permute-start.14
  26.3 0.0 collective-permute-done.10.refs_11_
  26.3 0.2 collective-permute-done.11.refs_12_
  26.5 0.2 collective-permute-done.12.refs_13_
  26.7 0.4 collective-permute-done.13.refs_14_
  27.0 0.2 collective-permute-done.14.refs_15_
  27.2 1.1 %attend.1 = (bf16[8,64,128]{2,1,0:T(8,128)(2,1)S(1)}, f32[8,16,128]{2,1,0:T(8,128)S(1)}, f32[8,16,128]{2,1,0:T(8,128)S(1)}) custom-call(bf16[304,128]{1,0:T(8,128)(2,1)S(1)} %copy-done.2, bf16[304,128]{1,0:T(8,128)(2,1)S(1)} %collective-permute-done.refs_1_, bf16[304,128]{1,0:T(8,128)(2,1)S(1)} %collective-permute-done.1.refs_2_, ...), custom_call_target="tpu_custom_call" | custom-call | tf_op jit(solution)/shard_map/attend/pallas_call | solution.py:528
  28.3 10.9 %all_to_all.20.own = bf16[8,64,128]{2,1,0:T(8,128)(2,1)S(1)} all-to-all(bf16[8,64,128]{2,1,0:T(8,128)(2,1)S(1)} %get-tuple-element.71), channel_id=1, replica_groups=mesh['groups'=2,'src'=2,'chan'=8] {'chan'}, dimensions={0} | all-to-all | bytes 262144 | tf_op jit(solution)/shard_map/all_to_all | solution.py:57
  39.2 0.0 collective-permute-start.15
  39.2 1.5 %fetch.1.fetched = bf16[2048,512]{1,0:T(8,128)(2,1)S(1)} custom-call(bf16[8192,512]{1,0:T(8,128)(2,1)} %weight.7), custom_call_target="tpu_custom_call" | custom-call | flops 3000000000 | tf_op jit(solution)/shard_map/fetch/pallas_call | solution.py:540
  40.7 0.0 collective-permute-done.15.other
  40.7 3.1 %out.1 = (bf16[16,512]{1,0:T(8,128)(2,1)S(1)}, bf16[8,32,512]{2,1,0:T(8,128)(2,1)S(1)}) custom-call(bf16[8,64,128]{2,1,0:T(8,128)(2,1)S(1)} %all_to_all.20.own, bf16[8,64,128]{2,1,0:T(8,128)(2,1)S(1)} %collective-permute-done.15.other, bf16[16,512]{1,0:T(8,128)(2,1)S(1)} %get-tuple-element.73.residual, bf16[8,16,512]{2,1,0:T(8,128)(2,1)S(1)} %get-tuple-element.74.cross, ...), custom_call_target="tpu_custom_call" | custom-call | tf_op jit(solution)/shard_map/out/pallas_call | solution.py:550
  43.9 0.0 copy-start
  43.9 0.0 copy-start.4
  43.9 0.0 copy-start.5
  43.9 12.4 %all_to_all.21.lhs.own = bf16[8,32,512]{2,1,0:T(8,128)(2,1)S(1)} all-to-all(bf16[8,32,512]{2,1,0:T(8,128)(2,1)S(1)} %get-tuple-element.76), channel_id=1, replica_groups=mesh['groups'=2,'src'=2,'chan'=8] {'chan'}, dimensions={0} | all-to-all | bytes 524288 | tf_op jit(solution)/shard_map/all_to_all | solution.py:57
  56.3 0.0 collective-permute-start.16
  56.4 2.4 %values_own.1.partial = f32[16,512]{1,0:T(8,128)S(1)} custom-call(bf16[8,32,512]{2,1,0:T(8,128)(2,1)S(1)} %all_to_all.21.lhs.own, bf16[8192,512]{1,0:T(8,128)(2,1)} %weight.9), custom_call_target="tpu_custom_call" | custom-call | flops 3000000000 | tf_op jit(solution)/shard_map/values_own/pallas_call | solution.py:566
  58.8 0.0 collective-permute-done.16.other.hid_other
  58.8 3.4 %values.1 = (f32[3,16,512]{2,1,0:T(8,128)}, f32[16,512]{1,0:T(8,128)S(1)}, f32[16,128]{1,0:T(8,128)S(1)}, bf16[8,144,128]{2,1,0:T(8,128)(2,1)}) custom-call(bf16[8,32,512]{2,1,0:T(8,128)(2,1)S(1)} %all_to_all.21.lhs.own, bf16[8,32,512]{2,1,0:T(8,128)(2,1)S(1)} %collective-permute-done.16.other.hid_other, f32[8,16,128]{2,1,0:T(8,128)S(1)} %get-tuple-element.77.own_conv, ...), custom_call_target="tpu_custom_call" | custom-call | tf_op jit(solution)/shard_map/values/pallas_call | solution.py:578
  62.2 3.6 %all-to-all-start.2 = ((bf16[8,144,128]{2,1,0:T(8,128)(2,1)}), bf16[8,144,128]{2,1,0:T(8,128)(2,1)S(1)}, u32[]{:S(2)}, u32[]{:S(2)}) async-start(bf16[8,144,128]{2,1,0:T(8,128)(2,1)} %get-tuple-element.81), calls=%async_computation.2 | async-start | bytes 589824 | tf_op jit(solution)/shard_map/all_to_all | solution.py:57
  65.8 0.0 copy-start.3
  65.8 0.0 copy-start.6
  65.8 0.0 copy-start.7
  65.8 3.9 %gates.1 = (f32[16,512]{1,0:T(8,128)S(1)}, bf16[512,1024]{1,0:T(8,128)(2,1)S(1)}) custom-call(bf16[8,32,512]{2,1,0:T(8,128)(2,1)S(1)} %all_to_all.21.lhs.own, bf16[8,32,512]{2,1,0:T(8,128)(2,1)S(1)} %collective-permute-done.16.other.hid_other, f32[16,128]{1,0:T(8,128)S(1)} %get-tuple-element.82.rms, bf16[8192,512]{1,0:T(8,128)(2,1)} %weight.10, ...), custom_call_target="tpu_custom_call" | custom-call | flops 3000000000 | tf_op jit(solution)/shard_map/gates/pallas_call | solution.py:596
  69.8 6.3 %all-to-all-done.2.own = bf16[8,144,128]{2,1,0:T(8,128)(2,1)S(1)} async-done(((bf16[8,144,128]{2,1,0:T(8,128)(2,1)}), bf16[8,144,128]{2,1,0:T(8,128)(2,1)S(1)}, u32[]{:S(2)}, u32[]{:S(2)}) %all-to-all-start.2) | async-done | bytes 294944 | tf_op jit(solution)/shard_map/all_to_all | solution.py:57
  76.0 0.0 collective-permute-start.17
  76.1 1.6 %collective-permute-done.17.other = bf16[8,144,128]{2,1,0:T(8,128)(2,1)S(1)} collective-permute-done((bf16[8,144,128]{2,1,0:T(8,128)(2,1)S(1)}, bf16[8,144,128]{2,1,0:T(8,128)(2,1)S(1)}, u32[]{:S(2)}, u32[]{:S(2)}) %collective-permute-start.17) | collective-permute-done | bytes 294944 | tf_op jit(solution)/shard_map/ppermute | solution.py:53
  77.7 2.5 %scan.1 = (f32[16,16,512]{2,1,0:T(8,128)}, bf16[16,512]{1,0:T(8,128)(2,1)S(1)}, bf16[8,16,512]{2,1,0:T(8,128)(2,1)S(1)}) custom-call(bf16[8,144,128]{2,1,0:T(8,128)(2,1)S(1)} %all-to-all-done.2.own, bf16[8,144,128]{2,1,0:T(8,128)(2,1)S(1)} %collective-permute-done.17.other, bf16[8,32,512]{2,1,0:T(8,128)(2,1)S(1)} %collective-permute-done.16.other.hid_other, ...), custom_call_target="tpu_custom_call" | custom-call | tf_op jit(solution)/shard_map/scan/pallas_call | solution.py:615
  80.2 0.2 collective-permute-start.18
  80.4 2.5 %down.1 = f32[8,16,512]{2,1,0:T(8,128)S(1)} custom-call(bf16[16,512]{1,0:T(8,128)(2,1)S(1)} %get-tuple-element.90.gated, bf16[512,8192]{1,0:T(8,128)(2,1)} %weight.12), custom_call_target="tpu_custom_call" | custom-call | flops 3000000000 | tf_op jit(solution)/shard_map/down/pallas_call | solution.py:641
  82.9 0.0 collective-permute-done.18
  82.9 10.9 %all_to_all.22.final = bf16[8,16,512]{2,1,0:T(8,128)(2,1)S(1)} all-to-all(bf16[8,16,512]{2,1,0:T(8,128)(2,1)S(1)} %add_convert_fusion), channel_id=1, replica_groups=mesh['groups'=2,'src'=2,'chan'=8] {'chan'}, dimensions={0} | all-to-all | bytes 262144 | tf_op jit(solution)/shard_map/all_to_all | solution.py:57
  93.9 0.6 finish.1
  (15 shorter events, 0.1 us)
Async XLA Ops:
  2.9 15.2 %copy-start.2 = (bf16[304,128]{1,0:T(8,128)(2,1)S(1)}, bf16[304,128]{1,0:T(8,128)(2,1)}, u32[]{:S(2)}) copy-start(bf16[304,128]{1,0:T(8,128)(2,1)} %get-tuple-element.63.refs_0_) | copy-start | bytes 233476
  2.9 10.7 %collective-permute-start = (bf16[304,128]{1,0:T(8,128)(2,1)}, bf16[304,128]{1,0:T(8,128)(2,1)S(1)}, u32[]{:S(2)}, u32[]{:S(2)}) collective-permute-start(bf16[304,128]{1,0:T(8,128)(2,1)} %get-tuple-element.64), channel_id=1, source_target_pairs={{0,1},{1,0},{2,3},{3,2},{4,5},{5,4},{6,7},{7,6},{8,9},{9,8},{10,11... | collective-permute-start | bytes 233480 | tf_op jit(solution)/shard_map/ppermute | solution.py:512
  5.9 12.1 %collective-permute-start.1 = (bf16[304,128]{1,0:T(8,128)(2,1)}, bf16[304,128]{1,0:T(8,128)(2,1)S(1)}, u32[]{:S(2)}, u32[]{:S(2)}) collective-permute-start(bf16[304,128]{1,0:T(8,128)(2,1)} %get-tuple-element.65), channel_id=1, source_target_pairs={{0,2},{1,3},{2,0},{3,1},{4,6},{5,7},{6,4},{7,5},{8,10},{9,11},{10,... | collective-permute-start | bytes 233480 | tf_op jit(solution)/shard_map/ppermute | solution.py:512
  7.5 10.5 %collective-permute-start.2 = (bf16[304,128]{1,0:T(8,128)(2,1)}, bf16[304,128]{1,0:T(8,128)(2,1)S(1)}, u32[]{:S(2)}, u32[]{:S(2)}) collective-permute-start(bf16[304,128]{1,0:T(8,128)(2,1)} %get-tuple-element.66), channel_id=1, source_target_pairs={{0,3},{1,2},{2,1},{3,0},{4,7},{5,6},{6,5},{7,4},{8,11},{9,10},{10,... | collective-permute-start | bytes 233480 | tf_op jit(solution)/shard_map/ppermute | solution.py:512
  7.5 10.6 %collective-permute-start.3 = (bf16[304,128]{1,0:T(8,128)(2,1)}, bf16[304,128]{1,0:T(8,128)(2,1)S(1)}, u32[]{:S(2)}, u32[]{:S(2)}) collective-permute-start(bf16[304,128]{1,0:T(8,128)(2,1)} %get-tuple-element.67), channel_id=1, source_target_pairs={{0,4},{1,5},{2,6},{3,7},{4,0},{5,1},{6,2},{7,3},{8,12},{9,13},{10,... | collective-permute-start | bytes 233480 | tf_op jit(solution)/shard_map/ppermute | solution.py:512
  10.5 12.0 %collective-permute-start.4 = (bf16[304,128]{1,0:T(8,128)(2,1)}, bf16[304,128]{1,0:T(8,128)(2,1)S(1)}, u32[]{:S(2)}, u32[]{:S(2)}) collective-permute-start(bf16[304,128]{1,0:T(8,128)(2,1)} %get-tuple-element.68), channel_id=1, source_target_pairs={{0,5},{1,4},{2,7},{3,6},{4,1},{5,0},{6,3},{7,2},{8,13},{9,12},{10,... | collective-permute-start | bytes 233480 | tf_op jit(solution)/shard_map/ppermute | solution.py:512
  11.8 1.0 %copy-start.8 = (f32[1,16,8192]{2,1,0:T(8,128)S(1)}, f32[1,16,8192]{2,1,0:T(8,128)}, u32[]{:S(2)}) copy-start(f32[1,16,8192]{2,1,0:T(8,128)} %state) | copy-start | bytes 1572868
  12.8 0.7 copy-start.9
  13.6 0.9 copy-start.11
  13.6 4.5 %copy-start.10 = (bf16[304,128]{1,0:T(8,128)(2,1)S(1)}, bf16[304,128]{1,0:T(8,128)(2,1)}, u32[]{:S(2)}) copy-start(bf16[304,128]{1,0:T(8,128)(2,1)} %get-tuple-element.70) | copy-start | bytes 233476
  14.4 8.1 %collective-permute-start.5 = (bf16[304,128]{1,0:T(8,128)(2,1)S(1)}, bf16[304,128]{1,0:T(8,128)(2,1)S(1)}, u32[]{:S(2)}, u32[]{:S(2)}) collective-permute-start(bf16[304,128]{1,0:T(8,128)(2,1)S(1)} %copy-done.11), channel_id=1, source_target_pairs={{0,6},{1,7},{2,4},{3,5},{4,2},{5,3},{6,0},{7,1},{8,14},{9,15},{10,... | collective-permute-start | bytes 233480 | tf_op jit(solution)/shard_map/ppermute | solution.py:512
  18.1 7.2 %collective-permute-start.6 = (bf16[304,128]{1,0:T(8,128)(2,1)S(1)}, bf16[304,128]{1,0:T(8,128)(2,1)S(1)}, u32[]{:S(2)}, u32[]{:S(2)}) collective-permute-start(bf16[304,128]{1,0:T(8,128)(2,1)S(1)} %copy-done.10), channel_id=1, source_target_pairs={{0,7},{1,6},{2,5},{3,4},{4,3},{5,2},{6,1},{7,0},{8,15},{9,14},{10,... | collective-permute-start | bytes 233480 | tf_op jit(solution)/shard_map/ppermute | solution.py:512
  18.1 7.2 %collective-permute-start.7 = (bf16[304,128]{1,0:T(8,128)(2,1)S(1)}, bf16[304,128]{1,0:T(8,128)(2,1)S(1)}, u32[]{:S(2)}, u32[]{:S(2)}) collective-permute-start(bf16[304,128]{1,0:T(8,128)(2,1)S(1)} %copy-done.2), channel_id=1, source_target_pairs={{0,8},{8,0},{1,9},{9,1},{2,10},{10,2},{3,11},{11,3},{4,12},{12,4},... | collective-permute-start | bytes 233480 | tf_op jit(solution)/shard_map/ppermute | solution.py:53
  18.2 7.6 %collective-permute-start.8 = (bf16[304,128]{1,0:T(8,128)(2,1)S(1)}, bf16[304,128]{1,0:T(8,128)(2,1)S(1)}, u32[]{:S(2)}, u32[]{:S(2)}) collective-permute-start(bf16[304,128]{1,0:T(8,128)(2,1)S(1)} %collective-permute-done.refs_1_), channel_id=1, source_target_pairs={{0,8},{8,0},{1,9},{9,1},{2,10},{10,2},{3,11},{11,3},{4,12},{12,4},... | collective-permute-start | bytes 233480 | tf_op jit(solution)/shard_map/ppermute | solution.py:53
  22.5 3.3 %collective-permute-start.9 = (bf16[304,128]{1,0:T(8,128)(2,1)S(1)}, bf16[304,128]{1,0:T(8,128)(2,1)S(1)}, u32[]{:S(2)}, u32[]{:S(2)}) collective-permute-start(bf16[304,128]{1,0:T(8,128)(2,1)S(1)} %collective-permute-done.1.refs_2_), channel_id=1, source_target_pairs={{0,8},{8,0},{1,9},{9,1},{2,10},{10,2},{3,11},{11,3},{4,12},{12,4},... | collective-permute-start | bytes 233480 | tf_op jit(solution)/shard_map/ppermute | solution.py:53
  22.5 3.8 %collective-permute-start.10 = (bf16[304,128]{1,0:T(8,128)(2,1)S(1)}, bf16[304,128]{1,0:T(8,128)(2,1)S(1)}, u32[]{:S(2)}, u32[]{:S(2)}) collective-permute-start(bf16[304,128]{1,0:T(8,128)(2,1)S(1)} %collective-permute-done.2.refs_3_), channel_id=1, source_target_pairs={{0,8},{8,0},{1,9},{9,1},{2,10},{10,2},{3,11},{11,3},{4,12},{12,4},... | collective-permute-start | bytes 233480 | tf_op jit(solution)/shard_map/ppermute | solution.py:53
  25.2 1.3 %collective-permute-start.11 = (bf16[304,128]{1,0:T(8,128)(2,1)S(1)}, bf16[304,128]{1,0:T(8,128)(2,1)S(1)}, u32[]{:S(2)}, u32[]{:S(2)}) collective-permute-start(bf16[304,128]{1,0:T(8,128)(2,1)S(1)} %collective-permute-done.3.refs_4_), channel_id=1, source_target_pairs={{0,8},{8,0},{1,9},{9,1},{2,10},{10,2},{3,11},{11,3},{4,12},{12,4},... | collective-permute-start | bytes 233480 | tf_op jit(solution)/shard_map/ppermute | solution.py:53
  25.3 1.4 %collective-permute-start.12 = (bf16[304,128]{1,0:T(8,128)(2,1)S(1)}, bf16[304,128]{1,0:T(8,128)(2,1)S(1)}, u32[]{:S(2)}, u32[]{:S(2)}) collective-permute-start(bf16[304,128]{1,0:T(8,128)(2,1)S(1)} %collective-permute-done.4.refs_5_), channel_id=1, source_target_pairs={{0,8},{8,0},{1,9},{9,1},{2,10},{10,2},{3,11},{11,3},{4,12},{12,4},... | collective-permute-start | bytes 233480 | tf_op jit(solution)/shard_map/ppermute | solution.py:53
  25.8 1.3 %collective-permute-start.13 = (bf16[304,128]{1,0:T(8,128)(2,1)S(1)}, bf16[304,128]{1,0:T(8,128)(2,1)S(1)}, u32[]{:S(2)}, u32[]{:S(2)}) collective-permute-start(bf16[304,128]{1,0:T(8,128)(2,1)S(1)} %collective-permute-done.5.refs_6_), channel_id=1, source_target_pairs={{0,8},{8,0},{1,9},{9,1},{2,10},{10,2},{3,11},{11,3},{4,12},{12,4},... | collective-permute-start | bytes 233480 | tf_op jit(solution)/shard_map/ppermute | solution.py:53
  25.8 1.4 %collective-permute-start.14 = (bf16[304,128]{1,0:T(8,128)(2,1)S(1)}, bf16[304,128]{1,0:T(8,128)(2,1)S(1)}, u32[]{:S(2)}, u32[]{:S(2)}) collective-permute-start(bf16[304,128]{1,0:T(8,128)(2,1)S(1)} %collective-permute-done.6.refs_7_), channel_id=1, source_target_pairs={{0,8},{8,0},{1,9},{9,1},{2,10},{10,2},{3,11},{11,3},{4,12},{12,4},... | collective-permute-start | bytes 233480 | tf_op jit(solution)/shard_map/ppermute | solution.py:53
  39.2 1.6 %collective-permute-start.15 = (bf16[8,64,128]{2,1,0:T(8,128)(2,1)S(1)}, bf16[8,64,128]{2,1,0:T(8,128)(2,1)S(1)}, u32[]{:S(2)}, u32[]{:S(2)}) collective-permute-start(bf16[8,64,128]{2,1,0:T(8,128)(2,1)S(1)} %all_to_all.20.own), channel_id=1, source_target_pairs={{0,8},{8,0},{1,9},{9,1},{2,10},{10,2},{3,11},{11,3},{4,12},{12,4},... | collective-permute-start | bytes 393224 | tf_op jit(solution)/shard_map/ppermute | solution.py:53
  43.9 14.9 %copy-start = (bf16[512,544]{0,1:T(8,128)(2,1)S(1)}, bf16[512,544]{0,1:T(8,128)(2,1)}, u32[]{:S(2)}) copy-start(bf16[512,544]{0,1:T(8,128)(2,1)} %param.34) | copy-start | bytes 1671172
  43.9 14.9 %copy-start.4 = (f32[4,512]{1,0:T(4,128)S(1)}, f32[4,512]{1,0:T(4,128)}, u32[]{:S(2)}) copy-start(f32[4,512]{1,0:T(4,128)} %taps.1) | copy-start | bytes 24580
  43.9 14.9 %copy-start.5 = (f32[512]{0:T(512)S(1)}, f32[512]{0:T(512)}, u32[]{:S(2)}) copy-start(f32[512]{0:T(512)} %param.33) | copy-start | bytes 6148
  56.3 2.4 %collective-permute-start.16 = (bf16[8,32,512]{2,1,0:T(8,128)(2,1)S(1)}, bf16[8,32,512]{2,1,0:T(8,128)(2,1)S(1)}, u32[]{:S(2)}, u32[]{:S(2)}) collective-permute-start(bf16[8,32,512]{2,1,0:T(8,128)(2,1)S(1)} %all_to_all.21.lhs.own), channel_id=1, source_target_pairs={{0,8},{8,0},{1,9},{9,1},{2,10},{10,2},{3,11},{11,3},{4,12},{12,4},... | collective-permute-start | bytes 786440 | tf_op jit(solution)/shard_map/ppermute | solution.py:53
  62.2 13.9 %all-to-all-start.2 = ((bf16[8,144,128]{2,1,0:T(8,128)(2,1)}), bf16[8,144,128]{2,1,0:T(8,128)(2,1)S(1)}, u32[]{:S(2)}, u32[]{:S(2)}) async-start(bf16[8,144,128]{2,1,0:T(8,128)(2,1)} %get-tuple-element.81), calls=%async_computation.2 | async-start | bytes 589824 | tf_op jit(solution)/shard_map/all_to_all | solution.py:57
  65.8 11.8 %copy-start.1 = (bf16[512,512]{1,0:T(8,128)(2,1)S(1)}, bf16[512,512]{1,0:T(8,128)(2,1)}, u32[]{:S(2)}) copy-start(bf16[512,512]{1,0:T(8,128)(2,1)} %step_proj.1) | copy-start | bytes 1572868
  65.8 11.8 %copy-start.3 = (f32[16,512]{1,0:T(8,128)S(1)}, f32[16,512]{1,0:T(8,128)}, u32[]{:S(2)}) copy-start(f32[16,512]{1,0:T(8,128)} %decay_log.1) | copy-start | bytes 98308
  65.8 11.8 %copy-start.6 = (f32[512]{0:T(512)S(1)}, f32[512]{0:T(512)}, u32[]{:S(2)}) copy-start(f32[512]{0:T(512)} %param.36) | copy-start | bytes 6148
  65.8 11.8 %copy-start.7 = (f32[512]{0:T(512)S(1)}, f32[512]{0:T(512)}, u32[]{:S(2)}) copy-start(f32[512]{0:T(512)} %param.38) | copy-start | bytes 6148
  76.0 1.6 %collective-permute-start.17 = (bf16[8,144,128]{2,1,0:T(8,128)(2,1)S(1)}, bf16[8,144,128]{2,1,0:T(8,128)(2,1)S(1)}, u32[]{:S(2)}, u32[]{:S(2)}) collective-permute-start(bf16[8,144,128]{2,1,0:T(8,128)(2,1)S(1)} %all-to-all-done.2.own), channel_id=1, source_target_pairs={{0,8},{8,0},{1,9},{9,1},{2,10},{10,2},{3,11},{11,3},{4,12},{12,4},... | collective-permute-start | bytes 884744 | tf_op jit(solution)/shard_map/ppermute | solution.py:53
  80.2 2.7 %collective-permute-start.18 = (bf16[8,16,512]{2,1,0:T(8,128)(2,1)S(1)}, bf16[8,16,512]{2,1,0:T(8,128)(2,1)S(1)}, u32[]{:S(2)}, u32[]{:S(2)}) collective-permute-start(bf16[8,16,512]{2,1,0:T(8,128)(2,1)S(1)} %get-tuple-element.91), channel_id=1, source_target_pairs={{0,8},{8,0},{1,9},{9,1},{2,10},{10,2},{3,11},{11,3},{4,12},{12,4},... | collective-permute-start | bytes 393224 | tf_op jit(solution)/shard_map/ppermute | solution.py:53
